TPU v7x, 32 devices: a whole 2x2x4 slice. The times are simulated.
32 devices in a mesh: gy: 8 (over z, core), gz: 4 (over y, x).
Axes of the slice: x: 2, y: 2, z: 4, core: 2. Of those that a mesh axis runs over, the one named last changes fastest.
Arguments:
- field_in: bfloat16 [64, 256, 128, 256], P(None, 'gy', 'gz'), may hold values from -42 to 42
- spectral_weight: bfloat16 [32, 32, 32, 64, 128], P('gz', 'gy'), may hold values from -1.5258789e-05 to 1.5258789e-05
- point_weight: bfloat16 [64, 64], replicated, may hold values from -0.75 to 0.75
- point_bias: float32 [64], replicated, may hold values from -3 to 3
- out_weight: bfloat16 [64, 3], replicated, may hold values from -0.75 to 0.75
- out_bias: float32 [3], replicated, may hold values from -4 to 4
Outputs:
- loss_value: float32 [], replicated
- grad_spectral: float32 [32, 32, 32, 64, 128], P('gz', 'gy')
- grad_point: float32 [64, 64], replicated
- grad_point_bias: float32 [64], replicated
- grad_out: float32 [64, 3], replicated
- grad_out_bias: float32 [3], replicated
All inputs are finite; a program needn't handle non-finite values.
Results may differ from a plain program's by a relative error of at most 0.01.
Values may be sent and summed in bfloat16 or wider, within the bound.
No kernel may reach another device: no remote copies, remote signals or barrier semaphores. Data moves between devices by JAX's collectives and lax.ppermute only.
A program may use at most 320 MiB of HBM per device.

v0:
```python
import math

import jax
import jax.numpy as jnp
from jax import lax
from jax.sharding import PartitionSpec as P

NX = 256
NY = 256
NZ = 128
MX = 32
MY = 32
MZ = 32


def with_halo(block, sides, width):
    for axis, dim in sides:
        count = lax.axis_size(axis)
        forward = [(i, i + 1) for i in range(count - 1)]
        backward = [(target, source) for source, target in forward]
        low = lax.ppermute(
            lax.slice_in_dim(block, block.shape[dim] - width, None, axis=dim), axis, forward
        )
        high = lax.ppermute(lax.slice_in_dim(block, 0, width, axis=dim), axis, backward)
        block = jnp.concatenate([low, block, high], axis=dim)
    return block


def frequencies(mode_count, mode_total):
    mode_index = jnp.arange(mode_count, dtype=jnp.int32)
    return jnp.where(mode_index < mode_total // 2, mode_index, mode_index - mode_total)


def twiddle(positions, wave_numbers, length):
    product = positions[:, None] * wave_numbers[None, :] % length
    phases = product.astype(jnp.float32) * (2.0 * math.pi / length)
    return (jnp.cos(phases).astype(jnp.bfloat16), jnp.sin(phases).astype(jnp.bfloat16))


def rotate(with_cos, with_sin, forward):
    half_width = with_cos.shape[-1] // 2
    cos_real, cos_imag = (with_cos[..., :half_width], with_cos[..., half_width:])
    sin_real, sin_imag = (with_sin[..., :half_width], with_sin[..., half_width:])
    if forward:
        return jnp.concatenate([cos_real + sin_imag, cos_imag - sin_real], axis=-1)
    return jnp.concatenate([cos_real - sin_imag, cos_imag + sin_real], axis=-1)


def x_tables(length, mode_total):
    cos_part, sin_part = twiddle(
        jnp.arange(length, dtype=jnp.int32), frequencies(mode_total, mode_total), length
    )
    forward_table = jnp.stack([cos_part, -sin_part], axis=1)
    inverse_table = jnp.stack([cos_part.T, -sin_part.T], axis=0)
    return (forward_table, inverse_table)


def cell_loss(field_b, slope_x, slope_y, slope_z):
    current_x = slope_y[2] - slope_z[1]
    current_y = slope_z[0] - slope_x[2]
    current_z = slope_x[1] - slope_y[0]
    force_x = current_y * field_b[2] - current_z * field_b[1]
    force_y = current_z * field_b[0] - current_x * field_b[2]
    force_z = current_x * field_b[1] - current_y * field_b[0]
    spread = slope_x[0] + slope_y[1] + slope_z[2]
    strength = field_b[0] * field_b[0] + field_b[1] * field_b[1] + field_b[2] * field_b[2] + 1.0
    return (force_x * force_x + force_y * force_y + force_z * force_z) / strength + spread * spread


def gelu_slope(pre_act):
    normal_cdf = 0.5 * (1.0 + lax.erf(pre_act * (1.0 / math.sqrt(2.0))))
    density = jnp.exp(-0.5 * pre_act * pre_act) * (1.0 / math.sqrt(2.0 * math.pi))
    return normal_cdf + pre_act * density


def to_modes(grid_field, factor, y_cells, forward_table):
    channels, local_rows, local_depth = (
        grid_field.shape[0],
        grid_field.shape[1],
        grid_field.shape[2],
    )
    products = jnp.einsum(
        "cyzx,xpk->yzkpc", grid_field, forward_table, preferred_element_type=jnp.float32
    )
    x_modes = products.reshape(local_rows, local_depth, MX, 2 * channels).astype(jnp.bfloat16)
    y_cos, y_sin = twiddle(
        y_cells, frequencies(MY // lax.axis_size("gy") * lax.axis_size("gy"), MY), NY
    )
    with_cos = jnp.einsum("yzkc,yj->jzkc", x_modes, y_cos, preferred_element_type=jnp.float32)
    with_sin = jnp.einsum("yzkc,yj->jzkc", x_modes, y_sin, preferred_element_type=jnp.float32)
    y_modes = lax.psum_scatter(
        rotate(with_cos, with_sin, True), "gy", scatter_dimension=0, tiled=True
    ).astype(jnp.bfloat16)
    portion = lax.all_to_all(y_modes, "gz", split_axis=2, concat_axis=1, tiled=True)
    all_depth = jnp.arange(portion.shape[1], dtype=jnp.int32)
    z_cos, z_sin = twiddle(all_depth, frequencies(MZ, MZ), portion.shape[1])
    with_cos = jnp.einsum("bzkc,zj->jbkc", portion, z_cos, preferred_element_type=jnp.float32)
    with_sin = jnp.einsum("bzkc,zj->jbkc", portion, z_sin, preferred_element_type=jnp.float32)
    rotated = (rotate(with_cos, with_sin, True) * factor).astype(jnp.bfloat16)
    return lax.all_to_all(rotated, "gz", split_axis=0, concat_axis=2, tiled=True)


def from_modes(modes_out, y_cells):
    portion = lax.all_to_all(modes_out, "gz", split_axis=2, concat_axis=0, tiled=True)
    all_depth = jnp.arange(NZ, dtype=jnp.int32)
    z_cos, z_sin = twiddle(all_depth, frequencies(portion.shape[0], MZ), NZ)
    with_cos = jnp.einsum("jbkc,zj->bzkc", portion, z_cos, preferred_element_type=jnp.float32)
    with_sin = jnp.einsum("jbkc,zj->bzkc", portion, z_sin, preferred_element_type=jnp.float32)
    rotated = rotate(with_cos, with_sin, False).astype(jnp.bfloat16)
    z_back = lax.all_to_all(rotated, "gz", split_axis=1, concat_axis=2, tiled=True)
    portion = lax.all_gather(z_back, "gy", axis=0, tiled=True)
    y_cos, y_sin = twiddle(y_cells, frequencies(portion.shape[0], MY), NY)
    with_cos = jnp.einsum("jzkc,yj->yzkc", portion, y_cos, preferred_element_type=jnp.float32)
    with_sin = jnp.einsum("jzkc,yj->yzkc", portion, y_sin, preferred_element_type=jnp.float32)
    return rotate(with_cos, with_sin, False).astype(jnp.bfloat16)


def mix_modes(modes_in, spectral_weight):
    channels = spectral_weight.shape[-2]
    with_real = jnp.einsum(
        "abki,abkio->abko",
        modes_in[..., :channels],
        spectral_weight,
        preferred_element_type=jnp.float32,
    )
    with_imag = jnp.einsum(
        "abki,abkio->abko",
        modes_in[..., channels:],
        spectral_weight,
        preferred_element_type=jnp.float32,
    )
    return jnp.concatenate(
        [
            with_real[..., :channels] - with_imag[..., channels:],
            with_real[..., channels:] + with_imag[..., :channels],
        ],
        axis=-1,
    ).astype(jnp.bfloat16)


def weight_grad(modes_in, grad_modes):
    channels = modes_in.shape[-1] // 2
    with_real = jnp.einsum(
        "abki,abko->abkio", modes_in[..., :channels], grad_modes, preferred_element_type=jnp.float32
    )
    with_imag = jnp.einsum(
        "abki,abko->abkio", modes_in[..., channels:], grad_modes, preferred_element_type=jnp.float32
    )
    return jnp.concatenate(
        [
            with_real[..., :channels] + with_imag[..., channels:],
            with_real[..., channels:] - with_imag[..., :channels],
        ],
        axis=-1,
    )


def on_device(field_in, spectral_weight, point_weight, point_bias, out_weight, out_bias):
    channels, local_rows, local_depth, x_count = field_in.shape
    y_cells = lax.axis_index("gy") * local_rows + jnp.arange(local_rows, dtype=jnp.int32)
    forward_table, inverse_table = x_tables(x_count, MX)
    modes_in = to_modes(field_in, math.sqrt(MX * MY * MZ / (NX * NY * NZ)), y_cells, forward_table)
    modes_out = mix_modes(modes_in, spectral_weight)
    y_back = from_modes(modes_out, y_cells)
    spectral = jnp.einsum(
        "yzkpc,pkx->cyzx",
        y_back.reshape(local_rows, local_depth, MX, 2, channels),
        inverse_table,
        preferred_element_type=jnp.float32,
    )
    pointwise = jnp.einsum(
        "cyzx,co->oyzx", field_in, point_weight, preferred_element_type=jnp.float32
    )
    pre_act = spectral + pointwise + point_bias[:, None, None, None]
    hidden = jax.nn.gelu(pre_act, approximate=False).astype(jnp.bfloat16)
    b_field = (
        jnp.einsum("cyzx,cb->byzx", hidden, out_weight, preferred_element_type=jnp.float32)
        + out_bias[:, None, None, None]
    )
    padded = with_halo(b_field, (("gy", 1), ("gz", 2)), 2)
    widened = padded[:, 1:-1, 1:-1]
    x_padded = jnp.pad(widened, ((0, 0), (0, 0), (0, 0), (1, 1)))
    slope_x = (x_padded[..., 2:] - x_padded[..., :-2]) * 0.5
    slope_y = (padded[:, 2:, 1:-1] - padded[:, :-2, 1:-1]) * 0.5
    slope_z = (padded[:, 1:-1, 2:] - padded[:, 1:-1, :-2]) * 0.5
    cell_terms, pullback = jax.vjp(cell_loss, widened, slope_x, slope_y, slope_z)
    y_wide = lax.axis_index("gy") * local_rows - 1 + jnp.arange(local_rows + 2, dtype=jnp.int32)
    z_wide = lax.axis_index("gz") * local_depth - 1 + jnp.arange(local_depth + 2, dtype=jnp.int32)
    inside = ((y_wide >= 0) & (y_wide < NY))[:, None] & ((z_wide >= 0) & (z_wide < NZ))[None, :]
    weight_map = jnp.broadcast_to(
        jnp.where(inside, 1.0, 0.0)[:, :, None] / (NX * NY * NZ), cell_terms.shape
    ).astype(jnp.float32)
    grad_wide, grad_x, grad_y, grad_z = pullback(weight_map)
    gx_inner = jnp.pad(grad_x[:, 1:-1, 1:-1], ((0, 0), (0, 0), (0, 0), (1, 1)))
    grad_b = grad_wide[:, 1:-1, 1:-1] + (gx_inner[..., :-2] - gx_inner[..., 2:]) * 0.5
    grad_b = grad_b + (grad_y[:, :-2, 1:-1] - grad_y[:, 2:, 1:-1]) * 0.5
    grad_b = grad_b + (grad_z[:, 1:-1, :-2] - grad_z[:, 1:-1, 2:]) * 0.5
    loss_local = jnp.sum(cell_terms[1:-1, 1:-1])
    weights_f = out_weight.astype(jnp.float32)
    grad_hidden = jnp.zeros_like(pre_act)
    for component in range(3):
        grad_hidden = (
            grad_hidden + weights_f[:, component][:, None, None, None] * grad_b[component][None]
        )
    grad_pre = (grad_hidden * gelu_slope(pre_act)).astype(jnp.bfloat16)
    out_part = jnp.einsum(
        "cyzx,byzx->cb",
        hidden,
        grad_b,
        preferred_element_type=jnp.float32,
        precision=lax.Precision.HIGHEST,
    )
    out_bias_part = jnp.sum(grad_b, axis=(1, 2, 3))
    point_part = jnp.einsum("iyzx,oyzx->io", field_in, grad_pre, preferred_element_type=jnp.float32)
    point_bias_part = jnp.sum(grad_pre.astype(jnp.float32), axis=(1, 2, 3))
    totals = lax.psum(
        (loss_local, point_part, point_bias_part, out_part, out_bias_part), ("gy", "gz")
    )
    grad_modes = to_modes(grad_pre, 1.0, y_cells, forward_table)
    grad_spectral = weight_grad(modes_in, grad_modes)
    return (totals[0] / (NX * NY * NZ), grad_spectral, totals[1], totals[2], totals[3], totals[4])


def solution(mesh):
    return jax.shard_map(
        on_device,
        mesh=mesh,
        in_specs=(P(None, "gy", "gz", None), P("gz", "gy", None, None, None), P(), P(), P(), P()),
        out_specs=(P(), P("gz", "gy", None, None, None), P(), P(), P(), P()),
        check_vma=False,
    )
```

profile of v0, /device:TPU:0, one launch (start us, length us, event | category | flops | bytes accessed | tf_op | source)
XLA Modules:
  0.0 1617.5 jit_solution(10281719878868618618)
XLA Ops:
  7.7 55.7 %convert_bitcast_fusion.1 = bf16[32,32,32,2,64]{4,2,1,0,3:T(8,128)(2,1)} fusion(bf16[64,32,32,256]{3,2,1,0:T(8,128)(2,1)} %param.6, bf16[256,1,32]{0,2,1:T(8,128)(2,1)S(1)} %fusion.89, bf16[256,1,32]{0,2,1:T(8,128)(2,1)S(1)} %cosine_convert_fusion), kind=kOutput, calls=%fused_computation.57 | convolution fusion | flops 2151743488 | bytes 41975808 | tf_op jit(solution)/shard_map/cyzx,xpk->yzkpc/dot_general | solution.py:82
  63.5 30.9 %copy.124 = bf16[32,32,32,2,64]{4,3,0,2,1:T(2,128)(2,1)} copy(bf16[32,32,32,2,64]{4,2,1,0,3:T(8,128)(2,1)} %convert_bitcast_fusion.1) | data formatting | bytes 16777216 | tf_op jit(solution)/shard_map/convert_element_type | solution.py:85
  94.4 26.9 %reshape.348 = bf16[32,32,32,128]{3,0,2,1:T(8,128)(2,1)} reshape(bf16[32,32,32,2,64]{4,3,0,2,1:T(2,128)(2,1)} %copy.124) | data formatting | bytes 16777216 | tf_op jit(solution)/shard_map/convert_element_type | solution.py:85
  121.3 12.2 fusion.111
  133.5 8.3 fusion.115
  141.7 37.9 %slice_add_fusion.3 = (f32[32,32,32,64]{3,0,2,1:T(8,128)}, f32[32,32,32,64]{3,0,2,1:T(8,128)}) fusion(f32[32,32,32,128]{3,0,2,1:T(8,128)} %fusion.111, f32[32,32,32,128]{3,0,2,1:T(8,128)} %fusion.115), kind=kLoop, calls=%fused_computation.49 | loop fusion | flops 4194304 | bytes 50331648 | tf_op jit(solution)/shard_map/add | solution.py:45
  179.7 12.0 pad_maximum_fusion.1
  191.7 19.5 %copy.76 = f32[32,32,32,128]{3,2,1,0:T(8,128)} copy(f32[32,32,32,128]{3,0,2,1:T(8,128)S(1)} %pad_maximum_fusion.1) | data formatting | bytes 33554432 | tf_op jit(solution)/shard_map/concatenate | solution.py:45
  211.3 171.0 %reduce-scatter.3.cloned.1.call-done = f32[4,32,32,128]{3,2,1,0:T(8,128)} async-done(((f32[32,32,32,128]{3,2,1,0:T(8,128)}), f32[4,32,32,128]{3,2,1,0:T(8,128)}) %reduce-scatter.3.cloned.1.call-update) | async-done | bytes 2097168 | tf_op jit(solution)/shard_map/reduce_scatter | solution.py:91
  382.4 1.8 convert_element_type.183
  385.0 15.7 all_to_all.99
  402.4 8.4 all_to_all.100
  412.1 8.2 fusion.60
  420.7 4.6 fusion.62
  426.6 8.1 all_to_all.101
  437.5 12.4 all_to_all.102
  452.7 44.4 %fusion.22 = f32[64,32,32,256]{3,0,2,1:T(8,128)} fusion(bf16[64,32,32,256]{3,2,1,0:T(8,128)(2,1)} %param.6, bf16[64,64]{1,0:T(8,128)(2,1)S(1)} %copy-done), kind=kOutput, calls=%fused_computation.39 | convolution fusion | flops 2147483648 | bytes 100671488 | tf_op jit(solution)/shard_map/cyzx,co->oyzx/dot_general | solution.py:171
  497.1 36.8 %all-gather.2.cloned.1.call-done = bf16[32,32,32,128]{3,2,1,0:T(8,128)(2,1)} async-done(((bf16[4,32,32,128]{3,2,1,0:T(8,128)(2,1)}), bf16[32,32,32,128]{3,2,1,0:T(8,128)(2,1)}) %all-gather.2.cloned.1.call-update) | async-done | bytes 8388624 | tf_op jit(solution)/shard_map/all_gather | solution.py:111
  533.9 14.9 fusion.34
  548.8 8.8 fusion.36
  557.6 29.8 %fusion.32 = (bf16[32,32,32,1,64]{4,0,2,1,3:T(8,128)(2,1)S(1)}, bf16[32,32,32,1,64]{4,0,2,1,3:T(8,128)(2,1)}) fusion(f32[32,32,32,128]{3,0,2,1:T(8,128)} %fusion.34, f32[32,32,32,128]{3,0,2,1:T(8,128)} %fusion.36), kind=kLoop, calls=%fused_computation.58 | loop fusion | flops 8388608 | bytes 41943040 | tf_op jit(solution)/shard_map/concatenate | solution.py:46
  587.3 11.7 pad_maximum_fusion.2
  599.0 64.7 %convert_reduce_fusion = (u32[64,32,256]{2,0,1:T(8,128)S(1)}, f32[64,32,32,256]{3,0,2,1:T(8,128)}) fusion(f32[64]{0:T(128)S(1)} %copy-done.30, f32[64,32,32,256]{3,0,2,1:T(8,128)} %fusion.22, bf16[32,32,32,2,64]{4,0,2,1,3:T(8,128)(2,1)} %pad_maximum_fusion.2, bf16[1,32,256]{2,1,0:T(8,128)(2,1)S(1)} %fusion.88, bf16[1,32,256]{2,1,0:T(8,128)(2,1)S(1)} %cosine_convert_fusion.1), kind=kOutput, calls=%fused_computation.12 | convolution fusion | flops 2281242624 | bytes 144736512 | tf_op jit(solution)/shard_map/yzkpc,pkx->cyzx/dot_general | solution.py:165
  663.7 151.9 %fusion.2 = bf16[64,32,32,256]{3,0,2,1:T(8,128)(2,1)} fusion(f32[64,32,32,256]{3,0,2,1:T(8,128)} %get-tuple-element.129, u32[64,32,256]{2,0,1:T(8,128)S(1)} %get-tuple-element.128), kind=kLoop, calls=%fused_computation.4 | loop fusion | flops 1124073472 | bytes 102760448 | tf_op jit(solution)/shard_map/convert_element_type | solution.py:175
  815.7 12.8 add_bitcast_fusion
  828.7 2.2 collective-permute-start
  832.5 1.8 collective-permute-done.1
  834.4 3.4 collective-permute-start.3
  839.2 2.9 collective-permute-done.3
  842.1 8.0 collective-permute-done.2
  850.1 4.2 pad_maximum_fusion.4
  854.4 4.8 fusion.176
  859.2 11.0 fusion.39
  870.2 10.1 fusion.42
  880.2 25.0 %add_multiply_fusion = (f32[1,34,34,256]{3,0,2,1:T(1,128)S(1)}, f32[1,34,34,256]{3,0,2,1:T(1,128)}, f32[1,34,34,256]{3,0,2,1:T(1,128)}, f32[1,34,34,256]{3,0,2,1...) fusion(f32[34,34]{1,0:T(8,128)S(1)} %select_multiply_fusion, ...), kind=kLoop, calls=%fused_computation.113 | loop fusion | flops 9765888 | bytes 28414480 | tf_op jit(solution)/shard_map/transpose(jvp())/add_any | solution.py:67
  905.3 7.8 negate_multiply_fusion.3
  913.2 5.9 negate_multiply_fusion.1
  919.0 11.0 slice_multiply_fusion.1
  930.0 3.4 add_add_fusion
  933.4 4.8 pad_add_fusion.2
  938.3 5.6 pad_add_fusion.1
  943.9 15.9 fusion.170
  959.8 2.0 copy-done.5
  961.8 3.2 fusion.177
  965.3 46.0 %convert_reduce_fusion.1 = (f32[64]{0:T(128)S(1)}, bf16[64,32,32,256]{3,0,2,1:T(8,128)(2,1)}) fusion(f32[64,32,32,256]{3,0,2,1:T(8,128)} %get-tuple-element.129, f32[32,32,256]{2,1,0:T(8,128)S(1)} %bitcast.186, f32[64]{0:T(128)S(1)} %get-tuple-element.126, f32[32,32,256]{2,1,0:T(8,128)S(1)} %bitcast.187, f32[64]{0:T(128)S(1)} %get-tuple-element.127, ...), kind=kLoop, calls=%fused_computation.15 | loop fusion | flops 285212608 | bytes 103810048 | tf_op jit(solution)/shard_map/reduce_sum | solution.py:215
  1011.4 22.9 %convert_bitcast_fusion = bf16[32,32,32,2,64]{4,2,1,0,3:T(8,128)(2,1)} fusion(bf16[64,32,32,256]{3,0,2,1:T(8,128)(2,1)} %get-tuple-element.38, bf16[256,1,32]{0,2,1:T(8,128)(2,1)S(1)} %copy-done.22, bf16[256,1,32]{0,2,1:T(8,128)(2,1)S(1)} %copy-done.24), kind=kOutput, calls=%fused_computation.56 | convolution fusion | flops 2151743488 | bytes 41975808 | tf_op jit(solution)/shard_map/cyzx,xpk->yzkpc/dot_general | solution.py:82
  1034.3 30.9 %copy.126 = bf16[32,32,32,2,64]{4,3,0,2,1:T(2,128)(2,1)} copy(bf16[32,32,32,2,64]{4,2,1,0,3:T(8,128)(2,1)} %convert_bitcast_fusion) | data formatting | bytes 16777216 | tf_op jit(solution)/shard_map/convert_element_type | solution.py:85
  1065.2 27.1 %reshape.349 = bf16[32,32,32,128]{3,0,2,1:T(8,128)(2,1)} reshape(bf16[32,32,32,2,64]{4,3,0,2,1:T(2,128)(2,1)} %copy.126) | data formatting | bytes 16777216 | tf_op jit(solution)/shard_map/convert_element_type | solution.py:85
  1092.4 11.8 fusion.109
  1104.2 8.2 fusion.113
  1112.4 38.2 %slice_add_fusion.1 = (f32[32,32,32,64]{3,0,2,1:T(8,128)}, f32[32,32,32,64]{3,0,2,1:T(8,128)}) fusion(f32[32,32,32,128]{3,0,2,1:T(8,128)} %fusion.109, f32[32,32,32,128]{3,0,2,1:T(8,128)} %fusion.113), kind=kLoop, calls=%fused_computation.43 | loop fusion | flops 4194304 | bytes 50331648 | tf_op jit(solution)/shard_map/add | solution.py:45
  1150.7 12.0 pad_maximum_fusion.3
  1162.7 19.3 %copy.96 = f32[32,32,32,128]{3,2,1,0:T(8,128)} copy(f32[32,32,32,128]{3,0,2,1:T(8,128)S(1)} %pad_maximum_fusion.3) | data formatting | bytes 33554432 | tf_op jit(solution)/shard_map/concatenate | solution.py:45
  1182.0 172.9 %reduce-scatter.5.cloned.1.call-done = f32[4,32,32,128]{3,2,1,0:T(8,128)} async-done(((f32[32,32,32,128]{3,2,1,0:T(8,128)}), f32[4,32,32,128]{3,2,1,0:T(8,128)}) %reduce-scatter.5.cloned.1.call-update) | async-done | bytes 2097168 | tf_op jit(solution)/shard_map/reduce_scatter | solution.py:91
  1354.9 1.8 convert_element_type.192
  1356.7 1.8 copy.97
  1358.6 4.1 all-to-all-start.4
  1362.6 45.6 %fusion.50 = f32[64,64]{0,1:T(8,128)S(1)} fusion(bf16[64,32,32,256]{3,0,2,1:T(8,128)(2,1)} %get-tuple-element.38, bf16[64,32,32,256]{3,2,1,0:T(8,128)(2,1)} %param.6), kind=kOutput, calls=%fused_computation.125 | convolution fusion | flops 2147483648 | bytes 67125248 | tf_op jit(solution)/shard_map/iyzx,oyzx->io/dot_general | solution.py:214
  1410.6 4.4 all-to-all-start.5
  1415.0 30.1 %convolution_bitcast_fusion.2 = f32[64,3]{0,1:T(4,128)S(1)} fusion(bf16[64,32,32,256]{3,0,2,1:T(8,128)(2,1)} %fusion.2, f32[3,32,32,256]{3,0,2,1:T(4,128)} %copy-done.5), kind=kOutput, calls=%fused_computation.126 | convolution fusion | flops 603979776 | bytes 36700928 | tf_op jit(solution)/shard_map/cyzx,byzx->cb/dot_general | solution.py:206
  1446.2 38.8 %all-reduce.20 = (f32[]{:T(128)}, f32[64,64]{0,1:T(8,128)S(1)}, f32[64]{0:T(128)}, f32[64,3]{0,1:T(4,128)}, f32[3]{0:T(128)}) all-reduce(f32[]{:T(128)} %slice_reduce_fusion, f32[64,64]{0,1:T(8,128)S(1)} %fusion.50, f32[64]{0:T(128)S(1)} %get-tuple-element.37, ...), channel_id=1, replica_groups=mesh['gy'=8,'gz'=4] {'gy','gz'}, use_global_device_ids=true, to_apply=%region_2.3 | all-reduce | flops 4356 | bytes 34848 | tf_op jit(solution)/shard_map/psum | solution.py:216
  1486.4 21.7 %broadcast_multiply_fusion.1 = (f32[8,4,32,64,128]{4,3,2,1,0:T(8,128)}, f32[8,4,32,64,128]{4,3,2,1,0:T(8,128)}) fusion(f32[8,4,32,128]{3,2,1,0:T(8,128)S(1)} %copy_bitcast_fusion.7, f32[8,4,32,64]{3,2,1,0:T(8,128)S(1)} %copy-done.19, f32[8,4,32,64]{3,2,1,0:T(8,128)S(1)} %copy-done.20), kind=kLoop, calls=%fused_computation.55 | loop fusion | flops 16777216 | bytes 68157440 | tf_op jit(solution)/shard_map/abki,abko->abkio/dot_general | solution.py:143
  1508.1 68.6 %slice_add_fusion = (f32[8,4,32,64,64]{4,3,2,1,0:T(8,128)}, f32[8,4,32,64,64]{4,3,2,1,0:T(8,128)}) fusion(f32[8,4,32,64,128]{4,3,2,1,0:T(8,128)} %get-tuple-element.120, f32[8,4,32,64,128]{4,3,2,1,0:T(8,128)} %get-tuple-element.119), kind=kLoop, calls=%fused_computation.31 | loop fusion | flops 8388608 | bytes 100663296 | tf_op jit(solution)/shard_map/add | solution.py:151
  1576.8 32.9 %pad_maximum_fusion = f32[8,4,32,64,128]{4,3,2,1,0:T(8,128)} fusion(f32[8,4,32,64,64]{4,3,2,1,0:T(8,128)} %get-tuple-element.65, f32[8,4,32,64,64]{4,3,2,1,0:T(8,128)} %get-tuple-element.64), kind=kLoop, calls=%fused_computation.32 | loop fusion | flops 8388608 | bytes 67108864 | tf_op jit(solution)/shard_map/concatenate | solution.py:149
  (137 shorter events, 19.2 us)
Async XLA Ops:
  7.2 445.5 %copy-start = (bf16[64,64]{1,0:T(8,128)(2,1)S(1)}, bf16[64,64]{1,0:T(8,128)(2,1)}, u32[]{:S(2)}) copy-start(bf16[64,64]{1,0:T(8,128)(2,1)} %param.8) | copy-start | bytes 24580
  7.2 375.2 %reduce-scatter.3.cloned.1.call-start = ((), (), s32[]{:S(2)}) async-start(), calls=%async_computation.8 | async-start | bytes 18874368 | tf_op jit(solution)/shard_map/reduce_scatter | solution.py:91
  7.2 541.5 %copy-start.25 = (s32[32]{0:T(128)}, s32[32]{0:T(128)S(1)}, u32[]{:S(2)}) copy-start(s32[32]{0:T(128)S(1)} %get-tuple-element.132) | copy-start | bytes 388
  7.3 541.5 %copy-start.27 = (s32[32]{0:T(128)}, s32[32]{0:T(128)S(1)}, u32[]{:S(2)}) copy-start(s32[32]{0:T(128)S(1)} %get-tuple-element.133) | copy-start | bytes 388
  7.5 56.0 %copy-start.21 = (bf16[256,1,32]{0,2,1:T(8,128)(2,1)}, bf16[256,1,32]{0,2,1:T(8,128)(2,1)S(1)}, u32[]{:S(2)}) copy-start(bf16[256,1,32]{0,2,1:T(8,128)(2,1)S(1)} %fusion.89) | copy-start | bytes 49156
  7.7 55.8 %copy-start.23 = (bf16[256,1,32]{0,2,1:T(8,128)(2,1)}, bf16[256,1,32]{0,2,1:T(8,128)(2,1)S(1)}, u32[]{:S(2)}) copy-start(bf16[256,1,32]{0,2,1:T(8,128)(2,1)S(1)} %cosine_convert_fusion) | copy-start | bytes 49156
  121.3 12.2 copy-start.2
  211.3 322.6 %all-gather.2.cloned.1.call-start = ((), (), s32[]{:S(2)}) async-start(), calls=%async_computation.9 | async-start | bytes 9437184 | tf_op jit(solution)/shard_map/all_gather | solution.py:111
  385.0 35.6 %slice-start = ((s8[16777216]{0:T(1024)(128)(4,1)}), s8[4194304]{0:T(1024)(128)(4,1)S(1)}, s32[]{:S(2)}) async-start(s8[16777216]{0:T(1024)(128)(4,1)} %bitcast.197), calls=%async_computation.11 | async-start | bytes 8388608
  401.8 18.9 %slice-start.1 = ((s8[16777216]{0:T(1024)(128)(4,1)}), s8[4194304]{0:T(1024)(128)(4,1)S(1)}, s32[]{:S(2)}) async-start(s8[16777216]{0:T(1024)(128)(4,1)} %bitcast.197), calls=%async_computation.12 | async-start | bytes 8388608
  412.1 8.6 slice-start.2
  412.1 8.6 slice-start.3
  435.4 15.7 copy-start.31
  451.1 903.8 %reduce-scatter.5.cloned.1.call-start = ((), (), s32[]{:S(2)}) async-start(), calls=%async_computation.10 | async-start | bytes 18874368 | tf_op jit(solution)/shard_map/reduce_scatter | solution.py:91
  533.9 14.9 copy-start.6
  587.3 11.7 copy-start.30
  663.7 152.0 %copy-start.32 = (bf16[64,3]{0,1:T(4,128)(2,1)S(1)}, bf16[64,3]{0,1:T(4,128)(2,1)}, u32[]{:S(2)}) copy-start(bf16[64,3]{0,1:T(4,128)(2,1)} %param.10) | copy-start | bytes 1156
  663.7 152.0 %copy-start.33 = (f32[3]{0:T(128)S(1)}, f32[3]{0:T(128)}, u32[]{:S(2)}) copy-start(f32[3]{0:T(128)} %param.11) | copy-start | bytes 40
  815.7 16.7 %copy-start.35 = (pred[34]{0:T(512)(128)(4,1)S(1)}, pred[34]{0:T(512)(128)(4,1)}, u32[]{:S(2)}) copy-start(pred[34]{0:T(512)(128)(4,1)} %get-tuple-element.130) | copy-start | bytes 106
  815.7 16.7 %copy-start.36 = (pred[34]{0:T(512)(128)(4,1)S(1)}, pred[34]{0:T(512)(128)(4,1)}, u32[]{:S(2)}) copy-start(pred[34]{0:T(512)(128)(4,1)} %get-tuple-element.131) | copy-start | bytes 106
  815.7 23.5 %copy-start.29 = (f32[64,3]{0,1:T(4,128)S(1)}, f32[64,3]{0,1:T(4,128)}, u32[]{:S(2)}) copy-start(f32[64,3]{0,1:T(4,128)} %convert_element_type.187) | copy-start | bytes 2308
  828.6 13.5 copy-start.4
  828.7 3.8 collective-permute-start
  830.9 3.4 collective-permute-start.1
  834.4 7.6 collective-permute-start.3
  837.9 12.2 collective-permute-start.2
  905.3 7.9 copy-start.7
  905.3 7.9 copy-start.16
  905.3 7.9 copy-start.17
  905.3 13.7 copy-start.8
  905.3 13.7 copy-start.18
  919.0 11.0 copy-start.15
  938.3 5.6 copy-start.9
  938.3 5.6 copy-start.10
  938.3 5.6 copy-start.12
  938.3 5.6 copy-start.13
  938.3 5.6 copy-start.14
  959.8 2.0 copy-start.5
  965.3 46.0 %copy-start.22 = (bf16[256,1,32]{0,2,1:T(8,128)(2,1)S(1)}, bf16[256,1,32]{0,2,1:T(8,128)(2,1)}, u32[]{:S(2)}) copy-start(bf16[256,1,32]{0,2,1:T(8,128)(2,1)} %copy-done.21) | copy-start | bytes 49156
  965.3 46.0 %copy-start.24 = (bf16[256,1,32]{0,2,1:T(8,128)(2,1)S(1)}, bf16[256,1,32]{0,2,1:T(8,128)(2,1)}, u32[]{:S(2)}) copy-start(bf16[256,1,32]{0,2,1:T(8,128)(2,1)} %copy-done.23) | copy-start | bytes 49156
  1065.2 27.2 %copy-start.26 = (s32[32]{0:T(128)S(1)}, s32[32]{0:T(128)}, u32[]{:S(2)}) copy-start(s32[32]{0:T(128)} %copy-done.25) | copy-start | bytes 388
  1065.2 27.2 %copy-start.28 = (s32[32]{0:T(128)S(1)}, s32[32]{0:T(128)}, u32[]{:S(2)}) copy-start(s32[32]{0:T(128)} %copy-done.27) | copy-start | bytes 388
  1092.4 11.8 copy-start.3
  1358.6 49.7 %all-to-all-start.4 = ((bf16[4,32,32,128]{3,0,1,2:T(4,128)(2,1)}), bf16[4,32,32,128]{3,0,1,2:T(4,128)(2,1)S(1)}, u32[]{:S(2)}, u32[]{:S(2)}) async-start(bf16[4,32,32,128]{3,0,1,2:T(4,128)(2,1)} %copy.97), calls=%async_computation.6 | async-start | bytes 2097152 | tf_op jit(solution)/shard_map/all_to_all | solution.py:94
  1410.6 75.7 %all-to-all-start.5 = ((bf16[32,4,8,128]{3,2,1,0:T(8,128)(2,1)}), bf16[32,4,8,128]{3,2,1,0:T(8,128)(2,1)S(1)}, u32[]{:S(2)}, u32[]{:S(2)}) async-start(bf16[32,4,8,128]{3,2,1,0:T(8,128)(2,1)} %copy.99), calls=%async_computation.7 | async-start | bytes 524288 | tf_op jit(solution)/shard_map/all_to_all | solution.py:100
  1415.0 30.1 %copy-start.11 = (f32[1,34,34,256]{3,0,2,1:T(1,128)S(1)}, f32[1,34,34,256]{3,0,2,1:T(1,128)}, u32[]{:S(2)}) copy-start(f32[1,34,34,256]{3,0,2,1:T(1,128)} %get-tuple-element.112) | copy-start | bytes 3551236
  1415.0 31.2 %copy-start.34 = (f32[3]{0:T(128)S(1)}, f32[3]{0:T(128)}, u32[]{:S(2)}) copy-start(f32[3]{0:T(128)} %get-tuple-element.35) | copy-start | bytes 40
  1415.0 71.4 %copy-start.19 = (f32[8,4,32,64]{3,2,1,0:T(8,128)S(1)}, f32[8,4,32,64]{3,2,1,0:T(8,128)}, u32[]{:S(2)}) copy-start(f32[8,4,32,64]{3,2,1,0:T(8,128)} %get-tuple-element.121) | copy-start | bytes 786436
  1415.0 71.4 %copy-start.20 = (f32[8,4,32,64]{3,2,1,0:T(8,128)S(1)}, f32[8,4,32,64]{3,2,1,0:T(8,128)}, u32[]{:S(2)}) copy-start(f32[8,4,32,64]{3,2,1,0:T(8,128)} %get-tuple-element.122) | copy-start | bytes 786436
  1576.8 32.9 %copy-start.1 = (bf16[64,64]{1,0:T(8,128)(2,1)S(1)}, bf16[64,64]{1,0:T(8,128)(2,1)}, u32[]{:S(2)}) copy-start(bf16[64,64]{1,0:T(8,128)(2,1)} %param.8) | copy-start | bytes 24580
Sparse Core Ops, SparseCore 0:
  211.4 170.9 reduce-scatter.2
  451.2 82.6 all-gather.1
  1182.1 172.7 reduce-scatter.4
where the time goes:
time: 1630 us; the launch traced here: 1620 us
  other arithmetic  583 us (36%)
  waiting for transfers between devices  394 us (24%)
  matrix products  356 us (22%)
  local copies, waits for them, and re-layouts  168 us (10%)
  blocking collectives  83.5 us (5%)
  starting transfers between devices  16.9 us (1%)
  between operations  16.6 us (1%)
    reduce_scatter x2, waiting for transfers between devices, to_modes(): lax.psum_scatter(rotate(with_cos, with_sin, True), 'gy', scatter_dimensio...  344 us
    convert_element_type x1, other arithmetic, on_device(): hidden = jax.nn.gelu(pre_act, approximate=False).astype(jnp.bfloat16)  152 us
    convert_element_type x4, local copies, waits for them, and re-layouts, to_modes(): products.reshape(local_rows, local_depth, MX, 2 * channels)  116 us
    dot_general x2, matrix products, to_modes(): jnp.einsum('cyzx,xpk->yzkpc', grid_field, forward_table, preferred_elemen...  78.6 us
    add x3, other arithmetic, rotate(): return jnp.concatenate([cos_real + sin_imag, cos_imag - sin_real], axis=-1)  76.5 us
    add x1, other arithmetic, weight_grad(): with_real[..., :channels] + with_imag[..., channels:]  68.6 us
    dot_general x1, matrix products, on_device(): jnp.einsum('yzkpc,pkx->cyzx', y_back.reshape(local_rows, local_depth, MX,...  64.7 us
    reduce_sum x1, other arithmetic, on_device(): point_bias_part = jnp.sum(grad_pre.astype(jnp.float32), axis=(1, 2, 3))  46 us
  transfers between devices with their start and end apart: 9, of which 6 were waited for; matrix products, arithmetic and copies ran while one was open for 8% of the time, Pallas kernels for 0%

commit v1 on v0

v1 whole, which is shorter than its diff:
```python
import functools
import math

import jax
import jax.numpy as jnp
from jax import lax
from jax.experimental import pallas as pl
from jax.experimental.pallas import tpu as pltpu
from jax.sharding import PartitionSpec as P

F32 = jnp.float32
BF16 = jnp.bfloat16
CORES = 2
LANES = 128
VMEM_LIMIT = 56 * 1024 * 1024
PARTS = 4


def params():
    return pltpu.CompilerParams(
        vmem_limit_bytes=VMEM_LIMIT, dimension_semantics=("arbitrary",)
    )


def whole(shape):
    return pl.BlockSpec(shape, lambda i: (0,) * len(shape), pipeline_mode=pl.Buffered(1))


ANY = pl.BlockSpec(memory_space=pl.ANY)


def cost(flops, moved):
    return pl.CostEstimate(flops=flops, bytes_accessed=moved, transcendentals=0)


def dot(a, b):
    return jnp.dot(a, b, preferred_element_type=F32)


def frequencies(mode_index, mode_total):
    return jnp.where(mode_index < mode_total // 2, mode_index, mode_index - mode_total)


def twiddle(product, length):
    phases = (product % length).astype(F32) * (2.0 * math.pi / length)
    return jnp.cos(phases).astype(BF16).astype(F32), jnp.sin(phases).astype(BF16).astype(F32)


def with_halo(block, sides, width):
    for axis, dim in sides:
        count = lax.axis_size(axis)
        forward = [(i, i + 1) for i in range(count - 1)]
        backward = [(target, source) for source, target in forward]
        low = lax.ppermute(
            lax.slice_in_dim(block, block.shape[dim] - width, None, axis=dim), axis, forward
        )
        high = lax.ppermute(lax.slice_in_dim(block, 0, width, axis=dim), axis, backward)
        block = jnp.concatenate([low, block, high], axis=dim)
    return block


class Layout:
    def __init__(self, field_in, spectral_weight):
        self.channels, self.rows, self.depth, self.width = field_in.shape
        self.kz, self.ky, self.mx = spectral_weight.shape[:3]
        self.n_gy, self.n_gz = lax.axis_size("gy"), lax.axis_size("gz")
        self.chips = self.n_gy // CORES
        self.ny, self.nz = self.rows * self.n_gy, self.depth * self.n_gz
        self.my, self.mz = self.ky * self.n_gy, self.kz * self.n_gz
        self.cells = self.rows * self.depth
        self.modes = self.my * self.mz
        self.pack = LANES // self.mx
        self.groups = self.channels // self.pack
        self.own = self.ky * self.kz
        self.band = min(LANES // self.depth, self.rows)
        self.blocks = self.rows // self.band
        self.step = min(LANES // self.rows, self.kz)
        self.tile = min(16, self.depth)
        self.gy, self.gz = lax.axis_index("gy"), lax.axis_index("gz")
        self.y0 = self.gy * self.rows
        self.z0 = self.gz * self.depth

    def mode_numbers(self):
        core, chip = self.gy % CORES, self.gy // CORES
        h = jnp.arange(CORES, dtype=jnp.int32) ^ core
        f = jnp.arange(self.chips, dtype=jnp.int32) ^ chip
        e = jnp.arange(self.n_gz, dtype=jnp.int32) ^ self.gz
        ky = (f[None, :, None] * CORES + h[:, None, None]) * self.ky
        ky = ky + jnp.arange(self.ky, dtype=jnp.int32)
        kz = e[:, None] * self.kz + jnp.arange(self.kz, dtype=jnp.int32)
        return frequencies(ky, self.my), frequencies(kz, self.mz)

    def grid_tables(self):
        ky, kz = self.mode_numbers()
        ky, kz = ky.reshape(self.my), kz.reshape(self.mz)
        y_cells = self.y0 + jnp.arange(self.rows, dtype=jnp.int32)
        z_cells = self.z0 + jnp.arange(self.depth, dtype=jnp.int32)
        y_both = jnp.stack(twiddle(ky[:, None] * y_cells, self.ny))
        y_both = y_both.reshape(2, self.my, self.blocks, self.band)
        z_both = jnp.stack(twiddle(kz[:, None] * z_cells, self.nz))
        band, step = jnp.eye(self.band, dtype=F32), jnp.eye(self.step, dtype=F32)
        z_modes, y_modes = self.mz * self.band, self.my * self.step
        z_cells, y_cells = self.band * self.depth, self.blocks * self.step * self.band
        z_forward = jnp.einsum("pkz,ab->kapbz", z_both, band)
        y_forward = jnp.einsum("pknb,st->kspntb", y_both, step)
        z_back = jnp.einsum("pkz,ab->azpkb", z_both, band)
        y_back = jnp.einsum("pknb,st->nsbpkt", y_both, step)
        return (
            z_forward.reshape(z_modes, 2 * z_cells).astype(BF16),
            y_forward.reshape(y_modes, 2 * y_cells).astype(BF16),
            y_back.reshape(y_cells, 2 * y_modes).astype(BF16),
            z_back.reshape(z_cells, 2 * z_modes).astype(BF16),
        )

    def x_tables(self):
        k = frequencies(jnp.arange(self.mx, dtype=jnp.int32), self.mx)
        cos, sin = twiddle(jnp.arange(self.width, dtype=jnp.int32)[:, None] * k, self.width)
        table = jnp.stack([cos, -sin], axis=1)
        eye = jnp.eye(self.pack, dtype=F32)
        forward = table[None, :, :, None, :] * eye[:, None, None, :, None]
        forward = forward.reshape(self.pack * self.width, 2 * LANES).astype(BF16)
        flipped = jnp.transpose(table, (1, 2, 0))
        inverse = flipped[:, None, :, None, :] * eye[None, :, None, :, None]
        inverse = inverse.reshape(2 * LANES, self.pack * self.width).astype(BF16)
        return forward, inverse


def turn(values, sign):
    real, imag = values[:, :LANES], values[:, LANES:]
    return jnp.concatenate([imag, -real] if sign > 0 else [-imag, real], axis=1)


def z_transform(x_modes, table_ref, part_ref, n):
    x_modes = x_modes.astype(BF16)
    rhs = jnp.concatenate([x_modes, turn(x_modes, 1)], axis=0)
    modes = dot(table_ref[...], rhs).astype(BF16)
    steps, _, _, size, _ = part_ref.shape
    part_ref[:, 0, n] = modes.reshape(steps, size, 2 * LANES)
    part_ref[:, 1, n] = turn(modes, 1).reshape(steps, size, 2 * LANES)


def y_transform(table_ref, part_ref, own_ref, send_ref):
    half = table_ref.shape[0] // 2
    steps, _, blocks, size, _ = part_ref.shape
    chips = own_ref.shape[1]
    rows = half // chips
    per = steps // own_ref.shape[0]
    for q in range(steps):
        modes = dot(table_ref[...], part_ref[q].reshape(2 * blocks * size, 2 * LANES))
        modes = modes.astype(BF16)
        here = pl.ds(q % per * rows, rows)
        own_ref[q // per, :, 0, here] = modes[:half].reshape(chips, rows, 2 * LANES)
        send_ref[q // per, :, 0, here] = modes[half:].reshape(chips, rows, 2 * LANES)


def modes_kernel(n_after, field_ref, x_ref, z_ref, y_ref, *refs):
    own_ref, send_ref, part_ref = refs[n_after:]
    pack, rows, depth, width = field_ref.shape
    blocks = part_ref.shape[2]
    band = rows // blocks
    for n in range(blocks):
        cells = [
            field_ref[c, n * band : (n + 1) * band].reshape(band * depth, width)
            for c in range(pack)
        ]
        z_transform(dot(jnp.concatenate(cells, axis=1), x_ref[...]), z_ref, part_ref, n)
    y_transform(y_ref, part_ref, own_ref, send_ref)


def mode_blocks(lay, count):
    shape = (lay.n_gz, lay.chips, count, lay.own, 2 * LANES)
    spec = pl.BlockSpec((lay.n_gz, lay.chips, 1, lay.own, 2 * LANES), lambda i: (0, 0, i, 0, 0))
    return jax.ShapeDtypeStruct(shape, BF16), spec


def part_scratch(lay):
    size = lay.step * lay.band
    return pltpu.VMEM((lay.mz // lay.step, 2, lay.blocks, size, 2 * LANES), BF16)


def forward_modes(lay, field_in, x_table, tables, first, count, after=()):
    out, spec = mode_blocks(lay, count)
    block = (lay.pack, lay.rows, lay.depth, lay.width)
    volume = lay.pack * lay.cells * lay.width
    return pl.pallas_call(
        functools.partial(modes_kernel, len(after)),
        grid=(count,),
        in_specs=[
            pl.BlockSpec(block, lambda i: (first + i, 0, 0, 0)),
            whole(x_table.shape),
            whole(tables[0].shape),
            whole(tables[1].shape),
        ]
        + [ANY] * len(after),
        out_specs=[spec, spec],
        out_shape=[out, out],
        scratch_shapes=[part_scratch(lay)],
        compiler_params=params(),
        cost_estimate=cost(count * volume * 2 * 2 * LANES, count * volume * 3),
        name="forward_modes",
    )(field_in, x_table, tables[0], tables[1], *after)


def exchange(value, axis, distance):
    count = lax.axis_size(axis)
    return lax.ppermute(value, axis, [(i, i ^ distance) for i in range(count)])


def sum_cores(own, send):
    return (own.astype(F32) + exchange(send, "gy", 1).astype(F32)).astype(BF16)


def sum_depth(lay, both):
    total = both[0].astype(F32)
    for d in range(1, lay.n_gz):
        total = total + exchange(both[d], "gz", d).astype(F32)
    return total.astype(BF16)


def sum_chips(lay, column, factor):
    total = column[0].astype(F32)
    for d in range(1, lay.chips):
        total = total + exchange(column[d], "gy", d * CORES).astype(F32)
    return (total * factor).astype(BF16)


def spread_chips(lay, mine):
    return jnp.stack([mine] + [exchange(mine, "gy", d * CORES) for d in range(1, lay.chips)])


def spread_depth(lay, column):
    return [column] + [exchange(column, "gz", d) for d in range(1, lay.n_gz)]


def by_mode(lay, modes):
    count = modes.shape[0]
    split = modes.reshape(
        count, lay.kz // lay.step, lay.ky, lay.step, 2, lay.pack, lay.mx
    )
    return jnp.transpose(split, (1, 3, 2, 4, 6, 0, 5)).reshape(
        lay.kz, lay.ky, 2 * lay.mx, count * lay.pack
    )


def by_group(lay, modes):
    split = modes.reshape(
        lay.kz // lay.step, lay.step, lay.ky, lay.mx, 2, lay.groups, lay.pack
    )
    return jnp.transpose(split, (5, 0, 2, 1, 4, 6, 3)).reshape(
        lay.groups, lay.own, 2 * LANES
    )


def mix_kernel(modes_ref, weight_ref, *refs):
    out_ref = refs[-1]
    count, channels, wide = weight_ref.shape[2:]
    modes = modes_ref[0, 0]
    per = wide // channels
    modes = jnp.concatenate([modes] * per, axis=1)
    shape = modes.shape
    row = lax.broadcasted_iota(jnp.int32, shape, 0) % count
    owner = lax.broadcasted_iota(jnp.int32, shape, 1) // channels
    zero = jnp.zeros_like(modes)
    spread = [jnp.where(row == owner + n * per, modes, zero) for n in range(count // per)]
    mixed = dot(jnp.concatenate(spread, axis=1), weight_ref[0, 0].reshape(count * channels, wide))
    real, imag = mixed[:count], mixed[count:]
    turned = jnp.concatenate([-imag[:, channels:], imag[:, :channels]], axis=1)
    out_ref[0, 0] = (real + turned).astype(BF16)


def mode_spec(lay, shape):
    return pl.BlockSpec((1, 1) + shape, lambda i: (i // lay.ky, i % lay.ky) + (0,) * len(shape))


def mix_modes(lay, modes_in, spectral_weight, after=()):
    shape = (lay.mx, 2 * lay.channels)
    return pl.pallas_call(
        mix_kernel,
        grid=(lay.own,),
        in_specs=[mode_spec(lay, modes_in.shape[2:]), mode_spec(lay, spectral_weight.shape[2:])]
        + [ANY] * len(after),
        out_specs=mode_spec(lay, shape),
        out_shape=jax.ShapeDtypeStruct((lay.kz, lay.ky) + shape, BF16),
        compiler_params=params(),
        cost_estimate=cost(spectral_weight.size * 8, spectral_weight.size * 2),
        name="mix_modes",
    )(modes_in, spectral_weight, *after)


def pointwise_kernel(tile, n_after, field_ref, weight_ref, *refs):
    out_ref, blocks_ref = refs[n_after:]
    channels, rows, depth, width = field_ref.shape
    count = out_ref.shape[0]

    @pl.when(pl.program_id(0) == 0)
    def _():
        shape = (tile * channels, tile * channels)
        split = lax.broadcasted_iota(jnp.int32, (shape[0], channels), 0) // tile
        split = (split == lax.broadcasted_iota(jnp.int32, (shape[0], channels), 1)).astype(BF16)
        wide = dot(split[: count * tile, :count], weight_ref[...]).astype(BF16)
        wide = lax.dot_general(
            wide, split, (((1,), (1,)), ((), ())), preferred_element_type=F32
        )
        row = lax.broadcasted_iota(jnp.int32, wide.shape, 0) % tile
        column = lax.broadcasted_iota(jnp.int32, wide.shape, 1) % tile
        blocks_ref[...] = jnp.where(row == column, wide, 0.0).astype(BF16)

    for y in range(rows):
        for z in range(0, depth, tile):
            cells = field_ref[:, y, z : z + tile, :].reshape(channels * tile, width)
            mixed = dot(blocks_ref[...], cells).astype(BF16)
            out_ref[:, y, z : z + tile, :] = mixed.reshape(count, tile, width)


def pointwise(lay, field_in, weight, after=()):
    span = 2
    count = weight.shape[0]
    size = lay.channels * lay.tile
    return pl.pallas_call(
        functools.partial(pointwise_kernel, lay.tile, len(after)),
        grid=(lay.rows // span,),
        in_specs=[
            pl.BlockSpec((lay.channels, span, lay.depth, lay.width), lambda i: (0, i, 0, 0)),
            whole(weight.shape),
        ]
        + [ANY] * len(after),
        out_specs=pl.BlockSpec((count, span, lay.depth, lay.width), lambda i: (0, i, 0, 0)),
        out_shape=jax.ShapeDtypeStruct((count,) + field_in.shape[1:], BF16),
        scratch_shapes=[pltpu.VMEM((count * lay.tile, size), BF16)],
        compiler_params=params(),
        cost_estimate=cost(2 * size * count * lay.cells * lay.width, 3 * field_in.size),
        name="pointwise",
    )(field_in, weight, *after)


def gelu_and_slope(v):
    bell = jnp.exp(v * v * -0.5)
    t = 1.0 / (1.0 + jnp.abs(v) * (0.3275911 / math.sqrt(2.0)))
    poly = 0.5 * 1.061405429
    for coefficient in (-1.453152027, 1.421413741, -0.284496736, 0.254829592):
        poly = poly * t + 0.5 * coefficient
    tail = poly * t * bell
    cdf = jnp.where(v >= 0.0, 1.0 - tail, tail)
    return v * cdf, cdf + v * (bell * (1.0 / math.sqrt(2.0 * math.pi)))


def dense_kernel(first, n_pieces, n_after, *refs):
    pieces = refs[:n_pieces]
    y_ref, z_ref, x_ref, point_ref, bias_ref, mix_ref, b_in_ref = refs[n_pieces : n_pieces + 7]
    hidden_ref, slope_ref, b_ref, part_ref = refs[n_pieces + 7 + n_after :]
    pack, rows, depth, width = point_ref.shape
    blocks, _, steps, size, _ = part_ref.shape
    band = rows // blocks
    tile = mix_ref.shape[2] // pack
    step = pl.program_id(0)

    @pl.when(step == 0)
    def _():
        b_ref[...] = b_in_ref[...]

    depths = n_pieces // CORES
    per = steps // depths
    for q in range(steps):
        chunks = []
        for h in range(CORES):
            piece = pieces[h * depths + q // per]
            rows_here = piece.shape[2] // per
            here = pl.ds(q % per * rows_here, rows_here)
            chunks.append(piece[:, 0, here].reshape(piece.shape[0] * rows_here, 2 * LANES))
        modes = jnp.concatenate(chunks, axis=0)
        back = dot(y_ref[...], jnp.concatenate([modes, turn(modes, -1)], axis=0)).astype(BF16)
        part_ref[:, 0, q] = back.reshape(blocks, size, 2 * LANES)
        part_ref[:, 1, q] = turn(back, -1).reshape(blocks, size, 2 * LANES)
    channel = (first + step) * pack

    def body(n, carry):
        here = pl.ds(n * band, band)
        cells = dot(z_ref[...], part_ref[n].reshape(2 * steps * size, 2 * LANES)).astype(BF16)
        hiddens = []
        for c in range(pack):
            value = dot(cells, x_ref[:, c * width : (c + 1) * width])
            value = value.reshape(band, depth, width)
            value = value + (point_ref[c, here].astype(F32) + bias_ref[channel + c])
            hidden, slope = gelu_and_slope(value)
            hiddens.append(hidden.astype(BF16))
            hidden_ref[c, here] = hiddens[c]
            slope_ref[c, here] = slope.astype(BF16)
        for y in range(band):
            for z in range(0, depth, tile):
                cells = jnp.concatenate([h[y, z : z + tile] for h in hiddens], axis=0)
                added = dot(mix_ref[0], cells).reshape(3, tile, width)
                b_ref[:, n * band + y, z : z + tile] += added
        return carry

    lax.fori_loop(0, blocks, body, 0)


def dense(lay, pieces, tables, x_table, point, bias, mixers, b_in, first, count, after=()):
    size = (lay.chips, 1, lay.own, 2 * LANES)
    block = (lay.pack, lay.rows, lay.depth, lay.width)
    part = pl.BlockSpec(block, lambda i: (i, 0, 0, 0))
    kept = jax.ShapeDtypeStruct((count * lay.pack,) + block[1:], BF16)
    volume = lay.pack * lay.cells * lay.width
    steps = lay.mz // lay.step
    return pl.pallas_call(
        functools.partial(dense_kernel, first, len(pieces), len(after)),
        grid=(count,),
        in_specs=[pl.BlockSpec(size, lambda i: (0, i, 0, 0)) for _ in pieces]
        + [
            whole(tables[2].shape),
            whole(tables[3].shape),
            whole(x_table.shape),
            part,
            pl.BlockSpec(memory_space=pltpu.SMEM),
            pl.BlockSpec((1,) + mixers.shape[1:], lambda i: (first + i, 0, 0)),
            whole(b_in.shape),
        ]
        + [ANY] * len(after),
        out_specs=[part, part, whole(b_in.shape)],
        out_shape=[kept, kept, jax.ShapeDtypeStruct(b_in.shape, F32)],
        scratch_shapes=[
            pltpu.VMEM((lay.blocks, 2, steps, lay.step * lay.band, 2 * LANES), BF16)
        ],
        compiler_params=params(),
        cost_estimate=cost(count * volume * 2 * 6 * LANES, count * volume * 24),
        name="dense",
    )(*pieces, tables[2], tables[3], x_table, point, bias, mixers, b_in, *after)


def stencil_kernel(total_y, total_z, origin_ref, b_ref, grad_ref, sums_ref, gy_ref, rest_ref):
    _, rows_wide, depth_wide, width = b_ref.shape
    rows, depth = grad_ref.shape[1:3]
    shape = (depth_wide, width)
    lane = lax.broadcasted_iota(jnp.int32, shape, 1)
    z_cell = origin_ref[1] + lax.broadcasted_iota(jnp.int32, shape, 0) - 2
    z_inside = (z_cell >= 0) & (z_cell < total_z)
    z_own = lax.broadcasted_iota(jnp.int32, shape, 0)
    z_own = (z_own >= 2) & (z_own < depth + 2)
    scale = 1.0 / (total_y * total_z * width)

    def next_x(v):
        return jnp.where(lane == width - 1, 0.0, pltpu.roll(v, width - 1, 1))

    def last_x(v):
        return jnp.where(lane == 0, 0.0, pltpu.roll(v, 1, 1))

    def next_z(v):
        return pltpu.roll(v, depth_wide - 1, 0)

    def last_z(v):
        return pltpu.roll(v, 1, 0)

    def terms(n, loss):
        b = [b_ref[a, n + 1] for a in range(3)]
        dx = [(next_x(v) - last_x(v)) * 0.5 for v in b]
        dy = [(b_ref[a, n + 2] - b_ref[a, n]) * 0.5 for a in range(3)]
        dz = [(next_z(v) - last_z(v)) * 0.5 for v in b]
        jx = dy[2] - dz[1]
        jy = dz[0] - dx[2]
        jz = dx[1] - dy[0]
        fx = jy * b[2] - jz * b[1]
        fy = jz * b[0] - jx * b[2]
        fz = jx * b[1] - jy * b[0]
        q = dx[0] + dy[1] + dz[2]
        strength = b[0] * b[0] + b[1] * b[1] + b[2] * b[2] + 1.0
        inverse = 1.0 / strength
        ratio = (fx * fx + fy * fy + fz * fz) * inverse
        y_cell = origin_ref[0] + n - 1
        y_inside = (y_cell >= 0) & (y_cell < total_y)
        own = z_own & (n >= 1) & (n <= rows)
        loss = loss + jnp.where(own, ratio + q * q, 0.0)
        weight = jnp.where(z_inside & y_inside, 2.0 * scale, 0.0)
        inverse = inverse * weight
        pull = ratio * inverse
        fx, fy, fz = fx * inverse, fy * inverse, fz * inverse
        q = q * weight
        cx = b[1] * fz - b[2] * fy
        cy = b[2] * fx - b[0] * fz
        cz = b[0] * fy - b[1] * fx
        db = [
            fy * jz - fz * jy - pull * b[0],
            fz * jx - fx * jz - pull * b[1],
            fx * jy - fy * jx - pull * b[2],
        ]
        gx = [q, cz, -cy]
        gy = [-cz, q, cx]
        gz = [cy, -cx, q]
        for a in range(3):
            gy_ref[a, n] = gy[a]
            back = last_x(gx[a]) - next_x(gx[a]) + last_z(gz[a]) - next_z(gz[a])
            rest_ref[a, n] = db[a] + back * 0.5
        return loss

    loss = lax.fori_loop(0, rows + 2, terms, jnp.zeros(shape, F32))

    def combine(n, sums):
        done = []
        for a in range(3):
            grad = rest_ref[a, n + 1] + (gy_ref[a, n] - gy_ref[a, n + 2]) * 0.5
            grad = grad[2 : depth + 2]
            grad_ref[a, n] = grad
            done.append(sums[a] + grad)
        return tuple(done)

    sums = lax.fori_loop(0, rows, combine, (jnp.zeros((depth, width), F32),) * 3)
    sums_ref[...] = jnp.zeros_like(sums_ref)
    for a in range(3):
        sums_ref[a : a + 1, :] = jnp.sum(sums[a], axis=0, keepdims=True)
    sums_ref[3:4, :] = jnp.sum(loss, axis=0, keepdims=True)


def stencil(lay, b_field):
    padded = with_halo(b_field, (("gy", 1), ("gz", 2)), 2)
    padded = jnp.pad(padded, ((0, 0), (0, 0), (0, 4), (0, 0)))
    origin = jnp.stack([lay.y0, lay.z0]).astype(jnp.int32)
    wide = (3, lay.rows + 2, padded.shape[2], lay.width)
    return pl.pallas_call(
        functools.partial(stencil_kernel, lay.ny, lay.nz),
        in_specs=[
            pl.BlockSpec(memory_space=pltpu.SMEM),
            pl.BlockSpec(memory_space=pltpu.VMEM),
        ],
        out_specs=[pl.BlockSpec(memory_space=pltpu.VMEM)] * 2,
        out_shape=[
            jax.ShapeDtypeStruct(b_field.shape, F32),
            jax.ShapeDtypeStruct((8, lay.width), F32),
        ],
        scratch_shapes=[pltpu.VMEM(wide, F32), pltpu.VMEM(wide, F32)],
        compiler_params=pltpu.CompilerParams(vmem_limit_bytes=VMEM_LIMIT),
        name="stencil",
    )(origin, padded)


def grad_kernel(first, n_after, weight_ref, hidden_ref, slope_ref, grad_ref, x_ref, z_ref, y_ref,
                *refs):
    pre_ref, own_ref, send_ref, sums_ref, part_ref = refs[n_after:]
    pack, rows, depth, width = hidden_ref.shape
    blocks = part_ref.shape[2]
    band = rows // blocks
    channel = (first + pl.program_id(0)) * pack

    def fold(v):
        return jnp.sum(v.reshape(-1, 8, width), axis=0)

    def body(n, sums):
        here = pl.ds(n * band, band)
        grads = [grad_ref[b, here] for b in range(3)]
        done, pres = [], []
        for c in range(pack):
            w = [weight_ref[channel + c, b] for b in range(3)]
            mixed = grads[0] * w[0] + grads[1] * w[1] + grads[2] * w[2]
            pre = (mixed * slope_ref[c, here].astype(F32)).astype(BF16)
            pre_ref[c, here] = pre
            pres.append(pre.reshape(band * depth, width))
            hidden = hidden_ref[c, here].astype(F32)
            for b in range(3):
                done.append(sums[3 * c + b] + fold(hidden * grads[b]))
        total = dot(jnp.concatenate(pres, axis=1), x_ref[...])
        done.append(sums[3 * pack] + fold(total))
        z_transform(total, z_ref, part_ref, n)
        return tuple(done)

    start = (jnp.zeros((8, width), F32),) * (3 * pack) + (jnp.zeros((8, 2 * LANES), F32),)
    sums = lax.fori_loop(0, blocks, body, start)
    sums_ref[...] = jnp.zeros_like(sums_ref)
    for n in range(3 * pack + 1):
        sums_ref[0, n : n + 1, :] = jnp.sum(sums[n], axis=0, keepdims=True)
    y_transform(y_ref, part_ref, own_ref, send_ref)


def grad_modes(lay, hidden, slope, grad_b, x_table, tables, weights, first, count, after=()):
    out, spec = mode_blocks(lay, count)
    block = (lay.pack, lay.rows, lay.depth, lay.width)
    part = pl.BlockSpec(block, lambda i: (i, 0, 0, 0))
    volume = lay.pack * lay.cells * lay.width
    lines = -(-(3 * lay.pack + 1) // 8) * 8
    return pl.pallas_call(
        functools.partial(grad_kernel, first, len(after)),
        grid=(count,),
        in_specs=[
            pl.BlockSpec(memory_space=pltpu.SMEM),
            part,
            part,
            whole(grad_b.shape),
            whole(x_table.shape),
            whole(tables[0].shape),
            whole(tables[1].shape),
        ]
        + [ANY] * len(after),
        out_specs=[
            part,
            spec,
            spec,
            pl.BlockSpec((1, lines, lay.width), lambda i: (i, 0, 0)),
        ],
        out_shape=[
            jax.ShapeDtypeStruct(hidden.shape, BF16),
            out,
            out,
            jax.ShapeDtypeStruct((count, lines, lay.width), F32),
        ],
        scratch_shapes=[part_scratch(lay)],
        compiler_params=params(),
        cost_estimate=cost(count * volume * 2 * 2 * LANES, count * volume * 10),
        name="grad_modes",
    )(weights, hidden, slope, grad_b, x_table, tables[0], tables[1], *after)


def point_kernel(tile, n_after, field_ref, grad_ref, *refs):
    out_ref, acc_ref = refs[n_after:]
    channels, rows, depth, width = field_ref.shape
    count = grad_ref.shape[0]
    step = pl.program_id(0)

    @pl.when(step == 0)
    def _():
        acc_ref[...] = jnp.zeros_like(acc_ref)

    total = 0.0
    for y in range(rows):
        for z in range(0, depth, tile):
            left = field_ref[:, y, z : z + tile, :].reshape(channels * tile, width)
            right = grad_ref[:, y, z : z + tile, :].reshape(count * tile, width)
            total = total + lax.dot_general(
                left, right, (((1,), (1,)), ((), ())), preferred_element_type=F32
            )
    acc_ref[...] += total

    @pl.when(step == pl.num_programs(0) - 1)
    def _():
        def pick(n):
            owner = lax.broadcasted_iota(jnp.int32, (n, n * tile), 1) // tile
            return (owner == lax.broadcasted_iota(jnp.int32, (n, n * tile), 0)).astype(F32)

        row = lax.broadcasted_iota(jnp.int32, acc_ref.shape, 0)
        column = lax.broadcasted_iota(jnp.int32, acc_ref.shape, 1)
        kept = jnp.where(row % tile == column % tile, acc_ref[...], 0.0)
        half = jnp.dot(
            pick(channels), kept, precision=lax.Precision.HIGHEST, preferred_element_type=F32
        )
        out_ref[...] = lax.dot_general(
            half,
            pick(count),
            (((1,), (1,)), ((), ())),
            precision=lax.Precision.HIGHEST,
            preferred_element_type=F32,
        )


def point_grad(lay, field_in, grad_pre, after=()):
    span = 4

    def block(count):
        return pl.BlockSpec((count, span, lay.depth, lay.width), lambda i: (0, i, 0, 0))

    count = grad_pre.shape[0]
    size = lay.channels * lay.tile
    return pl.pallas_call(
        functools.partial(point_kernel, lay.tile, len(after)),
        grid=(lay.rows // span,),
        in_specs=[block(lay.channels), block(count)] + [ANY] * len(after),
        out_specs=pl.BlockSpec((lay.channels, count), lambda i: (0, 0)),
        out_shape=jax.ShapeDtypeStruct((lay.channels, count), F32),
        scratch_shapes=[pltpu.VMEM((size, count * lay.tile), F32)],
        compiler_params=params(),
        cost_estimate=cost(2 * size * count * lay.cells * lay.width, 3 * field_in.size),
        name="point_grad",
    )(field_in, grad_pre, *after)


def outer_kernel(modes_ref, grads_ref, out_ref):
    count, channels, wide = out_ref.shape[2:]
    right = grads_ref[0, 0]
    turned = jnp.concatenate([right[:, channels:], -right[:, :channels]], axis=1)
    rows = jnp.concatenate([right, turned], axis=0)
    row = lax.broadcasted_iota(jnp.int32, rows.shape, 0) % count
    zero = jnp.zeros_like(rows)
    for k in range(0, count, 2):
        pair = [jnp.where(row == k + n, rows, zero) for n in range(2)]
        out = dot(modes_ref[0, 0], jnp.concatenate(pair, axis=1))
        out_ref[0, 0, k] = out[:, :wide]
        out_ref[0, 0, k + 1] = out[:, wide:]


def weight_grad(lay, modes_in, grads):
    columns = jnp.transpose(modes_in, (0, 1, 3, 2))
    rows = jnp.concatenate([grads[:, :, : lay.mx], grads[:, :, lay.mx :]], axis=-1)
    tile = (lay.mx, lay.channels, 2 * lay.channels)
    shape = (lay.kz, lay.ky) + tile
    return pl.pallas_call(
        outer_kernel,
        grid=(lay.own,),
        in_specs=[mode_spec(lay, columns.shape[2:]), mode_spec(lay, rows.shape[2:])],
        out_specs=mode_spec(lay, tile),
        out_shape=jax.ShapeDtypeStruct(shape, F32),
        compiler_params=params(),
        cost_estimate=cost(math.prod(shape) * 4, math.prod(shape) * 4),
        name="weight_grad",
    )(columns, rows)


def sum_everywhere(value, axes):
    for axis in axes:
        count = lax.axis_size(axis)
        d = 1
        while d < count:
            value = value + lax.ppermute(value, axis, [(i, i ^ d) for i in range(count)])
            d *= 2
    return value


def on_device(field_in, spectral_weight, point_weight, point_bias, out_weight, out_bias):
    lay = Layout(field_in, spectral_weight)
    tables = lay.grid_tables()
    x_table, x_back = lay.x_tables()
    weights = out_weight.astype(F32)
    per = lay.groups // PARTS
    parts = range(PARTS)
    scale = math.sqrt(lay.mx * lay.my * lay.mz / (lay.width * lay.ny * lay.nz))
    share = lay.channels // PARTS

    def point(n, after):
        return pointwise(lay, field_in, point_weight.T[n * share : (n + 1) * share], after)

    both, column, modes, points = [], [], [], []
    for n in parts:
        own, send = forward_modes(
            lay, field_in, x_table, tables, n * per, per, after=both[n - 2 : n - 1] if n > 1 else ()
        )
        both.append(sum_cores(own, send))
    for n in parts:
        column.append(sum_depth(lay, both[n]))
        modes.append(sum_chips(lay, column[n], scale))
    points.append(point(0, both[-1:]))
    points.append(point(1, column[:1]))
    points.append(point(2, column[1:2]))
    modes_in = by_mode(lay, jnp.concatenate(modes))
    mixed = mix_modes(lay, modes_in, spectral_weight, after=points)
    mine = by_group(
        lay, mixed.reshape(lay.kz, lay.ky, lay.mx, 2, lay.groups, lay.pack)
    )
    points.append(point(3, [mine]))

    b_field = jnp.broadcast_to(
        out_bias[:, None, None, None], (3, lay.rows, lay.depth, lay.width)
    ).astype(F32)
    eye = jnp.eye(lay.tile, dtype=BF16)
    mixers = jnp.einsum("gcb,zy->gbzcy", out_weight.reshape(lay.groups, lay.pack, 3), eye)
    mixers = mixers.reshape(lay.groups, 3 * lay.tile, lay.pack * lay.tile)
    hiddens, slopes = [], []
    columns = [spread_chips(lay, mine[n * per : (n + 1) * per]) for n in parts]
    for n in parts:
        pieces = spread_depth(lay, columns[n])
        pieces = pieces + [exchange(piece, "gy", 1) for piece in pieces]
        hidden, slope, b_field = dense(
            lay, pieces, tables, x_back, points[n], point_bias, mixers, b_field, n * per, per,
            after=columns[n + 1 : n + 2] + points[3:],
        )
        hiddens.append(hidden)
        slopes.append(slope)

    grad_b, edge = stencil(lay, b_field)

    both, column, grads, pres, sums = [], [], [], [], []
    for n in parts:
        pre, own, send, part = grad_modes(
            lay, hiddens[n], slopes[n], grad_b, x_table, tables, weights, n * per, per,
            after=both[n - 2 : n - 1] + column[n - 3 : n - 2] if n > 1 else (),
        )
        both.append(sum_cores(own, send))
        column.append(sum_depth(lay, both[n]))
        grads.append(sum_chips(lay, column[n], 1.0))
        pres.append(pre)
        sums.append(part)
    point_parts = [point_grad(lay, field_in, pres[0], both[2:3] + column[1:2])]
    point_parts.append(point_grad(lay, field_in, pres[1], both[3:4] + column[2:3]))
    point_parts.append(point_grad(lay, field_in, pres[2], column[3:4]))
    point_parts.append(point_grad(lay, field_in, pres[3]))
    sums = jnp.concatenate(sums)
    outs = jnp.sum(sums[:, : 3 * lay.pack], axis=-1).reshape(3 * lay.channels)
    bias = sums[:, 3 * lay.pack, :LANES].reshape(lay.groups, lay.pack, lay.mx)[..., 0]
    ends = jnp.sum(edge, axis=-1)
    square = lay.channels * lay.channels
    flat = jnp.concatenate(
        [
            jnp.concatenate(point_parts, axis=1).reshape(square),
            outs,
            bias.reshape(lay.channels),
            ends[:4],
        ]
    )
    flat = jnp.pad(flat, (0, -flat.shape[0] % 1024)).reshape(-1, LANES)
    flat = sum_everywhere(flat, ("gy", "gz")).reshape(-1)
    after = square + 3 * lay.channels
    ends = flat[after + lay.channels : after + lay.channels + 4]
    grad_spectral = weight_grad(lay, modes_in, by_mode(lay, jnp.concatenate(grads)))
    return (
        ends[3] / (lay.width * lay.ny * lay.nz),
        grad_spectral,
        flat[:square].reshape(lay.channels, lay.channels),
        flat[after : after + lay.channels],
        flat[square:after].reshape(lay.channels, 3),
        ends[:3],
    )


def solution(mesh):
    return jax.shard_map(
        on_device,
        mesh=mesh,
        in_specs=(P(None, "gy", "gz", None), P("gz", "gy", None, None, None), P(), P(), P(), P()),
        out_specs=(P(), P("gz", "gy", None, None, None), P(), P(), P(), P()),
        check_vma=False,
    )
```

time: 1630 us -> 821 us (0.50)
  other arithmetic: 583 us -> 37.9 us
  Pallas kernels: 0 us -> 535 us
  matrix products: 356 us -> 0 us
  waiting for transfers between devices: 394 us -> 38.9 us
  starting transfers between devices: 16.9 us -> 115 us
  local copies, waits for them, and re-layouts: 168 us -> 76.7 us
  blocking collectives: 83.5 us -> 0 us
    pallas_call x0 -> x23, Pallas kernels: none -> 535 us  [the longest x4 152 us: dense(): pl.pallas_call(functools.partial(dense_kernel, first, len(pieces), len(af...]
    dot_general x21 -> x0, matrix products: 356 us -> none  [the longest x2 78.6 us: to_modes(): jnp.einsum('cyzx,xpk->yzkpc', grid_field, forward_table, preferred_elemen...]
    reduce_scatter x2 -> x0, waiting for transfers between devices: 344 us -> none  [to_modes(): lax.psum_scatter(rotate(with_cos, with_sin, True), 'gy', scatter_dimensio...]
    add x4 -> x8, other arithmetic: 145 us -> 0.18 us  [the longest x1 0.07 us: mode_numbers(): ky = ky + jnp.arange(self.ky, dtype=jnp.int32)]
    convert_element_type x7 -> x33, other arithmetic: 157 us -> 24.9 us  [the longest x8 9.93 us: sum_depth(): return total.astype(BF16)]
    ppermute x0 -> x101, starting transfers between devices: none -> 107 us  [the longest x96 102 us: exchange(): return lax.ppermute(value, axis, [(i, i ^ distance) for i in range(count)])]
    concatenate x8 -> x4, other arithmetic: 99 us -> 1.81 us  [the longest x1 0.88 us: weight_grad(): jnp.concatenate([grads[:, :, :lay.mx], grads[:, :, lay.mx:]], axis=-1)]
    convert_element_type x7 -> x9, local copies, waits for them, and re-layouts: 119 us -> 28.6 us  [the longest x2 20 us: grid_tables(): y_forward.reshape(y_modes, 2 * y_cells).astype(BF16)]
  transfers between devices with their start and end apart: 9 -> 105, of which waited for: 6 -> 12; matrix products, arithmetic and copies ran while one was open for 8% -> 8% of each run, Pallas kernels for 0% -> 50%
where the time goes in v1:
time: 821 us; the launch traced here: 808 us
  Pallas kernels  535 us (65%)
  starting transfers between devices  115 us (14%)
  local copies, waits for them, and re-layouts  76.7 us (9%)
  waiting for transfers between devices  38.9 us (5%)
  other arithmetic  37.9 us (5%)
    pallas_call x4, Pallas kernels, dense(): pl.pallas_call(functools.partial(dense_kernel, first, len(pieces), len(af...  152 us
    ppermute x96, starting transfers between devices, exchange(): return lax.ppermute(value, axis, [(i, i ^ distance) for i in range(count)])  102 us
    pallas_call x4, Pallas kernels, grad_modes(): pl.pallas_call(functools.partial(grad_kernel, first, len(after)), grid=(c...  95.3 us
    pallas_call x4, Pallas kernels, pointwise(): pl.pallas_call(functools.partial(pointwise_kernel, lay.tile, len(after)),...  92.9 us
    pallas_call x4, Pallas kernels, point_grad(): pl.pallas_call(functools.partial(point_kernel, lay.tile, len(after)), gri...  75.8 us
    pallas_call x4, Pallas kernels, forward_modes(): pl.pallas_call(functools.partial(modes_kernel, len(after)), grid=(count,)...  56.3 us
    pallas_call x1, Pallas kernels, mix_modes(): pl.pallas_call(mix_kernel, grid=(lay.own,), in_specs=[mode_spec(lay, mode...  24.8 us
    pallas_call x1, Pallas kernels, weight_grad(): pl.pallas_call(outer_kernel, grid=(lay.own,), in_specs=[mode_spec(lay, co...  23.6 us
  transfers between devices with their start and end apart: 105, of which 12 were waited for; matrix products, arithmetic and copies ran while one was open for 8% of the time, Pallas kernels for 50%

profile of v1, /device:TPU:0, one launch (start us, length us, event | category | flops | bytes accessed | tf_op | source)
XLA Modules:
  0.0 807.9 jit_solution(1873107003313878238)
XLA Ops:
  1.3 2.5 fusion
  3.7 14.4 %copy.112 = bf16[32,4,2,8,4,4]{5,4,3,2,1,0:T(4,128)(2,1)} copy(bf16[32,4,2,8,4,4]{4,0,2,5,1,3:T(8,128)(2,1)} %get-tuple-element.157) | data formatting | bytes 131072 | tf_op jit(solution)/shard_map/convert_element_type | solution.py:110
  18.1 5.7 reshape.612.y_ref
  27.6 14.1 %forward_modes.4 = (bf16[4,4,4,32,256]{4,3,2,1,0:T(8,128)(2,1)}, bf16[4,4,4,32,256]{4,3,2,1,0:T(8,128)(2,1)}) custom-call(bf16[64,32,32,256]{3,2,1,0:T(8,128)(2,1)} %field_ref.23, bf16[1024,256]{1,0:T(8,128)(2,1)} %copy.72.x_ref, bf16[128,256]{1,0:T(8,128)(2,1)} %convert_element_type.597.z_ref, bf16[128,256]{1,0:T(8,128)(2,1)} %reshape.612.y_ref), custom_call_target="tpu_custom_call" | custom-call | flops 2147483648 | bytes 12582912 | tf_op jit(solution)/shard_map/forward_modes/pallas_call | solution.py:185
  42.1 14.0 %forward_modes.5 = (bf16[4,4,4,32,256]{4,3,2,1,0:T(8,128)(2,1)}, bf16[4,4,4,32,256]{4,3,2,1,0:T(8,128)(2,1)}) custom-call(bf16[64,32,32,256]{3,2,1,0:T(8,128)(2,1)} %field_ref.23, bf16[1024,256]{1,0:T(8,128)(2,1)} %copy.72.x_ref, bf16[128,256]{1,0:T(8,128)(2,1)} %convert_element_type.597.z_ref, bf16[128,256]{1,0:T(8,128)(2,1)} %reshape.612.y_ref), custom_call_target="tpu_custom_call" | custom-call | flops 2147483648 | bytes 12582912 | tf_op jit(solution)/shard_map/forward_modes/pallas_call | solution.py:185
  56.9 2.0 add_convert_fusion.7.refs_0_
  58.9 3.0 collective-permute-start.1
  66.0 14.0 %forward_modes.6 = (bf16[4,4,4,32,256]{4,3,2,1,0:T(8,128)(2,1)}, bf16[4,4,4,32,256]{4,3,2,1,0:T(8,128)(2,1)}) custom-call(bf16[64,32,32,256]{3,2,1,0:T(8,128)(2,1)} %field_ref.23, bf16[1024,256]{1,0:T(8,128)(2,1)} %copy.72.x_ref, bf16[128,256]{1,0:T(8,128)(2,1)} %convert_element_type.597.z_ref, bf16[128,256]{1,0:T(8,128)(2,1)} %reshape.612.y_ref, ...), custom_call_target="tpu_custom_call" | custom-call | flops 2147483648 | bytes 12582912 | tf_op jit(solution)/shard_map/forward_modes/pallas_call | solution.py:185
  80.1 2.9 collective-permute-start.10
  83.5 14.2 %forward_modes.7 = (bf16[4,4,4,32,256]{4,3,2,1,0:T(8,128)(2,1)}, bf16[4,4,4,32,256]{4,3,2,1,0:T(8,128)(2,1)}) custom-call(bf16[64,32,32,256]{3,2,1,0:T(8,128)(2,1)} %field_ref.23, bf16[1024,256]{1,0:T(8,128)(2,1)} %copy.72.x_ref, bf16[128,256]{1,0:T(8,128)(2,1)} %convert_element_type.597.z_ref, bf16[128,256]{1,0:T(8,128)(2,1)} %reshape.612.y_ref, ...), custom_call_target="tpu_custom_call" | custom-call | flops 2147483648 | bytes 12582912 | tf_op jit(solution)/shard_map/forward_modes/pallas_call | solution.py:185
  100.2 23.2 %pointwise.5.refs_1_.refs_11_ = bf16[16,32,32,256]{3,2,1,0:T(8,128)(2,1)} custom-call(bf16[64,32,32,256]{3,2,1,0:T(8,128)(2,1)} %field_ref.23, bf16[16,64]{1,0:T(8,128)(2,1)} %get-tuple-element.160.weight_ref, bf16[4,4,32,256]{3,2,1,0:T(8,128)(2,1)} %fusion.25.refs_0_), custom_call_target="tpu_custom_call" | custom-call | flops 8589934592 | bytes 50331648 | tf_op jit(solution)/shard_map/pointwise/pallas_call | solution.py:319
  123.5 2.0 collective-permute-start.4
  125.5 2.6 collective-permute-start.5
  130.0 23.3 %pointwise.6.refs_2_.refs_11_ = bf16[16,32,32,256]{3,2,1,0:T(8,128)(2,1)} custom-call(bf16[64,32,32,256]{3,2,1,0:T(8,128)(2,1)} %field_ref.23, bf16[16,64]{1,0:T(8,128)(2,1)} %get-tuple-element.159.weight_ref, bf16[4,4,32,256]{3,2,1,0:T(8,128)(2,1)} %fusion.22.refs_0_), custom_call_target="tpu_custom_call" | custom-call | flops 8589934592 | bytes 50331648 | tf_op jit(solution)/shard_map/pointwise/pallas_call | solution.py:319
  154.3 3.5 collective-permute-start.12
  157.8 3.9 collective-permute-done.12
  161.8 2.1 collective-permute-done.13
  172.9 23.2 %pointwise.4.refs_0_.refs_11_ = bf16[16,32,32,256]{3,2,1,0:T(8,128)(2,1)} custom-call(bf16[64,32,32,256]{3,2,1,0:T(8,128)(2,1)} %field_ref.23, bf16[16,64]{1,0:T(8,128)(2,1)} %get-tuple-element.161.weight_ref, bf16[4,4,4,32,256]{4,3,2,1,0:T(8,128)(2,1)} %copy-done.2), custom_call_target="tpu_custom_call" | custom-call | flops 8589934592 | bytes 50331648 | tf_op jit(solution)/shard_map/pointwise/pallas_call | solution.py:319
  198.4 2.7 collective-permute-start.20
  201.2 2.1 collective-permute-done.24
  206.2 2.7 collective-permute-start.27
  209.8 2.5 collective-permute-done.27
  212.8 2.1 copy.122
  214.9 2.4 reshape.584
  218.4 24.8 %mix_modes.1 = bf16[8,4,32,128]{3,2,1,0:T(8,128)(2,1)} custom-call(bf16[8,4,64,64]{3,2,1,0:T(8,128)(2,1)} %copy.82.modes_ref, bf16[8,4,32,64,128]{4,3,2,1,0:T(8,128)(2,1)} %weight_ref.1, bf16[16,32,32,256]{3,2,1,0:T(8,128)(2,1)} %pointwise.4.refs_0_.refs_11_, bf16[16,32,32,256]{3,2,1,0:T(8,128)(2,1)} %pointwise.5.refs_1_.refs_11_, ...), custom_call_target="tpu_custom_call" | custom-call | flops 67108864 | bytes 16777216 | tf_op jit(solution)/shard_map/mix_modes/pallas_call | solution.py:277
  247.7 2.4 collective-permute-start.29
  254.4 3.3 collective-permute-start.39
  264.3 3.2 collective-permute-start.52
  271.5 2.4 collective-permute-start.33
  277.4 3.2 collective-permute-start.42
  282.2 2.8 collective-permute-done.42
  287.4 3.9 collective-permute-done.43
  292.3 2.4 collective-permute-start.63
  295.4 4.6 convert_element_type.665.refs_8_
  307.9 2.4 collective-permute-start.56
  310.9 23.2 %pointwise.7.refs_16_.refs_11_.refs_15_ = bf16[16,32,32,256]{3,2,1,0:T(8,128)(2,1)} custom-call(bf16[64,32,32,256]{3,2,1,0:T(8,128)(2,1)} %field_ref.23, bf16[16,64]{1,0:T(8,128)(2,1)} %get-tuple-element.158.weight_ref, bf16[16,32,256]{2,1,0:T(8,128)(2,1)} %reshape.587.refs_0_), custom_call_target="tpu_custom_call" | custom-call | flops 8589934592 | bytes 50331648 | tf_op jit(solution)/shard_map/pointwise/pallas_call | solution.py:319
  336.9 2.1 broadcast_in_dim.2.refs_14_
  339.0 38.0 %dense.4 = (bf16[16,32,32,256]{3,2,1,0:T(8,128)(2,1)}, bf16[16,32,32,256]{3,2,1,0:T(8,128)(2,1)}, f32[3,32,32,256]{3,2,1,0:T(8,128)}) custom-call(bf16[4,4,32,256]{3,2,1,0:T(8,128)(2,1)} %pad_maximum_fusion.1.refs_0_, bf16[4,4,32,256]{3,2,1,0:T(8,128)(2,1)} %collective-permute-done.31.refs_1_, bf16[4,4,32,256]{3,2,1,0:T(8,128)(2,1)} %collective-permute-done.32.refs_2_, ...), custom_call_target="tpu_custom_call" | custom-call | flops 6442450944 | bytes 100663296 | tf_op jit(solution)/shard_map/dense/pallas_call | solution.py:405
  377.6 2.4 collective-permute-start.46
  381.3 37.9 %dense.5 = (bf16[16,32,32,256]{3,2,1,0:T(8,128)(2,1)}, bf16[16,32,32,256]{3,2,1,0:T(8,128)(2,1)}, f32[3,32,32,256]{3,2,1,0:T(8,128)}) custom-call(bf16[4,4,32,256]{3,2,1,0:T(8,128)(2,1)} %pad_maximum_fusion.2.refs_15_.refs_0_, bf16[4,4,32,256]{3,2,1,0:T(8,128)(2,1)} %collective-permute-done.61.refs_1_, ...), custom_call_target="tpu_custom_call" | custom-call | flops 6442450944 | bytes 100663296 | tf_op jit(solution)/shard_map/dense/pallas_call | solution.py:405
  421.2 37.8 %dense.6 = (bf16[16,32,32,256]{3,2,1,0:T(8,128)(2,1)}, bf16[16,32,32,256]{3,2,1,0:T(8,128)(2,1)}, f32[3,32,32,256]{3,2,1,0:T(8,128)}) custom-call(bf16[4,4,32,256]{3,2,1,0:T(8,128)(2,1)} %pad_maximum_fusion.4.refs_15_.refs_0_, bf16[4,4,32,256]{3,2,1,0:T(8,128)(2,1)} %collective-permute-done.54.refs_1_, bf16[4,4,32,256]{3,2,1,0:T(8,128)(2,1)} %copy-done.35, ...), custom_call_target="tpu_custom_call" | custom-call | flops 6442450944 | bytes 100663296 | tf_op jit(solution)/shard_map/dense/pallas_call | solution.py:405
  460.1 37.8 %dense.7 = (bf16[16,32,32,256]{3,2,1,0:T(8,128)(2,1)}, bf16[16,32,32,256]{3,2,1,0:T(8,128)(2,1)}, f32[3,32,32,256]{3,2,1,0:T(8,128)}) custom-call(bf16[4,4,32,256]{3,2,1,0:T(8,128)(2,1)} %copy-done.23, bf16[4,4,32,256]{3,2,1,0:T(8,128)(2,1)} %copy-done.37, bf16[4,4,32,256]{3,2,1,0:T(8,128)(2,1)} %copy-done.39, bf16[4,4,32,256]{3,2,1,0:T(8,128)(2,1)} %copy-done.40, ...), custom_call_target="tpu_custom_call" | custom-call | flops 6442450944 | bytes 100663296 | tf_op jit(solution)/shard_map/dense/pallas_call | solution.py:405
  499.0 2.0 collective-permute-start.68
  502.3 2.1 constant_dynamic-update-slice_fusion.1
  505.4 3.1 collective-permute-start.70
  511.8 7.2 collective-permute-done.71
  519.0 3.9 select_maximum_fusion.b_ref
  522.9 15.0 %stencil.1 = (f32[3,32,32,256]{3,2,1,0:T(8,128)}, f32[8,256]{1,0:T(8,128)}) custom-call(s32[2]{0:T(128)} %pad_add_fusion.origin_ref, f32[3,36,40,256]{3,2,1,0:T(8,128)} %select_maximum_fusion.b_ref), custom_call_target="tpu_custom_call" | custom-call | tf_op jit(solution)/shard_map/stencil/pallas_call | solution.py:517
  537.9 23.8 %grad_modes.4 = (bf16[16,32,32,256]{3,2,1,0:T(8,128)(2,1)}, bf16[4,4,4,32,256]{4,3,2,1,0:T(8,128)(2,1)}, bf16[4,4,4,32,256]{4,3,2,1,0:T(8,128)(2,1)}, f32[4,16,256]{2,1,0:T(8,128)}) custom-call(f32[64,3]{1,0:T(8,128)} %convert_element_type.583.weight_ref, bf16[16,32,32,256]{3,2,1,0:T(8,128)(2,1)} %get-tuple-element.52.hidden_ref, ...), custom_call_target="tpu_custom_call" | custom-call | flops 2147483648 | bytes 41943040 | tf_op jit(solution)/shard_map/grad_modes/pallas_call | solution.py:577
  563.3 23.8 %grad_modes.6 = (bf16[16,32,32,256]{3,2,1,0:T(8,128)(2,1)}, bf16[4,4,4,32,256]{4,3,2,1,0:T(8,128)(2,1)}, bf16[4,4,4,32,256]{4,3,2,1,0:T(8,128)(2,1)}, f32[4,16,256]{2,1,0:T(8,128)}) custom-call(f32[64,3]{1,0:T(8,128)} %convert_element_type.583.weight_ref, bf16[16,32,32,256]{3,2,1,0:T(8,128)(2,1)} %get-tuple-element.66.hidden_ref, ...), custom_call_target="tpu_custom_call" | custom-call | flops 2147483648 | bytes 41943040 | tf_op jit(solution)/shard_map/grad_modes/pallas_call | solution.py:577
  590.6 2.9 collective-permute-start.80
  594.8 23.8 %grad_modes.5 = (bf16[16,32,32,256]{3,2,1,0:T(8,128)(2,1)}, bf16[4,4,4,32,256]{4,3,2,1,0:T(8,128)(2,1)}, bf16[4,4,4,32,256]{4,3,2,1,0:T(8,128)(2,1)}, f32[4,16,256]{2,1,0:T(8,128)}) custom-call(f32[64,3]{1,0:T(8,128)} %convert_element_type.583.weight_ref, bf16[16,32,32,256]{3,2,1,0:T(8,128)(2,1)} %get-tuple-element.60.hidden_ref, ...), custom_call_target="tpu_custom_call" | custom-call | flops 2147483648 | bytes 41943040 | tf_op jit(solution)/shard_map/grad_modes/pallas_call | solution.py:577
  619.4 3.0 collective-permute-start.77
  624.3 3.8 collective-permute-start.93
  631.9 23.9 %grad_modes.7 = (bf16[16,32,32,256]{3,2,1,0:T(8,128)(2,1)}, bf16[4,4,4,32,256]{4,3,2,1,0:T(8,128)(2,1)}, bf16[4,4,4,32,256]{4,3,2,1,0:T(8,128)(2,1)}, f32[4,16,256]{2,1,0:T(8,128)}) custom-call(f32[64,3]{1,0:T(8,128)} %convert_element_type.583.weight_ref, bf16[16,32,32,256]{3,2,1,0:T(8,128)(2,1)} %get-tuple-element.71.hidden_ref, ...), custom_call_target="tpu_custom_call" | custom-call | flops 2147483648 | bytes 41943040 | tf_op jit(solution)/shard_map/grad_modes/pallas_call | solution.py:577
  656.9 18.9 %point_grad.7 = f32[64,16]{1,0:T(8,128)} custom-call(bf16[64,32,32,256]{3,2,1,0:T(8,128)(2,1)} %field_ref.23, bf16[16,32,32,256]{3,2,1,0:T(8,128)(2,1)} %get-tuple-element.76.grad_ref), custom_call_target="tpu_custom_call" | custom-call | flops 8589934592 | bytes 50331648 | tf_op jit(solution)/shard_map/point_grad/pallas_call | solution.py:658
  680.3 3.6 collective-permute-done.97
  688.1 18.9 %point_grad.4 = f32[64,16]{1,0:T(8,128)} custom-call(bf16[64,32,32,256]{3,2,1,0:T(8,128)(2,1)} %field_ref.23, bf16[16,32,32,256]{3,2,1,0:T(8,128)(2,1)} %get-tuple-element.59.grad_ref, bf16[4,4,4,32,256]{4,3,2,1,0:T(8,128)(2,1)} %copy-done.3, bf16[4,4,32,256]{3,2,1,0:T(8,128)(2,1)} %copy-done.9), custom_call_target="tpu_custom_call" | custom-call | flops 8589934592 | bytes 50331648 | tf_op jit(solution)/shard_map/point_grad/pallas_call | solution.py:658
  712.9 19.1 %point_grad.5 = f32[64,16]{1,0:T(8,128)} custom-call(bf16[64,32,32,256]{3,2,1,0:T(8,128)(2,1)} %field_ref.23, bf16[16,32,32,256]{3,2,1,0:T(8,128)(2,1)} %get-tuple-element.70.grad_ref, bf16[4,4,4,32,256]{4,3,2,1,0:T(8,128)(2,1)} %copy-done.4, bf16[4,4,32,256]{3,2,1,0:T(8,128)(2,1)} %fusion.7.refs_1_), custom_call_target="tpu_custom_call" | custom-call | flops 8589934592 | bytes 50331648 | tf_op jit(solution)/shard_map/point_grad/pallas_call | solution.py:658
  733.9 18.9 %point_grad.6 = f32[64,16]{1,0:T(8,128)} custom-call(bf16[64,32,32,256]{3,2,1,0:T(8,128)(2,1)} %field_ref.23, bf16[16,32,32,256]{3,2,1,0:T(8,128)(2,1)} %get-tuple-element.75.grad_ref, bf16[4,4,32,256]{3,2,1,0:T(8,128)(2,1)} %fusion.4.refs_0_), custom_call_target="tpu_custom_call" | custom-call | flops 8589934592 | bytes 50331648 | tf_op jit(solution)/shard_map/point_grad/pallas_call | solution.py:658
  757.6 2.1 collective-permute-start.89
  759.8 4.3 collective-permute-done.89
  768.2 5.1 collective-permute-done.90
  778.9 23.6 %weight_grad.1 = f32[8,4,32,64,128]{4,3,2,1,0:T(8,128)} custom-call(bf16[8,4,64,64]{3,2,1,0:T(8,128)(2,1)} %bitcast.242, bf16[8,4,32,128]{3,2,1,0:T(8,128)(2,1)} %pad_maximum_fusion.6.grads_ref), custom_call_target="tpu_custom_call" | custom-call | flops 33554432 | bytes 33554432 | tf_op jit(solution)/shard_map/weight_grad/pallas_call | solution.py:690
  (430 shorter events, 130.9 us)
Async XLA Ops:
  58.9 38.9 %collective-permute-start.1 = (bf16[4,4,32,256]{3,2,1,0:T(8,128)(2,1)S(1)}, bf16[4,4,32,256]{3,2,1,0:T(8,128)(2,1)S(1)}, u32[]{:S(2)}, u32[]{:S(2)}) collective-permute-start(bf16[4,4,32,256]{3,2,1,0:T(8,128)(2,1)S(1)} %get-tuple-element.114), channel_id=1, source_target_pairs={{0,1},{1,0},{2,3},{3,2},{4,5},{5,4},{6,7},{7,6},{8,9},{9,8},{10,11... | collective-permute-start | bytes 786440 | tf_op jit(solution)/shard_map/ppermute | solution.py:206
  61.9 35.9 %collective-permute-start.2 = (bf16[4,4,32,256]{3,2,1,0:T(8,128)(2,1)S(1)}, bf16[4,4,32,256]{3,2,1,0:T(8,128)(2,1)S(1)}, u32[]{:S(2)}, u32[]{:S(2)}) collective-permute-start(bf16[4,4,32,256]{3,2,1,0:T(8,128)(2,1)S(1)} %get-tuple-element.116), channel_id=1, source_target_pairs={{0,2},{1,3},{2,0},{3,1},{4,6},{5,7},{6,4},{7,5},{8,10},{9,11},{10,... | collective-permute-start | bytes 786440 | tf_op jit(solution)/shard_map/ppermute | solution.py:206
  63.4 34.4 %collective-permute-start.3 = (bf16[4,4,32,256]{3,2,1,0:T(8,128)(2,1)S(1)}, bf16[4,4,32,256]{3,2,1,0:T(8,128)(2,1)S(1)}, u32[]{:S(2)}, u32[]{:S(2)}) collective-permute-start(bf16[4,4,32,256]{3,2,1,0:T(8,128)(2,1)S(1)} %get-tuple-element.115), channel_id=1, source_target_pairs={{0,3},{1,2},{2,1},{3,0},{4,7},{5,6},{6,5},{7,4},{8,11},{9,10},{10,... | collective-permute-start | bytes 786440 | tf_op jit(solution)/shard_map/ppermute | solution.py:206
  80.1 43.4 %collective-permute-start.10 = (bf16[4,4,32,256]{3,2,1,0:T(8,128)(2,1)}, bf16[4,4,32,256]{3,2,1,0:T(8,128)(2,1)S(1)}, u32[]{:S(2)}, u32[]{:S(2)}) collective-permute-start(bf16[4,4,32,256]{3,2,1,0:T(8,128)(2,1)} %get-tuple-element.118), channel_id=1, source_target_pairs={{0,3},{1,2},{2,1},{3,0},{4,7},{5,6},{6,5},{7,4},{8,11},{9,10},{10,... | collective-permute-start | bytes 786440 | tf_op jit(solution)/shard_map/ppermute | solution.py:206
  83.0 42.6 %collective-permute-start.8 = (bf16[4,4,32,256]{3,2,1,0:T(8,128)(2,1)}, bf16[4,4,32,256]{3,2,1,0:T(8,128)(2,1)S(1)}, u32[]{:S(2)}, u32[]{:S(2)}) collective-permute-start(bf16[4,4,32,256]{3,2,1,0:T(8,128)(2,1)} %get-tuple-element.117), channel_id=1, source_target_pairs={{0,1},{1,0},{2,3},{3,2},{4,5},{5,4},{6,7},{7,6},{8,9},{9,8},{10,11... | collective-permute-start | bytes 786440 | tf_op jit(solution)/shard_map/ppermute | solution.py:206
  97.7 30.4 %collective-permute-start.9 = (bf16[4,4,32,256]{3,2,1,0:T(8,128)(2,1)S(1)}, bf16[4,4,32,256]{3,2,1,0:T(8,128)(2,1)S(1)}, u32[]{:S(2)}, u32[]{:S(2)}) collective-permute-start(bf16[4,4,32,256]{3,2,1,0:T(8,128)(2,1)S(1)} %get-tuple-element.119), channel_id=1, source_target_pairs={{0,2},{1,3},{2,0},{3,1},{4,6},{5,7},{6,4},{7,5},{8,10},{9,11},{10,... | collective-permute-start | bytes 786440 | tf_op jit(solution)/shard_map/ppermute | solution.py:206
  97.8 66.7 %collective-permute-start.14 = (bf16[4,4,4,32,256]{4,3,2,1,0:T(8,128)(2,1)}, bf16[4,4,4,32,256]{4,3,2,1,0:T(8,128)(2,1)S(1)}, u32[]{:S(2)}, u32[]{:S(2)}) collective-permute-start(bf16[4,4,4,32,256]{4,3,2,1,0:T(8,128)(2,1)} %get-tuple-element.49), channel_id=1, source_target_pairs={{0,4},{4,0},{8,12},{12,8},{16,20},{20,16},{24,28},{28,24},{1,5},{5... | collective-permute-start | bytes 3145736 | tf_op jit(solution)/shard_map/ppermute | solution.py:206
  97.9 71.4 %collective-permute-start.21 = (bf16[4,4,4,32,256]{4,3,2,1,0:T(8,128)(2,1)}, bf16[4,4,4,32,256]{4,3,2,1,0:T(8,128)(2,1)S(1)}, u32[]{:S(2)}, u32[]{:S(2)}) collective-permute-start(bf16[4,4,4,32,256]{4,3,2,1,0:T(8,128)(2,1)} %get-tuple-element.51), channel_id=1, source_target_pairs={{0,4},{4,0},{8,12},{12,8},{16,20},{20,16},{24,28},{28,24},{1,5},{5... | collective-permute-start | bytes 3145736 | tf_op jit(solution)/shard_map/ppermute | solution.py:206
  123.5 29.8 %collective-permute-start.4 = (bf16[4,32,256]{2,1,0:T(8,128)(2,1)S(1)}, bf16[4,32,256]{2,1,0:T(8,128)(2,1)S(1)}, u32[]{:S(2)}, u32[]{:S(2)}) collective-permute-start(bf16[4,32,256]{2,1,0:T(8,128)(2,1)S(1)} %get-tuple-element.140), channel_id=1, source_target_pairs={{0,8},{4,12},{8,0},{12,4},{16,24},{20,28},{24,16},{28,20},{1,9},{5... | collective-permute-start | bytes 196616 | tf_op jit(solution)/shard_map/ppermute | solution.py:206
  125.5 28.8 %collective-permute-start.5 = (bf16[4,32,256]{2,1,0:T(8,128)(2,1)S(1)}, bf16[4,32,256]{2,1,0:T(8,128)(2,1)S(1)}, u32[]{:S(2)}, u32[]{:S(2)}) collective-permute-start(bf16[4,32,256]{2,1,0:T(8,128)(2,1)S(1)} %get-tuple-element.142), channel_id=1, source_target_pairs={{0,16},{4,20},{8,24},{12,28},{16,0},{20,4},{24,8},{28,12},{1,17},{... | collective-permute-start | bytes 196616 | tf_op jit(solution)/shard_map/ppermute | solution.py:206
  128.1 29.7 %collective-permute-start.6 = (bf16[4,32,256]{2,1,0:T(8,128)(2,1)S(1)}, bf16[4,32,256]{2,1,0:T(8,128)(2,1)S(1)}, u32[]{:S(2)}, u32[]{:S(2)}) collective-permute-start(bf16[4,32,256]{2,1,0:T(8,128)(2,1)S(1)} %get-tuple-element.141), channel_id=1, source_target_pairs={{0,24},{4,28},{8,16},{12,20},{16,8},{20,12},{24,0},{28,4},{1,25},{... | collective-permute-start | bytes 196616 | tf_op jit(solution)/shard_map/ppermute | solution.py:206
  165.8 30.2 %collective-permute-start.15 = (bf16[4,4,32,256]{3,2,1,0:T(8,128)(2,1)}, bf16[4,4,32,256]{3,2,1,0:T(8,128)(2,1)S(1)}, u32[]{:S(2)}, u32[]{:S(2)}) collective-permute-start(bf16[4,4,32,256]{3,2,1,0:T(8,128)(2,1)} %get-tuple-element.120), channel_id=1, source_target_pairs={{0,1},{1,0},{2,3},{3,2},{4,5},{5,4},{6,7},{7,6},{8,9},{9,8},{10,11... | collective-permute-start | bytes 786440 | tf_op jit(solution)/shard_map/ppermute | solution.py:206
  167.3 29.2 %collective-permute-start.16 = (bf16[4,4,32,256]{3,2,1,0:T(8,128)(2,1)}, bf16[4,4,32,256]{3,2,1,0:T(8,128)(2,1)S(1)}, u32[]{:S(2)}, u32[]{:S(2)}) collective-permute-start(bf16[4,4,32,256]{3,2,1,0:T(8,128)(2,1)} %get-tuple-element.122), channel_id=1, source_target_pairs={{0,2},{1,3},{2,0},{3,1},{4,6},{5,7},{6,4},{7,5},{8,10},{9,11},{10,... | collective-permute-start | bytes 786440 | tf_op jit(solution)/shard_map/ppermute | solution.py:206
  168.8 27.7 %collective-permute-start.17 = (bf16[4,4,32,256]{3,2,1,0:T(8,128)(2,1)S(1)}, bf16[4,4,32,256]{3,2,1,0:T(8,128)(2,1)S(1)}, u32[]{:S(2)}, u32[]{:S(2)}) collective-permute-start(bf16[4,4,32,256]{3,2,1,0:T(8,128)(2,1)S(1)} %get-tuple-element.121), channel_id=1, source_target_pairs={{0,3},{1,2},{2,1},{3,0},{4,7},{5,6},{6,5},{7,4},{8,11},{9,10},{10,... | collective-permute-start | bytes 786440 | tf_op jit(solution)/shard_map/ppermute | solution.py:206
  169.8 28.6 %collective-permute-start.22 = (bf16[4,4,32,256]{3,2,1,0:T(8,128)(2,1)S(1)}, bf16[4,4,32,256]{3,2,1,0:T(8,128)(2,1)S(1)}, u32[]{:S(2)}, u32[]{:S(2)}) collective-permute-start(bf16[4,4,32,256]{3,2,1,0:T(8,128)(2,1)S(1)} %get-tuple-element.123), channel_id=1, source_target_pairs={{0,1},{1,0},{2,3},{3,2},{4,5},{5,4},{6,7},{7,6},{8,9},{9,8},{10,11... | collective-permute-start | bytes 786440 | tf_op jit(solution)/shard_map/ppermute | solution.py:206
  171.4 29.8 %collective-permute-start.23 = (bf16[4,4,32,256]{3,2,1,0:T(8,128)(2,1)S(1)}, bf16[4,4,32,256]{3,2,1,0:T(8,128)(2,1)S(1)}, u32[]{:S(2)}, u32[]{:S(2)}) collective-permute-start(bf16[4,4,32,256]{3,2,1,0:T(8,128)(2,1)S(1)} %get-tuple-element.125), channel_id=1, source_target_pairs={{0,2},{1,3},{2,0},{3,1},{4,6},{5,7},{6,4},{7,5},{8,10},{9,11},{10,... | collective-permute-start | bytes 786440 | tf_op jit(solution)/shard_map/ppermute | solution.py:206
  246.9 16.3 %collective-permute-start.28 = (bf16[4,32,256]{2,1,0:T(8,128)(2,1)}, bf16[4,32,256]{2,1,0:T(8,128)(2,1)}, u32[]{:S(2)}, u32[]{:S(2)}) collective-permute-start(bf16[4,32,256]{2,1,0:T(8,128)(2,1)} %slice.313), channel_id=1, source_target_pairs={{0,8},{4,12},{8,0},{12,4},{16,24},{20,28},{24,16},{28,20},{1,9},{5... | collective-permute-start | bytes 196616 | tf_op jit(solution)/shard_map/ppermute | solution.py:206
  247.7 16.6 %collective-permute-start.29 = (bf16[4,32,256]{2,1,0:T(8,128)(2,1)}, bf16[4,32,256]{2,1,0:T(8,128)(2,1)}, u32[]{:S(2)}, u32[]{:S(2)}) collective-permute-start(bf16[4,32,256]{2,1,0:T(8,128)(2,1)} %slice.313), channel_id=1, source_target_pairs={{0,16},{4,20},{8,24},{12,28},{16,0},{20,4},{24,8},{28,12},{1,17},{... | collective-permute-start | bytes 196616 | tf_op jit(solution)/shard_map/ppermute | solution.py:206
  270.4 21.4 %collective-permute-start.31 = (bf16[4,4,32,256]{3,2,1,0:T(8,128)(2,1)}, bf16[4,4,32,256]{3,2,1,0:T(8,128)(2,1)}, u32[]{:S(2)}, u32[]{:S(2)}) collective-permute-start(bf16[4,4,32,256]{3,2,1,0:T(8,128)(2,1)} %pad_maximum_fusion.1.refs_0_), channel_id=1, source_target_pairs={{0,1},{1,0},{2,3},{3,2},{4,5},{5,4},{6,7},{7,6},{8,9},{9,8},{10,11... | collective-permute-start | bytes 786440 | tf_op jit(solution)/shard_map/ppermute | solution.py:206
  271.0 21.3 %collective-permute-start.32 = (bf16[4,4,32,256]{3,2,1,0:T(8,128)(2,1)}, bf16[4,4,32,256]{3,2,1,0:T(8,128)(2,1)}, u32[]{:S(2)}, u32[]{:S(2)}) collective-permute-start(bf16[4,4,32,256]{3,2,1,0:T(8,128)(2,1)} %pad_maximum_fusion.1.refs_0_), channel_id=1, source_target_pairs={{0,2},{1,3},{2,0},{3,1},{4,6},{5,7},{6,4},{7,5},{8,10},{9,11},{10,... | collective-permute-start | bytes 786440 | tf_op jit(solution)/shard_map/ppermute | solution.py:206
  271.5 23.3 %collective-permute-start.33 = (bf16[4,4,32,256]{3,2,1,0:T(8,128)(2,1)}, bf16[4,4,32,256]{3,2,1,0:T(8,128)(2,1)}, u32[]{:S(2)}, u32[]{:S(2)}) collective-permute-start(bf16[4,4,32,256]{3,2,1,0:T(8,128)(2,1)} %pad_maximum_fusion.1.refs_0_), channel_id=1, source_target_pairs={{0,3},{1,2},{2,1},{3,0},{4,7},{5,6},{6,5},{7,4},{8,11},{9,10},{10,... | collective-permute-start | bytes 786440 | tf_op jit(solution)/shard_map/ppermute | solution.py:206
  274.0 20.8 %collective-permute-start.34 = (bf16[4,4,32,256]{3,2,1,0:T(8,128)(2,1)}, bf16[4,4,32,256]{3,2,1,0:T(8,128)(2,1)}, u32[]{:S(2)}, u32[]{:S(2)}) collective-permute-start(bf16[4,4,32,256]{3,2,1,0:T(8,128)(2,1)} %pad_maximum_fusion.1.refs_0_), channel_id=1, source_target_pairs={{0,4},{4,0},{8,12},{12,8},{16,20},{20,16},{24,28},{28,24},{1,5},{5... | collective-permute-start | bytes 786440 | tf_op jit(solution)/shard_map/ppermute | solution.py:206
  291.3 16.1 %collective-permute-start.61 = (bf16[4,4,32,256]{3,2,1,0:T(8,128)(2,1)}, bf16[4,4,32,256]{3,2,1,0:T(8,128)(2,1)}, u32[]{:S(2)}, u32[]{:S(2)}) collective-permute-start(bf16[4,4,32,256]{3,2,1,0:T(8,128)(2,1)} %pad_maximum_fusion.2.refs_15_.refs_0_), channel_id=1, source_target_pairs={{0,1},{1,0},{2,3},{3,2},{4,5},{5,4},{6,7},{7,6},{8,9},{9,8},{10,11... | collective-permute-start | bytes 786440 | tf_op jit(solution)/shard_map/ppermute | solution.py:206
  291.8 16.1 %collective-permute-start.62 = (bf16[4,4,32,256]{3,2,1,0:T(8,128)(2,1)}, bf16[4,4,32,256]{3,2,1,0:T(8,128)(2,1)}, u32[]{:S(2)}, u32[]{:S(2)}) collective-permute-start(bf16[4,4,32,256]{3,2,1,0:T(8,128)(2,1)} %pad_maximum_fusion.2.refs_15_.refs_0_), channel_id=1, source_target_pairs={{0,2},{1,3},{2,0},{3,1},{4,6},{5,7},{6,4},{7,5},{8,10},{9,11},{10,... | collective-permute-start | bytes 786440 | tf_op jit(solution)/shard_map/ppermute | solution.py:206
  292.3 18.0 %collective-permute-start.63 = (bf16[4,4,32,256]{3,2,1,0:T(8,128)(2,1)}, bf16[4,4,32,256]{3,2,1,0:T(8,128)(2,1)}, u32[]{:S(2)}, u32[]{:S(2)}) collective-permute-start(bf16[4,4,32,256]{3,2,1,0:T(8,128)(2,1)} %pad_maximum_fusion.2.refs_15_.refs_0_), channel_id=1, source_target_pairs={{0,3},{1,2},{2,1},{3,0},{4,7},{5,6},{6,5},{7,4},{8,11},{9,10},{10,... | collective-permute-start | bytes 786440 | tf_op jit(solution)/shard_map/ppermute | solution.py:206
  294.8 16.1 %collective-permute-start.54 = (bf16[4,4,32,256]{3,2,1,0:T(8,128)(2,1)}, bf16[4,4,32,256]{3,2,1,0:T(8,128)(2,1)}, u32[]{:S(2)}, u32[]{:S(2)}) collective-permute-start(bf16[4,4,32,256]{3,2,1,0:T(8,128)(2,1)} %pad_maximum_fusion.4.refs_15_.refs_0_), channel_id=1, source_target_pairs={{0,1},{1,0},{2,3},{3,2},{4,5},{5,4},{6,7},{7,6},{8,9},{9,8},{10,11... | collective-permute-start | bytes 786440 | tf_op jit(solution)/shard_map/ppermute | solution.py:206
  307.4 27.8 %collective-permute-start.55 = (bf16[4,4,32,256]{3,2,1,0:T(8,128)(2,1)}, bf16[4,4,32,256]{3,2,1,0:T(8,128)(2,1)S(1)}, u32[]{:S(2)}, u32[]{:S(2)}) collective-permute-start(bf16[4,4,32,256]{3,2,1,0:T(8,128)(2,1)} %pad_maximum_fusion.4.refs_15_.refs_0_), channel_id=1, source_target_pairs={{0,2},{1,3},{2,0},{3,1},{4,6},{5,7},{6,4},{7,5},{8,10},{9,11},{10,... | collective-permute-start | bytes 786440 | tf_op jit(solution)/shard_map/ppermute | solution.py:206
  307.9 27.9 %collective-permute-start.56 = (bf16[4,4,32,256]{3,2,1,0:T(8,128)(2,1)}, bf16[4,4,32,256]{3,2,1,0:T(8,128)(2,1)S(1)}, u32[]{:S(2)}, u32[]{:S(2)}) collective-permute-start(bf16[4,4,32,256]{3,2,1,0:T(8,128)(2,1)} %pad_maximum_fusion.4.refs_15_.refs_0_), channel_id=1, source_target_pairs={{0,3},{1,2},{2,1},{3,0},{4,7},{5,6},{6,5},{7,4},{8,11},{9,10},{10,... | collective-permute-start | bytes 786440 | tf_op jit(solution)/shard_map/ppermute | solution.py:206
  310.3 25.9 %collective-permute-start.35 = (bf16[4,4,32,256]{3,2,1,0:T(8,128)(2,1)}, bf16[4,4,32,256]{3,2,1,0:T(8,128)(2,1)S(1)}, u32[]{:S(2)}, u32[]{:S(2)}) collective-permute-start(bf16[4,4,32,256]{3,2,1,0:T(8,128)(2,1)} %collective-permute-done.31.refs_1_), channel_id=1, source_target_pairs={{0,4},{4,0},{8,12},{12,8},{16,20},{20,16},{24,28},{28,24},{1,5},{5... | collective-permute-start | bytes 786440 | tf_op jit(solution)/shard_map/ppermute | solution.py:206
  310.3 26.0 %collective-permute-start.36 = (bf16[4,4,32,256]{3,2,1,0:T(8,128)(2,1)}, bf16[4,4,32,256]{3,2,1,0:T(8,128)(2,1)S(1)}, u32[]{:S(2)}, u32[]{:S(2)}) collective-permute-start(bf16[4,4,32,256]{3,2,1,0:T(8,128)(2,1)} %collective-permute-done.32.refs_2_), channel_id=1, source_target_pairs={{0,4},{4,0},{8,12},{12,8},{16,20},{20,16},{24,28},{28,24},{1,5},{5... | collective-permute-start | bytes 786440 | tf_op jit(solution)/shard_map/ppermute | solution.py:206
  310.9 26.0 %collective-permute-start.37 = (bf16[4,4,32,256]{3,2,1,0:T(8,128)(2,1)}, bf16[4,4,32,256]{3,2,1,0:T(8,128)(2,1)S(1)}, u32[]{:S(2)}, u32[]{:S(2)}) collective-permute-start(bf16[4,4,32,256]{3,2,1,0:T(8,128)(2,1)} %collective-permute-done.33.refs_3_), channel_id=1, source_target_pairs={{0,4},{4,0},{8,12},{12,8},{16,20},{20,16},{24,28},{28,24},{1,5},{5... | collective-permute-start | bytes 786440 | tf_op jit(solution)/shard_map/ppermute | solution.py:206
  335.2 41.8 %collective-permute-start.57 = (bf16[4,4,32,256]{3,2,1,0:T(8,128)(2,1)}, bf16[4,4,32,256]{3,2,1,0:T(8,128)(2,1)S(1)}, u32[]{:S(2)}, u32[]{:S(2)}) collective-permute-start(bf16[4,4,32,256]{3,2,1,0:T(8,128)(2,1)} %pad_maximum_fusion.4.refs_15_.refs_0_), channel_id=1, source_target_pairs={{0,4},{4,0},{8,12},{12,8},{16,20},{20,16},{24,28},{28,24},{1,5},{5... | collective-permute-start | bytes 786440 | tf_op jit(solution)/shard_map/ppermute | solution.py:206
  335.7 41.9 %collective-permute-start.44 = (bf16[4,4,32,256]{3,2,1,0:T(8,128)(2,1)S(1)}, bf16[4,4,32,256]{3,2,1,0:T(8,128)(2,1)S(1)}, u32[]{:S(2)}, u32[]{:S(2)}) collective-permute-start(bf16[4,4,32,256]{3,2,1,0:T(8,128)(2,1)S(1)} %pad_maximum_fusion.3.refs_15_.refs_0_), channel_id=1, source_target_pairs={{0,1},{1,0},{2,3},{3,2},{4,5},{5,4},{6,7},{7,6},{8,9},{9,8},{10,11... | collective-permute-start | bytes 786440 | tf_op jit(solution)/shard_map/ppermute | solution.py:206
  336.3 43.8 %collective-permute-start.65 = (bf16[4,4,32,256]{3,2,1,0:T(8,128)(2,1)}, bf16[4,4,32,256]{3,2,1,0:T(8,128)(2,1)S(1)}, u32[]{:S(2)}, u32[]{:S(2)}) collective-permute-start(bf16[4,4,32,256]{3,2,1,0:T(8,128)(2,1)} %collective-permute-done.61.refs_1_), channel_id=1, source_target_pairs={{0,4},{4,0},{8,12},{12,8},{16,20},{20,16},{24,28},{28,24},{1,5},{5... | collective-permute-start | bytes 786440 | tf_op jit(solution)/shard_map/ppermute | solution.py:206
  336.3 43.8 %collective-permute-start.66 = (bf16[4,4,32,256]{3,2,1,0:T(8,128)(2,1)}, bf16[4,4,32,256]{3,2,1,0:T(8,128)(2,1)S(1)}, u32[]{:S(2)}, u32[]{:S(2)}) collective-permute-start(bf16[4,4,32,256]{3,2,1,0:T(8,128)(2,1)} %collective-permute-done.62.refs_2_), channel_id=1, source_target_pairs={{0,4},{4,0},{8,12},{12,8},{16,20},{20,16},{24,28},{28,24},{1,5},{5... | collective-permute-start | bytes 786440 | tf_op jit(solution)/shard_map/ppermute | solution.py:206
  336.8 43.8 %collective-permute-start.67 = (bf16[4,4,32,256]{3,2,1,0:T(8,128)(2,1)}, bf16[4,4,32,256]{3,2,1,0:T(8,128)(2,1)S(1)}, u32[]{:S(2)}, u32[]{:S(2)}) collective-permute-start(bf16[4,4,32,256]{3,2,1,0:T(8,128)(2,1)} %collective-permute-done.63.refs_3_), channel_id=1, source_target_pairs={{0,4},{4,0},{8,12},{12,8},{16,20},{20,16},{24,28},{28,24},{1,5},{5... | collective-permute-start | bytes 786440 | tf_op jit(solution)/shard_map/ppermute | solution.py:206
  377.0 42.3 %collective-permute-start.45 = (bf16[4,4,32,256]{3,2,1,0:T(8,128)(2,1)S(1)}, bf16[4,4,32,256]{3,2,1,0:T(8,128)(2,1)S(1)}, u32[]{:S(2)}, u32[]{:S(2)}) collective-permute-start(bf16[4,4,32,256]{3,2,1,0:T(8,128)(2,1)S(1)} %pad_maximum_fusion.3.refs_15_.refs_0_), channel_id=1, source_target_pairs={{0,2},{1,3},{2,0},{3,1},{4,6},{5,7},{6,4},{7,5},{8,10},{9,11},{10,... | collective-permute-start | bytes 786440 | tf_op jit(solution)/shard_map/ppermute | solution.py:206
  377.6 41.8 %collective-permute-start.46 = (bf16[4,4,32,256]{3,2,1,0:T(8,128)(2,1)S(1)}, bf16[4,4,32,256]{3,2,1,0:T(8,128)(2,1)S(1)}, u32[]{:S(2)}, u32[]{:S(2)}) collective-permute-start(bf16[4,4,32,256]{3,2,1,0:T(8,128)(2,1)S(1)} %pad_maximum_fusion.3.refs_15_.refs_0_), channel_id=1, source_target_pairs={{0,3},{1,2},{2,1},{3,0},{4,7},{5,6},{6,5},{7,4},{8,11},{9,10},{10,... | collective-permute-start | bytes 786440 | tf_op jit(solution)/shard_map/ppermute | solution.py:206
  380.1 39.9 %collective-permute-start.58 = (bf16[4,4,32,256]{3,2,1,0:T(8,128)(2,1)}, bf16[4,4,32,256]{3,2,1,0:T(8,128)(2,1)S(1)}, u32[]{:S(2)}, u32[]{:S(2)}) collective-permute-start(bf16[4,4,32,256]{3,2,1,0:T(8,128)(2,1)} %collective-permute-done.54.refs_1_), channel_id=1, source_target_pairs={{0,4},{4,0},{8,12},{12,8},{16,20},{20,16},{24,28},{28,24},{1,5},{5... | collective-permute-start | bytes 786440 | tf_op jit(solution)/shard_map/ppermute | solution.py:206
  380.1 40.0 %collective-permute-start.59 = (bf16[4,4,32,256]{3,2,1,0:T(8,128)(2,1)S(1)}, bf16[4,4,32,256]{3,2,1,0:T(8,128)(2,1)S(1)}, u32[]{:S(2)}, u32[]{:S(2)}) collective-permute-start(bf16[4,4,32,256]{3,2,1,0:T(8,128)(2,1)S(1)} %collective-permute-done.55.refs_2_), channel_id=1, source_target_pairs={{0,4},{4,0},{8,12},{12,8},{16,20},{20,16},{24,28},{28,24},{1,5},{5... | collective-permute-start | bytes 786440 | tf_op jit(solution)/shard_map/ppermute | solution.py:206
  380.6 39.9 %collective-permute-start.60 = (bf16[4,4,32,256]{3,2,1,0:T(8,128)(2,1)S(1)}, bf16[4,4,32,256]{3,2,1,0:T(8,128)(2,1)S(1)}, u32[]{:S(2)}, u32[]{:S(2)}) collective-permute-start(bf16[4,4,32,256]{3,2,1,0:T(8,128)(2,1)S(1)} %collective-permute-done.56.refs_3_), channel_id=1, source_target_pairs={{0,4},{4,0},{8,12},{12,8},{16,20},{20,16},{24,28},{28,24},{1,5},{5... | collective-permute-start | bytes 786440 | tf_op jit(solution)/shard_map/ppermute | solution.py:206
  419.3 39.7 %collective-permute-start.47 = (bf16[4,4,32,256]{3,2,1,0:T(8,128)(2,1)S(1)}, bf16[4,4,32,256]{3,2,1,0:T(8,128)(2,1)S(1)}, u32[]{:S(2)}, u32[]{:S(2)}) collective-permute-start(bf16[4,4,32,256]{3,2,1,0:T(8,128)(2,1)S(1)} %pad_maximum_fusion.3.refs_15_.refs_0_), channel_id=1, source_target_pairs={{0,4},{4,0},{8,12},{12,8},{16,20},{20,16},{24,28},{28,24},{1,5},{5... | collective-permute-start | bytes 786440 | tf_op jit(solution)/shard_map/ppermute | solution.py:206
  419.5 39.6 %collective-permute-start.48 = (bf16[4,4,32,256]{3,2,1,0:T(8,128)(2,1)S(1)}, bf16[4,4,32,256]{3,2,1,0:T(8,128)(2,1)S(1)}, u32[]{:S(2)}, u32[]{:S(2)}) collective-permute-start(bf16[4,4,32,256]{3,2,1,0:T(8,128)(2,1)S(1)} %collective-permute-done.44.refs_1_), channel_id=1, source_target_pairs={{0,4},{4,0},{8,12},{12,8},{16,20},{20,16},{24,28},{28,24},{1,5},{5... | collective-permute-start | bytes 786440 | tf_op jit(solution)/shard_map/ppermute | solution.py:206
  420.0 39.1 %collective-permute-start.49 = (bf16[4,4,32,256]{3,2,1,0:T(8,128)(2,1)S(1)}, bf16[4,4,32,256]{3,2,1,0:T(8,128)(2,1)S(1)}, u32[]{:S(2)}, u32[]{:S(2)}) collective-permute-start(bf16[4,4,32,256]{3,2,1,0:T(8,128)(2,1)S(1)} %collective-permute-done.45.refs_2_), channel_id=1, source_target_pairs={{0,4},{4,0},{8,12},{12,8},{16,20},{20,16},{24,28},{28,24},{1,5},{5... | collective-permute-start | bytes 786440 | tf_op jit(solution)/shard_map/ppermute | solution.py:206
  420.1 39.1 %collective-permute-start.50 = (bf16[4,4,32,256]{3,2,1,0:T(8,128)(2,1)S(1)}, bf16[4,4,32,256]{3,2,1,0:T(8,128)(2,1)S(1)}, u32[]{:S(2)}, u32[]{:S(2)}) collective-permute-start(bf16[4,4,32,256]{3,2,1,0:T(8,128)(2,1)S(1)} %collective-permute-done.46.refs_3_), channel_id=1, source_target_pairs={{0,4},{4,0},{8,12},{12,8},{16,20},{20,16},{24,28},{28,24},{1,5},{5... | collective-permute-start | bytes 786440 | tf_op jit(solution)/shard_map/ppermute | solution.py:206
  561.6 26.7 %collective-permute-start.72 = (bf16[4,4,4,32,256]{4,3,2,1,0:T(8,128)(2,1)}, bf16[4,4,4,32,256]{4,3,2,1,0:T(8,128)(2,1)}, u32[]{:S(2)}, u32[]{:S(2)}) collective-permute-start(bf16[4,4,4,32,256]{4,3,2,1,0:T(8,128)(2,1)} %get-tuple-element.63), channel_id=1, source_target_pairs={{0,4},{4,0},{8,12},{12,8},{16,20},{20,16},{24,28},{28,24},{1,5},{5... | collective-permute-start | bytes 3145736 | tf_op jit(solution)/shard_map/ppermute | solution.py:206
  590.0 29.4 %collective-permute-start.78 = (bf16[4,4,32,256]{3,2,1,0:T(8,128)(2,1)S(1)}, bf16[4,4,32,256]{3,2,1,0:T(8,128)(2,1)S(1)}, u32[]{:S(2)}, u32[]{:S(2)}) collective-permute-start(bf16[4,4,32,256]{3,2,1,0:T(8,128)(2,1)S(1)} %get-tuple-element.107), channel_id=1, source_target_pairs={{0,1},{1,0},{2,3},{3,2},{4,5},{5,4},{6,7},{7,6},{8,9},{9,8},{10,11... | collective-permute-start | bytes 786440 | tf_op jit(solution)/shard_map/ppermute | solution.py:206
  590.6 31.8 %collective-permute-start.79 = (bf16[4,4,32,256]{3,2,1,0:T(8,128)(2,1)S(1)}, bf16[4,4,32,256]{3,2,1,0:T(8,128)(2,1)S(1)}, u32[]{:S(2)}, u32[]{:S(2)}) collective-permute-start(bf16[4,4,32,256]{3,2,1,0:T(8,128)(2,1)S(1)} %get-tuple-element.109), channel_id=1, source_target_pairs={{0,2},{1,3},{2,0},{3,1},{4,6},{5,7},{6,4},{7,5},{8,10},{9,11},{10,... | collective-permute-start | bytes 786440 | tf_op jit(solution)/shard_map/ppermute | solution.py:206
  590.6 31.8 %collective-permute-start.80 = (bf16[4,4,32,256]{3,2,1,0:T(8,128)(2,1)S(1)}, bf16[4,4,32,256]{3,2,1,0:T(8,128)(2,1)S(1)}, u32[]{:S(2)}, u32[]{:S(2)}) collective-permute-start(bf16[4,4,32,256]{3,2,1,0:T(8,128)(2,1)S(1)} %get-tuple-element.108), channel_id=1, source_target_pairs={{0,3},{1,2},{2,1},{3,0},{4,7},{5,6},{6,5},{7,4},{8,11},{9,10},{10,... | collective-permute-start | bytes 786440 | tf_op jit(solution)/shard_map/ppermute | solution.py:206
  594.1 34.0 %collective-permute-start.75 = (bf16[4,4,32,256]{3,2,1,0:T(8,128)(2,1)S(1)}, bf16[4,4,32,256]{3,2,1,0:T(8,128)(2,1)S(1)}, u32[]{:S(2)}, u32[]{:S(2)}) collective-permute-start(bf16[4,4,32,256]{3,2,1,0:T(8,128)(2,1)S(1)} %get-tuple-element.98), channel_id=1, source_target_pairs={{0,1},{1,0},{2,3},{3,2},{4,5},{5,4},{6,7},{7,6},{8,9},{9,8},{10,11... | collective-permute-start | bytes 786440 | tf_op jit(solution)/shard_map/ppermute | solution.py:206
  594.7 33.9 %collective-permute-start.76 = (bf16[4,4,32,256]{3,2,1,0:T(8,128)(2,1)S(1)}, bf16[4,4,32,256]{3,2,1,0:T(8,128)(2,1)S(1)}, u32[]{:S(2)}, u32[]{:S(2)}) collective-permute-start(bf16[4,4,32,256]{3,2,1,0:T(8,128)(2,1)S(1)} %get-tuple-element.100), channel_id=1, source_target_pairs={{0,2},{1,3},{2,0},{3,1},{4,6},{5,7},{6,4},{7,5},{8,10},{9,11},{10,... | collective-permute-start | bytes 786440 | tf_op jit(solution)/shard_map/ppermute | solution.py:206
  622.4 61.6 %collective-permute-start.73 = (bf16[4,4,4,32,256]{4,3,2,1,0:T(8,128)(2,1)}, bf16[4,4,4,32,256]{4,3,2,1,0:T(8,128)(2,1)S(1)}, u32[]{:S(2)}, u32[]{:S(2)}) collective-permute-start(bf16[4,4,4,32,256]{4,3,2,1,0:T(8,128)(2,1)} %get-tuple-element.65), channel_id=1, source_target_pairs={{0,4},{4,0},{8,12},{12,8},{16,20},{20,16},{24,28},{28,24},{1,5},{5... | collective-permute-start | bytes 3145736 | tf_op jit(solution)/shard_map/ppermute | solution.py:206
  624.3 51.8 %collective-permute-start.93 = (bf16[4,32,256]{2,1,0:T(8,128)(2,1)}, bf16[4,32,256]{2,1,0:T(8,128)(2,1)S(1)}, u32[]{:S(2)}, u32[]{:S(2)}) collective-permute-start(bf16[4,32,256]{2,1,0:T(8,128)(2,1)} %get-tuple-element.128), channel_id=1, source_target_pairs={{0,8},{4,12},{8,0},{12,4},{16,24},{20,28},{24,16},{28,20},{1,9},{5... | collective-permute-start | bytes 196616 | tf_op jit(solution)/shard_map/ppermute | solution.py:206
  628.1 49.5 %collective-permute-start.94 = (bf16[4,32,256]{2,1,0:T(8,128)(2,1)S(1)}, bf16[4,32,256]{2,1,0:T(8,128)(2,1)S(1)}, u32[]{:S(2)}, u32[]{:S(2)}) collective-permute-start(bf16[4,32,256]{2,1,0:T(8,128)(2,1)S(1)} %get-tuple-element.130), channel_id=1, source_target_pairs={{0,16},{4,20},{8,24},{12,28},{16,0},{20,4},{24,8},{28,12},{1,17},{... | collective-permute-start | bytes 196616 | tf_op jit(solution)/shard_map/ppermute | solution.py:206
  628.6 50.8 %collective-permute-start.95 = (bf16[4,32,256]{2,1,0:T(8,128)(2,1)S(1)}, bf16[4,32,256]{2,1,0:T(8,128)(2,1)S(1)}, u32[]{:S(2)}, u32[]{:S(2)}) collective-permute-start(bf16[4,32,256]{2,1,0:T(8,128)(2,1)S(1)} %get-tuple-element.129), channel_id=1, source_target_pairs={{0,24},{4,28},{8,16},{12,20},{16,8},{20,12},{24,0},{28,4},{1,25},{... | collective-permute-start | bytes 196616 | tf_op jit(solution)/shard_map/ppermute | solution.py:206
  630.7 49.6 %collective-permute-start.96 = (bf16[4,32,256]{2,1,0:T(8,128)(2,1)S(1)}, bf16[4,32,256]{2,1,0:T(8,128)(2,1)S(1)}, u32[]{:S(2)}, u32[]{:S(2)}) collective-permute-start(bf16[4,32,256]{2,1,0:T(8,128)(2,1)S(1)} %get-tuple-element.131), channel_id=1, source_target_pairs={{0,8},{4,12},{8,0},{12,4},{16,24},{20,28},{24,16},{28,20},{1,9},{5... | collective-permute-start | bytes 196616 | tf_op jit(solution)/shard_map/ppermute | solution.py:206
  679.4 27.6 %collective-permute-start.81 = (bf16[4,4,4,32,256]{4,3,2,1,0:T(8,128)(2,1)}, bf16[4,4,4,32,256]{4,3,2,1,0:T(8,128)(2,1)S(1)}, u32[]{:S(2)}, u32[]{:S(2)}) collective-permute-start(bf16[4,4,4,32,256]{4,3,2,1,0:T(8,128)(2,1)} %get-tuple-element.74), channel_id=1, source_target_pairs={{0,4},{4,0},{8,12},{12,8},{16,20},{20,16},{24,28},{28,24},{1,5},{5... | collective-permute-start | bytes 3145736 | tf_op jit(solution)/shard_map/ppermute | solution.py:206
  684.5 25.0 %collective-permute-start.82 = (bf16[4,4,32,256]{3,2,1,0:T(8,128)(2,1)S(1)}, bf16[4,4,32,256]{3,2,1,0:T(8,128)(2,1)S(1)}, u32[]{:S(2)}, u32[]{:S(2)}) collective-permute-start(bf16[4,4,32,256]{3,2,1,0:T(8,128)(2,1)S(1)} %get-tuple-element.101), channel_id=1, source_target_pairs={{0,1},{1,0},{2,3},{3,2},{4,5},{5,4},{6,7},{7,6},{8,9},{9,8},{10,11... | collective-permute-start | bytes 786440 | tf_op jit(solution)/shard_map/ppermute | solution.py:206
  685.1 25.9 %collective-permute-start.83 = (bf16[4,4,32,256]{3,2,1,0:T(8,128)(2,1)S(1)}, bf16[4,4,32,256]{3,2,1,0:T(8,128)(2,1)S(1)}, u32[]{:S(2)}, u32[]{:S(2)}) collective-permute-start(bf16[4,4,32,256]{3,2,1,0:T(8,128)(2,1)S(1)} %get-tuple-element.103), channel_id=1, source_target_pairs={{0,2},{1,3},{2,0},{3,1},{4,6},{5,7},{6,4},{7,5},{8,10},{9,11},{10,... | collective-permute-start | bytes 786440 | tf_op jit(solution)/shard_map/ppermute | solution.py:206
  686.6 24.5 %collective-permute-start.84 = (bf16[4,4,32,256]{3,2,1,0:T(8,128)(2,1)S(1)}, bf16[4,4,32,256]{3,2,1,0:T(8,128)(2,1)S(1)}, u32[]{:S(2)}, u32[]{:S(2)}) collective-permute-start(bf16[4,4,32,256]{3,2,1,0:T(8,128)(2,1)S(1)} %get-tuple-element.102), channel_id=1, source_target_pairs={{0,3},{1,2},{2,1},{3,0},{4,7},{5,6},{6,5},{7,4},{8,11},{9,10},{10,... | collective-permute-start | bytes 786440 | tf_op jit(solution)/shard_map/ppermute | solution.py:206
  707.5 24.5 %collective-permute-start.85 = (bf16[4,4,32,256]{3,2,1,0:T(8,128)(2,1)S(1)}, bf16[4,4,32,256]{3,2,1,0:T(8,128)(2,1)S(1)}, u32[]{:S(2)}, u32[]{:S(2)}) collective-permute-start(bf16[4,4,32,256]{3,2,1,0:T(8,128)(2,1)S(1)} %get-tuple-element.104), channel_id=1, source_target_pairs={{0,1},{1,0},{2,3},{3,2},{4,5},{5,4},{6,7},{7,6},{8,9},{9,8},{10,11... | collective-permute-start | bytes 786440 | tf_op jit(solution)/shard_map/ppermute | solution.py:206
  708.1 23.9 %collective-permute-start.86 = (bf16[4,4,32,256]{3,2,1,0:T(8,128)(2,1)S(1)}, bf16[4,4,32,256]{3,2,1,0:T(8,128)(2,1)S(1)}, u32[]{:S(2)}, u32[]{:S(2)}) collective-permute-start(bf16[4,4,32,256]{3,2,1,0:T(8,128)(2,1)S(1)} %get-tuple-element.106), channel_id=1, source_target_pairs={{0,2},{1,3},{2,0},{3,1},{4,6},{5,7},{6,4},{7,5},{8,10},{9,11},{10,... | collective-permute-start | bytes 786440 | tf_op jit(solution)/shard_map/ppermute | solution.py:206
  709.6 22.4 %collective-permute-start.87 = (bf16[4,4,32,256]{3,2,1,0:T(8,128)(2,1)S(1)}, bf16[4,4,32,256]{3,2,1,0:T(8,128)(2,1)S(1)}, u32[]{:S(2)}, u32[]{:S(2)}) collective-permute-start(bf16[4,4,32,256]{3,2,1,0:T(8,128)(2,1)S(1)} %get-tuple-element.105), channel_id=1, source_target_pairs={{0,3},{1,2},{2,1},{3,0},{4,7},{5,6},{6,5},{7,4},{8,11},{9,10},{10,... | collective-permute-start | bytes 786440 | tf_op jit(solution)/shard_map/ppermute | solution.py:206
  777.1 25.4 %collective-permute-start.92 = (f32[40,128]{1,0:T(8,128)S(1)}, f32[40,128]{1,0:T(8,128)S(1)}, u32[]{:S(2)}, u32[]{:S(2)}) collective-permute-start(f32[40,128]{1,0:T(8,128)S(1)} %add.405), channel_id=1, source_target_pairs={{0,2},{1,3},{2,0},{3,1},{4,6},{5,7},{6,4},{7,5},{8,10},{9,11},{10,... | collective-permute-start | bytes 61448 | tf_op jit(solution)/shard_map/ppermute | solution.py:707
  (95 other events, 1307.4 us)

commit v2 on v1

v2 whole, which is shorter than its diff:
```python
import functools
import math

import jax
import jax.numpy as jnp
from jax import lax
from jax.experimental import pallas as pl
from jax.experimental.pallas import tpu as pltpu
from jax.sharding import PartitionSpec as P

F32 = jnp.float32
BF16 = jnp.bfloat16
CORES = 2
LANES = 128
VMEM_LIMIT = 56 * 1024 * 1024
PARTS = 2
CHUNK = 256


def params():
    return pltpu.CompilerParams(
        vmem_limit_bytes=VMEM_LIMIT, dimension_semantics=("arbitrary",)
    )


def whole(shape):
    return pl.BlockSpec(shape, lambda i: (0,) * len(shape), pipeline_mode=pl.Buffered(1))


ANY = pl.BlockSpec(memory_space=pl.ANY)


def cost(flops, moved):
    return pl.CostEstimate(flops=flops, bytes_accessed=moved, transcendentals=0)


def dot(a, b):
    return jnp.dot(a, b, preferred_element_type=F32)


def frequencies(mode_index, mode_total):
    return jnp.where(mode_index < mode_total // 2, mode_index, mode_index - mode_total)


def twiddle(product, length):
    phases = (product % length).astype(F32) * (2.0 * math.pi / length)
    return jnp.cos(phases).astype(BF16).astype(F32), jnp.sin(phases).astype(BF16).astype(F32)


def halo(lay, block):
    sizes = {"gy": lay.n_gy, "gz": lay.n_gz}

    def cut(dim, step):
        count = block.shape[dim]
        return slice(None) if step == 0 else slice(count - 2, count) if step > 0 else slice(0, 2)

    def moved(y_step, z_step):
        pairs = [
            (y * lay.n_gz + z, (y + y_step) * lay.n_gz + z + z_step)
            for y in range(sizes["gy"])
            for z in range(sizes["gz"])
            if 0 <= y + y_step < sizes["gy"] and 0 <= z + z_step < sizes["gz"]
        ]
        return lax.ppermute(block[:, cut(1, y_step), cut(2, z_step)], ("gy", "gz"), pairs)

    steps = [(1, 0), (-1, 0), (0, 1), (0, -1), (1, 1), (1, -1), (-1, 1), (-1, -1)]
    return [moved(*step) for step in steps]


class Layout:
    def __init__(self, field_in, spectral_weight):
        self.channels, self.rows, self.depth, self.width = field_in.shape
        self.kz, self.ky, self.mx = spectral_weight.shape[:3]
        self.n_gy, self.n_gz = lax.axis_size("gy"), lax.axis_size("gz")
        self.chips = self.n_gy // CORES
        self.ny, self.nz = self.rows * self.n_gy, self.depth * self.n_gz
        self.my, self.mz = self.ky * self.n_gy, self.kz * self.n_gz
        self.cells = self.rows * self.depth
        self.modes = self.my * self.mz
        self.pack = LANES // self.mx
        self.groups = self.channels // self.pack
        self.own = self.ky * self.kz
        self.band = min(LANES // self.depth, self.rows)
        self.blocks = self.rows // self.band
        self.step = min(LANES // self.rows, self.kz)
        self.tile = 8
        self.gy, self.gz = lax.axis_index("gy"), lax.axis_index("gz")
        self.y0 = self.gy * self.rows
        self.z0 = self.gz * self.depth

    def grid_table(self, mode, cell, first, length, same):
        real, imag = twiddle(mode * (first + cell[0]), length)
        return jnp.where(same, jnp.where(cell[1] == 0, real, imag), 0.0).astype(BF16)

    def grid_tables(self):
        core, chip = self.gy % CORES, self.gy // CORES

        def iotas(rows, columns):
            shape = (rows, columns)
            row = lax.broadcasted_iota(jnp.int32, shape, 0)
            return row, lax.broadcasted_iota(jnp.int32, shape, 1)

        def kz(n):
            return frequencies(((n // self.kz) ^ self.gz) * self.kz + n % self.kz, self.mz)

        def ky(n):
            h, f = n // (self.chips * self.ky), n // self.ky % self.chips
            return frequencies(((f ^ chip) * CORES + (h ^ core)) * self.ky + n % self.ky, self.my)

        band, step, depth = self.band, self.step, self.depth
        z_modes, y_modes = self.mz * band, self.my * step
        z_cells, y_cells = band * depth, self.blocks * step * band
        m, c = iotas(z_modes, 2 * z_cells)
        z_forward = self.grid_table(
            kz(m // band), (c % depth, c // z_cells), self.z0, self.nz,
            m % band == c // depth % band,
        )
        c, m = iotas(z_cells, 2 * z_modes)
        z_back = self.grid_table(
            kz(m % z_modes // band), (c % depth, m // z_modes), self.z0, self.nz,
            m % band == c // depth,
        )

        def row_of(c):
            return c // (step * band) % self.blocks * band + c % band

        m, c = iotas(y_modes, 2 * y_cells)
        y_forward = self.grid_table(
            ky(m // step), (row_of(c), c // y_cells), self.y0, self.ny,
            m % step == c // band % step,
        )
        c, m = iotas(y_cells, 2 * y_modes)
        y_back = self.grid_table(
            ky(m % y_modes // step), (row_of(c), m // y_modes), self.y0, self.ny,
            m % step == c // band % step,
        )
        return z_forward, y_forward, y_back, z_back

    def x_tables(self):
        shape = (self.width, 2 * LANES)
        x = lax.broadcasted_iota(jnp.int32, shape, 0)
        lane = lax.broadcasted_iota(jnp.int32, shape, 1)
        cos, sin = twiddle(x * frequencies(lane % self.mx, self.mx), self.width)
        table = jnp.where(lane < LANES, cos, -sin).astype(BF16)
        owner = lane % LANES // self.mx
        forward = [jnp.where(owner == c, table, 0) for c in range(self.pack)]
        lane, x = (lax.broadcasted_iota(jnp.int32, shape[::-1], d) for d in range(2))
        cos, sin = twiddle(x * frequencies(lane % self.mx, self.mx), self.width)
        table = jnp.where(lane < LANES, cos, -sin).astype(BF16)
        owner = lane % LANES // self.mx
        inverse = [jnp.where(owner == c, table, 0) for c in range(self.pack)]
        return jnp.concatenate(forward, axis=0), jnp.concatenate(inverse, axis=1)


def turn(values, sign):
    real, imag = values[:, :LANES], values[:, LANES:]
    return jnp.concatenate([imag, -real] if sign > 0 else [-imag, real], axis=1)


def z_transform(x_modes, table_ref, part_ref, n):
    x_modes = x_modes.astype(BF16)
    rhs = jnp.concatenate([x_modes, turn(x_modes, 1)], axis=0)
    modes = dot(table_ref[...], rhs).astype(BF16)
    steps, _, _, size, _ = part_ref.shape
    part_ref[:, 0, n] = modes.reshape(steps, size, 2 * LANES)
    part_ref[:, 1, n] = turn(modes, 1).reshape(steps, size, 2 * LANES)


def y_transform(table_ref, part_ref, own_ref, send_ref):
    half = table_ref.shape[0] // 2
    steps, _, blocks, size, _ = part_ref.shape
    chips = own_ref.shape[1]
    rows = half // chips
    per = steps // own_ref.shape[0]
    for q in range(steps):
        modes = dot(table_ref[...], part_ref[q].reshape(2 * blocks * size, 2 * LANES))
        modes = modes.astype(BF16)
        here = pl.ds(q % per * rows, rows)
        own_ref[q // per, :, 0, here] = modes[:half].reshape(chips, rows, 2 * LANES)
        send_ref[q // per, :, 0, here] = modes[half:].reshape(chips, rows, 2 * LANES)


def x_transform(source_ref, x_ref):
    pack, rows, depth, width = source_ref.shape
    cells = [source_ref[c].reshape(rows * depth, width) for c in range(pack)]
    return dot(jnp.concatenate(cells, axis=1), x_ref[...])


def modes_kernel(n_after, field_ref, x_ref, z_ref, y_ref, *refs):
    own_ref, send_ref, part_ref = refs[n_after:]
    total = x_transform(field_ref, x_ref)
    blocks = part_ref.shape[2]
    size = total.shape[0] // blocks
    for n in range(blocks):
        z_transform(total[n * size : (n + 1) * size], z_ref, part_ref, n)
    y_transform(y_ref, part_ref, own_ref, send_ref)


def mode_blocks(lay, count):
    shape = (lay.n_gz, lay.chips, count, lay.own, 2 * LANES)
    spec = pl.BlockSpec((lay.n_gz, lay.chips, 1, lay.own, 2 * LANES), lambda i: (0, 0, i, 0, 0))
    return jax.ShapeDtypeStruct(shape, BF16), spec


def part_scratch(lay):
    size = lay.step * lay.band
    return pltpu.VMEM((lay.mz // lay.step, 2, lay.blocks, size, 2 * LANES), BF16)


def forward_modes(lay, field_in, x_table, tables, first, count, after=()):
    out, spec = mode_blocks(lay, count)
    block = (lay.pack, lay.rows, lay.depth, lay.width)
    volume = lay.pack * lay.cells * lay.width
    return pl.pallas_call(
        functools.partial(modes_kernel, len(after)),
        grid=(count,),
        in_specs=[
            pl.BlockSpec(block, lambda i: (first + i, 0, 0, 0)),
            whole(x_table.shape),
            whole(tables[0].shape),
            whole(tables[1].shape),
        ]
        + [ANY] * len(after),
        out_specs=[spec, spec],
        out_shape=[out, out],
        scratch_shapes=[part_scratch(lay)],
        compiler_params=params(),
        cost_estimate=cost(count * volume * 2 * 2 * LANES, count * volume * 3),
        name="forward_modes",
    )(field_in, x_table, tables[0], tables[1], *after)


def exchange(value, axis, distance):
    count = lax.axis_size(axis)
    return lax.ppermute(value, axis, [(i, i ^ distance) for i in range(count)])


def sum_kernel(n_in, n_out, factor, *refs):
    total = refs[0][...].astype(F32)
    for ref in refs[1:n_in]:
        total = total + ref[...].astype(F32)
    total = (total * factor).astype(BF16)
    for n, out_ref in enumerate(refs[-n_out:]):
        out_ref[...] = total[n] if n_out > 1 else total


def sum_blocks(values, split, factor=1.0, after=()):
    shape = values[0].shape
    out = shape[1:] if split else shape
    count = shape[-3]

    def spec(sizes):
        lead = len(sizes) - 3
        block = sizes[:lead] + (1,) + sizes[lead + 1 :]
        return pl.BlockSpec(block, lambda i: (0,) * lead + (i, 0, 0))

    n_out = shape[0] if split else 1
    total = math.prod(shape)
    outs = pl.pallas_call(
        functools.partial(sum_kernel, len(values), n_out, factor),
        grid=(count,),
        in_specs=[spec(shape)] * len(values) + [ANY] * len(after),
        out_specs=[spec(out)] * n_out,
        out_shape=[jax.ShapeDtypeStruct(out, BF16)] * n_out,
        compiler_params=params(),
        cost_estimate=cost(total * len(values), total * 2 * (len(values) + 1)),
        name="sum_blocks",
    )(*values, *after)
    return list(outs)


def from_cores(own, send, after=()):
    return sum_blocks([own, exchange(send, "gy", 1)], True, after=after)


def from_depth(blocks, after=()):
    return sum_blocks(
        blocks[:1] + [exchange(block, "gz", d) for d, block in enumerate(blocks) if d], True,
        after=after,
    )


def from_chips(blocks, factor, after=()):
    got = [exchange(block, "gy", d * CORES) for d, block in enumerate(blocks) if d]
    return sum_blocks(blocks[:1] + got, False, factor, after)[0]


def stack_kernel(n_in, *refs):
    for n in range(n_in):
        refs[-1][n] = refs[n][...]


def stack_blocks(values, after=()):
    shape = values[0].shape
    count = shape[-3]

    def spec(sizes):
        lead = len(sizes) - 3
        block = sizes[:lead] + (1,) + sizes[lead + 1 :]
        return pl.BlockSpec(block, lambda i: (0,) * lead + (i, 0, 0))

    out = (len(values),) + shape
    return pl.pallas_call(
        functools.partial(stack_kernel, len(values)),
        grid=(count,),
        in_specs=[spec(shape)] * len(values) + [ANY] * len(after),
        out_specs=spec(out),
        out_shape=jax.ShapeDtypeStruct(out, BF16),
        compiler_params=params(),
        cost_estimate=cost(math.prod(out), 4 * math.prod(out)),
        name="stack_blocks",
    )(*values, *after)


def spread_chips(lay, mine):
    return stack_blocks([mine] + [exchange(mine, "gy", d * CORES) for d in range(1, lay.chips)])


def spread_depth(lay, column, after=()):
    pieces = [column] + [exchange(column, "gz", d) for d in range(1, lay.n_gz)]
    return stack_blocks(pieces, after)


def by_mode(lay, modes):
    count = modes.shape[0]
    split = modes.reshape(
        count, lay.kz // lay.step, lay.ky, lay.step, 2, lay.pack, lay.mx
    )
    return jnp.transpose(split, (1, 3, 2, 4, 6, 0, 5)).reshape(
        lay.kz, lay.ky, 2 * lay.mx, count * lay.pack
    )


def by_group(lay, modes):
    split = modes.reshape(
        lay.kz // lay.step, lay.step, lay.ky, lay.mx, 2, lay.groups, lay.pack
    )
    return jnp.transpose(split, (5, 0, 2, 1, 4, 6, 3)).reshape(
        lay.groups, lay.own, 2 * LANES
    )


def mix_kernel(modes_ref, weight_ref, *refs):
    out_ref = refs[-1]
    pair, count, channels, wide = weight_ref.shape[1:]
    per = wide // channels
    spread = []
    for a in range(pair):
        modes = jnp.concatenate([modes_ref[0, a]] * per, axis=1)
        row = lax.broadcasted_iota(jnp.int32, modes.shape, 0) % count
        owner = lax.broadcasted_iota(jnp.int32, modes.shape, 1) // channels
        zero = jnp.zeros_like(modes)
        parts = [jnp.where(row == owner + n * per, modes, zero) for n in range(count // per)]
        spread.append(jnp.concatenate(parts, axis=1))
    weights = [weight_ref[0, a].reshape(count * channels, wide) for a in range(pair)]
    mixed = dot(jnp.concatenate(spread, axis=0), jnp.concatenate(weights, axis=1))
    for a in range(pair):
        own = mixed[2 * count * a : 2 * count * (a + 1), wide * a : wide * (a + 1)]
        real, imag = own[:count], own[count:]
        turned = jnp.concatenate([-imag[:, channels:], imag[:, :channels]], axis=1)
        out_ref[0, a] = (real + turned).astype(BF16)


def mode_spec(lay, shape):
    per = lay.ky // 2
    return pl.BlockSpec((1, 2) + shape, lambda i: (i // per, i % per) + (0,) * len(shape))


def mix_modes(lay, modes_in, spectral_weight, after=()):
    shape = (lay.mx, 2 * lay.channels)
    return pl.pallas_call(
        mix_kernel,
        grid=(lay.own // 2,),
        in_specs=[mode_spec(lay, modes_in.shape[2:]), mode_spec(lay, spectral_weight.shape[2:])]
        + [ANY] * len(after),
        out_specs=mode_spec(lay, shape),
        out_shape=jax.ShapeDtypeStruct((lay.kz, lay.ky) + shape, BF16),
        compiler_params=params(),
        cost_estimate=cost(spectral_weight.size * 8, spectral_weight.size * 2),
        name="mix_modes",
    )(modes_in, spectral_weight, *after)


def pointwise_kernel(tile, field_ref, weight_ref, bias_ref, *refs):
    out_ref, blocks_ref, shift_ref = refs[-3:]
    channels, rows, depth, width = field_ref.shape

    @pl.when(pl.program_id(0) == 0)
    def _():
        shape = (tile * channels, channels)
        split = lax.broadcasted_iota(jnp.int32, shape, 0) // tile
        split = split == lax.broadcasted_iota(jnp.int32, shape, 1)
        shift = jnp.sum(jnp.where(split, bias_ref[...], 0.0), axis=1, keepdims=True)
        shift_ref[...] = jnp.broadcast_to(shift, shift_ref.shape)
        split = split.astype(BF16)
        wide = dot(split, weight_ref[...]).astype(BF16)
        wide = lax.dot_general(
            wide, split, (((1,), (1,)), ((), ())), preferred_element_type=F32
        )
        row = lax.broadcasted_iota(jnp.int32, wide.shape, 0) % tile
        column = lax.broadcasted_iota(jnp.int32, wide.shape, 1) % tile
        blocks_ref[...] = jnp.where(row == column, wide, 0.0).astype(BF16)

    for y in range(rows):
        for z in range(0, depth, tile):
            cells = field_ref[:, y, z : z + tile, :].reshape(channels * tile, width)
            mixed = (dot(blocks_ref[...], cells) + shift_ref[...]).astype(BF16)
            out_ref[:, y, z : z + tile, :] = mixed.reshape(channels, tile, width)


def pointwise(lay, field_in, weight, bias, first, count, done=None, after=()):
    span = 2
    size = lay.channels * lay.tile
    given = [] if done is None else [done]
    block = pl.BlockSpec(
        (lay.channels, span, lay.depth, lay.width), lambda i: (0, first // span + i, 0, 0)
    )
    return pl.pallas_call(
        functools.partial(pointwise_kernel, lay.tile),
        grid=(count // span,),
        in_specs=[block, whole(weight.shape), whole(bias.shape)]
        + [ANY] * (len(given) + len(after)),
        out_specs=block,
        out_shape=jax.ShapeDtypeStruct(field_in.shape, BF16),
        scratch_shapes=[pltpu.VMEM((size, size), BF16), pltpu.VMEM((size, lay.width), F32)],
        input_output_aliases={3: 0} if given else {},
        compiler_params=params(),
        cost_estimate=cost(
            2 * size * lay.channels * count * lay.depth * lay.width,
            4 * lay.channels * count * lay.depth * lay.width,
        ),
        name="pointwise",
    )(field_in, weight, bias, *given, *after)


def gelu_and_slope(v):
    bell = jnp.exp2(v * v * (-0.5 * math.log2(math.e)))
    base = 1.0 + jnp.abs(v) * (0.3275911 / math.sqrt(2.0))
    t = pl.reciprocal(base, approx=True)
    poly = 0.5 * 1.061405429
    for coefficient in (-1.453152027, 1.421413741, -0.284496736, 0.254829592):
        poly = poly * t + 0.5 * coefficient
    tail = poly * t * bell
    cdf = jnp.where(v >= 0.0, 1.0 - tail, tail)
    return v * cdf, cdf + v * (bell * (1.0 / math.sqrt(2.0 * math.pi)))


def dense_kernel(
    first, own_ref, other_ref, y_ref, z_ref, x_ref, point_ref, weight_ref, b_in_ref, *refs
):
    hidden_ref, slope_ref, b_ref, part_ref, even_ref, odd_ref = refs[-6:]
    pack, rows, depth, width = point_ref.shape
    blocks, _, steps, size, _ = part_ref.shape
    band = rows // blocks
    step = pl.program_id(0)

    @pl.when(step == 0)
    def _():
        b_ref[...] = b_in_ref[...]

    depths, chips = own_ref.shape[:2]
    per = steps // depths
    rows_here = own_ref.shape[3] // per
    for q in range(steps):
        here = pl.ds(q % per * rows_here, rows_here)
        chunks = [
            piece[q // per, :, 0, here].reshape(chips * rows_here, 2 * LANES)
            for piece in (own_ref, other_ref)
        ]
        modes = jnp.concatenate(chunks, axis=0)
        back = dot(y_ref[...], jnp.concatenate([modes, turn(modes, -1)], axis=0)).astype(BF16)
        part_ref[:, 0, q] = back.reshape(blocks, size, 2 * LANES)
        part_ref[:, 1, q] = turn(back, -1).reshape(blocks, size, 2 * LANES)
    channel = (first + step) * pack

    per = even_ref.shape[0] // (band * depth)
    span = per * band
    count = rows // span

    def spectral(out_ref, n):
        cells = [
            dot(z_ref[...], part_ref[n * per + m].reshape(2 * steps * size, 2 * LANES))
            for m in range(per)
        ]
        out_ref[...] = dot(jnp.concatenate(cells, axis=0).astype(BF16), x_ref[...])

    def activate(spectral_ref, n):
        for m in range(span):
            y = n * span + m
            parts = [b_ref[b, y] for b in range(3)]
            for c in range(pack):
                value = spectral_ref[m * depth : (m + 1) * depth, c * width : (c + 1) * width]
                value = value + point_ref[c, y].astype(F32)
                hidden, slope = gelu_and_slope(value)
                hidden = hidden.astype(BF16)
                hidden_ref[c, y] = hidden
                slope_ref[c, y] = slope.astype(BF16)
                hidden = hidden.astype(F32)
                parts = [parts[b] + hidden * weight_ref[channel + c, b] for b in range(3)]
            for b in range(3):
                b_ref[b, y] = parts[b]

    spectral(even_ref, 0)
    if count == 1:
        activate(even_ref, 0)
        return

    def body(m, carry):
        spectral(odd_ref, 2 * m + 1)
        activate(even_ref, 2 * m)
        spectral(even_ref, jnp.minimum(2 * m + 2, count - 1))
        activate(odd_ref, 2 * m + 1)
        return carry

    lax.fori_loop(0, count // 2, body, 0)


def dense(lay, own, other, tables, x_table, point, weights, b_in, first, count, after=()):
    size = (lay.n_gz, lay.chips, 1, lay.own, 2 * LANES)
    modes = pl.BlockSpec(size, lambda i: (0, 0, i, 0, 0))
    block = (lay.pack, lay.rows, lay.depth, lay.width)
    part = pl.BlockSpec(block, lambda i: (i, 0, 0, 0))
    kept = jax.ShapeDtypeStruct((count * lay.pack,) + block[1:], BF16)
    volume = lay.pack * lay.cells * lay.width
    steps = lay.mz // lay.step
    return pl.pallas_call(
        functools.partial(dense_kernel, first),
        grid=(count,),
        in_specs=[
            modes,
            modes,
            whole(tables[2].shape),
            whole(tables[3].shape),
            whole(x_table.shape),
            pl.BlockSpec(block, lambda i: (first + i, 0, 0, 0)),
            pl.BlockSpec(memory_space=pltpu.SMEM),
            whole(b_in.shape),
        ]
        + [ANY] * len(after),
        out_specs=[part, part, whole(b_in.shape)],
        out_shape=[kept, kept, jax.ShapeDtypeStruct(b_in.shape, F32)],
        scratch_shapes=[
            pltpu.VMEM((lay.blocks, 2, steps, lay.step * lay.band, 2 * LANES), BF16),
            pltpu.VMEM((CHUNK, lay.pack * lay.width), F32),
            pltpu.VMEM((CHUNK, lay.pack * lay.width), F32),
        ],
        compiler_params=params(),
        cost_estimate=cost(count * volume * 2 * 6 * LANES, count * volume * 24),
        name="dense",
    )(own, other, tables[2], tables[3], x_table, point, weights, b_in, *after)


def stencil_kernel(total_y, total_z, origin_ref, field_ref, *refs):
    halos, (grad_ref, sums_ref, b_ref, gy_ref, rest_ref) = refs[:8], refs[8:]
    _, rows_wide, depth_wide, width = b_ref.shape
    rows, depth = grad_ref.shape[1:3]
    low_y, high_y = pl.ds(0, 2), pl.ds(rows + 2, 2)
    low_z, high_z = pl.ds(0, 2), pl.ds(depth + 2, 2)
    mid_y, mid_z = pl.ds(2, rows), pl.ds(2, depth)
    b_ref[:, :, depth + 4 :] = jnp.zeros_like(b_ref[:, :, depth + 4 :])
    b_ref[:, mid_y, mid_z] = field_ref[...]
    places = [
        (low_y, mid_z), (high_y, mid_z), (mid_y, low_z), (mid_y, high_z),
        (low_y, low_z), (low_y, high_z), (high_y, low_z), (high_y, high_z),
    ]
    for ref, (y, z) in zip(halos, places):
        b_ref[:, y, z] = ref[...]
    shape = (depth_wide, width)
    lane = lax.broadcasted_iota(jnp.int32, shape, 1)
    z_cell = origin_ref[1] + lax.broadcasted_iota(jnp.int32, shape, 0) - 2
    z_inside = (z_cell >= 0) & (z_cell < total_z)
    z_own = lax.broadcasted_iota(jnp.int32, shape, 0)
    z_own = (z_own >= 2) & (z_own < depth + 2)
    scale = 1.0 / (total_y * total_z * width)

    def next_x(v):
        return jnp.where(lane == width - 1, 0.0, pltpu.roll(v, width - 1, 1))

    def last_x(v):
        return jnp.where(lane == 0, 0.0, pltpu.roll(v, 1, 1))

    def next_z(v):
        return pltpu.roll(v, depth_wide - 1, 0)

    def last_z(v):
        return pltpu.roll(v, 1, 0)

    def terms(n, loss):
        b = [b_ref[a, n + 1] for a in range(3)]
        dx = [(next_x(v) - last_x(v)) * 0.5 for v in b]
        dy = [(b_ref[a, n + 2] - b_ref[a, n]) * 0.5 for a in range(3)]
        dz = [(next_z(v) - last_z(v)) * 0.5 for v in b]
        jx = dy[2] - dz[1]
        jy = dz[0] - dx[2]
        jz = dx[1] - dy[0]
        fx = jy * b[2] - jz * b[1]
        fy = jz * b[0] - jx * b[2]
        fz = jx * b[1] - jy * b[0]
        q = dx[0] + dy[1] + dz[2]
        strength = b[0] * b[0] + b[1] * b[1] + b[2] * b[2] + 1.0
        inverse = 1.0 / strength
        ratio = (fx * fx + fy * fy + fz * fz) * inverse
        y_cell = origin_ref[0] + n - 1
        y_inside = (y_cell >= 0) & (y_cell < total_y)
        own = z_own & (n >= 1) & (n <= rows)
        loss = loss + jnp.where(own, ratio + q * q, 0.0)
        weight = jnp.where(z_inside & y_inside, 2.0 * scale, 0.0)
        inverse = inverse * weight
        pull = ratio * inverse
        fx, fy, fz = fx * inverse, fy * inverse, fz * inverse
        q = q * weight
        cx = b[1] * fz - b[2] * fy
        cy = b[2] * fx - b[0] * fz
        cz = b[0] * fy - b[1] * fx
        db = [
            fy * jz - fz * jy - pull * b[0],
            fz * jx - fx * jz - pull * b[1],
            fx * jy - fy * jx - pull * b[2],
        ]
        gx = [q, cz, -cy]
        gy = [-cz, q, cx]
        gz = [cy, -cx, q]
        for a in range(3):
            gy_ref[a, n] = gy[a]
            back = last_x(gx[a]) - next_x(gx[a]) + last_z(gz[a]) - next_z(gz[a])
            rest_ref[a, n] = db[a] + back * 0.5
        return loss

    loss = lax.fori_loop(0, rows + 2, terms, jnp.zeros(shape, F32))

    def combine(n, sums):
        done = []
        for a in range(3):
            grad = rest_ref[a, n + 1] + (gy_ref[a, n] - gy_ref[a, n + 2]) * 0.5
            grad = grad[2 : depth + 2]
            grad_ref[a, n] = grad
            done.append(sums[a] + grad)
        return tuple(done)

    sums = lax.fori_loop(0, rows, combine, (jnp.zeros((depth, width), F32),) * 3)
    sums_ref[...] = jnp.zeros_like(sums_ref)
    for a in range(3):
        sums_ref[a : a + 1, :] = jnp.sum(sums[a], axis=0, keepdims=True)
    sums_ref[3:4, :] = jnp.sum(loss, axis=0, keepdims=True)


def stencil(lay, b_field):
    halos = halo(lay, b_field)
    origin = jnp.stack([lay.y0, lay.z0]).astype(jnp.int32)
    wide = (3, lay.rows + 2, lay.depth + 8, lay.width)
    return pl.pallas_call(
        functools.partial(stencil_kernel, lay.ny, lay.nz),
        in_specs=[
            pl.BlockSpec(memory_space=pltpu.SMEM),
        ]
        + [pl.BlockSpec(memory_space=pltpu.VMEM)] * 9,
        out_specs=[pl.BlockSpec(memory_space=pltpu.VMEM)] * 2,
        out_shape=[
            jax.ShapeDtypeStruct(b_field.shape, F32),
            jax.ShapeDtypeStruct((8, lay.width), F32),
        ],
        scratch_shapes=[
            pltpu.VMEM((3, lay.rows + 4) + wide[2:], F32),
            pltpu.VMEM(wide, F32),
            pltpu.VMEM(wide, F32),
        ],
        compiler_params=pltpu.CompilerParams(vmem_limit_bytes=VMEM_LIMIT),
        name="stencil",
    )(origin, b_field, *halos)


def grad_kernel(first, n_after, weight_ref, hidden_ref, slope_ref, grad_ref, x_ref, z_ref, y_ref,
                *refs):
    pre_ref, own_ref, send_ref, sums_ref, part_ref = refs[n_after:]
    pack, rows, depth, width = hidden_ref.shape
    blocks = part_ref.shape[2]
    band = rows // blocks
    channel = (first + pl.program_id(0)) * pack

    def fold(v):
        return jnp.sum(v.reshape(-1, 8, width), axis=0)

    per = max(CHUNK // (band * depth), 1)
    span = per * band
    count = rows // span

    def slopes(n):
        sums = [0.0] * (3 * pack)
        for y in range(n * span, (n + 1) * span):
            grads = [grad_ref[b, y] for b in range(3)]
            for c in range(pack):
                w = [weight_ref[channel + c, b] for b in range(3)]
                mixed = grads[0] * w[0] + grads[1] * w[1] + grads[2] * w[2]
                pre_ref[c, y] = (mixed * slope_ref[c, y].astype(F32)).astype(BF16)
                hidden = hidden_ref[c, y].astype(F32)
                for b in range(3):
                    sums[3 * c + b] = sums[3 * c + b] + fold(hidden * grads[b])
        return sums

    def transform(n):
        total = x_transform(pre_ref.at[:, n * span : (n + 1) * span], x_ref)
        for m in range(per):
            here = total[m * band * depth : (m + 1) * band * depth]
            z_transform(here, z_ref, part_ref, n * per + m)
        return fold(total)

    parts = [slopes(0)]
    totals = []
    for n in range(1, count):
        parts.append(slopes(n))
        totals.append(transform(n - 1))
    totals.append(transform(count - 1))
    sums = [sum(column[1:], column[0]) for column in zip(*parts)]
    sums.append(sum(totals[1:], totals[0]))
    sums_ref[...] = jnp.zeros_like(sums_ref)
    for n, part in enumerate(sums):
        sums_ref[0, n : n + 1, :] = jnp.sum(part, axis=0, keepdims=True)
    y_transform(y_ref, part_ref, own_ref, send_ref)


def grad_modes(lay, hidden, slope, grad_b, x_table, tables, weights, first, count, after=()):
    out, spec = mode_blocks(lay, count)
    block = (lay.pack, lay.rows, lay.depth, lay.width)
    part = pl.BlockSpec(block, lambda i: (i, 0, 0, 0))
    volume = lay.pack * lay.cells * lay.width
    lines = -(-(3 * lay.pack + 1) // 8) * 8
    return pl.pallas_call(
        functools.partial(grad_kernel, first, len(after)),
        grid=(count,),
        in_specs=[
            pl.BlockSpec(memory_space=pltpu.SMEM),
            part,
            part,
            whole(grad_b.shape),
            whole(x_table.shape),
            whole(tables[0].shape),
            whole(tables[1].shape),
        ]
        + [ANY] * len(after),
        out_specs=[
            part,
            spec,
            spec,
            pl.BlockSpec((1, lines, lay.width), lambda i: (i, 0, 0)),
        ],
        out_shape=[
            jax.ShapeDtypeStruct(hidden.shape, BF16),
            out,
            out,
            jax.ShapeDtypeStruct((count, lines, lay.width), F32),
        ],
        scratch_shapes=[part_scratch(lay)],
        compiler_params=params(),
        cost_estimate=cost(count * volume * 2 * 2 * LANES, count * volume * 10),
        name="grad_modes",
    )(weights, hidden, slope, grad_b, x_table, tables[0], tables[1], *after)


def point_kernel(tile, n_after, field_ref, grad_ref, *refs):
    out_ref, acc_ref = refs[n_after:]
    channels, rows, depth, width = field_ref.shape
    count = grad_ref.shape[0]
    step = pl.program_id(0)

    @pl.when(step == 0)
    def _():
        acc_ref[...] = jnp.zeros_like(acc_ref)

    left, right = [], []
    for y in range(rows):
        for z in range(0, depth, tile):
            left.append(field_ref[:, y, z : z + tile, :].reshape(channels * tile, width))
            right.append(grad_ref[:, y, z : z + tile, :].reshape(count * tile, width))
    acc_ref[...] += lax.dot_general(
        jnp.concatenate(left, axis=1),
        jnp.concatenate(right, axis=1),
        (((1,), (1,)), ((), ())),
        preferred_element_type=F32,
    )

    @pl.when(step == pl.num_programs(0) - 1)
    def _():
        def pick(n):
            owner = lax.broadcasted_iota(jnp.int32, (n, n * tile), 1) // tile
            return (owner == lax.broadcasted_iota(jnp.int32, (n, n * tile), 0)).astype(F32)

        row = lax.broadcasted_iota(jnp.int32, acc_ref.shape, 0)
        column = lax.broadcasted_iota(jnp.int32, acc_ref.shape, 1)
        kept = jnp.where(row % tile == column % tile, acc_ref[...], 0.0)
        half = jnp.dot(
            pick(channels), kept, precision=lax.Precision.HIGHEST, preferred_element_type=F32
        )
        out_ref[...] = lax.dot_general(
            half,
            pick(count),
            (((1,), (1,)), ((), ())),
            precision=lax.Precision.HIGHEST,
            preferred_element_type=F32,
        )


def point_grad(lay, field_in, grad_pre, after=()):
    span = 4

    def block(count):
        return pl.BlockSpec((count, span, lay.depth, lay.width), lambda i: (0, i, 0, 0))

    count = grad_pre.shape[0]
    size = lay.channels * lay.tile
    return pl.pallas_call(
        functools.partial(point_kernel, lay.tile, len(after)),
        grid=(lay.rows // span,),
        in_specs=[block(lay.channels), block(count)] + [ANY] * len(after),
        out_specs=pl.BlockSpec((lay.channels, count), lambda i: (0, 0)),
        out_shape=jax.ShapeDtypeStruct((lay.channels, count), F32),
        scratch_shapes=[pltpu.VMEM((size, count * lay.tile), F32)],
        compiler_params=params(),
        cost_estimate=cost(2 * size * count * lay.cells * lay.width, 3 * field_in.size),
        name="point_grad",
    )(field_in, grad_pre, *after)


def join_kernel(n_in, *refs):
    refs[-1][...] = jnp.concatenate([ref[...] for ref in refs[:n_in]], axis=1)


def join(values, after=()):
    vmem = pl.BlockSpec(memory_space=pltpu.VMEM)
    rows = values[0].shape[0]
    out = (rows, sum(value.shape[1] for value in values))
    return pl.pallas_call(
        functools.partial(join_kernel, len(values)),
        in_specs=[vmem] * len(values) + [ANY] * len(after),
        out_specs=vmem,
        out_shape=jax.ShapeDtypeStruct(out, values[0].dtype),
        name="join",
    )(*values, *after)


def outer_kernel(modes_ref, grads_ref, out_ref):
    pair, count, channels, wide = out_ref.shape[1:]
    columns = jnp.concatenate([modes_ref[0, a] for a in range(pair)], axis=1)
    rows = []
    for a in range(pair):
        right = grads_ref[0, a]
        turned = jnp.concatenate([right[:, channels:], -right[:, :channels]], axis=1)
        right = jnp.concatenate([right, turned], axis=0)
        zero = jnp.zeros_like(right)
        rows.append(jnp.concatenate([right if n == a else zero for n in range(pair)], axis=1))
    rows = jnp.concatenate(rows, axis=0)
    owner = lax.broadcasted_iota(jnp.int32, columns.shape, 1) % count
    zero = jnp.zeros_like(columns)
    some = 8
    for k in range(0, count, some):
        left = [jnp.where(owner == k + n, columns, zero) for n in range(some)]
        out = dot(jnp.concatenate(left, axis=0), rows)
        for a in range(pair):
            here = out[:, wide * a : wide * (a + 1)]
            out_ref[0, a, k : k + some] = here.reshape(some, channels, wide)


def weight_grad(lay, modes_in, grads):
    columns = jnp.transpose(modes_in, (0, 1, 3, 2))
    rows = jnp.concatenate([grads[:, :, : lay.mx], grads[:, :, lay.mx :]], axis=-1)
    tile = (lay.mx, lay.channels, 2 * lay.channels)
    shape = (lay.kz, lay.ky) + tile
    return pl.pallas_call(
        outer_kernel,
        grid=(lay.own // 2,),
        in_specs=[mode_spec(lay, columns.shape[2:]), mode_spec(lay, rows.shape[2:])],
        out_specs=mode_spec(lay, tile),
        out_shape=jax.ShapeDtypeStruct(shape, F32),
        compiler_params=params(),
        cost_estimate=cost(math.prod(shape) * 4, math.prod(shape) * 4),
        name="weight_grad",
    )(columns, rows)


def on_device(field_in, spectral_weight, point_weight, point_bias, out_weight, out_bias):
    lay = Layout(field_in, spectral_weight)
    tables = lay.grid_tables()
    x_table, x_back = lay.x_tables()
    weights = out_weight.astype(F32)
    per = lay.groups // PARTS
    parts = range(PARTS)
    scale = math.sqrt(lay.mx * lay.my * lay.mz / (lay.width * lay.ny * lay.nz))
    half = lay.rows // 2

    def point(n, done, after):
        bias = point_bias.reshape(1, lay.channels)
        return pointwise(lay, field_in, point_weight.T, bias, n * half, half, done, after)

    both, column = [], []
    for n in parts:
        own, send = forward_modes(
            lay, field_in, x_table, tables, n * per, per, after=[b[0] for b in both[n - 1 : n]]
        )
        both.append(from_cores(own, send))
    column.append(from_depth(both[0], both[1][:1]))
    done = point(0, None, column[0][:1])
    column.append(from_depth(both[1], [done]))
    modes = [from_chips(column[0], scale, [done])]
    done = point(1, done, column[1][:1] + modes)
    modes.append(from_chips(column[1], scale, [done]))
    modes_in = by_mode(lay, jnp.concatenate(modes))
    mixed = mix_modes(lay, modes_in, spectral_weight, after=[done])
    mine = by_group(lay, mixed.reshape(lay.kz, lay.ky, lay.mx, 2, lay.groups, lay.pack))

    b_field = jnp.broadcast_to(
        out_bias[:, None, None, None], (3, lay.rows, lay.depth, lay.width)
    ).astype(F32)
    hiddens, slopes = [], []
    columns = [spread_chips(lay, mine[n * per : (n + 1) * per]) for n in parts]
    for n in parts:
        own = spread_depth(lay, columns[n], columns[n + 1 : n + 2] if n == 0 else [b_field])
        hidden, slope, b_field = dense(
            lay, own, exchange(own, "gy", 1), tables, x_back, done, weights, b_field,
            n * per, per,
        )
        hiddens.append(hidden)
        slopes.append(slope)

    grad_b, edge = stencil(lay, b_field)

    both, column, pres, sums = [], [], [], []
    for n in parts:
        pre, own, send, part = grad_modes(
            lay, hiddens[n], slopes[n], grad_b, x_table, tables, weights, n * per, per,
            after=[b[0] for b in both[n - 1 : n]],
        )
        both.append(from_cores(own, send))
        pres.append(pre)
        sums.append(part)
    column.append(from_depth(both[0], both[1][:1]))
    point_parts = [point_grad(lay, field_in, pres[0], column[0][:1])]
    column.append(from_depth(both[1], point_parts[:1]))
    grads = [from_chips(column[0], 1.0, point_parts)]
    point_parts.append(point_grad(lay, field_in, pres[1], column[1][:1] + grads))
    grads.append(from_chips(column[1], 1.0, point_parts[1:]))
    sums = jnp.concatenate(sums)
    outs = jnp.sum(sums[:, : 3 * lay.pack], axis=-1).reshape(3 * lay.channels)
    bias = sums[:, 3 * lay.pack, :LANES].reshape(lay.groups, lay.pack, lay.mx)[..., 0]
    ends = jnp.sum(edge, axis=-1)
    square = lay.channels * lay.channels
    flat = jnp.concatenate(
        [
            join(point_parts, grads[-1:]).reshape(square),
            outs,
            bias.reshape(lay.channels),
            ends[:4],
        ]
    )
    flat = jnp.pad(flat, (0, -flat.shape[0] % 1024)).reshape(-1, LANES)
    flat = jnp.sum(lax.all_gather(flat, ("gy", "gz")), axis=0).reshape(-1)
    after = square + 3 * lay.channels
    ends = flat[after + lay.channels : after + lay.channels + 4]
    grad_spectral = weight_grad(lay, modes_in, by_mode(lay, jnp.concatenate(grads)))
    return (
        ends[3] / (lay.width * lay.ny * lay.nz),
        grad_spectral,
        flat[:square].reshape(lay.channels, lay.channels),
        flat[after : after + lay.channels],
        flat[square:after].reshape(lay.channels, 3),
        ends[:3],
    )


def solution(mesh):
    return jax.shard_map(
        on_device,
        mesh=mesh,
        in_specs=(P(None, "gy", "gz", None), P("gz", "gy", None, None, None), P(), P(), P(), P()),
        out_specs=(P(), P("gz", "gy", None, None, None), P(), P(), P(), P()),
        check_vma=False,
    )
```

time: 821 us -> 699 us (0.85)
  Pallas kernels: 535 us -> 413 us
  blocking collectives: 0 us -> 67.6 us
  starting transfers between devices: 115 us -> 77.8 us
  local copies, waits for them, and re-layouts: 76.7 us -> 43.8 us
  waiting for transfers between devices: 38.9 us -> 67.5 us
  other arithmetic: 37.9 us -> 14.5 us
    all_gather x0 -> x1, blocking collectives: none -> 67.6 us  [on_device(): flat = jnp.sum(lax.all_gather(flat, ('gy', 'gz')), axis=0).reshape(-1)]
    ppermute x96 -> x42, starting transfers between devices: 102 us -> 49.2 us  [exchange(): return lax.ppermute(value, axis, [(i, i ^ distance) for i in range(count)])]
    pallas_call x4 -> x2, Pallas kernels: 95.3 us -> 53.7 us  [grad_modes(): pl.pallas_call(functools.partial(grad_kernel, first, len(after)), grid=(c...]
    ppermute x96 -> x42, waiting for transfers between devices: 21.9 us -> 61.9 us  [exchange(): return lax.ppermute(value, axis, [(i, i ^ distance) for i in range(count)])]
    pallas_call x4 -> x2, Pallas kernels: 75.8 us -> 40.6 us  [point_grad(): pl.pallas_call(functools.partial(point_kernel, lay.tile, len(after)), gri...]
    convert_element_type x9 -> x0, local copies, waits for them, and re-layouts: 28.6 us -> none  [the longest x2 20 us: grid_tables(): y_forward.reshape(y_modes, 2 * y_cells).astype(BF16)]
    pallas_call x4 -> x2, Pallas kernels: 56.3 us -> 31.4 us  [forward_modes(): pl.pallas_call(functools.partial(modes_kernel, len(after)), grid=(count,)...]
    pallas_call x10 -> x23, Pallas kernels: 293 us -> 272 us  [the longest x2 120 us: dense(): pl.pallas_call(functools.partial(dense_kernel, first), grid=(count,), in_...]
  transfers between devices with their start and end apart: 105 -> 50, of which waited for: 12 -> 17; matrix products, arithmetic and copies ran while one was open for 8% -> 2% of each run, Pallas kernels for 50% -> 23%
where the time goes in v2:
time: 699 us; the launch traced here: 688 us
  Pallas kernels  413 us (59%)
  starting transfers between devices  77.8 us (11%)
  blocking collectives  67.6 us (10%)
  waiting for transfers between devices  67.5 us (10%)
  local copies, waits for them, and re-layouts  43.8 us (6%)
  other arithmetic  14.5 us (2%)
    pallas_call x2, Pallas kernels, dense(): pl.pallas_call(functools.partial(dense_kernel, first), grid=(count,), in_...  120 us
    all_gather x1, blocking collectives, on_device(): flat = jnp.sum(lax.all_gather(flat, ('gy', 'gz')), axis=0).reshape(-1)  67.6 us
    pallas_call x12, Pallas kernels, sum_blocks(): pl.pallas_call(functools.partial(sum_kernel, len(values), n_out, factor),...  63.4 us
    ppermute x42, waiting for transfers between devices, exchange(): return lax.ppermute(value, axis, [(i, i ^ distance) for i in range(count)])  61.9 us
    pallas_call x2, Pallas kernels, grad_modes(): pl.pallas_call(functools.partial(grad_kernel, first, len(after)), grid=(c...  53.7 us
    ppermute x42, starting transfers between devices, exchange(): return lax.ppermute(value, axis, [(i, i ^ distance) for i in range(count)])  49.2 us
    pallas_call x2, Pallas kernels, point_grad(): pl.pallas_call(functools.partial(point_kernel, lay.tile, len(after)), gri...  40.6 us
    pallas_call x2, Pallas kernels, pointwise(): pl.pallas_call(functools.partial(pointwise_kernel, lay.tile), grid=(count...  35.1 us
  transfers between devices with their start and end apart: 50, of which 17 were waited for; matrix products, arithmetic and copies ran while one was open for 2% of the time, Pallas kernels for 23%

profile of v2, /device:TPU:0, one launch (start us, length us, event | category | flops | bytes accessed | tf_op | source)
XLA Modules:
  0.0 687.9 jit_solution(17514994424338737986)
XLA Ops:
  0.8 2.9 compare_select_fusion.9
  7.4 15.6 %forward_modes.2 = (bf16[4,4,8,32,256]{4,3,2,1,0:T(8,128)(2,1)}, bf16[4,4,8,32,256]{4,3,2,1,0:T(8,128)(2,1)}) custom-call(bf16[64,32,32,256]{3,2,1,0:T(8,128)(2,1)} %field_ref.11, bf16[1024,256]{1,0:T(8,128)(2,1)} %pad_maximum_fusion.x_ref, bf16[128,256]{1,0:T(8,128)(2,1)} %select_convert_fusion.5.z_ref, bf16[128,256]{1,0:T(8,128)(2,1)} %select_convert_fusion.4.y_ref), custom_call_target="tpu_custom_call" | custom-call | flops 4294967296 | bytes 25165824 | tf_op jit(solution)/shard_map/forward_modes/pallas_call | solution.py:214
  23.5 4.0 collective-permute-done.refs_1_
  28.8 6.2 sum_blocks.12
  35.0 15.8 %forward_modes.3 = (bf16[4,4,8,32,256]{4,3,2,1,0:T(8,128)(2,1)}, bf16[4,4,8,32,256]{4,3,2,1,0:T(8,128)(2,1)}) custom-call(bf16[64,32,32,256]{3,2,1,0:T(8,128)(2,1)} %field_ref.11, bf16[1024,256]{1,0:T(8,128)(2,1)} %pad_maximum_fusion.x_ref, bf16[128,256]{1,0:T(8,128)(2,1)} %select_convert_fusion.5.z_ref, bf16[128,256]{1,0:T(8,128)(2,1)} %select_convert_fusion.4.y_ref, ...), custom_call_target="tpu_custom_call" | custom-call | flops 4294967296 | bytes 25165824 | tf_op jit(solution)/shard_map/forward_modes/pallas_call | solution.py:214
  51.1 2.6 collective-permute-start.1
  53.8 1.5 collective-permute-start.2
  56.7 6.2 sum_blocks.13
  62.9 3.6 collective-permute-done.1.refs_1_
  66.5 12.4 %collective-permute-done.2.refs_2_ = bf16[4,8,32,256]{3,2,1,0:T(8,128)(2,1)S(1)} collective-permute-done((bf16[4,8,32,256]{3,2,1,0:T(8,128)(2,1)S(1)}, bf16[4,8,32,256]{3,2,1,0:T(8,128)(2,1)S(1)}, u32[]{:S(2)}, u32[]{:S(2)}) %collective-permute-start.2) | collective-permute-done | bytes 524320 | tf_op jit(solution)/shard_map/ppermute | solution.py:235
  79.9 5.3 sum_blocks.14
  85.2 1.6 collective-permute-start.5
  87.5 2.6 collective-permute-start.6
  93.8 17.6 %pointwise.2.refs_4_.refs_0_ = bf16[64,32,32,256]{3,2,1,0:T(8,128)(2,1)} custom-call(bf16[64,32,32,256]{3,2,1,0:T(8,128)(2,1)} %field_ref.11, bf16[64,64]{1,0:T(8,128)(2,1)} %bitcast.27, f32[1,64]{1,0:T(1,128)} %bitcast.33, bf16[8,32,256]{2,1,0:T(8,128)(2,1)} %get-tuple-element.67.refs_0_), custom_call_target="tpu_custom_call" | custom-call | flops 8589934592 | bytes 33554432 | tf_op jit(solution)/shard_map/pointwise/pallas_call | solution.py:418
  112.7 4.4 sum_blocks.15.refs_2_
  118.8 5.3 sum_blocks.16
  124.8 3.5 collective-permute-start.12
  128.5 17.6 %pointwise.3.refs_4_.refs_0_.point_ref = bf16[64,32,32,256]{3,2,1,0:T(8,128)(2,1)} custom-call(bf16[64,32,32,256]{3,2,1,0:T(8,128)(2,1)} %field_ref.11, bf16[64,64]{1,0:T(8,128)(2,1)} %bitcast.28, f32[1,64]{1,0:T(1,128)} %bitcast.34, bf16[64,32,32,256]{3,2,1,0:T(8,128)(2,1)} %pointwise.2.refs_4_.refs_0_, ...), custom_call_target="tpu_custom_call", output_to_operand_aliasing={{}: (3, {})} | custom-call | flops 8589934592 | bytes 33554432 | tf_op jit(solution)/shard_map/pointwise/pallas_call | solution.py:418
  147.5 4.4 sum_blocks.17
  155.8 15.5 %mix_modes.1 = bf16[8,4,32,128]{3,2,1,0:T(8,128)(2,1)} custom-call(bf16[8,4,64,64]{3,2,1,0:T(8,128)(2,1)} %copy.35.modes_ref, bf16[8,4,32,64,128]{4,3,2,1,0:T(8,128)(2,1)} %weight_ref.1, bf16[64,32,32,256]{3,2,1,0:T(8,128)(2,1)} %pointwise.3.refs_4_.refs_0_.point_ref), custom_call_target="tpu_custom_call" | custom-call | flops 67108864 | bytes 16777216 | tf_op jit(solution)/shard_map/mix_modes/pallas_call | solution.py:371
  174.0 3.7 collective-permute-start.16
  178.4 3.1 collective-permute-done.16.refs_3_
  181.5 3.4 collective-permute-done.15.refs_2_
  186.3 4.4 stack_blocks.4.refs_0_
  192.1 1.5 collective-permute-start.18
  194.8 2.8 collective-permute-start.22
  197.6 5.2 collective-permute-done.22.refs_3_
  202.8 2.5 collective-permute-start.20
  206.2 2.1 collective-permute-done.20.refs_1_
  208.9 4.4 stack_blocks.5.refs_4_.refs_0_
  213.4 2.2 collective-permute-done.18.refs_2_
  217.2 5.7 stack_blocks.6.own_ref
  225.8 1.5 select_convert_fusion.3.y_ref
  228.4 1.8 collective-permute-start.25
  230.8 2.1 broadcast_in_dim.26.b_in_ref
  232.9 55.8 %dense.2 = (bf16[32,32,32,256]{3,2,1,0:T(8,128)(2,1)}, bf16[32,32,32,256]{3,2,1,0:T(8,128)(2,1)}, f32[3,32,32,256]{3,2,1,0:T(8,128)}) custom-call(bf16[4,4,8,32,256]{4,3,2,1,0:T(8,128)(2,1)} %stack_blocks.6.own_ref, bf16[4,4,8,32,256]{4,3,2,1,0:T(8,128)(2,1)} %collective-permute-done.23.other_ref, bf16[128,256]{1,0:T(8,128)(2,1)} %select_convert_fusion.3.y_ref, ...), custom_call_target="tpu_custom_call" | custom-call | flops 12884901888 | bytes 201326592 | tf_op jit(solution)/shard_map/dense/pallas_call | solution.py:526
  289.9 5.7 stack_blocks.7.own_ref
  295.5 4.4 collective-permute-done.27.other_ref
  301.3 64.6 %dense.3 = (bf16[32,32,32,256]{3,2,1,0:T(8,128)(2,1)}, bf16[32,32,32,256]{3,2,1,0:T(8,128)(2,1)}, f32[3,32,32,256]{3,2,1,0:T(8,128)}) custom-call(bf16[4,4,8,32,256]{4,3,2,1,0:T(8,128)(2,1)} %stack_blocks.7.own_ref, bf16[4,4,8,32,256]{4,3,2,1,0:T(8,128)(2,1)} %copy-done.58, bf16[128,256]{1,0:T(8,128)(2,1)} %select_convert_fusion.3.y_ref, ...), custom_call_target="tpu_custom_call" | custom-call | flops 12884901888 | bytes 201326592 | tf_op jit(solution)/shard_map/dense/pallas_call | solution.py:526
  365.9 1.5 fusion.97
  369.7 4.6 collective-permute-start.30
  375.6 3.0 collective-permute-start.28
  380.9 4.8 collective-permute-done.35.refs_7_
  387.0 15.9 %collective-permute-start.32 = (f32[3,2,2,256]{3,2,1,0:T(2,128)S(1)}, f32[3,2,2,256]{3,2,1,0:T(2,128)S(1)}, u32[]{:S(2)}, u32[]{:S(2)}) collective-permute-start(f32[3,2,2,256]{3,2,1,0:T(2,128)S(1)} %get-tuple-element.125), channel_id=1, source_target_pairs={{0,5},{1,6},{2,7},{4,9},{5,10},{6,11},{8,13},{9,14},{10,15},{12,17... | collective-permute-start | bytes 36872 | tf_op jit(solution)/shard_map/ppermute | solution.py:64
  405.8 15.4 %stencil.1 = (f32[3,32,32,256]{3,2,1,0:T(8,128)}, f32[8,256]{1,0:T(8,128)}) custom-call(s32[2]{0:T(128)} %pad_add_fusion.origin_ref, f32[3,32,32,256]{3,2,1,0:T(8,128)} %get-tuple-element.81.field_ref, f32[3,2,32,256]{3,2,1,0:T(8,128)} %copy-done.30, f32[3,2,32,256]{3,2,1,0:T(8,128)} %copy-done.29, f32[3,32,2,256]{3,2,1,0:T(2,128)} %copy-done.28, ...), custom_call_target="tpu_custom_call" | custom-call | tf_op jit(solution)/shard_map/stencil/pallas_call | solution.py:651
  421.2 26.8 %grad_modes.2 = (bf16[32,32,32,256]{3,2,1,0:T(8,128)(2,1)}, bf16[4,4,8,32,256]{4,3,2,1,0:T(8,128)(2,1)}, bf16[4,4,8,32,256]{4,3,2,1,0:T(8,128)(2,1)}, f32[8,16,256]{2,1,0:T(8,128)}) custom-call(f32[64,3]{1,0:T(8,128)} %convert_element_type.194.weight_ref, bf16[32,32,32,256]{3,2,1,0:T(8,128)(2,1)} %get-tuple-element.78.hidden_ref, ...), custom_call_target="tpu_custom_call" | custom-call | flops 4294967296 | bytes 83886080 | tf_op jit(solution)/shard_map/grad_modes/pallas_call | solution.py:727
  448.0 4.4 collective-permute-done.36.refs_1_
  453.7 6.2 sum_blocks.18
  459.9 26.9 %grad_modes.3 = (bf16[32,32,32,256]{3,2,1,0:T(8,128)(2,1)}, bf16[4,4,8,32,256]{4,3,2,1,0:T(8,128)(2,1)}, bf16[4,4,8,32,256]{4,3,2,1,0:T(8,128)(2,1)}, f32[8,16,256]{2,1,0:T(8,128)}) custom-call(f32[64,3]{1,0:T(8,128)} %convert_element_type.194.weight_ref, bf16[32,32,32,256]{3,2,1,0:T(8,128)(2,1)} %get-tuple-element.90.hidden_ref, ...), custom_call_target="tpu_custom_call" | custom-call | flops 4294967296 | bytes 83886080 | tf_op jit(solution)/shard_map/grad_modes/pallas_call | solution.py:727
  487.0 2.0 collective-permute-start.37
  489.0 1.5 collective-permute-start.39
  493.0 6.2 sum_blocks.19
  499.2 2.7 collective-permute-done.37.refs_1_
  502.0 12.2 %collective-permute-done.38.refs_2_ = bf16[4,8,32,256]{3,2,1,0:T(8,128)(2,1)S(1)} collective-permute-done((bf16[4,8,32,256]{3,2,1,0:T(8,128)(2,1)}, bf16[4,8,32,256]{3,2,1,0:T(8,128)(2,1)S(1)}, u32[]{:S(2)}, u32[]{:S(2)}) %collective-permute-start.38) | collective-permute-done | bytes 524320 | tf_op jit(solution)/shard_map/ppermute | solution.py:235
  515.0 5.3 sum_blocks.20
  520.9 4.2 collective-permute-start.46
  528.6 20.3 %point_grad.2.refs_4_.refs_0_ = f32[64,32]{1,0:T(8,128)} custom-call(bf16[64,32,32,256]{3,2,1,0:T(8,128)(2,1)} %field_ref.11, bf16[32,32,32,256]{3,2,1,0:T(8,128)(2,1)} %get-tuple-element.83.grad_ref, bf16[8,32,256]{2,1,0:T(8,128)(2,1)} %get-tuple-element.95.refs_0_), custom_call_target="tpu_custom_call" | custom-call | flops 8589934592 | bytes 50331648 | tf_op jit(solution)/shard_map/point_grad/pallas_call | solution.py:810
  550.2 4.4 sum_blocks.22.refs_1_
  556.4 5.3 sum_blocks.21
  562.7 3.4 collective-permute-start.49
  566.1 20.3 %point_grad.3.refs_4_.refs_1_ = f32[64,32]{1,0:T(8,128)} custom-call(bf16[64,32,32,256]{3,2,1,0:T(8,128)(2,1)} %field_ref.11, bf16[32,32,32,256]{3,2,1,0:T(8,128)(2,1)} %get-tuple-element.96.grad_ref, bf16[8,32,256]{2,1,0:T(8,128)(2,1)} %get-tuple-element.100.refs_0_, bf16[8,32,256]{2,1,0:T(8,128)(2,1)} %sum_blocks.22.refs_1_), custom_call_target="tpu_custom_call" | custom-call | flops 8589934592 | bytes 50331648 | tf_op jit(solution)/shard_map/point_grad/pallas_call | solution.py:810
  587.8 4.4 sum_blocks.23.refs_2_
  595.5 67.6 %all_gather.3 = f32[32,40,128]{2,1,0:T(8,128)S(1)} all-gather(f32[1,40,128]{2,1,0:T(8,128)S(1)} %pad_bitcast_fusion), channel_id=1, replica_groups=mesh['gy'=8,'gz'=4] {'gy','gz'}, dimensions={0}, use_global_device_ids=true | all-gather | bytes 675840 | tf_op jit(solution)/shard_map/all_gather | solution.py:954
  670.5 16.0 %weight_grad.1 = f32[8,4,32,64,128]{4,3,2,1,0:T(8,128)} custom-call(bf16[8,4,64,64]{3,2,1,0:T(8,128)(2,1)} %bitcast.23, bf16[8,4,32,128]{3,2,1,0:T(8,128)(2,1)} %pad_maximum_fusion.4.grads_ref), custom_call_target="tpu_custom_call" | custom-call | flops 33554432 | bytes 33554432 | tf_op jit(solution)/shard_map/weight_grad/pallas_call | solution.py:867
  (266 shorter events, 73.9 us)
Async XLA Ops:
  23.0 4.4 collective-permute-start
  35.0 18.8 %copy-start.60 = (bf16[4,8,32,256]{3,2,1,0:T(8,128)(2,1)S(1)}, bf16[4,8,32,256]{3,2,1,0:T(8,128)(2,1)}, u32[]{:S(2)}) copy-start(bf16[4,8,32,256]{3,2,1,0:T(8,128)(2,1)} %get-tuple-element.62) | copy-start | bytes 1572868
  35.0 20.3 %copy-start.59 = (bf16[4,8,32,256]{3,2,1,0:T(8,128)(2,1)S(1)}, bf16[4,8,32,256]{3,2,1,0:T(8,128)(2,1)}, u32[]{:S(2)}) copy-start(bf16[4,8,32,256]{3,2,1,0:T(8,128)(2,1)} %get-tuple-element.63) | copy-start | bytes 1572868
  50.8 4.6 collective-permute-start.4
  51.1 15.4 %collective-permute-start.1 = (bf16[4,8,32,256]{3,2,1,0:T(8,128)(2,1)S(1)}, bf16[4,8,32,256]{3,2,1,0:T(8,128)(2,1)S(1)}, u32[]{:S(2)}, u32[]{:S(2)}) collective-permute-start(bf16[4,8,32,256]{3,2,1,0:T(8,128)(2,1)S(1)} %copy-done.61), channel_id=1, source_target_pairs={{0,1},{1,0},{2,3},{3,2},{4,5},{5,4},{6,7},{7,6},{8,9},{9,8},{10,11... | collective-permute-start | bytes 1572872 | tf_op jit(solution)/shard_map/ppermute | solution.py:235
  53.8 25.1 %collective-permute-start.2 = (bf16[4,8,32,256]{3,2,1,0:T(8,128)(2,1)S(1)}, bf16[4,8,32,256]{3,2,1,0:T(8,128)(2,1)S(1)}, u32[]{:S(2)}, u32[]{:S(2)}) collective-permute-start(bf16[4,8,32,256]{3,2,1,0:T(8,128)(2,1)S(1)} %copy-done.60), channel_id=1, source_target_pairs={{0,2},{1,3},{2,0},{3,1},{4,6},{5,7},{6,4},{7,5},{8,10},{9,11},{10,... | collective-permute-start | bytes 1572872 | tf_op jit(solution)/shard_map/ppermute | solution.py:235
  55.3 23.6 %collective-permute-start.3 = (bf16[4,8,32,256]{3,2,1,0:T(8,128)(2,1)S(1)}, bf16[4,8,32,256]{3,2,1,0:T(8,128)(2,1)S(1)}, u32[]{:S(2)}, u32[]{:S(2)}) collective-permute-start(bf16[4,8,32,256]{3,2,1,0:T(8,128)(2,1)S(1)} %copy-done.59), channel_id=1, source_target_pairs={{0,3},{1,2},{2,1},{3,0},{4,7},{5,6},{6,5},{7,4},{8,11},{9,10},{10,... | collective-permute-start | bytes 1572872 | tf_op jit(solution)/shard_map/ppermute | solution.py:235
  56.7 30.1 %copy-start.50 = (bf16[64,64]{1,0:T(8,128)(2,1)S(1)}, bf16[64,64]{1,0:T(8,128)(2,1)}, u32[]{:S(2)}) copy-start(bf16[64,64]{1,0:T(8,128)(2,1)} %param.8) | copy-start | bytes 24580
  85.2 7.2 %collective-permute-start.5 = (bf16[8,32,256]{2,1,0:T(8,128)(2,1)}, bf16[8,32,256]{2,1,0:T(8,128)(2,1)S(1)}, u32[]{:S(2)}, u32[]{:S(2)}) collective-permute-start(bf16[8,32,256]{2,1,0:T(8,128)(2,1)} %get-tuple-element.68), channel_id=1, source_target_pairs={{0,8},{4,12},{8,0},{12,4},{16,24},{20,28},{24,16},{28,20},{1,9},{5... | collective-permute-start | bytes 393224 | tf_op jit(solution)/shard_map/ppermute | solution.py:235
  87.5 23.9 %collective-permute-start.6 = (bf16[8,32,256]{2,1,0:T(8,128)(2,1)}, bf16[8,32,256]{2,1,0:T(8,128)(2,1)S(1)}, u32[]{:S(2)}, u32[]{:S(2)}) collective-permute-start(bf16[8,32,256]{2,1,0:T(8,128)(2,1)} %get-tuple-element.69), channel_id=1, source_target_pairs={{0,16},{4,20},{8,24},{12,28},{16,0},{20,4},{24,8},{28,12},{1,17},{... | collective-permute-start | bytes 393224 | tf_op jit(solution)/shard_map/ppermute | solution.py:235
  90.1 21.3 %collective-permute-start.7 = (bf16[8,32,256]{2,1,0:T(8,128)(2,1)}, bf16[8,32,256]{2,1,0:T(8,128)(2,1)S(1)}, u32[]{:S(2)}, u32[]{:S(2)}) collective-permute-start(bf16[8,32,256]{2,1,0:T(8,128)(2,1)} %get-tuple-element.70), channel_id=1, source_target_pairs={{0,24},{4,28},{8,16},{12,20},{16,8},{20,12},{24,0},{28,4},{1,25},{... | collective-permute-start | bytes 393224 | tf_op jit(solution)/shard_map/ppermute | solution.py:235
  90.3 26.8 %collective-permute-start.8 = (bf16[4,8,32,256]{3,2,1,0:T(8,128)(2,1)}, bf16[4,8,32,256]{3,2,1,0:T(8,128)(2,1)S(1)}, u32[]{:S(2)}, u32[]{:S(2)}) collective-permute-start(bf16[4,8,32,256]{3,2,1,0:T(8,128)(2,1)} %get-tuple-element.71), channel_id=1, source_target_pairs={{0,1},{1,0},{2,3},{3,2},{4,5},{5,4},{6,7},{7,6},{8,9},{9,8},{10,11... | collective-permute-start | bytes 1572872 | tf_op jit(solution)/shard_map/ppermute | solution.py:235
  91.4 25.7 %collective-permute-start.9 = (bf16[4,8,32,256]{3,2,1,0:T(8,128)(2,1)}, bf16[4,8,32,256]{3,2,1,0:T(8,128)(2,1)S(1)}, u32[]{:S(2)}, u32[]{:S(2)}) collective-permute-start(bf16[4,8,32,256]{3,2,1,0:T(8,128)(2,1)} %get-tuple-element.72), channel_id=1, source_target_pairs={{0,2},{1,3},{2,0},{3,1},{4,6},{5,7},{6,4},{7,5},{8,10},{9,11},{10,... | collective-permute-start | bytes 1572872 | tf_op jit(solution)/shard_map/ppermute | solution.py:235
  92.4 19.0 %copy-start.31 = (bf16[8,32,256]{2,1,0:T(8,128)(2,1)}, bf16[8,32,256]{2,1,0:T(8,128)(2,1)S(1)}, u32[]{:S(2)}) copy-start(bf16[8,32,256]{2,1,0:T(8,128)(2,1)S(1)} %collective-permute-done.5.refs_1_) | copy-start | bytes 393220
  92.4 24.7 %collective-permute-start.10 = (bf16[4,8,32,256]{3,2,1,0:T(8,128)(2,1)}, bf16[4,8,32,256]{3,2,1,0:T(8,128)(2,1)S(1)}, u32[]{:S(2)}, u32[]{:S(2)}) collective-permute-start(bf16[4,8,32,256]{3,2,1,0:T(8,128)(2,1)} %get-tuple-element.73), channel_id=1, source_target_pairs={{0,3},{1,2},{2,1},{3,0},{4,7},{5,6},{6,5},{7,4},{8,11},{9,10},{10,... | collective-permute-start | bytes 1572872 | tf_op jit(solution)/shard_map/ppermute | solution.py:235
  124.1 22.0 %collective-permute-start.11 = (bf16[8,32,256]{2,1,0:T(8,128)(2,1)}, bf16[8,32,256]{2,1,0:T(8,128)(2,1)S(1)}, u32[]{:S(2)}, u32[]{:S(2)}) collective-permute-start(bf16[8,32,256]{2,1,0:T(8,128)(2,1)} %get-tuple-element.75), channel_id=1, source_target_pairs={{0,8},{4,12},{8,0},{12,4},{16,24},{20,28},{24,16},{28,20},{1,9},{5... | collective-permute-start | bytes 393224 | tf_op jit(solution)/shard_map/ppermute | solution.py:235
  124.8 21.3 %collective-permute-start.12 = (bf16[8,32,256]{2,1,0:T(8,128)(2,1)}, bf16[8,32,256]{2,1,0:T(8,128)(2,1)S(1)}, u32[]{:S(2)}, u32[]{:S(2)}) collective-permute-start(bf16[8,32,256]{2,1,0:T(8,128)(2,1)} %get-tuple-element.76), channel_id=1, source_target_pairs={{0,16},{4,20},{8,24},{12,28},{16,0},{20,4},{24,8},{28,12},{1,17},{... | collective-permute-start | bytes 393224 | tf_op jit(solution)/shard_map/ppermute | solution.py:235
  128.3 17.8 %collective-permute-start.13 = (bf16[8,32,256]{2,1,0:T(8,128)(2,1)}, bf16[8,32,256]{2,1,0:T(8,128)(2,1)S(1)}, u32[]{:S(2)}, u32[]{:S(2)}) collective-permute-start(bf16[8,32,256]{2,1,0:T(8,128)(2,1)} %get-tuple-element.77), channel_id=1, source_target_pairs={{0,24},{4,28},{8,16},{12,20},{16,8},{20,12},{24,0},{28,4},{1,25},{... | collective-permute-start | bytes 393224 | tf_op jit(solution)/shard_map/ppermute | solution.py:235
  154.8 16.5 %copy-start = (bf16[8,4,64,64]{2,3,1,0:T(8,128)(2,1)}, bf16[8,4,64,64]{2,3,1,0:T(8,128)(2,1)S(1)}, u32[]{:S(2)}) copy-start(bf16[8,4,64,64]{2,3,1,0:T(8,128)(2,1)S(1)} %reshape.53) | copy-start | bytes 786436
  174.0 7.5 %collective-permute-start.16 = (bf16[8,32,256]{2,1,0:T(8,128)(2,1)S(1)}, bf16[8,32,256]{2,1,0:T(8,128)(2,1)S(1)}, u32[]{:S(2)}, u32[]{:S(2)}) collective-permute-start(bf16[8,32,256]{2,1,0:T(8,128)(2,1)S(1)} %slice.74.refs_0_), channel_id=1, source_target_pairs={{0,24},{4,28},{8,16},{12,20},{16,8},{20,12},{24,0},{28,4},{1,25},{... | collective-permute-start | bytes 393224 | tf_op jit(solution)/shard_map/ppermute | solution.py:235
  177.6 7.3 %collective-permute-start.15 = (bf16[8,32,256]{2,1,0:T(8,128)(2,1)S(1)}, bf16[8,32,256]{2,1,0:T(8,128)(2,1)S(1)}, u32[]{:S(2)}, u32[]{:S(2)}) collective-permute-start(bf16[8,32,256]{2,1,0:T(8,128)(2,1)S(1)} %slice.74.refs_0_), channel_id=1, source_target_pairs={{0,16},{4,20},{8,24},{12,28},{16,0},{20,4},{24,8},{28,12},{1,17},{... | collective-permute-start | bytes 393224 | tf_op jit(solution)/shard_map/ppermute | solution.py:235
  177.6 7.3 %collective-permute-start.14 = (bf16[8,32,256]{2,1,0:T(8,128)(2,1)S(1)}, bf16[8,32,256]{2,1,0:T(8,128)(2,1)S(1)}, u32[]{:S(2)}, u32[]{:S(2)}) collective-permute-start(bf16[8,32,256]{2,1,0:T(8,128)(2,1)S(1)} %slice.74.refs_0_), channel_id=1, source_target_pairs={{0,8},{4,12},{8,0},{12,4},{16,24},{20,28},{24,16},{28,20},{1,9},{5... | collective-permute-start | bytes 393224 | tf_op jit(solution)/shard_map/ppermute | solution.py:235
  190.7 22.7 %collective-permute-start.19 = (bf16[4,8,32,256]{3,2,1,0:T(8,128)(2,1)}, bf16[4,8,32,256]{3,2,1,0:T(8,128)(2,1)S(1)}, u32[]{:S(2)}, u32[]{:S(2)}) collective-permute-start(bf16[4,8,32,256]{3,2,1,0:T(8,128)(2,1)} %stack_blocks.4.refs_0_), channel_id=1, source_target_pairs={{0,3},{1,2},{2,1},{3,0},{4,7},{5,6},{6,5},{7,4},{8,11},{9,10},{10,... | collective-permute-start | bytes 1572872 | tf_op jit(solution)/shard_map/ppermute | solution.py:235
  192.1 23.5 %collective-permute-start.18 = (bf16[4,8,32,256]{3,2,1,0:T(8,128)(2,1)}, bf16[4,8,32,256]{3,2,1,0:T(8,128)(2,1)S(1)}, u32[]{:S(2)}, u32[]{:S(2)}) collective-permute-start(bf16[4,8,32,256]{3,2,1,0:T(8,128)(2,1)} %stack_blocks.4.refs_0_), channel_id=1, source_target_pairs={{0,2},{1,3},{2,0},{3,1},{4,6},{5,7},{6,4},{7,5},{8,10},{9,11},{10,... | collective-permute-start | bytes 1572872 | tf_op jit(solution)/shard_map/ppermute | solution.py:235
  193.6 22.2 %collective-permute-start.17 = (bf16[4,8,32,256]{3,2,1,0:T(8,128)(2,1)}, bf16[4,8,32,256]{3,2,1,0:T(8,128)(2,1)S(1)}, u32[]{:S(2)}, u32[]{:S(2)}) collective-permute-start(bf16[4,8,32,256]{3,2,1,0:T(8,128)(2,1)} %stack_blocks.4.refs_0_), channel_id=1, source_target_pairs={{0,1},{1,0},{2,3},{3,2},{4,5},{5,4},{6,7},{7,6},{8,9},{9,8},{10,11... | collective-permute-start | bytes 1572872 | tf_op jit(solution)/shard_map/ppermute | solution.py:235
  194.4 28.5 %copy-start.56 = (bf16[64,3]{0,1:T(4,128)(2,1)S(1)}, bf16[64,3]{0,1:T(4,128)(2,1)}, u32[]{:S(2)}) copy-start(bf16[64,3]{0,1:T(4,128)(2,1)} %param.10) | copy-start | bytes 1156
  194.8 8.0 %collective-permute-start.22 = (bf16[8,32,256]{2,1,0:T(8,128)(2,1)S(1)}, bf16[8,32,256]{2,1,0:T(8,128)(2,1)S(1)}, u32[]{:S(2)}, u32[]{:S(2)}) collective-permute-start(bf16[8,32,256]{2,1,0:T(8,128)(2,1)S(1)} %slice.76.refs_0_), channel_id=1, source_target_pairs={{0,24},{4,28},{8,16},{12,20},{16,8},{20,12},{24,0},{28,4},{1,25},{... | collective-permute-start | bytes 393224 | tf_op jit(solution)/shard_map/ppermute | solution.py:235
  197.6 8.6 %collective-permute-start.21 = (bf16[8,32,256]{2,1,0:T(8,128)(2,1)S(1)}, bf16[8,32,256]{2,1,0:T(8,128)(2,1)S(1)}, u32[]{:S(2)}, u32[]{:S(2)}) collective-permute-start(bf16[8,32,256]{2,1,0:T(8,128)(2,1)S(1)} %slice.76.refs_0_), channel_id=1, source_target_pairs={{0,16},{4,20},{8,24},{12,28},{16,0},{20,4},{24,8},{28,12},{1,17},{... | collective-permute-start | bytes 393224 | tf_op jit(solution)/shard_map/ppermute | solution.py:235
  202.8 5.4 collective-permute-start.20
  213.4 17.4 %copy-start.57 = (f32[3]{0:T(128)S(1)}, f32[3]{0:T(128)}, u32[]{:S(2)}) copy-start(f32[3]{0:T(128)} %param.11) | copy-start | bytes 40
  222.9 8.0 %collective-permute-start.23 = (bf16[4,4,8,32,256]{4,3,2,1,0:T(8,128)(2,1)}, bf16[4,4,8,32,256]{4,3,2,1,0:T(8,128)(2,1)}, u32[]{:S(2)}, u32[]{:S(2)}) collective-permute-start(bf16[4,4,8,32,256]{4,3,2,1,0:T(8,128)(2,1)} %stack_blocks.6.own_ref), channel_id=1, source_target_pairs={{0,4},{4,0},{8,12},{12,8},{16,20},{20,16},{24,28},{28,24},{1,5},{5... | collective-permute-start | bytes 6291464 | tf_op jit(solution)/shard_map/ppermute | solution.py:235
  227.3 61.4 %collective-permute-start.26 = (bf16[4,8,32,256]{3,2,1,0:T(8,128)(2,1)S(1)}, bf16[4,8,32,256]{3,2,1,0:T(8,128)(2,1)S(1)}, u32[]{:S(2)}, u32[]{:S(2)}) collective-permute-start(bf16[4,8,32,256]{3,2,1,0:T(8,128)(2,1)S(1)} %copy-done.1), channel_id=1, source_target_pairs={{0,3},{1,2},{2,1},{3,0},{4,7},{5,6},{6,5},{7,4},{8,11},{9,10},{10,... | collective-permute-start | bytes 1572872 | tf_op jit(solution)/shard_map/ppermute | solution.py:235
  228.4 60.3 %collective-permute-start.25 = (bf16[4,8,32,256]{3,2,1,0:T(8,128)(2,1)S(1)}, bf16[4,8,32,256]{3,2,1,0:T(8,128)(2,1)S(1)}, u32[]{:S(2)}, u32[]{:S(2)}) collective-permute-start(bf16[4,8,32,256]{3,2,1,0:T(8,128)(2,1)S(1)} %copy-done.1), channel_id=1, source_target_pairs={{0,2},{1,3},{2,0},{3,1},{4,6},{5,7},{6,4},{7,5},{8,10},{9,11},{10,... | collective-permute-start | bytes 1572872 | tf_op jit(solution)/shard_map/ppermute | solution.py:235
  230.3 58.5 %collective-permute-start.24 = (bf16[4,8,32,256]{3,2,1,0:T(8,128)(2,1)S(1)}, bf16[4,8,32,256]{3,2,1,0:T(8,128)(2,1)S(1)}, u32[]{:S(2)}, u32[]{:S(2)}) collective-permute-start(bf16[4,8,32,256]{3,2,1,0:T(8,128)(2,1)S(1)} %copy-done.1), channel_id=1, source_target_pairs={{0,1},{1,0},{2,3},{3,2},{4,5},{5,4},{6,7},{7,6},{8,9},{9,8},{10,11... | collective-permute-start | bytes 1572872 | tf_op jit(solution)/shard_map/ppermute | solution.py:235
  295.5 4.4 collective-permute-start.27
  368.4 35.8 %collective-permute-start.31 = (f32[3,32,2,256]{3,2,1,0:T(2,128)S(1)}, f32[3,32,2,256]{3,2,1,0:T(2,128)S(1)}, u32[]{:S(2)}, u32[]{:S(2)}) collective-permute-start(f32[3,32,2,256]{3,2,1,0:T(2,128)S(1)} %get-tuple-element.126), channel_id=1, source_target_pairs={{1,0},{2,1},{3,2},{5,4},{6,5},{7,6},{9,8},{10,9},{11,10},{13,12},{... | collective-permute-start | bytes 589832 | tf_op jit(solution)/shard_map/ppermute | solution.py:64
  369.7 34.5 %collective-permute-start.30 = (f32[3,32,2,256]{3,2,1,0:T(2,128)S(1)}, f32[3,32,2,256]{3,2,1,0:T(2,128)S(1)}, u32[]{:S(2)}, u32[]{:S(2)}) collective-permute-start(f32[3,32,2,256]{3,2,1,0:T(2,128)S(1)} %get-tuple-element.127), channel_id=1, source_target_pairs={{0,1},{1,2},{2,3},{4,5},{5,6},{6,7},{8,9},{9,10},{10,11},{12,13},{... | collective-permute-start | bytes 589832 | tf_op jit(solution)/shard_map/ppermute | solution.py:64
  374.3 30.0 %collective-permute-start.29 = (f32[3,2,32,256]{3,2,1,0:T(8,128)S(1)}, f32[3,2,32,256]{3,2,1,0:T(8,128)S(1)}, u32[]{:S(2)}, u32[]{:S(2)}) collective-permute-start(f32[3,2,32,256]{3,2,1,0:T(8,128)S(1)} %get-tuple-element.128), channel_id=1, source_target_pairs={{4,0},{5,1},{6,2},{7,3},{8,4},{9,5},{10,6},{11,7},{12,8},{13,9},{1... | collective-permute-start | bytes 589832 | tf_op jit(solution)/shard_map/ppermute | solution.py:64
  375.6 28.7 %collective-permute-start.28 = (f32[3,2,32,256]{3,2,1,0:T(8,128)S(1)}, f32[3,2,32,256]{3,2,1,0:T(8,128)S(1)}, u32[]{:S(2)}, u32[]{:S(2)}) collective-permute-start(f32[3,2,32,256]{3,2,1,0:T(8,128)S(1)} %get-tuple-element.129), channel_id=1, source_target_pairs={{0,4},{1,5},{2,6},{3,7},{4,8},{5,9},{6,10},{7,11},{8,12},{9,13},{1... | collective-permute-start | bytes 589832 | tf_op jit(solution)/shard_map/ppermute | solution.py:64
  379.6 6.1 collective-permute-start.35
  385.6 18.7 %copy-start.51 = (f32[3,2,2,256]{3,2,1,0:T(2,128)}, f32[3,2,2,256]{3,2,1,0:T(2,128)S(1)}, u32[]{:S(2)}) copy-start(f32[3,2,2,256]{3,2,1,0:T(2,128)S(1)} %collective-permute-done.35.refs_7_) | copy-start | bytes 36868
  385.6 0.7 collective-permute-start.34
  386.3 18.0 %copy-start.52 = (f32[3,2,2,256]{3,2,1,0:T(2,128)}, f32[3,2,2,256]{3,2,1,0:T(2,128)S(1)}, u32[]{:S(2)}) copy-start(f32[3,2,2,256]{3,2,1,0:T(2,128)S(1)} %collective-permute-done.34.refs_6_) | copy-start | bytes 36868
  386.3 0.7 collective-permute-start.33
  387.0 17.3 %copy-start.53 = (f32[3,2,2,256]{3,2,1,0:T(2,128)}, f32[3,2,2,256]{3,2,1,0:T(2,128)S(1)}, u32[]{:S(2)}) copy-start(f32[3,2,2,256]{3,2,1,0:T(2,128)S(1)} %collective-permute-done.33.refs_5_) | copy-start | bytes 36868
  387.0 17.3 %collective-permute-start.32 = (f32[3,2,2,256]{3,2,1,0:T(2,128)S(1)}, f32[3,2,2,256]{3,2,1,0:T(2,128)S(1)}, u32[]{:S(2)}, u32[]{:S(2)}) collective-permute-start(f32[3,2,2,256]{3,2,1,0:T(2,128)S(1)} %get-tuple-element.125), channel_id=1, source_target_pairs={{0,5},{1,6},{2,7},{4,9},{5,10},{6,11},{8,13},{9,14},{10,15},{12,17... | collective-permute-start | bytes 36872 | tf_op jit(solution)/shard_map/ppermute | solution.py:64
  447.9 4.4 collective-permute-start.36
  459.9 30.6 %copy-start.55 = (f32[8,256]{1,0:T(8,128)S(1)}, f32[8,256]{1,0:T(8,128)}, u32[]{:S(2)}) copy-start(f32[8,256]{1,0:T(8,128)} %get-tuple-element.109) | copy-start | bytes 24580
  459.9 30.7 %copy-start.37 = (f32[8,16,256]{2,1,0:T(8,128)S(1)}, f32[8,16,256]{2,1,0:T(8,128)}, u32[]{:S(2)}) copy-start(f32[8,16,256]{2,1,0:T(8,128)} %get-tuple-element.107) | copy-start | bytes 393220
  486.8 4.9 collective-permute-start.40
  487.0 15.0 %collective-permute-start.37 = (bf16[4,8,32,256]{3,2,1,0:T(8,128)(2,1)}, bf16[4,8,32,256]{3,2,1,0:T(8,128)(2,1)S(1)}, u32[]{:S(2)}, u32[]{:S(2)}) collective-permute-start(bf16[4,8,32,256]{3,2,1,0:T(8,128)(2,1)} %get-tuple-element.87), channel_id=1, source_target_pairs={{0,1},{1,0},{2,3},{3,2},{4,5},{5,4},{6,7},{7,6},{8,9},{9,8},{10,11... | collective-permute-start | bytes 1572872 | tf_op jit(solution)/shard_map/ppermute | solution.py:235
  489.0 25.2 %collective-permute-start.38 = (bf16[4,8,32,256]{3,2,1,0:T(8,128)(2,1)}, bf16[4,8,32,256]{3,2,1,0:T(8,128)(2,1)S(1)}, u32[]{:S(2)}, u32[]{:S(2)}) collective-permute-start(bf16[4,8,32,256]{3,2,1,0:T(8,128)(2,1)} %get-tuple-element.88), channel_id=1, source_target_pairs={{0,2},{1,3},{2,0},{3,1},{4,6},{5,7},{6,4},{7,5},{8,10},{9,11},{10,... | collective-permute-start | bytes 1572872 | tf_op jit(solution)/shard_map/ppermute | solution.py:235
  489.0 25.2 %collective-permute-start.39 = (bf16[4,8,32,256]{3,2,1,0:T(8,128)(2,1)}, bf16[4,8,32,256]{3,2,1,0:T(8,128)(2,1)}, u32[]{:S(2)}, u32[]{:S(2)}) collective-permute-start(bf16[4,8,32,256]{3,2,1,0:T(8,128)(2,1)} %get-tuple-element.89), channel_id=1, source_target_pairs={{0,3},{1,2},{2,1},{3,0},{4,7},{5,6},{6,5},{7,4},{8,11},{9,10},{10,... | collective-permute-start | bytes 1572872 | tf_op jit(solution)/shard_map/ppermute | solution.py:235
  520.2 7.2 %collective-permute-start.44 = (bf16[8,32,256]{2,1,0:T(8,128)(2,1)}, bf16[8,32,256]{2,1,0:T(8,128)(2,1)S(1)}, u32[]{:S(2)}, u32[]{:S(2)}) collective-permute-start(bf16[8,32,256]{2,1,0:T(8,128)(2,1)} %get-tuple-element.101), channel_id=1, source_target_pairs={{0,8},{4,12},{8,0},{12,4},{16,24},{20,28},{24,16},{28,20},{1,9},{5... | collective-permute-start | bytes 393224 | tf_op jit(solution)/shard_map/ppermute | solution.py:235
  520.9 28.1 %collective-permute-start.45 = (bf16[8,32,256]{2,1,0:T(8,128)(2,1)}, bf16[8,32,256]{2,1,0:T(8,128)(2,1)S(1)}, u32[]{:S(2)}, u32[]{:S(2)}) collective-permute-start(bf16[8,32,256]{2,1,0:T(8,128)(2,1)} %get-tuple-element.102), channel_id=1, source_target_pairs={{0,16},{4,20},{8,24},{12,28},{16,0},{20,4},{24,8},{28,12},{1,17},{... | collective-permute-start | bytes 393224 | tf_op jit(solution)/shard_map/ppermute | solution.py:235
  520.9 28.0 %collective-permute-start.46 = (bf16[8,32,256]{2,1,0:T(8,128)(2,1)}, bf16[8,32,256]{2,1,0:T(8,128)(2,1)S(1)}, u32[]{:S(2)}, u32[]{:S(2)}) collective-permute-start(bf16[8,32,256]{2,1,0:T(8,128)(2,1)} %get-tuple-element.103), channel_id=1, source_target_pairs={{0,24},{4,28},{8,16},{12,20},{16,8},{20,12},{24,0},{28,4},{1,25},{... | collective-permute-start | bytes 393224 | tf_op jit(solution)/shard_map/ppermute | solution.py:235
  525.1 29.5 %collective-permute-start.41 = (bf16[4,8,32,256]{3,2,1,0:T(8,128)(2,1)}, bf16[4,8,32,256]{3,2,1,0:T(8,128)(2,1)S(1)}, u32[]{:S(2)}, u32[]{:S(2)}) collective-permute-start(bf16[4,8,32,256]{3,2,1,0:T(8,128)(2,1)} %get-tuple-element.97), channel_id=1, source_target_pairs={{0,1},{1,0},{2,3},{3,2},{4,5},{5,4},{6,7},{7,6},{8,9},{9,8},{10,11... | collective-permute-start | bytes 1572872 | tf_op jit(solution)/shard_map/ppermute | solution.py:235
  525.4 29.2 %collective-permute-start.42 = (bf16[4,8,32,256]{3,2,1,0:T(8,128)(2,1)}, bf16[4,8,32,256]{3,2,1,0:T(8,128)(2,1)S(1)}, u32[]{:S(2)}, u32[]{:S(2)}) collective-permute-start(bf16[4,8,32,256]{3,2,1,0:T(8,128)(2,1)} %get-tuple-element.98), channel_id=1, source_target_pairs={{0,2},{1,3},{2,0},{3,1},{4,6},{5,7},{6,4},{7,5},{8,10},{9,11},{10,... | collective-permute-start | bytes 1572872 | tf_op jit(solution)/shard_map/ppermute | solution.py:235
  527.4 21.5 %copy-start.38 = (bf16[8,32,256]{2,1,0:T(8,128)(2,1)}, bf16[8,32,256]{2,1,0:T(8,128)(2,1)S(1)}, u32[]{:S(2)}) copy-start(bf16[8,32,256]{2,1,0:T(8,128)(2,1)S(1)} %collective-permute-done.44.refs_1_) | copy-start | bytes 393220
  527.4 27.2 %collective-permute-start.43 = (bf16[4,8,32,256]{3,2,1,0:T(8,128)(2,1)}, bf16[4,8,32,256]{3,2,1,0:T(8,128)(2,1)S(1)}, u32[]{:S(2)}, u32[]{:S(2)}) collective-permute-start(bf16[4,8,32,256]{3,2,1,0:T(8,128)(2,1)} %get-tuple-element.99), channel_id=1, source_target_pairs={{0,3},{1,2},{2,1},{3,0},{4,7},{5,6},{6,5},{7,4},{8,11},{9,10},{10,... | collective-permute-start | bytes 1572872 | tf_op jit(solution)/shard_map/ppermute | solution.py:235
  561.7 24.8 %collective-permute-start.47 = (bf16[8,32,256]{2,1,0:T(8,128)(2,1)}, bf16[8,32,256]{2,1,0:T(8,128)(2,1)S(1)}, u32[]{:S(2)}, u32[]{:S(2)}) collective-permute-start(bf16[8,32,256]{2,1,0:T(8,128)(2,1)} %get-tuple-element.104), channel_id=1, source_target_pairs={{0,8},{4,12},{8,0},{12,4},{16,24},{20,28},{24,16},{28,20},{1,9},{5... | collective-permute-start | bytes 393224 | tf_op jit(solution)/shard_map/ppermute | solution.py:235
  562.7 23.8 %collective-permute-start.48 = (bf16[8,32,256]{2,1,0:T(8,128)(2,1)}, bf16[8,32,256]{2,1,0:T(8,128)(2,1)S(1)}, u32[]{:S(2)}, u32[]{:S(2)}) collective-permute-start(bf16[8,32,256]{2,1,0:T(8,128)(2,1)} %get-tuple-element.105), channel_id=1, source_target_pairs={{0,16},{4,20},{8,24},{12,28},{16,0},{20,4},{24,8},{28,12},{1,17},{... | collective-permute-start | bytes 393224 | tf_op jit(solution)/shard_map/ppermute | solution.py:235
  562.7 23.8 %collective-permute-start.49 = (bf16[8,32,256]{2,1,0:T(8,128)(2,1)}, bf16[8,32,256]{2,1,0:T(8,128)(2,1)S(1)}, u32[]{:S(2)}, u32[]{:S(2)}) collective-permute-start(bf16[8,32,256]{2,1,0:T(8,128)(2,1)} %get-tuple-element.106), channel_id=1, source_target_pairs={{0,24},{4,28},{8,16},{12,20},{16,8},{20,12},{24,0},{28,4},{1,25},{... | collective-permute-start | bytes 393224 | tf_op jit(solution)/shard_map/ppermute | solution.py:235
  566.1 27.5 %copy-start.7 = (bf16[8,32,256]{2,1,0:T(8,128)(2,1)S(1)}, bf16[8,32,256]{2,1,0:T(8,128)(2,1)}, u32[]{:S(2)}) copy-start(bf16[8,32,256]{2,1,0:T(8,128)(2,1)} %sum_blocks.22.refs_1_) | copy-start | bytes 393220
  (48 other events, 129.2 us)

commit v3 on v2

--- a/solution.py
+++ b/solution.py
@@ -13,7 +13,6 @@
 CORES = 2
 LANES = 128
 VMEM_LIMIT = 56 * 1024 * 1024
-PARTS = 2
 CHUNK = 256
 
 
@@ -47,24 +46,19 @@
     return jnp.cos(phases).astype(BF16).astype(F32), jnp.sin(phases).astype(BF16).astype(F32)
 
 
-def halo(lay, block):
-    sizes = {"gy": lay.n_gy, "gz": lay.n_gz}
-
-    def cut(dim, step):
-        count = block.shape[dim]
-        return slice(None) if step == 0 else slice(count - 2, count) if step > 0 else slice(0, 2)
-
-    def moved(y_step, z_step):
-        pairs = [
-            (y * lay.n_gz + z, (y + y_step) * lay.n_gz + z + z_step)
-            for y in range(sizes["gy"])
-            for z in range(sizes["gz"])
-            if 0 <= y + y_step < sizes["gy"] and 0 <= z + z_step < sizes["gz"]
-        ]
-        return lax.ppermute(block[:, cut(1, y_step), cut(2, z_step)], ("gy", "gz"), pairs)
-
-    steps = [(1, 0), (-1, 0), (0, 1), (0, -1), (1, 1), (1, -1), (-1, 1), (-1, -1)]
-    return [moved(*step) for step in steps]
+def halo(block):
+    def moved(value, axis, step):
+        count = lax.axis_size(axis)
+        pairs = [(n, n + step) for n in range(count) if 0 <= n + step < count]
+        return lax.ppermute(value, axis, pairs)
+
+    low = moved(block[:, -2:], "gy", 1)
+    high = moved(block[:, :2], "gy", -1)
+    ends = [
+        jnp.concatenate([part[:, :, cut] for part in (low, block, high)], axis=1)
+        for cut in (slice(-2, None), slice(0, 2))
+    ]
+    return [low, high, moved(ends[0], "gz", 1), moved(ends[1], "gz", -1)]
 
 
 class Layout:
@@ -236,48 +230,81 @@
 
 
 def sum_kernel(n_in, n_out, factor, *refs):
-    total = refs[0][...].astype(F32)
-    for ref in refs[1:n_in]:
-        total = total + ref[...].astype(F32)
-    total = (total * factor).astype(BF16)
-    for n, out_ref in enumerate(refs[-n_out:]):
-        out_ref[...] = total[n] if n_out > 1 else total
-
-
-def sum_blocks(values, split, factor=1.0, after=()):
+    rows = refs[0].shape[1]
+    chunk = math.gcd(rows, 256)
+
+    def body(n, carry):
+        here = pl.ds(pl.multiple_of(n * chunk, chunk), chunk)
+        for m, out_ref in enumerate(refs[-n_out:]):
+            total = refs[0][m, here].astype(F32)
+            for ref in refs[1:n_in]:
+                total = total + ref[m, here].astype(F32)
+            out_ref[here] = (total * factor).astype(out_ref.dtype)
+        return carry
+
+    lax.fori_loop(0, rows // chunk, body, 0)
+
+
+VMEM = pl.BlockSpec(memory_space=pltpu.VMEM)
+
+
+def sum_blocks(values, split, factor=1.0, after=(), weight=2):
     shape = values[0].shape
-    out = shape[1:] if split else shape
-    count = shape[-3]
-
-    def spec(sizes):
-        lead = len(sizes) - 3
-        block = sizes[:lead] + (1,) + sizes[lead + 1 :]
-        return pl.BlockSpec(block, lambda i: (0,) * lead + (i, 0, 0))
-
     n_out = shape[0] if split else 1
-    total = math.prod(shape)
+    rows = math.prod(shape[:-1]) // n_out
+    values = [value.reshape(n_out, rows, shape[-1]) for value in values]
     outs = pl.pallas_call(
         functools.partial(sum_kernel, len(values), n_out, factor),
-        grid=(count,),
-        in_specs=[spec(shape)] * len(values) + [ANY] * len(after),
-        out_specs=[spec(out)] * n_out,
-        out_shape=[jax.ShapeDtypeStruct(out, BF16)] * n_out,
-        compiler_params=params(),
-        cost_estimate=cost(total * len(values), total * 2 * (len(values) + 1)),
+        in_specs=[VMEM] * len(values) + [ANY] * len(after),
+        out_specs=[VMEM] * n_out,
+        out_shape=[jax.ShapeDtypeStruct((rows, shape[-1]), values[0].dtype)] * n_out,
+        compiler_params=pltpu.CompilerParams(vmem_limit_bytes=VMEM_LIMIT),
+        cost_estimate=cost(math.prod(shape) * len(values), math.prod(shape) * weight * len(values)),
         name="sum_blocks",
     )(*values, *after)
-    return list(outs)
-
-
-def from_cores(own, send, after=()):
-    return sum_blocks([own, exchange(send, "gy", 1)], True, after=after)
-
-
-def from_depth(blocks, after=()):
-    return sum_blocks(
-        blocks[:1] + [exchange(block, "gz", d) for d, block in enumerate(blocks) if d], True,
-        after=after,
-    )
+    return [out.reshape(shape[1:] if split else shape) for out in outs]
+
+
+def core_kernel(own_ref, other_ref, *refs):
+    count = own_ref.shape[0]
+    for n, out_ref in enumerate(refs[len(refs) - count :]):
+        out_ref[0] = (own_ref[n, 0].astype(F32) + other_ref[n, 0].astype(F32)).astype(BF16)
+
+
+def from_cores(lay, own, other, half, after=()):
+    size = lay.groups // 2
+    tail = (size, lay.own, 2 * LANES)
+    given = pl.BlockSpec((lay.n_gz, 1) + tail, lambda i: (0, i, half, 0, 0))
+    return list(
+        pl.pallas_call(
+            core_kernel,
+            grid=(lay.chips,),
+            in_specs=[given, given] + [ANY] * len(after),
+            out_specs=[pl.BlockSpec((1,) + tail, lambda i: (i, 0, 0, 0))] * lay.n_gz,
+            out_shape=[jax.ShapeDtypeStruct((lay.chips,) + tail, BF16)] * lay.n_gz,
+            compiler_params=params(),
+            cost_estimate=cost(own.size // 2, own.size * 3),
+            name="core_sums",
+        )(own, other, *after)
+    )
+
+
+def sum_all(lay, own, send, factor, work):
+    other = exchange(send, "gy", 1)
+    early = from_cores(lay, own, other, 0)
+    done = work(0, early[:1])
+    early = to_depth(early)
+    late = to_depth(from_cores(lay, own, other, 1, [done, early[1]]))
+    done = work(1, late[:1])
+    early = sum_blocks(early, True, after=[done])
+    done = work(2, early[:1])
+    first = from_chips(early, factor, [done])
+    late = sum_blocks(late, True, after=[first])
+    return [first, from_chips(late, factor)]
+
+
+def to_depth(blocks):
+    return blocks[:1] + [exchange(block, "gz", d) for d, block in enumerate(blocks) if d]
 
 
 def from_chips(blocks, factor, after=()):
@@ -286,27 +313,22 @@
 
 
 def stack_kernel(n_in, *refs):
-    for n in range(n_in):
-        refs[-1][n] = refs[n][...]
+    out_ref, sems = refs[-2:]
+    copies = [pltpu.make_async_copy(refs[n], out_ref.at[n], sems.at[n]) for n in range(n_in)]
+    for copy in copies:
+        copy.start()
+    for copy in copies:
+        copy.wait()
 
 
 def stack_blocks(values, after=()):
-    shape = values[0].shape
-    count = shape[-3]
-
-    def spec(sizes):
-        lead = len(sizes) - 3
-        block = sizes[:lead] + (1,) + sizes[lead + 1 :]
-        return pl.BlockSpec(block, lambda i: (0,) * lead + (i, 0, 0))
-
-    out = (len(values),) + shape
+    out = (len(values),) + values[0].shape
     return pl.pallas_call(
         functools.partial(stack_kernel, len(values)),
-        grid=(count,),
-        in_specs=[spec(shape)] * len(values) + [ANY] * len(after),
-        out_specs=spec(out),
-        out_shape=jax.ShapeDtypeStruct(out, BF16),
-        compiler_params=params(),
+        in_specs=[ANY] * (len(values) + len(after)),
+        out_specs=ANY,
+        out_shape=jax.ShapeDtypeStruct(out, values[0].dtype),
+        scratch_shapes=[pltpu.SemaphoreType.DMA((len(values),))],
         cost_estimate=cost(math.prod(out), 4 * math.prod(out)),
         name="stack_blocks",
     )(*values, *after)
@@ -515,12 +537,12 @@
     lax.fori_loop(0, count // 2, body, 0)
 
 
-def dense(lay, own, other, tables, x_table, point, weights, b_in, first, count, after=()):
+def dense(lay, own, other, tables, x_table, point, weights, b_in, first, count, kept=()):
     size = (lay.n_gz, lay.chips, 1, lay.own, 2 * LANES)
     modes = pl.BlockSpec(size, lambda i: (0, 0, i, 0, 0))
     block = (lay.pack, lay.rows, lay.depth, lay.width)
-    part = pl.BlockSpec(block, lambda i: (i, 0, 0, 0))
-    kept = jax.ShapeDtypeStruct((count * lay.pack,) + block[1:], BF16)
+    part = pl.BlockSpec(block, lambda i: (first + i, 0, 0, 0))
+    out = jax.ShapeDtypeStruct(point.shape, BF16)
     volume = lay.pack * lay.cells * lay.width
     steps = lay.mz // lay.step
     return pl.pallas_call(
@@ -532,13 +554,14 @@
             whole(tables[2].shape),
             whole(tables[3].shape),
             whole(x_table.shape),
-            pl.BlockSpec(block, lambda i: (first + i, 0, 0, 0)),
+            part,
             pl.BlockSpec(memory_space=pltpu.SMEM),
             whole(b_in.shape),
         ]
-        + [ANY] * len(after),
+        + [ANY] * len(kept),
         out_specs=[part, part, whole(b_in.shape)],
-        out_shape=[kept, kept, jax.ShapeDtypeStruct(b_in.shape, F32)],
+        out_shape=[out, out, jax.ShapeDtypeStruct(b_in.shape, F32)],
+        input_output_aliases={8 + n: n for n in range(len(kept))},
         scratch_shapes=[
             pltpu.VMEM((lay.blocks, 2, steps, lay.step * lay.band, 2 * LANES), BF16),
             pltpu.VMEM((CHUNK, lay.pack * lay.width), F32),
@@ -547,11 +570,11 @@
         compiler_params=params(),
         cost_estimate=cost(count * volume * 2 * 6 * LANES, count * volume * 24),
         name="dense",
-    )(own, other, tables[2], tables[3], x_table, point, weights, b_in, *after)
+    )(own, other, tables[2], tables[3], x_table, point, weights, b_in, *kept)
 
 
 def stencil_kernel(total_y, total_z, origin_ref, field_ref, *refs):
-    halos, (grad_ref, sums_ref, b_ref, gy_ref, rest_ref) = refs[:8], refs[8:]
+    halos, (grad_ref, sums_ref, b_ref, gy_ref, rest_ref) = refs[:4], refs[4:]
     _, rows_wide, depth_wide, width = b_ref.shape
     rows, depth = grad_ref.shape[1:3]
     low_y, high_y = pl.ds(0, 2), pl.ds(rows + 2, 2)
@@ -559,10 +582,8 @@
     mid_y, mid_z = pl.ds(2, rows), pl.ds(2, depth)
     b_ref[:, :, depth + 4 :] = jnp.zeros_like(b_ref[:, :, depth + 4 :])
     b_ref[:, mid_y, mid_z] = field_ref[...]
-    places = [
-        (low_y, mid_z), (high_y, mid_z), (mid_y, low_z), (mid_y, high_z),
-        (low_y, low_z), (low_y, high_z), (high_y, low_z), (high_y, high_z),
-    ]
+    all_y = pl.ds(0, rows_wide)
+    places = [(low_y, mid_z), (high_y, mid_z), (all_y, low_z), (all_y, high_z)]
     for ref, (y, z) in zip(halos, places):
         b_ref[:, y, z] = ref[...]
     shape = (depth_wide, width)
@@ -645,7 +666,7 @@
 
 
 def stencil(lay, b_field):
-    halos = halo(lay, b_field)
+    halos = halo(b_field)
     origin = jnp.stack([lay.y0, lay.z0]).astype(jnp.int32)
     wide = (3, lay.rows + 2, lay.depth + 8, lay.width)
     return pl.pallas_call(
@@ -653,7 +674,7 @@
         in_specs=[
             pl.BlockSpec(memory_space=pltpu.SMEM),
         ]
-        + [pl.BlockSpec(memory_space=pltpu.VMEM)] * 9,
+        + [VMEM] * 5,
         out_specs=[pl.BlockSpec(memory_space=pltpu.VMEM)] * 2,
         out_shape=[
             jax.ShapeDtypeStruct(b_field.shape, F32),
@@ -722,6 +743,7 @@
     out, spec = mode_blocks(lay, count)
     block = (lay.pack, lay.rows, lay.depth, lay.width)
     part = pl.BlockSpec(block, lambda i: (i, 0, 0, 0))
+    given = pl.BlockSpec(block, lambda i: (first + i, 0, 0, 0))
     volume = lay.pack * lay.cells * lay.width
     lines = -(-(3 * lay.pack + 1) // 8) * 8
     return pl.pallas_call(
@@ -729,8 +751,8 @@
         grid=(count,),
         in_specs=[
             pl.BlockSpec(memory_space=pltpu.SMEM),
-            part,
-            part,
+            given,
+            given,
             whole(grad_b.shape),
             whole(x_table.shape),
             whole(tables[0].shape),
@@ -744,7 +766,7 @@
             pl.BlockSpec((1, lines, lay.width), lambda i: (i, 0, 0)),
         ],
         out_shape=[
-            jax.ShapeDtypeStruct(hidden.shape, BF16),
+            jax.ShapeDtypeStruct((count * lay.pack,) + block[1:], BF16),
             out,
             out,
             jax.ShapeDtypeStruct((count, lines, lay.width), F32),
@@ -799,17 +821,18 @@
         )
 
 
-def point_grad(lay, field_in, grad_pre, after=()):
-    span = 4
+def point_grad(lay, field_in, grad_pre, first, rows, after=()):
+    span = math.gcd(4, rows)
 
     def block(count):
-        return pl.BlockSpec((count, span, lay.depth, lay.width), lambda i: (0, i, 0, 0))
+        size = (count, span, lay.depth, lay.width)
+        return pl.BlockSpec(size, lambda i: (0, first // span + i, 0, 0))
 
     count = grad_pre.shape[0]
     size = lay.channels * lay.tile
     return pl.pallas_call(
         functools.partial(point_kernel, lay.tile, len(after)),
-        grid=(lay.rows // span,),
+        grid=(rows // span,),
         in_specs=[block(lay.channels), block(count)] + [ANY] * len(after),
         out_specs=pl.BlockSpec((lay.channels, count), lambda i: (0, 0)),
         out_shape=jax.ShapeDtypeStruct((lay.channels, count), F32),
@@ -820,24 +843,8 @@
     )(field_in, grad_pre, *after)
 
 
-def join_kernel(n_in, *refs):
-    refs[-1][...] = jnp.concatenate([ref[...] for ref in refs[:n_in]], axis=1)
-
-
-def join(values, after=()):
-    vmem = pl.BlockSpec(memory_space=pltpu.VMEM)
-    rows = values[0].shape[0]
-    out = (rows, sum(value.shape[1] for value in values))
-    return pl.pallas_call(
-        functools.partial(join_kernel, len(values)),
-        in_specs=[vmem] * len(values) + [ANY] * len(after),
-        out_specs=vmem,
-        out_shape=jax.ShapeDtypeStruct(out, values[0].dtype),
-        name="join",
-    )(*values, *after)
-
-
-def outer_kernel(modes_ref, grads_ref, out_ref):
+def outer_kernel(modes_ref, grads_ref, *refs):
+    out_ref = refs[-1]
     pair, count, channels, wide = out_ref.shape[1:]
     columns = jnp.concatenate([modes_ref[0, a] for a in range(pair)], axis=1)
     rows = []
@@ -859,21 +866,29 @@
             out_ref[0, a, k : k + some] = here.reshape(some, channels, wide)
 
 
-def weight_grad(lay, modes_in, grads):
-    columns = jnp.transpose(modes_in, (0, 1, 3, 2))
-    rows = jnp.concatenate([grads[:, :, : lay.mx], grads[:, :, lay.mx :]], axis=-1)
+def weight_grad(lay, columns, rows, half, done=(), after=()):
     tile = (lay.mx, lay.channels, 2 * lay.channels)
     shape = (lay.kz, lay.ky) + tile
+    per = lay.ky // 2
+    first = half * lay.kz // 2
+
+    def spec(block):
+        return pl.BlockSpec(
+            (1, 2) + block, lambda i: (first + i // per, i % per) + (0,) * len(block)
+        )
+
     return pl.pallas_call(
         outer_kernel,
-        grid=(lay.own // 2,),
-        in_specs=[mode_spec(lay, columns.shape[2:]), mode_spec(lay, rows.shape[2:])],
-        out_specs=mode_spec(lay, tile),
+        grid=(lay.own // 4,),
+        in_specs=[spec(columns.shape[2:]), spec(rows.shape[2:])]
+        + [ANY] * (len(done) + len(after)),
+        out_specs=spec(tile),
         out_shape=jax.ShapeDtypeStruct(shape, F32),
+        input_output_aliases={2: 0} if done else {},
         compiler_params=params(),
-        cost_estimate=cost(math.prod(shape) * 4, math.prod(shape) * 4),
+        cost_estimate=cost(math.prod(shape) * 2, math.prod(shape) * 2),
         name="weight_grad",
-    )(columns, rows)
+    )(columns, rows, *done, *after)
 
 
 def on_device(field_in, spectral_weight, point_weight, point_bias, out_weight, out_bias):
@@ -881,27 +896,23 @@
     tables = lay.grid_tables()
     x_table, x_back = lay.x_tables()
     weights = out_weight.astype(F32)
-    per = lay.groups // PARTS
-    parts = range(PARTS)
     scale = math.sqrt(lay.mx * lay.my * lay.mz / (lay.width * lay.ny * lay.nz))
-    half = lay.rows // 2
+    cuts = [0, lay.rows // 4, lay.rows * 5 // 8, lay.rows]
 
     def point(n, done, after):
         bias = point_bias.reshape(1, lay.channels)
-        return pointwise(lay, field_in, point_weight.T, bias, n * half, half, done, after)
-
-    both, column = [], []
-    for n in parts:
-        own, send = forward_modes(
-            lay, field_in, x_table, tables, n * per, per, after=[b[0] for b in both[n - 1 : n]]
-        )
-        both.append(from_cores(own, send))
-    column.append(from_depth(both[0], both[1][:1]))
-    done = point(0, None, column[0][:1])
-    column.append(from_depth(both[1], [done]))
-    modes = [from_chips(column[0], scale, [done])]
-    done = point(1, done, column[1][:1] + modes)
-    modes.append(from_chips(column[1], scale, [done]))
+        first, count = cuts[n], cuts[n + 1] - cuts[n]
+        return pointwise(lay, field_in, point_weight.T, bias, first, count, done, after)
+
+    own, send = forward_modes(lay, field_in, x_table, tables, 0, lay.groups)
+    points = [None]
+
+    def point_part(n, after):
+        points.append(point(n, points[-1], after))
+        return points[-1]
+
+    modes = sum_all(lay, own, send, scale, point_part)
+    done = points[-1]
     modes_in = by_mode(lay, jnp.concatenate(modes))
     mixed = mix_modes(lay, modes_in, spectral_weight, after=[done])
     mine = by_group(lay, mixed.reshape(lay.kz, lay.ky, lay.mx, 2, lay.groups, lay.pack))
@@ -909,52 +920,58 @@
     b_field = jnp.broadcast_to(
         out_bias[:, None, None, None], (3, lay.rows, lay.depth, lay.width)
     ).astype(F32)
-    hiddens, slopes = [], []
-    columns = [spread_chips(lay, mine[n * per : (n + 1) * per]) for n in parts]
-    for n in parts:
-        own = spread_depth(lay, columns[n], columns[n + 1 : n + 2] if n == 0 else [b_field])
-        hidden, slope, b_field = dense(
-            lay, own, exchange(own, "gy", 1), tables, x_back, done, weights, b_field,
-            n * per, per,
-        )
-        hiddens.append(hidden)
-        slopes.append(slope)
+    first = max(lay.groups * 5 // 16, 1)
+    columns = [spread_chips(lay, mine[:first]), spread_chips(lay, mine[first:])]
+    own = spread_depth(lay, columns[0], columns[1:])
+    *kept, b_field = dense(
+        lay, own, exchange(own, "gy", 1), tables, x_back, done, weights, b_field, 0, first
+    )
+    own = spread_depth(lay, columns[1], [b_field])
+    hidden, slope, b_field = dense(
+        lay, own, exchange(own, "gy", 1), tables, x_back, done, weights, b_field,
+        first, lay.groups - first, kept,
+    )
 
     grad_b, edge = stencil(lay, b_field)
 
-    both, column, pres, sums = [], [], [], []
-    for n in parts:
-        pre, own, send, part = grad_modes(
-            lay, hiddens[n], slopes[n], grad_b, x_table, tables, weights, n * per, per,
-            after=[b[0] for b in both[n - 1 : n]],
-        )
-        both.append(from_cores(own, send))
-        pres.append(pre)
-        sums.append(part)
-    column.append(from_depth(both[0], both[1][:1]))
-    point_parts = [point_grad(lay, field_in, pres[0], column[0][:1])]
-    column.append(from_depth(both[1], point_parts[:1]))
-    grads = [from_chips(column[0], 1.0, point_parts)]
-    point_parts.append(point_grad(lay, field_in, pres[1], column[1][:1] + grads))
-    grads.append(from_chips(column[1], 1.0, point_parts[1:]))
-    sums = jnp.concatenate(sums)
+    pre, own, send, sums = grad_modes(
+        lay, hidden, slope, grad_b, x_table, tables, weights, 0, lay.groups
+    )
+    point_parts = []
+
+    def grad_part(n, after):
+        count = cuts[n + 1] - cuts[n]
+        point_parts.append(point_grad(lay, field_in, pre, cuts[n], count, after))
+        return point_parts[-1]
+
+    grads = sum_all(lay, own, send, 1.0, grad_part)
     outs = jnp.sum(sums[:, : 3 * lay.pack], axis=-1).reshape(3 * lay.channels)
     bias = sums[:, 3 * lay.pack, :LANES].reshape(lay.groups, lay.pack, lay.mx)[..., 0]
     ends = jnp.sum(edge, axis=-1)
     square = lay.channels * lay.channels
     flat = jnp.concatenate(
         [
-            join(point_parts, grads[-1:]).reshape(square),
+            sum_blocks(point_parts, False, 1.0, grads[-1:])[0].reshape(square),
             outs,
             bias.reshape(lay.channels),
             ends[:4],
         ]
     )
     flat = jnp.pad(flat, (0, -flat.shape[0] % 1024)).reshape(-1, LANES)
-    flat = jnp.sum(lax.all_gather(flat, ("gy", "gz")), axis=0).reshape(-1)
+    rows = by_mode(lay, jnp.concatenate(grads))
+    rows = jnp.concatenate([rows[:, :, : lay.mx], rows[:, :, lay.mx :]], axis=-1)
+    columns = jnp.transpose(modes_in, (0, 1, 3, 2))
+
+    def gathered(axis, steps, after):
+        return sum_blocks([flat] + [exchange(flat, axis, d) for d in steps], False, 1.0, after)[0]
+
+    flat = gathered("gz", range(1, lay.n_gz), [rows])
+    grad_spectral = weight_grad(lay, columns, rows, 0, after=[flat])
+    flat = gathered("gy", range(CORES, lay.n_gy, CORES), [grad_spectral])
+    grad_spectral = weight_grad(lay, columns, rows, 1, [grad_spectral], [flat])
+    flat = gathered("gy", [1], [grad_spectral]).reshape(-1)
     after = square + 3 * lay.channels
     ends = flat[after + lay.channels : after + lay.channels + 4]
-    grad_spectral = weight_grad(lay, modes_in, by_mode(lay, jnp.concatenate(grads)))
     return (
         ends[3] / (lay.width * lay.ny * lay.nz),
         grad_spectral,

time: 699 us -> 718 us (1.027)
  Pallas kernels: 413 us -> 517 us
  blocking collectives: 67.6 us -> 0 us
  waiting for transfers between devices: 67.5 us -> 53.8 us
  starting transfers between devices: 77.8 us -> 70.1 us
    pallas_call x6 -> x10, Pallas kernels: 37.7 us -> 198 us  [the longest x4 163 us: stack_blocks(): pl.pallas_call(functools.partial(stack_kernel, len(values)), in_specs=[AN...]
    all_gather x1 -> x0, blocking collectives: 67.6 us -> none  [on_device(): flat = jnp.sum(lax.all_gather(flat, ('gy', 'gz')), axis=0).reshape(-1)]
    pallas_call x12, Pallas kernels: 63.4 us -> 22.7 us  [sum_blocks(): pl.pallas_call(functools.partial(sum_kernel, len(values), n_out, factor),...]
    ppermute x8 -> x4, starting transfers between devices: 28.7 us -> 8.01 us  [moved(): return lax.ppermute(value, axis, pairs)]
    ppermute x42 -> x47, waiting for transfers between devices: 61.9 us -> 44.7 us  [exchange(): return lax.ppermute(value, axis, [(i, i ^ distance) for i in range(count)])]
    ppermute x42 -> x47, starting transfers between devices: 49.2 us -> 62.1 us  [exchange(): return lax.ppermute(value, axis, [(i, i ^ distance) for i in range(count)])]
    pallas_call x2, Pallas kernels: 120 us -> 112 us  [dense(): pl.pallas_call(functools.partial(dense_kernel, first), grid=(count,), in_...]
    pallas_call x2 -> x1, Pallas kernels: 53.7 us -> 49.6 us  [grad_modes(): pl.pallas_call(functools.partial(grad_kernel, first, len(after)), grid=(c...]
  transfers between devices with their start and end apart: 50 -> 51, of which waited for: 17 -> 17; matrix products, arithmetic and copies ran while one was open for 2% -> 3% of each run, Pallas kernels for 23% -> 25%
where the time goes in v3:
time: 718 us; the launch traced here: 709 us
  Pallas kernels  517 us (72%)
  starting transfers between devices  70.1 us (10%)
  waiting for transfers between devices  53.8 us (7%)
  local copies, waits for them, and re-layouts  48.3 us (7%)
  other arithmetic  16 us (2%)
    pallas_call x4, Pallas kernels, stack_blocks(): pl.pallas_call(functools.partial(stack_kernel, len(values)), in_specs=[AN...  163 us
    pallas_call x2, Pallas kernels, dense(): pl.pallas_call(functools.partial(dense_kernel, first), grid=(count,), in_...  112 us
    ppermute x47, starting transfers between devices, exchange(): return lax.ppermute(value, axis, [(i, i ^ distance) for i in range(count)])  62.1 us
    pallas_call x1, Pallas kernels, grad_modes(): pl.pallas_call(functools.partial(grad_kernel, first, len(after)), grid=(c...  49.6 us
    ppermute x47, waiting for transfers between devices, exchange(): return lax.ppermute(value, axis, [(i, i ^ distance) for i in range(count)])  44.7 us
    pallas_call x3, Pallas kernels, pointwise(): pl.pallas_call(functools.partial(pointwise_kernel, lay.tile), grid=(count...  37.6 us
    pallas_call x3, Pallas kernels, point_grad(): pl.pallas_call(functools.partial(point_kernel, lay.tile, len(after)), gri...  37.1 us
    pallas_call x1, Pallas kernels, forward_modes(): pl.pallas_call(functools.partial(modes_kernel, len(after)), grid=(count,)...  28.9 us
  transfers between devices with their start and end apart: 51, of which 17 were waited for; matrix products, arithmetic and copies ran while one was open for 3% of the time, Pallas kernels for 25%

profile of v3, /device:TPU:0, one launch (start us, length us, event | category | flops | bytes accessed | tf_op | source)
XLA Modules:
  0.0 708.6 jit_solution(7103951836252716690)
XLA Ops:
  0.8 2.9 compare_select_fusion.9
  7.4 28.9 %forward_modes.1 = (bf16[4,4,16,32,256]{4,3,2,1,0:T(8,128)(2,1)}, bf16[4,4,16,32,256]{4,3,2,1,0:T(8,128)(2,1)}) custom-call(bf16[64,32,32,256]{3,2,1,0:T(8,128)(2,1)} %field_ref.13, bf16[1024,256]{1,0:T(8,128)(2,1)} %pad_maximum_fusion.x_ref, bf16[128,256]{1,0:T(8,128)(2,1)} %select_convert_fusion.5.z_ref, bf16[128,256]{1,0:T(8,128)(2,1)} %select_convert_fusion.4.y_ref), custom_call_target="tpu_custom_call" | custom-call | flops 8589934592 | bytes 50331648 | tf_op jit(solution)/shard_map/forward_modes/pallas_call | solution.py:208
  36.8 7.0 collective-permute-done.other_ref
  43.8 2.0 copy-done.1
  45.8 4.2 core_sums.4
  50.0 2.9 collective-permute-start.1
  55.1 9.8 %pointwise.3.refs_0_ = bf16[64,32,32,256]{3,2,1,0:T(8,128)(2,1)} custom-call(bf16[64,32,32,256]{3,2,1,0:T(8,128)(2,1)} %field_ref.13, bf16[64,64]{1,0:T(8,128)(2,1)} %bitcast.114, f32[1,64]{1,0:T(1,128)} %bitcast.144, bf16[4,8,32,256]{3,2,1,0:T(8,128)(2,1)} %get-tuple-element.54.refs_0_), custom_call_target="tpu_custom_call" | custom-call | flops 4294967296 | bytes 16777216 | tf_op jit(solution)/shard_map/pointwise/pallas_call | solution.py:440
  66.6 4.2 core_sums.5
  70.8 13.7 %pointwise.4.refs_4_.refs_0_ = bf16[64,32,32,256]{3,2,1,0:T(8,128)(2,1)} custom-call(bf16[64,32,32,256]{3,2,1,0:T(8,128)(2,1)} %field_ref.13, bf16[64,64]{1,0:T(8,128)(2,1)} %bitcast.115, f32[1,64]{1,0:T(1,128)} %bitcast.145, bf16[64,32,32,256]{3,2,1,0:T(8,128)(2,1)} %pointwise.3.refs_0_, ...), custom_call_target="tpu_custom_call", output_to_operand_aliasing={{}: (3, {})} | custom-call | flops 6442450944 | bytes 25165824 | tf_op jit(solution)/shard_map/pointwise/pallas_call | solution.py:440
  85.5 2.5 sum_blocks.12
  88.0 3.2 collective-permute-start.5
  96.0 3.0 collective-permute-done.5
  99.0 2.5 collective-permute-start.9
  101.4 14.1 %pointwise.5.refs_4_.refs_0_.point_ref = bf16[64,32,32,256]{3,2,1,0:T(8,128)(2,1)} custom-call(bf16[64,32,32,256]{3,2,1,0:T(8,128)(2,1)} %field_ref.13, bf16[64,64]{1,0:T(8,128)(2,1)} %bitcast.116, f32[1,64]{1,0:T(1,128)} %bitcast.146, bf16[64,32,32,256]{3,2,1,0:T(8,128)(2,1)} %pointwise.4.refs_4_.refs_0_, ...), custom_call_target="tpu_custom_call", output_to_operand_aliasing={{}: (3, {})} | custom-call | flops 6442450944 | bytes 25165824 | tf_op jit(solution)/shard_map/pointwise/pallas_call | solution.py:440
  116.3 1.8 sum_blocks.13
  119.3 2.4 sum_blocks.14
  121.7 2.2 collective-permute-start.10
  123.9 3.2 collective-permute-start.11
  128.9 3.3 collective-permute-done.11
  132.3 2.0 collective-permute-done.12
  134.9 1.8 sum_blocks.15
  141.6 15.2 %mix_modes.1 = bf16[8,4,32,128]{3,2,1,0:T(8,128)(2,1)} custom-call(bf16[8,4,64,64]{3,2,1,0:T(8,128)(2,1)} %copy.30.modes_ref, bf16[8,4,32,64,128]{4,3,2,1,0:T(8,128)(2,1)} %weight_ref.1, bf16[64,32,32,256]{3,2,1,0:T(8,128)(2,1)} %pointwise.5.refs_4_.refs_0_.point_ref), custom_call_target="tpu_custom_call" | custom-call | flops 67108864 | bytes 16777216 | tf_op jit(solution)/shard_map/mix_modes/pallas_call | solution.py:393
  158.8 2.0 collective-permute-start.21
  164.4 2.0 collective-permute-start.15
  166.4 1.8 collective-permute-done.20.refs_2_
  169.4 11.1 %stack_blocks.5.refs_0_ = bf16[4,5,32,256]{3,2,1,0:T(8,128)(2,1)} custom-call(bf16[5,32,256]{2,1,0:T(8,128)(2,1)} %copy-done.25, bf16[5,32,256]{2,1,0:T(8,128)(2,1)} %copy-done.48, bf16[5,32,256]{2,1,0:T(8,128)(2,1)} %copy-done.47, bf16[5,32,256]{2,1,0:T(8,128)(2,1)} %copy-done.46), custom_call_target="tpu_custom_call" | custom-call | flops 163840 | bytes 655360 | tf_op jit(solution)/shard_map/stack_blocks/pallas_call | solution.py:326
  184.8 2.3 collective-permute-start.13
  187.1 4.9 collective-permute-done.14.refs_2_
  193.4 23.0 %stack_blocks.4.refs_4_.refs_0_ = bf16[4,11,32,256]{3,2,1,0:T(8,128)(2,1)} custom-call(bf16[11,32,256]{2,1,0:T(8,128)(2,1)} %copy-done.8, bf16[11,32,256]{2,1,0:T(8,128)(2,1)} %copy-done.33, bf16[11,32,256]{2,1,0:T(8,128)(2,1)} %copy-done.32, bf16[11,32,256]{2,1,0:T(8,128)(2,1)} %copy-done.31), custom_call_target="tpu_custom_call" | custom-call | flops 360448 | bytes 1441792 | tf_op jit(solution)/shard_map/stack_blocks/pallas_call | solution.py:326
  217.9 40.8 %stack_blocks.6.own_ref = bf16[4,4,5,32,256]{4,3,2,1,0:T(8,128)(2,1)} custom-call(bf16[4,5,32,256]{3,2,1,0:T(8,128)(2,1)} %stack_blocks.5.refs_0_, bf16[4,5,32,256]{3,2,1,0:T(8,128)(2,1)} %copy-done.24, bf16[4,5,32,256]{3,2,1,0:T(8,128)(2,1)} %copy-done.23, bf16[4,5,32,256]{3,2,1,0:T(8,128)(2,1)} %copy-done.22, ...), custom_call_target="tpu_custom_call" | custom-call | flops 655360 | bytes 2621440 | tf_op jit(solution)/shard_map/stack_blocks/pallas_call | solution.py:326
  266.8 2.1 broadcast_in_dim.26.b_in_ref
  268.9 37.3 %dense.2 = (bf16[64,32,32,256]{3,2,1,0:T(8,128)(2,1)}, bf16[64,32,32,256]{3,2,1,0:T(8,128)(2,1)}, f32[3,32,32,256]{3,2,1,0:T(8,128)}) custom-call(bf16[4,4,5,32,256]{4,3,2,1,0:T(8,128)(2,1)} %stack_blocks.6.own_ref, bf16[4,4,5,32,256]{4,3,2,1,0:T(8,128)(2,1)} %copy-done.7, bf16[128,256]{1,0:T(8,128)(2,1)} %select_convert_fusion.3.y_ref, ...), custom_call_target="tpu_custom_call" | custom-call | flops 8053063680 | bytes 125829120 | tf_op jit(solution)/shard_map/dense/pallas_call | solution.py:548
  307.6 88.5 %stack_blocks.7.own_ref = bf16[4,4,11,32,256]{4,3,2,1,0:T(8,128)(2,1)} custom-call(bf16[4,11,32,256]{3,2,1,0:T(8,128)(2,1)} %stack_blocks.4.refs_4_.refs_0_, bf16[4,11,32,256]{3,2,1,0:T(8,128)(2,1)} %copy-done.11, bf16[4,11,32,256]{3,2,1,0:T(8,128)(2,1)} %copy-done.10, bf16[4,11,32,256]{3,2,1,0:T(8,128)(2,1)} %copy-done.9, ...), custom_call_target="tpu_custom_call" | custom-call | flops 1441792 | bytes 5767168 | tf_op jit(solution)/shard_map/stack_blocks/pallas_call | solution.py:326
  396.2 5.5 collective-permute-done.26.other_ref
  401.6 1.7 copy-done.4
  403.4 74.6 %dense.3 = (bf16[64,32,32,256]{3,2,1,0:T(8,128)(2,1)}, bf16[64,32,32,256]{3,2,1,0:T(8,128)(2,1)}, f32[3,32,32,256]{3,2,1,0:T(8,128)}) custom-call(bf16[4,4,11,32,256]{4,3,2,1,0:T(8,128)(2,1)} %stack_blocks.7.own_ref, bf16[4,4,11,32,256]{4,3,2,1,0:T(8,128)(2,1)} %copy-done.4, ...), custom_call_target="tpu_custom_call", output_to_operand_aliasing={{0}: (8, {}), {1}: (9, {})} | custom-call | flops 17716740096 | bytes 276824064 | tf_op jit(solution)/shard_map/dense/pallas_call | solution.py:548
  480.3 3.0 collective-permute-start.27
  485.1 2.4 collective-permute-start.29
  489.4 2.3 collective-permute-done.29.refs_2_
  491.8 6.7 collective-permute-done.30.refs_3_
  499.2 15.7 %stencil.1 = (f32[3,32,32,256]{3,2,1,0:T(8,128)}, f32[8,256]{1,0:T(8,128)}) custom-call(s32[2]{0:T(128)} %pad_add_fusion.origin_ref, f32[3,32,32,256]{3,2,1,0:T(8,128)} %get-tuple-element.75.field_ref, f32[3,2,32,256]{3,2,1,0:T(8,128)} %copy-done.28, f32[3,2,32,256]{3,2,1,0:T(8,128)} %copy-done.27, f32[3,36,2,256]{3,2,1,0:T(2,128)} %copy-done.29, ...), custom_call_target="tpu_custom_call" | custom-call | tf_op jit(solution)/shard_map/stencil/pallas_call | solution.py:672
  514.9 49.6 %grad_modes.1 = (bf16[64,32,32,256]{3,2,1,0:T(8,128)(2,1)}, bf16[4,4,16,32,256]{4,3,2,1,0:T(8,128)(2,1)}, bf16[4,4,16,32,256]{4,3,2,1,0:T(8,128)(2,1)}, f32[16,16,256]{2,1,0:T(8,128)}) custom-call(f32[64,3]{1,0:T(8,128)} %convert_element_type.194.weight_ref, bf16[64,32,32,256]{3,2,1,0:T(8,128)(2,1)} %get-tuple-element.73.hidden_ref, ...), custom_call_target="tpu_custom_call" | custom-call | flops 8589934592 | bytes 167772160 | tf_op jit(solution)/shard_map/grad_modes/pallas_call | solution.py:749
  565.9 7.0 collective-permute-done.31.other_ref
  572.9 2.0 copy-done
  574.9 4.2 core_sums.6
  579.5 3.1 collective-permute-start.34
  582.6 9.9 %point_grad.3.refs_0_ = f32[64,64]{1,0:T(8,128)} custom-call(bf16[64,32,32,256]{3,2,1,0:T(8,128)(2,1)} %field_ref.13, bf16[64,32,32,256]{3,2,1,0:T(8,128)(2,1)} %get-tuple-element.77.grad_ref, bf16[4,8,32,256]{3,2,1,0:T(8,128)(2,1)} %get-tuple-element.80.refs_0_), custom_call_target="tpu_custom_call" | custom-call | flops 17179869184 | bytes 50331648 | tf_op jit(solution)/shard_map/point_grad/pallas_call | solution.py:833
  594.9 4.2 core_sums.7
  599.1 13.5 %point_grad.4.refs_4_ = f32[64,64]{1,0:T(8,128)} custom-call(bf16[64,32,32,256]{3,2,1,0:T(8,128)(2,1)} %field_ref.13, bf16[64,32,32,256]{3,2,1,0:T(8,128)(2,1)} %get-tuple-element.77.grad_ref, bf16[4,8,32,256]{3,2,1,0:T(8,128)(2,1)} %get-tuple-element.82.refs_0_), custom_call_target="tpu_custom_call" | custom-call | flops 17179869184 | bytes 50331648 | tf_op jit(solution)/shard_map/point_grad/pallas_call | solution.py:833
  613.6 2.4 sum_blocks.16
  616.1 2.7 collective-permute-start.39
  619.5 2.9 collective-permute-start.37
  622.5 2.3 collective-permute-done.39
  625.4 13.7 %point_grad.5.refs_4_ = f32[64,64]{1,0:T(8,128)} custom-call(bf16[64,32,32,256]{3,2,1,0:T(8,128)(2,1)} %field_ref.13, bf16[64,32,32,256]{3,2,1,0:T(8,128)(2,1)} %get-tuple-element.77.grad_ref, bf16[8,32,256]{2,1,0:T(8,128)(2,1)} %bitcast.101), custom_call_target="tpu_custom_call" | custom-call | flops 17179869184 | bytes 50331648 | tf_op jit(solution)/shard_map/point_grad/pallas_call | solution.py:833
  639.8 1.8 sum_blocks.17
  643.5 2.4 sum_blocks.18
  646.9 2.2 collective-permute-start.42
  653.0 3.6 collective-permute-done.42
  657.3 1.8 sum_blocks.19
  662.1 2.4 collective-permute-start.46
  664.5 1.7 collective-permute-start.45
  673.8 1.7 collective-permute-start.49
  678.1 8.8 %weight_grad.2.refs_4_.refs_0_ = f32[8,4,32,64,128]{4,3,2,1,0:T(8,128)} custom-call(bf16[8,4,64,64]{3,2,1,0:T(8,128)(2,1)} %bitcast.84, bf16[8,4,32,128]{3,2,1,0:T(8,128)(2,1)} %pad_maximum_fusion.2.refs_4_.grads_ref, f32[40,128]{1,0:T(8,128)} %sum_blocks.21.refs_0_), custom_call_target="tpu_custom_call" | custom-call | flops 16777216 | bytes 16777216 | tf_op jit(solution)/shard_map/weight_grad/pallas_call | solution.py:880
  689.0 8.8 %weight_grad.3.refs_2_ = f32[8,4,32,64,128]{4,3,2,1,0:T(8,128)} custom-call(bf16[8,4,64,64]{3,2,1,0:T(8,128)(2,1)} %bitcast.85, bf16[8,4,32,128]{3,2,1,0:T(8,128)(2,1)} %pad_maximum_fusion.2.refs_4_.grads_ref, f32[8,4,32,64,128]{4,3,2,1,0:T(8,128)} %weight_grad.2.refs_4_.refs_0_, f32[40,128]{1,0:T(8,128)} %sum_blocks.22.refs_1_), custom_call_target="tpu_custom_call", output_to_operand_aliasing={{}: (2, {})} | custom-call | flops 16777216 | bytes 16777216 | tf_op jit(solution)/shard_map/weight_grad/pallas_call | solution.py:880
  (284 shorter events, 91.3 us)
Async XLA Ops:
  36.3 7.4 %collective-permute-start = (bf16[4,4,16,32,256]{4,3,2,1,0:T(8,128)(2,1)}, bf16[4,4,16,32,256]{4,3,2,1,0:T(8,128)(2,1)S(1)}, u32[]{:S(2)}, u32[]{:S(2)}) collective-permute-start(bf16[4,4,16,32,256]{4,3,2,1,0:T(8,128)(2,1)} %get-tuple-element.53), channel_id=1, source_target_pairs={{0,4},{4,0},{8,12},{12,8},{16,20},{20,16},{24,28},{28,24},{1,5},{5... | collective-permute-start | bytes 12582920 | tf_op jit(solution)/shard_map/ppermute | solution.py:229
  50.0 15.8 %collective-permute-start.1 = (bf16[4,8,32,256]{3,2,1,0:T(8,128)(2,1)}, bf16[4,8,32,256]{3,2,1,0:T(8,128)(2,1)S(1)}, u32[]{:S(2)}, u32[]{:S(2)}) collective-permute-start(bf16[4,8,32,256]{3,2,1,0:T(8,128)(2,1)} %get-tuple-element.55), channel_id=1, source_target_pairs={{0,1},{1,0},{2,3},{3,2},{4,5},{5,4},{6,7},{7,6},{8,9},{9,8},{10,11... | collective-permute-start | bytes 1572872 | tf_op jit(solution)/shard_map/ppermute | solution.py:229
  53.6 30.9 %collective-permute-start.2 = (bf16[4,8,32,256]{3,2,1,0:T(8,128)(2,1)}, bf16[4,8,32,256]{3,2,1,0:T(8,128)(2,1)S(1)}, u32[]{:S(2)}, u32[]{:S(2)}) collective-permute-start(bf16[4,8,32,256]{3,2,1,0:T(8,128)(2,1)} %get-tuple-element.56), channel_id=1, source_target_pairs={{0,2},{1,3},{2,0},{3,1},{4,6},{5,7},{6,4},{7,5},{8,10},{9,11},{10,... | collective-permute-start | bytes 1572872 | tf_op jit(solution)/shard_map/ppermute | solution.py:229
  55.1 29.4 %collective-permute-start.3 = (bf16[4,8,32,256]{3,2,1,0:T(8,128)(2,1)}, bf16[4,8,32,256]{3,2,1,0:T(8,128)(2,1)S(1)}, u32[]{:S(2)}, u32[]{:S(2)}) collective-permute-start(bf16[4,8,32,256]{3,2,1,0:T(8,128)(2,1)} %get-tuple-element.57), channel_id=1, source_target_pairs={{0,3},{1,2},{2,1},{3,0},{4,7},{5,6},{6,5},{7,4},{8,11},{9,10},{10,... | collective-permute-start | bytes 1572872 | tf_op jit(solution)/shard_map/ppermute | solution.py:229
  88.0 11.0 %collective-permute-start.5 = (bf16[8,32,256]{2,1,0:T(8,128)(2,1)}, bf16[8,32,256]{2,1,0:T(8,128)(2,1)S(1)}, u32[]{:S(2)}, u32[]{:S(2)}) collective-permute-start(bf16[8,32,256]{2,1,0:T(8,128)(2,1)} %bitcast.157), channel_id=1, source_target_pairs={{0,16},{4,20},{8,24},{12,28},{16,0},{20,4},{24,8},{28,12},{1,17},{... | collective-permute-start | bytes 393224 | tf_op jit(solution)/shard_map/ppermute | solution.py:229
  91.2 24.4 %collective-permute-start.4 = (bf16[8,32,256]{2,1,0:T(8,128)(2,1)}, bf16[8,32,256]{2,1,0:T(8,128)(2,1)S(1)}, u32[]{:S(2)}, u32[]{:S(2)}) collective-permute-start(bf16[8,32,256]{2,1,0:T(8,128)(2,1)} %bitcast.153), channel_id=1, source_target_pairs={{0,8},{4,12},{8,0},{12,4},{16,24},{20,28},{24,16},{28,20},{1,9},{5... | collective-permute-start | bytes 393224 | tf_op jit(solution)/shard_map/ppermute | solution.py:229
  92.7 22.9 %collective-permute-start.6 = (bf16[8,32,256]{2,1,0:T(8,128)(2,1)}, bf16[8,32,256]{2,1,0:T(8,128)(2,1)S(1)}, u32[]{:S(2)}, u32[]{:S(2)}) collective-permute-start(bf16[8,32,256]{2,1,0:T(8,128)(2,1)} %bitcast.150), channel_id=1, source_target_pairs={{0,24},{4,28},{8,16},{12,20},{16,8},{20,12},{24,0},{28,4},{1,25},{... | collective-permute-start | bytes 393224 | tf_op jit(solution)/shard_map/ppermute | solution.py:229
  92.7 25.4 %collective-permute-start.7 = (bf16[4,8,32,256]{3,2,1,0:T(8,128)(2,1)S(1)}, bf16[4,8,32,256]{3,2,1,0:T(8,128)(2,1)S(1)}, u32[]{:S(2)}, u32[]{:S(2)}) collective-permute-start(bf16[4,8,32,256]{3,2,1,0:T(8,128)(2,1)S(1)} %copy-done.64), channel_id=1, source_target_pairs={{0,1},{1,0},{2,3},{3,2},{4,5},{5,4},{6,7},{7,6},{8,9},{9,8},{10,11... | collective-permute-start | bytes 1572872 | tf_op jit(solution)/shard_map/ppermute | solution.py:229
  94.5 23.7 %collective-permute-start.8 = (bf16[4,8,32,256]{3,2,1,0:T(8,128)(2,1)S(1)}, bf16[4,8,32,256]{3,2,1,0:T(8,128)(2,1)S(1)}, u32[]{:S(2)}, u32[]{:S(2)}) collective-permute-start(bf16[4,8,32,256]{3,2,1,0:T(8,128)(2,1)S(1)} %copy-done.62), channel_id=1, source_target_pairs={{0,2},{1,3},{2,0},{3,1},{4,6},{5,7},{6,4},{7,5},{8,10},{9,11},{10,... | collective-permute-start | bytes 1572872 | tf_op jit(solution)/shard_map/ppermute | solution.py:229
  99.0 16.6 %copy-start.34 = (bf16[8,32,256]{2,1,0:T(8,128)(2,1)}, bf16[8,32,256]{2,1,0:T(8,128)(2,1)S(1)}, u32[]{:S(2)}) copy-start(bf16[8,32,256]{2,1,0:T(8,128)(2,1)S(1)} %collective-permute-done.5) | copy-start | bytes 393220
  99.0 19.1 %collective-permute-start.9 = (bf16[4,8,32,256]{3,2,1,0:T(8,128)(2,1)S(1)}, bf16[4,8,32,256]{3,2,1,0:T(8,128)(2,1)S(1)}, u32[]{:S(2)}, u32[]{:S(2)}) collective-permute-start(bf16[4,8,32,256]{3,2,1,0:T(8,128)(2,1)S(1)} %copy-done.60), channel_id=1, source_target_pairs={{0,3},{1,2},{2,1},{3,0},{4,7},{5,6},{6,5},{7,4},{8,11},{9,10},{10,... | collective-permute-start | bytes 1572872 | tf_op jit(solution)/shard_map/ppermute | solution.py:229
  121.7 7.2 %collective-permute-start.10 = (bf16[8,32,256]{2,1,0:T(8,128)(2,1)}, bf16[8,32,256]{2,1,0:T(8,128)(2,1)S(1)}, u32[]{:S(2)}, u32[]{:S(2)}) collective-permute-start(bf16[8,32,256]{2,1,0:T(8,128)(2,1)} %bitcast.159), channel_id=1, source_target_pairs={{0,8},{4,12},{8,0},{12,4},{16,24},{20,28},{24,16},{28,20},{1,9},{5... | collective-permute-start | bytes 393224 | tf_op jit(solution)/shard_map/ppermute | solution.py:229
  123.9 8.3 %collective-permute-start.11 = (bf16[8,32,256]{2,1,0:T(8,128)(2,1)}, bf16[8,32,256]{2,1,0:T(8,128)(2,1)S(1)}, u32[]{:S(2)}, u32[]{:S(2)}) collective-permute-start(bf16[8,32,256]{2,1,0:T(8,128)(2,1)} %bitcast.158), channel_id=1, source_target_pairs={{0,16},{4,20},{8,24},{12,28},{16,0},{20,4},{24,8},{28,12},{1,17},{... | collective-permute-start | bytes 393224 | tf_op jit(solution)/shard_map/ppermute | solution.py:229
  127.2 7.1 collective-permute-start.12
  140.6 16.2 %copy-start.2 = (bf16[8,4,64,64]{2,3,1,0:T(8,128)(2,1)}, bf16[8,4,64,64]{2,3,1,0:T(8,128)(2,1)S(1)}, u32[]{:S(2)}) copy-start(bf16[8,4,64,64]{2,3,1,0:T(8,128)(2,1)S(1)} %reshape.254) | copy-start | bytes 786436
  158.8 7.6 %collective-permute-start.21 = (bf16[5,32,256]{2,1,0:T(8,128)(2,1)S(1)}, bf16[5,32,256]{2,1,0:T(8,128)(2,1)S(1)}, u32[]{:S(2)}, u32[]{:S(2)}) collective-permute-start(bf16[5,32,256]{2,1,0:T(8,128)(2,1)S(1)} %slice.76.refs_0_), channel_id=1, source_target_pairs={{0,24},{4,28},{8,16},{12,20},{16,8},{20,12},{24,0},{28,4},{1,25},{... | collective-permute-start | bytes 245768 | tf_op jit(solution)/shard_map/ppermute | solution.py:229
  160.7 7.4 %collective-permute-start.20 = (bf16[5,32,256]{2,1,0:T(8,128)(2,1)S(1)}, bf16[5,32,256]{2,1,0:T(8,128)(2,1)S(1)}, u32[]{:S(2)}, u32[]{:S(2)}) collective-permute-start(bf16[5,32,256]{2,1,0:T(8,128)(2,1)S(1)} %slice.76.refs_0_), channel_id=1, source_target_pairs={{0,16},{4,20},{8,24},{12,28},{16,0},{20,4},{24,8},{28,12},{1,17},{... | collective-permute-start | bytes 245768 | tf_op jit(solution)/shard_map/ppermute | solution.py:229
  161.7 6.5 collective-permute-start.19
  163.5 95.4 %copy-start.58 = (bf16[64,3]{0,1:T(4,128)(2,1)S(1)}, bf16[64,3]{0,1:T(4,128)(2,1)}, u32[]{:S(2)}) copy-start(bf16[64,3]{0,1:T(4,128)(2,1)} %param.10) | copy-start | bytes 1156
  163.9 102.9 %copy-start.59 = (f32[3]{0:T(128)S(1)}, f32[3]{0:T(128)}, u32[]{:S(2)}) copy-start(f32[3]{0:T(128)} %param.11) | copy-start | bytes 40
  164.4 28.1 %copy-start.8 = (bf16[11,32,256]{2,1,0:T(8,128)(2,1)}, bf16[11,32,256]{2,1,0:T(8,128)(2,1)S(1)}, u32[]{:S(2)}) copy-start(bf16[11,32,256]{2,1,0:T(8,128)(2,1)S(1)} %slice.74.refs_0_) | copy-start | bytes 540676
  164.4 20.4 %collective-permute-start.15 = (bf16[11,32,256]{2,1,0:T(8,128)(2,1)S(1)}, bf16[11,32,256]{2,1,0:T(8,128)(2,1)S(1)}, u32[]{:S(2)}, u32[]{:S(2)}) collective-permute-start(bf16[11,32,256]{2,1,0:T(8,128)(2,1)S(1)} %slice.74.refs_0_), channel_id=1, source_target_pairs={{0,24},{4,28},{8,16},{12,20},{16,8},{20,12},{24,0},{28,4},{1,25},{... | collective-permute-start | bytes 540680 | tf_op jit(solution)/shard_map/ppermute | solution.py:229
  180.5 35.9 %collective-permute-start.24 = (bf16[4,5,32,256]{3,2,1,0:T(8,128)(2,1)}, bf16[4,5,32,256]{3,2,1,0:T(8,128)(2,1)S(1)}, u32[]{:S(2)}, u32[]{:S(2)}) collective-permute-start(bf16[4,5,32,256]{3,2,1,0:T(8,128)(2,1)} %stack_blocks.5.refs_0_), channel_id=1, source_target_pairs={{0,3},{1,2},{2,1},{3,0},{4,7},{5,6},{6,5},{7,4},{8,11},{9,10},{10,... | collective-permute-start | bytes 983048 | tf_op jit(solution)/shard_map/ppermute | solution.py:229
  181.0 35.3 %collective-permute-start.23 = (bf16[4,5,32,256]{3,2,1,0:T(8,128)(2,1)}, bf16[4,5,32,256]{3,2,1,0:T(8,128)(2,1)S(1)}, u32[]{:S(2)}, u32[]{:S(2)}) collective-permute-start(bf16[4,5,32,256]{3,2,1,0:T(8,128)(2,1)} %stack_blocks.5.refs_0_), channel_id=1, source_target_pairs={{0,2},{1,3},{2,0},{3,1},{4,6},{5,7},{6,4},{7,5},{8,10},{9,11},{10,... | collective-permute-start | bytes 983048 | tf_op jit(solution)/shard_map/ppermute | solution.py:229
  182.6 33.8 %collective-permute-start.22 = (bf16[4,5,32,256]{3,2,1,0:T(8,128)(2,1)}, bf16[4,5,32,256]{3,2,1,0:T(8,128)(2,1)S(1)}, u32[]{:S(2)}, u32[]{:S(2)}) collective-permute-start(bf16[4,5,32,256]{3,2,1,0:T(8,128)(2,1)} %stack_blocks.5.refs_0_), channel_id=1, source_target_pairs={{0,1},{1,0},{2,3},{3,2},{4,5},{5,4},{6,7},{7,6},{8,9},{9,8},{10,11... | collective-permute-start | bytes 983048 | tf_op jit(solution)/shard_map/ppermute | solution.py:229
  184.1 8.0 %collective-permute-start.14 = (bf16[11,32,256]{2,1,0:T(8,128)(2,1)S(1)}, bf16[11,32,256]{2,1,0:T(8,128)(2,1)S(1)}, u32[]{:S(2)}, u32[]{:S(2)}) collective-permute-start(bf16[11,32,256]{2,1,0:T(8,128)(2,1)S(1)} %slice.74.refs_0_), channel_id=1, source_target_pairs={{0,16},{4,20},{8,24},{12,28},{16,0},{20,4},{24,8},{28,12},{1,17},{... | collective-permute-start | bytes 540680 | tf_op jit(solution)/shard_map/ppermute | solution.py:229
  184.8 7.7 %collective-permute-start.13 = (bf16[11,32,256]{2,1,0:T(8,128)(2,1)S(1)}, bf16[11,32,256]{2,1,0:T(8,128)(2,1)S(1)}, u32[]{:S(2)}, u32[]{:S(2)}) collective-permute-start(bf16[11,32,256]{2,1,0:T(8,128)(2,1)S(1)} %slice.74.refs_0_), channel_id=1, source_target_pairs={{0,8},{4,12},{8,0},{12,4},{16,24},{20,28},{24,16},{28,20},{1,9},{5... | collective-permute-start | bytes 540680 | tf_op jit(solution)/shard_map/ppermute | solution.py:229
  216.3 47.0 %copy-start.3 = (bf16[4,11,32,256]{3,2,1,0:T(8,128)(2,1)S(1)}, bf16[4,11,32,256]{3,2,1,0:T(8,128)(2,1)}, u32[]{:S(2)}) copy-start(bf16[4,11,32,256]{3,2,1,0:T(8,128)(2,1)} %stack_blocks.4.refs_4_.refs_0_) | copy-start | bytes 2162692
  258.8 8.0 %collective-permute-start.25 = (bf16[4,4,5,32,256]{4,3,2,1,0:T(8,128)(2,1)}, bf16[4,4,5,32,256]{4,3,2,1,0:T(8,128)(2,1)S(1)}, u32[]{:S(2)}, u32[]{:S(2)}) collective-permute-start(bf16[4,4,5,32,256]{4,3,2,1,0:T(8,128)(2,1)} %stack_blocks.6.own_ref), channel_id=1, source_target_pairs={{0,4},{4,0},{8,12},{12,8},{16,20},{20,16},{24,28},{28,24},{1,5},{5... | collective-permute-start | bytes 3932168 | tf_op jit(solution)/shard_map/ppermute | solution.py:229
  263.3 42.9 %collective-permute-start.18 = (bf16[4,11,32,256]{3,2,1,0:T(8,128)(2,1)S(1)}, bf16[4,11,32,256]{3,2,1,0:T(8,128)(2,1)S(1)}, u32[]{:S(2)}, u32[]{:S(2)}) collective-permute-start(bf16[4,11,32,256]{3,2,1,0:T(8,128)(2,1)S(1)} %copy-done.3), channel_id=1, source_target_pairs={{0,3},{1,2},{2,1},{3,0},{4,7},{5,6},{6,5},{7,4},{8,11},{9,10},{10,... | collective-permute-start | bytes 2162696 | tf_op jit(solution)/shard_map/ppermute | solution.py:229
  263.8 42.4 %collective-permute-start.17 = (bf16[4,11,32,256]{3,2,1,0:T(8,128)(2,1)S(1)}, bf16[4,11,32,256]{3,2,1,0:T(8,128)(2,1)S(1)}, u32[]{:S(2)}, u32[]{:S(2)}) collective-permute-start(bf16[4,11,32,256]{3,2,1,0:T(8,128)(2,1)S(1)} %copy-done.3), channel_id=1, source_target_pairs={{0,2},{1,3},{2,0},{3,1},{4,6},{5,7},{6,4},{7,5},{8,10},{9,11},{10,... | collective-permute-start | bytes 2162696 | tf_op jit(solution)/shard_map/ppermute | solution.py:229
  265.3 40.9 %collective-permute-start.16 = (bf16[4,11,32,256]{3,2,1,0:T(8,128)(2,1)S(1)}, bf16[4,11,32,256]{3,2,1,0:T(8,128)(2,1)S(1)}, u32[]{:S(2)}, u32[]{:S(2)}) collective-permute-start(bf16[4,11,32,256]{3,2,1,0:T(8,128)(2,1)S(1)} %copy-done.3), channel_id=1, source_target_pairs={{0,1},{1,0},{2,3},{3,2},{4,5},{5,4},{6,7},{7,6},{8,9},{9,8},{10,11... | collective-permute-start | bytes 2162696 | tf_op jit(solution)/shard_map/ppermute | solution.py:229
  396.1 5.6 collective-permute-start.26
  479.0 5.9 collective-permute-start.28
  480.3 4.6 collective-permute-start.27
  484.9 13.6 %copy-start.27 = (f32[3,2,32,256]{3,2,1,0:T(8,128)}, f32[3,2,32,256]{3,2,1,0:T(8,128)S(1)}, u32[]{:S(2)}) copy-start(f32[3,2,32,256]{3,2,1,0:T(8,128)S(1)} %collective-permute-done.28.refs_1_) | copy-start | bytes 589828
  485.1 6.7 collective-permute-start.29
  487.6 11.0 %collective-permute-start.30 = (f32[3,36,2,256]{3,2,1,0:T(2,128)S(1)}, f32[3,36,2,256]{3,2,1,0:T(2,128)S(1)}, u32[]{:S(2)}, u32[]{:S(2)}) collective-permute-start(f32[3,36,2,256]{3,2,1,0:T(2,128)S(1)} %pad_maximum_fusion.4), channel_id=1, source_target_pairs={{1,0},{2,1},{3,2},{5,4},{6,5},{7,6},{9,8},{10,9},{11,10},{13,12},{... | collective-permute-start | bytes 663560 | tf_op jit(solution)/shard_map/ppermute | solution.py:53
  564.5 8.3 %collective-permute-start.31 = (bf16[4,4,16,32,256]{4,3,2,1,0:T(8,128)(2,1)}, bf16[4,4,16,32,256]{4,3,2,1,0:T(8,128)(2,1)S(1)}, u32[]{:S(2)}, u32[]{:S(2)}) collective-permute-start(bf16[4,4,16,32,256]{4,3,2,1,0:T(8,128)(2,1)} %get-tuple-element.79), channel_id=1, source_target_pairs={{0,4},{4,0},{8,12},{12,8},{16,20},{20,16},{24,28},{28,24},{1,5},{5... | collective-permute-start | bytes 12582920 | tf_op jit(solution)/shard_map/ppermute | solution.py:229
  579.1 15.0 %collective-permute-start.32 = (bf16[4,8,32,256]{3,2,1,0:T(8,128)(2,1)}, bf16[4,8,32,256]{3,2,1,0:T(8,128)(2,1)S(1)}, u32[]{:S(2)}, u32[]{:S(2)}) collective-permute-start(bf16[4,8,32,256]{3,2,1,0:T(8,128)(2,1)} %get-tuple-element.81), channel_id=1, source_target_pairs={{0,1},{1,0},{2,3},{3,2},{4,5},{5,4},{6,7},{7,6},{8,9},{9,8},{10,11... | collective-permute-start | bytes 1572872 | tf_op jit(solution)/shard_map/ppermute | solution.py:229
  579.5 33.1 %collective-permute-start.33 = (bf16[4,8,32,256]{3,2,1,0:T(8,128)(2,1)}, bf16[4,8,32,256]{3,2,1,0:T(8,128)(2,1)S(1)}, u32[]{:S(2)}, u32[]{:S(2)}) collective-permute-start(bf16[4,8,32,256]{3,2,1,0:T(8,128)(2,1)} %get-tuple-element.83), channel_id=1, source_target_pairs={{0,2},{1,3},{2,0},{3,1},{4,6},{5,7},{6,4},{7,5},{8,10},{9,11},{10,... | collective-permute-start | bytes 1572872 | tf_op jit(solution)/shard_map/ppermute | solution.py:229
  579.5 33.1 %collective-permute-start.34 = (bf16[4,8,32,256]{3,2,1,0:T(8,128)(2,1)}, bf16[4,8,32,256]{3,2,1,0:T(8,128)(2,1)S(1)}, u32[]{:S(2)}, u32[]{:S(2)}) collective-permute-start(bf16[4,8,32,256]{3,2,1,0:T(8,128)(2,1)} %get-tuple-element.84), channel_id=1, source_target_pairs={{0,3},{1,2},{2,1},{3,0},{4,7},{5,6},{6,5},{7,4},{8,11},{9,10},{10,... | collective-permute-start | bytes 1572872 | tf_op jit(solution)/shard_map/ppermute | solution.py:229
  599.1 19.7 %copy-start.26 = (f32[16,16,256]{2,1,0:T(8,128)S(1)}, f32[16,16,256]{2,1,0:T(8,128)}, u32[]{:S(2)}) copy-start(f32[16,16,256]{2,1,0:T(8,128)} %get-tuple-element.96) | copy-start | bytes 786436
  599.1 19.8 %copy-start.65 = (bf16[4,8,32,256]{3,2,1,0:T(8,128)(2,1)S(1)}, bf16[4,8,32,256]{3,2,1,0:T(8,128)(2,1)}, u32[]{:S(2)}) copy-start(bf16[4,8,32,256]{3,2,1,0:T(8,128)(2,1)} %get-tuple-element.86) | copy-start | bytes 1572868
  599.1 20.4 %copy-start.63 = (bf16[4,8,32,256]{3,2,1,0:T(8,128)(2,1)S(1)}, bf16[4,8,32,256]{3,2,1,0:T(8,128)(2,1)}, u32[]{:S(2)}) copy-start(bf16[4,8,32,256]{3,2,1,0:T(8,128)(2,1)} %get-tuple-element.87) | copy-start | bytes 1572868
  599.1 20.4 %copy-start.61 = (bf16[4,8,32,256]{3,2,1,0:T(8,128)(2,1)S(1)}, bf16[4,8,32,256]{3,2,1,0:T(8,128)(2,1)}, u32[]{:S(2)}) copy-start(bf16[4,8,32,256]{3,2,1,0:T(8,128)(2,1)} %get-tuple-element.88) | copy-start | bytes 1572868
  616.1 8.6 %collective-permute-start.39 = (bf16[8,32,256]{2,1,0:T(8,128)(2,1)}, bf16[8,32,256]{2,1,0:T(8,128)(2,1)S(1)}, u32[]{:S(2)}, u32[]{:S(2)}) collective-permute-start(bf16[8,32,256]{2,1,0:T(8,128)(2,1)} %bitcast.155), channel_id=1, source_target_pairs={{0,16},{4,20},{8,24},{12,28},{16,0},{20,4},{24,8},{28,12},{1,17},{... | collective-permute-start | bytes 393224 | tf_op jit(solution)/shard_map/ppermute | solution.py:229
  618.9 22.7 %collective-permute-start.35 = (bf16[4,8,32,256]{3,2,1,0:T(8,128)(2,1)S(1)}, bf16[4,8,32,256]{3,2,1,0:T(8,128)(2,1)S(1)}, u32[]{:S(2)}, u32[]{:S(2)}) collective-permute-start(bf16[4,8,32,256]{3,2,1,0:T(8,128)(2,1)S(1)} %copy-done.65), channel_id=1, source_target_pairs={{0,1},{1,0},{2,3},{3,2},{4,5},{5,4},{6,7},{7,6},{8,9},{9,8},{10,11... | collective-permute-start | bytes 1572872 | tf_op jit(solution)/shard_map/ppermute | solution.py:229
  619.5 23.0 %collective-permute-start.36 = (bf16[4,8,32,256]{3,2,1,0:T(8,128)(2,1)S(1)}, bf16[4,8,32,256]{3,2,1,0:T(8,128)(2,1)S(1)}, u32[]{:S(2)}, u32[]{:S(2)}) collective-permute-start(bf16[4,8,32,256]{3,2,1,0:T(8,128)(2,1)S(1)} %copy-done.63), channel_id=1, source_target_pairs={{0,2},{1,3},{2,0},{3,1},{4,6},{5,7},{6,4},{7,5},{8,10},{9,11},{10,... | collective-permute-start | bytes 1572872 | tf_op jit(solution)/shard_map/ppermute | solution.py:229
  619.5 23.0 %collective-permute-start.37 = (bf16[4,8,32,256]{3,2,1,0:T(8,128)(2,1)S(1)}, bf16[4,8,32,256]{3,2,1,0:T(8,128)(2,1)S(1)}, u32[]{:S(2)}, u32[]{:S(2)}) collective-permute-start(bf16[4,8,32,256]{3,2,1,0:T(8,128)(2,1)S(1)} %copy-done.61), channel_id=1, source_target_pairs={{0,3},{1,2},{2,1},{3,0},{4,7},{5,6},{6,5},{7,4},{8,11},{9,10},{10,... | collective-permute-start | bytes 1572872 | tf_op jit(solution)/shard_map/ppermute | solution.py:229
  622.5 16.6 %collective-permute-start.38 = (bf16[8,32,256]{2,1,0:T(8,128)(2,1)}, bf16[8,32,256]{2,1,0:T(8,128)(2,1)S(1)}, u32[]{:S(2)}, u32[]{:S(2)}) collective-permute-start(bf16[8,32,256]{2,1,0:T(8,128)(2,1)} %bitcast.152), channel_id=1, source_target_pairs={{0,8},{4,12},{8,0},{12,4},{16,24},{20,28},{24,16},{28,20},{1,9},{5... | collective-permute-start | bytes 393224 | tf_op jit(solution)/shard_map/ppermute | solution.py:229
  624.7 14.3 %copy-start.43 = (bf16[8,32,256]{2,1,0:T(8,128)(2,1)}, bf16[8,32,256]{2,1,0:T(8,128)(2,1)S(1)}, u32[]{:S(2)}) copy-start(bf16[8,32,256]{2,1,0:T(8,128)(2,1)S(1)} %collective-permute-done.39) | copy-start | bytes 393220
  624.7 14.4 %collective-permute-start.40 = (bf16[8,32,256]{2,1,0:T(8,128)(2,1)}, bf16[8,32,256]{2,1,0:T(8,128)(2,1)S(1)}, u32[]{:S(2)}, u32[]{:S(2)}) collective-permute-start(bf16[8,32,256]{2,1,0:T(8,128)(2,1)} %bitcast.149), channel_id=1, source_target_pairs={{0,24},{4,28},{8,16},{12,20},{16,8},{20,12},{24,0},{28,4},{1,25},{... | collective-permute-start | bytes 393224 | tf_op jit(solution)/shard_map/ppermute | solution.py:229
  625.4 25.3 %copy-start.57 = (f32[8,256]{1,0:T(8,128)S(1)}, f32[8,256]{1,0:T(8,128)}, u32[]{:S(2)}) copy-start(f32[8,256]{1,0:T(8,128)} %get-tuple-element.97) | copy-start | bytes 24580
  646.0 7.0 collective-permute-start.41
  646.9 9.7 %collective-permute-start.42 = (bf16[8,32,256]{2,1,0:T(8,128)(2,1)}, bf16[8,32,256]{2,1,0:T(8,128)(2,1)S(1)}, u32[]{:S(2)}, u32[]{:S(2)}) collective-permute-start(bf16[8,32,256]{2,1,0:T(8,128)(2,1)} %bitcast.151), channel_id=1, source_target_pairs={{0,16},{4,20},{8,24},{12,28},{16,0},{20,4},{24,8},{28,12},{1,17},{... | collective-permute-start | bytes 393224 | tf_op jit(solution)/shard_map/ppermute | solution.py:229
  649.1 7.5 %collective-permute-start.43 = (bf16[8,32,256]{2,1,0:T(8,128)(2,1)}, bf16[8,32,256]{2,1,0:T(8,128)(2,1)S(1)}, u32[]{:S(2)}, u32[]{:S(2)}) collective-permute-start(bf16[8,32,256]{2,1,0:T(8,128)(2,1)} %bitcast.148), channel_id=1, source_target_pairs={{0,24},{4,28},{8,16},{12,20},{16,8},{20,12},{24,0},{28,4},{1,25},{... | collective-permute-start | bytes 393224 | tf_op jit(solution)/shard_map/ppermute | solution.py:229
  662.1 9.6 %collective-permute-start.46 = (f32[40,128]{1,0:T(8,128)S(1)}, f32[40,128]{1,0:T(8,128)S(1)}, u32[]{:S(2)}, u32[]{:S(2)}) collective-permute-start(f32[40,128]{1,0:T(8,128)S(1)} %get-tuple-element.114), channel_id=1, source_target_pairs={{0,3},{1,2},{2,1},{3,0},{4,7},{5,6},{6,5},{7,4},{8,11},{9,10},{10,... | collective-permute-start | bytes 61448 | tf_op jit(solution)/shard_map/ppermute | solution.py:229
  664.5 7.2 %collective-permute-start.45 = (f32[40,128]{1,0:T(8,128)S(1)}, f32[40,128]{1,0:T(8,128)S(1)}, u32[]{:S(2)}, u32[]{:S(2)}) collective-permute-start(f32[40,128]{1,0:T(8,128)S(1)} %get-tuple-element.114), channel_id=1, source_target_pairs={{0,2},{1,3},{2,0},{3,1},{4,6},{5,7},{6,4},{7,5},{8,10},{9,11},{10,... | collective-permute-start | bytes 61448 | tf_op jit(solution)/shard_map/ppermute | solution.py:229
  666.3 5.5 collective-permute-start.44
  673.8 13.2 %collective-permute-start.49 = (f32[40,128]{1,0:T(8,128)}, f32[40,128]{1,0:T(8,128)S(1)}, u32[]{:S(2)}, u32[]{:S(2)}) collective-permute-start(f32[40,128]{1,0:T(8,128)} %sum_blocks.21.refs_0_), channel_id=1, source_target_pairs={{0,24},{4,28},{8,16},{12,20},{16,8},{20,12},{24,0},{28,4},{1,25},{... | collective-permute-start | bytes 61448 | tf_op jit(solution)/shard_map/ppermute | solution.py:229
  675.5 11.5 %collective-permute-start.48 = (f32[40,128]{1,0:T(8,128)}, f32[40,128]{1,0:T(8,128)S(1)}, u32[]{:S(2)}, u32[]{:S(2)}) collective-permute-start(f32[40,128]{1,0:T(8,128)} %sum_blocks.21.refs_0_), channel_id=1, source_target_pairs={{0,16},{4,20},{8,24},{12,28},{16,0},{20,4},{24,8},{28,12},{1,17},{... | collective-permute-start | bytes 61448 | tf_op jit(solution)/shard_map/ppermute | solution.py:229
  677.1 9.9 %collective-permute-start.47 = (f32[40,128]{1,0:T(8,128)}, f32[40,128]{1,0:T(8,128)S(1)}, u32[]{:S(2)}, u32[]{:S(2)}) collective-permute-start(f32[40,128]{1,0:T(8,128)} %sum_blocks.21.refs_0_), channel_id=1, source_target_pairs={{0,8},{4,12},{8,0},{12,4},{16,24},{20,28},{24,16},{28,20},{1,9},{5... | collective-permute-start | bytes 61448 | tf_op jit(solution)/shard_map/ppermute | solution.py:229
  689.0 8.8 %collective-permute-start.50 = (f32[40,128]{1,0:T(8,128)}, f32[40,128]{1,0:T(8,128)S(1)}, u32[]{:S(2)}, u32[]{:S(2)}) collective-permute-start(f32[40,128]{1,0:T(8,128)} %sum_blocks.22.refs_1_), channel_id=1, source_target_pairs={{0,4},{4,0},{8,12},{12,8},{16,20},{20,16},{24,28},{28,24},{1,5},{5... | collective-permute-start | bytes 61448 | tf_op jit(solution)/shard_map/ppermute | solution.py:229
  (53 other events, 123.7 us)

commit v4 on v3

--- a/solution.py
+++ b/solution.py
@@ -267,39 +267,37 @@
 
 def core_kernel(own_ref, other_ref, *refs):
     count = own_ref.shape[0]
-    for n, out_ref in enumerate(refs[len(refs) - count :]):
-        out_ref[0] = (own_ref[n, 0].astype(F32) + other_ref[n, 0].astype(F32)).astype(BF16)
-
-
-def from_cores(lay, own, other, half, after=()):
-    size = lay.groups // 2
-    tail = (size, lay.own, 2 * LANES)
-    given = pl.BlockSpec((lay.n_gz, 1) + tail, lambda i: (0, i, half, 0, 0))
-    return list(
-        pl.pallas_call(
-            core_kernel,
-            grid=(lay.chips,),
-            in_specs=[given, given] + [ANY] * len(after),
-            out_specs=[pl.BlockSpec((1,) + tail, lambda i: (i, 0, 0, 0))] * lay.n_gz,
-            out_shape=[jax.ShapeDtypeStruct((lay.chips,) + tail, BF16)] * lay.n_gz,
-            compiler_params=params(),
-            cost_estimate=cost(own.size // 2, own.size * 3),
-            name="core_sums",
-        )(own, other, *after)
-    )
+    half = refs[0].shape[1]
+    for n in range(count):
+        total = (own_ref[n, 0].astype(F32) + other_ref[n, 0].astype(F32)).astype(BF16)
+        refs[n][0] = total[:half]
+        refs[count + n][0] = total[half:]
+
+
+def from_cores(lay, own, other):
+    tail = (lay.own, 2 * LANES)
+    half = lay.groups // 2
+    given = pl.BlockSpec((lay.n_gz, 1, lay.groups) + tail, lambda i: (0, i, 0, 0, 0))
+    outs = pl.pallas_call(
+        core_kernel,
+        grid=(lay.chips,),
+        in_specs=[given, given],
+        out_specs=[pl.BlockSpec((1, half) + tail, lambda i: (i, 0, 0, 0))] * (2 * lay.n_gz),
+        out_shape=[jax.ShapeDtypeStruct((lay.chips, half) + tail, BF16)] * (2 * lay.n_gz),
+        compiler_params=params(),
+        cost_estimate=cost(own.size, own.size * 6),
+        name="core_sums",
+    )(own, other)
+    return list(outs[: lay.n_gz]), list(outs[lay.n_gz :])
 
 
 def sum_all(lay, own, send, factor, work):
-    other = exchange(send, "gy", 1)
-    early = from_cores(lay, own, other, 0)
+    early, late = from_cores(lay, own, exchange(send, "gy", 1))
     done = work(0, early[:1])
-    early = to_depth(early)
-    late = to_depth(from_cores(lay, own, other, 1, [done, early[1]]))
-    done = work(1, late[:1])
-    early = sum_blocks(early, True, after=[done])
-    done = work(2, early[:1])
+    early = sum_blocks(to_depth(early), True, after=[done])
+    done = work(1, early[:1])
     first = from_chips(early, factor, [done])
-    late = sum_blocks(late, True, after=[first])
+    late = sum_blocks(to_depth(late), True, after=[first])
     return [first, from_chips(late, factor)]
 
 
@@ -313,25 +311,32 @@
 
 
 def stack_kernel(n_in, *refs):
-    out_ref, sems = refs[-2:]
-    copies = [pltpu.make_async_copy(refs[n], out_ref.at[n], sems.at[n]) for n in range(n_in)]
-    for copy in copies:
-        copy.start()
-    for copy in copies:
-        copy.wait()
+    rows = refs[0].shape[0]
+    chunk = math.gcd(rows, 256)
+
+    def body(n, carry):
+        here = pl.ds(pl.multiple_of(n * chunk, chunk), chunk)
+        for m in range(n_in):
+            refs[-1][m, here] = refs[m][here]
+        return carry
+
+    lax.fori_loop(0, rows // chunk, body, 0)
 
 
 def stack_blocks(values, after=()):
-    out = (len(values),) + values[0].shape
-    return pl.pallas_call(
+    shape = values[0].shape
+    flat = [value.reshape(-1, shape[-1]) for value in values]
+    out = (len(values),) + flat[0].shape
+    stacked = pl.pallas_call(
         functools.partial(stack_kernel, len(values)),
-        in_specs=[ANY] * (len(values) + len(after)),
-        out_specs=ANY,
+        in_specs=[VMEM] * len(values) + [ANY] * len(after),
+        out_specs=VMEM,
         out_shape=jax.ShapeDtypeStruct(out, values[0].dtype),
-        scratch_shapes=[pltpu.SemaphoreType.DMA((len(values),))],
+        compiler_params=pltpu.CompilerParams(vmem_limit_bytes=VMEM_LIMIT),
         cost_estimate=cost(math.prod(out), 4 * math.prod(out)),
         name="stack_blocks",
-    )(*values, *after)
+    )(*flat, *after)
+    return stacked.reshape((len(values),) + shape)
 
 
 def spread_chips(lay, mine):
@@ -891,13 +896,54 @@
     )(columns, rows, *done, *after)
 
 
+def pack_kernel(n_parts, *refs):
+    small_ref, out_ref = refs[n_parts], refs[-1]
+    count = refs[0].shape[0]
+    total = refs[0][...]
+    for ref in refs[1:n_parts]:
+        total = total + ref[...]
+    out_ref[...] = small_ref[...]
+    out_ref[:count, :count] = total
+
+
+def pack_sums(lay, parts, small, after):
+    return pl.pallas_call(
+        functools.partial(pack_kernel, len(parts)),
+        in_specs=[VMEM] * (len(parts) + 1) + [ANY] * len(after),
+        out_specs=VMEM,
+        out_shape=jax.ShapeDtypeStruct(small.shape, F32),
+        name="pack_sums",
+    )(*parts, small, *after)
+
+
+def unpack_kernel(left_ref, right_ref, *refs):
+    ends_ref, point_ref, bias_ref, outs_ref = refs[-4:]
+    count = point_ref.shape[0]
+    total = left_ref[...] + right_ref[...]
+    point_ref[...] = total[:count, :count]
+    outs_ref[...] = total[:count, count : count + 3]
+    bias_ref[...] = total[count : count + 1, :count]
+    ends_ref[...] = total[count + 1 : count + 2, :4]
+
+
+def unpack_sums(lay, left, right, after):
+    shapes = [(1, 4), (lay.channels, lay.channels), (1, lay.channels), (lay.channels, 3)]
+    return pl.pallas_call(
+        unpack_kernel,
+        in_specs=[VMEM] * 2 + [ANY] * len(after),
+        out_specs=[VMEM] * 4,
+        out_shape=[jax.ShapeDtypeStruct(shape, F32) for shape in shapes],
+        name="unpack_sums",
+    )(left, right, *after)
+
+
 def on_device(field_in, spectral_weight, point_weight, point_bias, out_weight, out_bias):
     lay = Layout(field_in, spectral_weight)
     tables = lay.grid_tables()
     x_table, x_back = lay.x_tables()
     weights = out_weight.astype(F32)
     scale = math.sqrt(lay.mx * lay.my * lay.mz / (lay.width * lay.ny * lay.nz))
-    cuts = [0, lay.rows // 4, lay.rows * 5 // 8, lay.rows]
+    cuts = [0, lay.rows * 5 // 8, lay.rows]
 
     def point(n, done, after):
         bias = point_bias.reshape(1, lay.channels)
@@ -945,40 +991,34 @@
         return point_parts[-1]
 
     grads = sum_all(lay, own, send, 1.0, grad_part)
-    outs = jnp.sum(sums[:, : 3 * lay.pack], axis=-1).reshape(3 * lay.channels)
+    outs = jnp.sum(sums[:, : 3 * lay.pack], axis=-1).reshape(lay.channels, 3)
     bias = sums[:, 3 * lay.pack, :LANES].reshape(lay.groups, lay.pack, lay.mx)[..., 0]
-    ends = jnp.sum(edge, axis=-1)
-    square = lay.channels * lay.channels
-    flat = jnp.concatenate(
-        [
-            sum_blocks(point_parts, False, 1.0, grads[-1:])[0].reshape(square),
-            outs,
-            bias.reshape(lay.channels),
-            ends[:4],
-        ]
-    )
-    flat = jnp.pad(flat, (0, -flat.shape[0] % 1024)).reshape(-1, LANES)
+    ends = jnp.sum(edge[:4], axis=-1)
+    small = jnp.zeros((lay.channels + 8, LANES), F32)
+    small = small.at[: lay.channels, lay.channels : lay.channels + 3].set(outs)
+    small = small.at[lay.channels, : lay.channels].set(bias.reshape(lay.channels))
+    small = small.at[lay.channels + 1, :4].set(ends)
+    flat = pack_sums(lay, point_parts, small, grads[-1:])
     rows = by_mode(lay, jnp.concatenate(grads))
     rows = jnp.concatenate([rows[:, :, : lay.mx], rows[:, :, lay.mx :]], axis=-1)
     columns = jnp.transpose(modes_in, (0, 1, 3, 2))
 
-    def gathered(axis, steps, after):
-        return sum_blocks([flat] + [exchange(flat, axis, d) for d in steps], False, 1.0, after)[0]
-
-    flat = gathered("gz", range(1, lay.n_gz), [rows])
+    def gathered(axis, steps):
+        return [flat] + [exchange(flat, axis, d) for d in steps]
+
+    flat = sum_blocks(gathered("gz", range(1, lay.n_gz)), False, 1.0, [rows])[0]
     grad_spectral = weight_grad(lay, columns, rows, 0, after=[flat])
-    flat = gathered("gy", range(CORES, lay.n_gy, CORES), [grad_spectral])
+    flat = sum_blocks(gathered("gy", range(CORES, lay.n_gy, CORES)), False, 1.0, [grad_spectral])
+    flat = flat[0]
     grad_spectral = weight_grad(lay, columns, rows, 1, [grad_spectral], [flat])
-    flat = gathered("gy", [1], [grad_spectral]).reshape(-1)
-    after = square + 3 * lay.channels
-    ends = flat[after + lay.channels : after + lay.channels + 4]
+    ends, grad_point, bias, outs = unpack_sums(lay, *gathered("gy", [1]), [grad_spectral])
     return (
-        ends[3] / (lay.width * lay.ny * lay.nz),
+        ends[0, 3] / (lay.width * lay.ny * lay.nz),
         grad_spectral,
-        flat[:square].reshape(lay.channels, lay.channels),
-        flat[after : after + lay.channels],
-        flat[square:after].reshape(lay.channels, 3),
-        ends[:3],
+        grad_point,
+        bias.reshape(lay.channels),
+        outs,
+        ends[0, :3],
     )
 
 

time: 718 us -> 559 us (0.78)
  Pallas kernels: 517 us -> 352 us
  starting transfers between devices: 70.1 us -> 77.4 us
    pallas_call x8, Pallas kernels: 180 us -> 24.6 us  [the longest x2 11.7 us: from_cores(): pl.pallas_call(core_kernel, grid=(lay.chips,), in_specs=[given, given], o...]
    unnamed x137 -> x131, local copies, waits for them, and re-layouts: 23.6 us -> 17.2 us
    pallas_call x3 -> x2, Pallas kernels: 37.1 us -> 32.7 us  [point_grad(): pl.pallas_call(functools.partial(point_kernel, lay.tile, len(after)), gri...]
    pallas_call x12 -> x10, Pallas kernels: 22.7 us -> 20 us  [sum_blocks(): pl.pallas_call(functools.partial(sum_kernel, len(values), n_out, factor),...]
    pallas_call x3 -> x2, Pallas kernels: 37.6 us -> 35.4 us  [pointwise(): pl.pallas_call(functools.partial(pointwise_kernel, lay.tile), grid=(count...]
  transfers between devices with their start and end apart: 51 -> 51, of which waited for: 17 -> 16; matrix products, arithmetic and copies ran while one was open for 3% -> 5% of each run, Pallas kernels for 25% -> 24%
where the time goes in v4:
time: 559 us; the launch traced here: 550 us
  Pallas kernels  352 us (63%)
  starting transfers between devices  77.4 us (14%)
  waiting for transfers between devices  55.8 us (10%)
  local copies, waits for them, and re-layouts  43.3 us (8%)
  other arithmetic  18.2 us (3%)
    pallas_call x2, Pallas kernels, dense(): pl.pallas_call(functools.partial(dense_kernel, first), grid=(count,), in_...  112 us
    ppermute x47, starting transfers between devices, exchange(): return lax.ppermute(value, axis, [(i, i ^ distance) for i in range(count)])  68.2 us
    pallas_call x1, Pallas kernels, grad_modes(): pl.pallas_call(functools.partial(grad_kernel, first, len(after)), grid=(c...  49.6 us
    ppermute x47, waiting for transfers between devices, exchange(): return lax.ppermute(value, axis, [(i, i ^ distance) for i in range(count)])  49.4 us
    pallas_call x2, Pallas kernels, pointwise(): pl.pallas_call(functools.partial(pointwise_kernel, lay.tile), grid=(count...  35.4 us
    pallas_call x2, Pallas kernels, point_grad(): pl.pallas_call(functools.partial(point_kernel, lay.tile, len(after)), gri...  32.7 us
    pallas_call x1, Pallas kernels, forward_modes(): pl.pallas_call(functools.partial(modes_kernel, len(after)), grid=(count,)...  29 us
    pallas_call x10, Pallas kernels, sum_blocks(): pl.pallas_call(functools.partial(sum_kernel, len(values), n_out, factor),...  20 us
  transfers between devices with their start and end apart: 51, of which 16 were waited for; matrix products, arithmetic and copies ran while one was open for 5% of the time, Pallas kernels for 24%

profile of v4, /device:TPU:0, one launch (start us, length us, event | category | flops | bytes accessed | tf_op | source)
XLA Modules:
  0.0 550.3 jit_solution(607000184563926973)
XLA Ops:
  0.8 2.9 compare_select_fusion.9
  7.4 29.0 %forward_modes.1 = (bf16[4,4,16,32,256]{4,3,2,1,0:T(8,128)(2,1)}, bf16[4,4,16,32,256]{4,3,2,1,0:T(8,128)(2,1)}) custom-call(bf16[64,32,32,256]{3,2,1,0:T(8,128)(2,1)} %field_ref.9, bf16[1024,256]{1,0:T(8,128)(2,1)} %pad_maximum_fusion.x_ref, bf16[128,256]{1,0:T(8,128)(2,1)} %select_convert_fusion.5.z_ref, bf16[128,256]{1,0:T(8,128)(2,1)} %select_convert_fusion.4.y_ref), custom_call_target="tpu_custom_call" | custom-call | flops 8589934592 | bytes 50331648 | tf_op jit(solution)/shard_map/forward_modes/pallas_call | solution.py:208
  37.5 6.4 %collective-permute-done.other_ref = bf16[4,4,16,32,256]{4,3,2,1,0:T(8,128)(2,1)} collective-permute-done((bf16[4,4,16,32,256]{4,3,2,1,0:T(8,128)(2,1)}, bf16[4,4,16,32,256]{4,3,2,1,0:T(8,128)(2,1)}, u32[]{:S(2)}, u32[]{:S(2)}) %collective-permute-start) | collective-permute-done | bytes 4194336 | tf_op jit(solution)/shard_map/ppermute | solution.py:229
  43.9 5.9 %core_sums.2 = (bf16[4,8,32,256]{3,2,1,0:T(8,128)(2,1)}, bf16[4,8,32,256]{3,2,1,0:T(8,128)(2,1)}, bf16[4,8,32,256]{3,2,1,0:T(8,128)(2,1)}, bf16[4,8,32,256]{3,2,...) custom-call(bf16[4,4,16,32,256]{4,3,2,1,0:T(8,128)(2,1)} %get-tuple-, ...), custom_call_target="tpu_custom_call" | custom-call | flops 2097152 | bytes 12582912 | tf_op jit(solution)/shard_map/core_sums/pallas_call | solution.py:281
  49.8 2.9 collective-permute-start.1
  54.3 21.5 %pointwise.2.refs_4_.refs_0_ = bf16[64,32,32,256]{3,2,1,0:T(8,128)(2,1)} custom-call(bf16[64,32,32,256]{3,2,1,0:T(8,128)(2,1)} %field_ref.9, bf16[64,64]{1,0:T(8,128)(2,1)} %bitcast.149, f32[1,64]{1,0:T(1,128)} %bitcast.174, bf16[4,8,32,256]{3,2,1,0:T(8,128)(2,1)} %get-tuple-element.94.refs_0_), custom_call_target="tpu_custom_call" | custom-call | flops 10737418240 | bytes 41943040 | tf_op jit(solution)/shard_map/pointwise/pallas_call | solution.py:445
  75.7 2.1 collective-permute-done.2
  78.8 2.5 sum_blocks.10
  81.4 2.6 collective-permute-start.5
  88.8 2.6 collective-permute-done.5
  91.5 2.4 collective-permute-start.4
  93.9 13.9 %pointwise.3.refs_4_.refs_0_.point_ref = bf16[64,32,32,256]{3,2,1,0:T(8,128)(2,1)} custom-call(bf16[64,32,32,256]{3,2,1,0:T(8,128)(2,1)} %field_ref.9, bf16[64,64]{1,0:T(8,128)(2,1)} %bitcast.150, f32[1,64]{1,0:T(1,128)} %bitcast.175, bf16[64,32,32,256]{3,2,1,0:T(8,128)(2,1)} %pointwise.2.refs_4_.refs_0_, ...), custom_call_target="tpu_custom_call", output_to_operand_aliasing={{}: (3, {})} | custom-call | flops 6442450944 | bytes 25165824 | tf_op jit(solution)/shard_map/pointwise/pallas_call | solution.py:445
  108.5 1.8 sum_blocks.11
  111.5 2.4 sum_blocks.12
  114.0 3.4 collective-permute-start.11
  120.6 5.5 %collective-permute-done.11 = bf16[8,32,256]{2,1,0:T(8,128)(2,1)S(1)} collective-permute-done((bf16[8,32,256]{2,1,0:T(8,128)(2,1)}, bf16[8,32,256]{2,1,0:T(8,128)(2,1)S(1)}, u32[]{:S(2)}, u32[]{:S(2)}) %collective-permute-start.11) | collective-permute-done | bytes 131104 | tf_op jit(solution)/shard_map/ppermute | solution.py:229
  126.9 1.8 sum_blocks.13
  130.4 1.6 maximum_bitcast_fusion
  133.6 15.2 %mix_modes.1 = bf16[8,4,32,128]{3,2,1,0:T(8,128)(2,1)} custom-call(bf16[8,4,64,64]{3,2,1,0:T(8,128)(2,1)} %copy.44.modes_ref, bf16[8,4,32,64,128]{4,3,2,1,0:T(8,128)(2,1)} %weight_ref.1, bf16[64,32,32,256]{3,2,1,0:T(8,128)(2,1)} %pointwise.3.refs_4_.refs_0_.point_ref), custom_call_target="tpu_custom_call" | custom-call | flops 67108864 | bytes 16777216 | tf_op jit(solution)/shard_map/mix_modes/pallas_call | solution.py:398
  150.7 2.0 collective-permute-start.19
  159.2 2.3 collective-permute-done.21
  162.2 1.8 stack_blocks.5
  164.0 3.8 collective-permute-start.22
  169.2 2.4 collective-permute-start.14
  173.9 10.4 %collective-permute-done.14 = bf16[11,32,256]{2,1,0:T(8,128)(2,1)S(1)} collective-permute-done((bf16[11,32,256]{2,1,0:T(8,128)(2,1)S(1)}, bf16[11,32,256]{2,1,0:T(8,128)(2,1)S(1)}, u32[]{:S(2)}, u32[]{:S(2)}) %collective-permute-start.14) | collective-permute-done | bytes 180256 | tf_op jit(solution)/shard_map/ppermute | solution.py:229
  185.0 2.1 stack_blocks.4
  188.1 2.5 stack_blocks.6
  195.0 1.7 collective-permute-start.16
  198.5 2.1 broadcast_in_dim.29.b_in_ref
  200.6 37.6 %dense.2 = (bf16[64,32,32,256]{3,2,1,0:T(8,128)(2,1)}, bf16[64,32,32,256]{3,2,1,0:T(8,128)(2,1)}, f32[3,32,32,256]{3,2,1,0:T(8,128)}) custom-call(bf16[4,4,5,32,256]{4,3,2,1,0:T(8,128)(2,1)} %bitcast.108, bf16[4,4,5,32,256]{4,3,2,1,0:T(8,128)(2,1)} %copy-done.3, bf16[128,256]{1,0:T(8,128)(2,1)} %select_convert_fusion.3.y_ref, ...), custom_call_target="tpu_custom_call" | custom-call | flops 8053063680 | bytes 125829120 | tf_op jit(solution)/shard_map/dense/pallas_call | solution.py:553
  239.6 3.5 stack_blocks.7
  243.1 5.5 collective-permute-done.26.other_ref
  248.6 1.7 copy-done.2
  250.4 74.5 %dense.3 = (bf16[64,32,32,256]{3,2,1,0:T(8,128)(2,1)}, bf16[64,32,32,256]{3,2,1,0:T(8,128)(2,1)}, f32[3,32,32,256]{3,2,1,0:T(8,128)}) custom-call(bf16[4,4,11,32,256]{4,3,2,1,0:T(8,128)(2,1)} %bitcast.99, bf16[4,4,11,32,256]{4,3,2,1,0:T(8,128)(2,1)} %copy-done.2, ...), custom_call_target="tpu_custom_call", output_to_operand_aliasing={{0}: (8, {}), {1}: (9, {})} | custom-call | flops 17716740096 | bytes 276824064 | tf_op jit(solution)/shard_map/dense/pallas_call | solution.py:553
  325.9 2.1 collective-permute-start.27
  330.8 3.6 collective-permute-done.28.refs_1_
  336.0 4.6 collective-permute-start.29
  344.7 15.7 %stencil.1 = (f32[3,32,32,256]{3,2,1,0:T(8,128)}, f32[8,256]{1,0:T(8,128)}) custom-call(s32[2]{0:T(128)} %pad_add_fusion.origin_ref, f32[3,32,32,256]{3,2,1,0:T(8,128)} %get-tuple-element.115.field_ref, f32[3,2,32,256]{3,2,1,0:T(8,128)} %copy-done.22, f32[3,2,32,256]{3,2,1,0:T(8,128)} %copy-done.23, f32[3,36,2,256]{3,2,1,0:T(2,128)} %copy-done.25, ...), custom_call_target="tpu_custom_call" | custom-call | tf_op jit(solution)/shard_map/stencil/pallas_call | solution.py:677
  360.3 49.6 %grad_modes.1 = (bf16[64,32,32,256]{3,2,1,0:T(8,128)(2,1)}, bf16[4,4,16,32,256]{4,3,2,1,0:T(8,128)(2,1)}, bf16[4,4,16,32,256]{4,3,2,1,0:T(8,128)(2,1)}, f32[16,16,256]{2,1,0:T(8,128)}) custom-call(f32[64,3]{1,0:T(8,128)} %convert_element_type.192.weight_ref, bf16[64,32,32,256]{3,2,1,0:T(8,128)(2,1)} %get-tuple-element.113.hidden_ref, ...), custom_call_target="tpu_custom_call" | custom-call | flops 8589934592 | bytes 167772160 | tf_op jit(solution)/shard_map/grad_modes/pallas_call | solution.py:754
  409.9 3.1 collective-permute-start.31
  416.2 3.9 collective-permute-done.31.other_ref
  420.1 5.9 %core_sums.3 = (bf16[4,8,32,256]{3,2,1,0:T(8,128)(2,1)}, bf16[4,8,32,256]{3,2,1,0:T(8,128)(2,1)}, bf16[4,8,32,256]{3,2,1,0:T(8,128)(2,1)}, bf16[4,8,32,256]{3,2,...) custom-call(bf16[4,4,16,32,256]{4,3,2,1,0:T(8,128)(2,1)} %get-tuple-, ...), custom_call_target="tpu_custom_call" | custom-call | flops 2097152 | bytes 12582912 | tf_op jit(solution)/shard_map/core_sums/pallas_call | solution.py:281
  426.0 3.3 collective-permute-start.32
  429.3 2.3 collective-permute-start.33
  432.1 19.3 %point_grad.2.refs_4_.refs_0_ = f32[64,64]{1,0:T(8,128)} custom-call(bf16[64,32,32,256]{3,2,1,0:T(8,128)(2,1)} %field_ref.9, bf16[64,32,32,256]{3,2,1,0:T(8,128)(2,1)} %get-tuple-element.117.grad_ref, bf16[4,8,32,256]{3,2,1,0:T(8,128)(2,1)} %get-tuple-element.120.refs_0_), custom_call_target="tpu_custom_call" | custom-call | flops 17179869184 | bytes 50331648 | tf_op jit(solution)/shard_map/point_grad/pallas_call | solution.py:838
  451.4 3.1 collective-permute-done.33
  456.5 2.4 sum_blocks.14
  458.9 3.4 collective-permute-start.38
  466.7 2.3 collective-permute-start.40
  469.0 13.4 %point_grad.3.refs_4_.refs_1_ = f32[64,64]{1,0:T(8,128)} custom-call(bf16[64,32,32,256]{3,2,1,0:T(8,128)(2,1)} %field_ref.9, bf16[64,32,32,256]{3,2,1,0:T(8,128)(2,1)} %get-tuple-element.117.grad_ref, bf16[8,32,256]{2,1,0:T(8,128)(2,1)} %bitcast.128), custom_call_target="tpu_custom_call" | custom-call | flops 17179869184 | bytes 50331648 | tf_op jit(solution)/shard_map/point_grad/pallas_call | solution.py:838
  483.1 1.8 sum_blocks.15
  484.9 3.5 collective-permute-done.36
  489.4 2.4 sum_blocks.16
  492.1 1.6 collective-permute-start.42
  493.7 2.5 collective-permute-start.43
  496.5 2.3 scatter.10
  501.4 1.8 collective-permute-done.42
  503.9 1.8 sum_blocks.17
  508.8 1.8 collective-permute-start.45
  512.4 1.6 maximum_bitcast_fusion.1
  518.2 1.9 collective-permute-start.47
  520.1 2.5 collective-permute-start.49
  522.6 8.8 %weight_grad.2.refs_4_.refs_0_ = f32[8,4,32,64,128]{4,3,2,1,0:T(8,128)} custom-call(bf16[8,4,64,64]{3,2,1,0:T(8,128)(2,1)} %bitcast.100, bf16[8,4,32,128]{3,2,1,0:T(8,128)(2,1)} %pad_maximum_fusion.2.refs_4_.grads_ref, f32[72,128]{1,0:T(8,128)} %sum_blocks.18.refs_0_), custom_call_target="tpu_custom_call" | custom-call | flops 16777216 | bytes 16777216 | tf_op jit(solution)/shard_map/weight_grad/pallas_call | solution.py:885
  533.5 8.8 %weight_grad.3.refs_0_ = f32[8,4,32,64,128]{4,3,2,1,0:T(8,128)} custom-call(bf16[8,4,64,64]{3,2,1,0:T(8,128)(2,1)} %bitcast.101, bf16[8,4,32,128]{3,2,1,0:T(8,128)(2,1)} %pad_maximum_fusion.2.refs_4_.grads_ref, f32[8,4,32,64,128]{4,3,2,1,0:T(8,128)} %weight_grad.2.refs_4_.refs_0_, f32[72,128]{1,0:T(8,128)} %sum_blocks.19.refs_1_.left_ref), custom_call_target="tpu_custom_call", output_to_operand_aliasing={{}: (2, {})} | custom-call | flops 16777216 | bytes 16777216 | tf_op jit(solution)/shard_map/weight_grad/pallas_call | solution.py:885
  (276 shorter events, 85.0 us)
Async XLA Ops:
  7.4 29.4 %copy-start.52 = (bf16[64,64]{1,0:T(8,128)(2,1)S(1)}, bf16[64,64]{1,0:T(8,128)(2,1)}, u32[]{:S(2)}) copy-start(bf16[64,64]{1,0:T(8,128)(2,1)} %param.14) | copy-start | bytes 24580
  36.4 7.6 %collective-permute-start = (bf16[4,4,16,32,256]{4,3,2,1,0:T(8,128)(2,1)}, bf16[4,4,16,32,256]{4,3,2,1,0:T(8,128)(2,1)}, u32[]{:S(2)}, u32[]{:S(2)}) collective-permute-start(bf16[4,4,16,32,256]{4,3,2,1,0:T(8,128)(2,1)} %get-tuple-element.93), channel_id=1, source_target_pairs={{0,4},{4,0},{8,12},{12,8},{16,20},{20,16},{24,28},{28,24},{1,5},{5... | collective-permute-start | bytes 12582920 | tf_op jit(solution)/shard_map/ppermute | solution.py:229
  49.8 25.9 %collective-permute-start.1 = (bf16[4,8,32,256]{3,2,1,0:T(8,128)(2,1)}, bf16[4,8,32,256]{3,2,1,0:T(8,128)(2,1)S(1)}, u32[]{:S(2)}, u32[]{:S(2)}) collective-permute-start(bf16[4,8,32,256]{3,2,1,0:T(8,128)(2,1)} %get-tuple-element.95), channel_id=1, source_target_pairs={{0,1},{1,0},{2,3},{3,2},{4,5},{5,4},{6,7},{7,6},{8,9},{9,8},{10,11... | collective-permute-start | bytes 1572872 | tf_op jit(solution)/shard_map/ppermute | solution.py:229
  52.7 25.1 %collective-permute-start.2 = (bf16[4,8,32,256]{3,2,1,0:T(8,128)(2,1)}, bf16[4,8,32,256]{3,2,1,0:T(8,128)(2,1)S(1)}, u32[]{:S(2)}, u32[]{:S(2)}) collective-permute-start(bf16[4,8,32,256]{3,2,1,0:T(8,128)(2,1)} %get-tuple-element.96), channel_id=1, source_target_pairs={{0,2},{1,3},{2,0},{3,1},{4,6},{5,7},{6,4},{7,5},{8,10},{9,11},{10,... | collective-permute-start | bytes 1572872 | tf_op jit(solution)/shard_map/ppermute | solution.py:229
  54.2 23.6 %collective-permute-start.3 = (bf16[4,8,32,256]{3,2,1,0:T(8,128)(2,1)}, bf16[4,8,32,256]{3,2,1,0:T(8,128)(2,1)S(1)}, u32[]{:S(2)}, u32[]{:S(2)}) collective-permute-start(bf16[4,8,32,256]{3,2,1,0:T(8,128)(2,1)} %get-tuple-element.97), channel_id=1, source_target_pairs={{0,3},{1,2},{2,1},{3,0},{4,7},{5,6},{6,5},{7,4},{8,11},{9,10},{10,... | collective-permute-start | bytes 1572872 | tf_op jit(solution)/shard_map/ppermute | solution.py:229
  81.4 10.1 %collective-permute-start.5 = (bf16[8,32,256]{2,1,0:T(8,128)(2,1)}, bf16[8,32,256]{2,1,0:T(8,128)(2,1)S(1)}, u32[]{:S(2)}, u32[]{:S(2)}) collective-permute-start(bf16[8,32,256]{2,1,0:T(8,128)(2,1)} %bitcast.186), channel_id=1, source_target_pairs={{0,16},{4,20},{8,24},{12,28},{16,0},{20,4},{24,8},{28,12},{1,17},{... | collective-permute-start | bytes 393224 | tf_op jit(solution)/shard_map/ppermute | solution.py:229
  84.0 26.4 %collective-permute-start.7 = (bf16[4,8,32,256]{3,2,1,0:T(8,128)(2,1)S(1)}, bf16[4,8,32,256]{3,2,1,0:T(8,128)(2,1)S(1)}, u32[]{:S(2)}, u32[]{:S(2)}) collective-permute-start(bf16[4,8,32,256]{3,2,1,0:T(8,128)(2,1)S(1)} %copy-done.61), channel_id=1, source_target_pairs={{0,1},{1,0},{2,3},{3,2},{4,5},{5,4},{6,7},{7,6},{8,9},{9,8},{10,11... | collective-permute-start | bytes 1572872 | tf_op jit(solution)/shard_map/ppermute | solution.py:229
  85.0 25.4 %collective-permute-start.8 = (bf16[4,8,32,256]{3,2,1,0:T(8,128)(2,1)S(1)}, bf16[4,8,32,256]{3,2,1,0:T(8,128)(2,1)S(1)}, u32[]{:S(2)}, u32[]{:S(2)}) collective-permute-start(bf16[4,8,32,256]{3,2,1,0:T(8,128)(2,1)S(1)} %copy-done.59), channel_id=1, source_target_pairs={{0,2},{1,3},{2,0},{3,1},{4,6},{5,7},{6,4},{7,5},{8,10},{9,11},{10,... | collective-permute-start | bytes 1572872 | tf_op jit(solution)/shard_map/ppermute | solution.py:229
  86.0 24.4 %collective-permute-start.9 = (bf16[4,8,32,256]{3,2,1,0:T(8,128)(2,1)S(1)}, bf16[4,8,32,256]{3,2,1,0:T(8,128)(2,1)S(1)}, u32[]{:S(2)}, u32[]{:S(2)}) collective-permute-start(bf16[4,8,32,256]{3,2,1,0:T(8,128)(2,1)S(1)} %copy-done.57), channel_id=1, source_target_pairs={{0,3},{1,2},{2,1},{3,0},{4,7},{5,6},{6,5},{7,4},{8,11},{9,10},{10,... | collective-permute-start | bytes 1572872 | tf_op jit(solution)/shard_map/ppermute | solution.py:229
  87.5 20.4 %collective-permute-start.6 = (bf16[8,32,256]{2,1,0:T(8,128)(2,1)}, bf16[8,32,256]{2,1,0:T(8,128)(2,1)S(1)}, u32[]{:S(2)}, u32[]{:S(2)}) collective-permute-start(bf16[8,32,256]{2,1,0:T(8,128)(2,1)} %bitcast.183), channel_id=1, source_target_pairs={{0,24},{4,28},{8,16},{12,20},{16,8},{20,12},{24,0},{28,4},{1,25},{... | collective-permute-start | bytes 393224 | tf_op jit(solution)/shard_map/ppermute | solution.py:229
  91.5 16.4 %copy-start.30 = (bf16[8,32,256]{2,1,0:T(8,128)(2,1)}, bf16[8,32,256]{2,1,0:T(8,128)(2,1)S(1)}, u32[]{:S(2)}) copy-start(bf16[8,32,256]{2,1,0:T(8,128)(2,1)S(1)} %collective-permute-done.5) | copy-start | bytes 393220
  91.5 16.4 %collective-permute-start.4 = (bf16[8,32,256]{2,1,0:T(8,128)(2,1)}, bf16[8,32,256]{2,1,0:T(8,128)(2,1)S(1)}, u32[]{:S(2)}, u32[]{:S(2)}) collective-permute-start(bf16[8,32,256]{2,1,0:T(8,128)(2,1)} %bitcast.181), channel_id=1, source_target_pairs={{0,8},{4,12},{8,0},{12,4},{16,24},{20,28},{24,16},{28,20},{1,9},{5... | collective-permute-start | bytes 393224 | tf_op jit(solution)/shard_map/ppermute | solution.py:229
  113.9 6.7 %collective-permute-start.10 = (bf16[8,32,256]{2,1,0:T(8,128)(2,1)}, bf16[8,32,256]{2,1,0:T(8,128)(2,1)S(1)}, u32[]{:S(2)}, u32[]{:S(2)}) collective-permute-start(bf16[8,32,256]{2,1,0:T(8,128)(2,1)} %bitcast.188), channel_id=1, source_target_pairs={{0,8},{4,12},{8,0},{12,4},{16,24},{20,28},{24,16},{28,20},{1,9},{5... | collective-permute-start | bytes 393224 | tf_op jit(solution)/shard_map/ppermute | solution.py:229
  114.0 12.2 %collective-permute-start.11 = (bf16[8,32,256]{2,1,0:T(8,128)(2,1)}, bf16[8,32,256]{2,1,0:T(8,128)(2,1)S(1)}, u32[]{:S(2)}, u32[]{:S(2)}) collective-permute-start(bf16[8,32,256]{2,1,0:T(8,128)(2,1)} %bitcast.187), channel_id=1, source_target_pairs={{0,16},{4,20},{8,24},{12,28},{16,0},{20,4},{24,8},{28,12},{1,17},{... | collective-permute-start | bytes 393224 | tf_op jit(solution)/shard_map/ppermute | solution.py:229
  117.4 8.7 %collective-permute-start.12 = (bf16[8,32,256]{2,1,0:T(8,128)(2,1)}, bf16[8,32,256]{2,1,0:T(8,128)(2,1)S(1)}, u32[]{:S(2)}, u32[]{:S(2)}) collective-permute-start(bf16[8,32,256]{2,1,0:T(8,128)(2,1)} %bitcast.185), channel_id=1, source_target_pairs={{0,24},{4,28},{8,16},{12,20},{16,8},{20,12},{24,0},{28,4},{1,25},{... | collective-permute-start | bytes 393224 | tf_op jit(solution)/shard_map/ppermute | solution.py:229
  132.5 16.2 %copy-start = (bf16[8,4,64,64]{2,3,1,0:T(8,128)(2,1)}, bf16[8,4,64,64]{2,3,1,0:T(8,128)(2,1)S(1)}, u32[]{:S(2)}) copy-start(bf16[8,4,64,64]{2,3,1,0:T(8,128)(2,1)S(1)} %reshape.381) | copy-start | bytes 786436
  150.7 7.6 %collective-permute-start.19 = (bf16[5,32,256]{2,1,0:T(8,128)(2,1)S(1)}, bf16[5,32,256]{2,1,0:T(8,128)(2,1)S(1)}, u32[]{:S(2)}, u32[]{:S(2)}) collective-permute-start(bf16[5,32,256]{2,1,0:T(8,128)(2,1)S(1)} %slice.127), channel_id=1, source_target_pairs={{0,8},{4,12},{8,0},{12,4},{16,24},{20,28},{24,16},{28,20},{1,9},{5... | collective-permute-start | bytes 245768 | tf_op jit(solution)/shard_map/ppermute | solution.py:229
  152.7 6.5 %collective-permute-start.20 = (bf16[5,32,256]{2,1,0:T(8,128)(2,1)S(1)}, bf16[5,32,256]{2,1,0:T(8,128)(2,1)S(1)}, u32[]{:S(2)}, u32[]{:S(2)}) collective-permute-start(bf16[5,32,256]{2,1,0:T(8,128)(2,1)S(1)} %slice.127), channel_id=1, source_target_pairs={{0,16},{4,20},{8,24},{12,28},{16,0},{20,4},{24,8},{28,12},{1,17},{... | collective-permute-start | bytes 245768 | tf_op jit(solution)/shard_map/ppermute | solution.py:229
  153.8 7.7 %collective-permute-start.21 = (bf16[5,32,256]{2,1,0:T(8,128)(2,1)S(1)}, bf16[5,32,256]{2,1,0:T(8,128)(2,1)S(1)}, u32[]{:S(2)}, u32[]{:S(2)}) collective-permute-start(bf16[5,32,256]{2,1,0:T(8,128)(2,1)S(1)} %slice.127), channel_id=1, source_target_pairs={{0,24},{4,28},{8,16},{12,20},{16,8},{20,12},{24,0},{28,4},{1,25},{... | collective-permute-start | bytes 245768 | tf_op jit(solution)/shard_map/ppermute | solution.py:229
  155.8 34.7 %copy-start.54 = (bf16[64,3]{0,1:T(4,128)(2,1)S(1)}, bf16[64,3]{0,1:T(4,128)(2,1)}, u32[]{:S(2)}) copy-start(bf16[64,3]{0,1:T(4,128)(2,1)} %param.16) | copy-start | bytes 1156
  156.3 42.2 %copy-start.55 = (f32[3]{0:T(128)S(1)}, f32[3]{0:T(128)}, u32[]{:S(2)}) copy-start(f32[3]{0:T(128)} %param.17) | copy-start | bytes 40
  156.3 15.3 %collective-permute-start.13 = (bf16[11,32,256]{2,1,0:T(8,128)(2,1)S(1)}, bf16[11,32,256]{2,1,0:T(8,128)(2,1)S(1)}, u32[]{:S(2)}, u32[]{:S(2)}) collective-permute-start(bf16[11,32,256]{2,1,0:T(8,128)(2,1)S(1)} %slice.125), channel_id=1, source_target_pairs={{0,8},{4,12},{8,0},{12,4},{16,24},{20,28},{24,16},{28,20},{1,9},{5... | collective-permute-start | bytes 540680 | tf_op jit(solution)/shard_map/ppermute | solution.py:229
  164.0 23.2 %collective-permute-start.22 = (bf16[4,5,32,256]{3,2,1,0:T(8,128)(2,1)}, bf16[4,5,32,256]{3,2,1,0:T(8,128)(2,1)S(1)}, u32[]{:S(2)}, u32[]{:S(2)}) collective-permute-start(bf16[4,5,32,256]{3,2,1,0:T(8,128)(2,1)} %bitcast.113), channel_id=1, source_target_pairs={{0,1},{1,0},{2,3},{3,2},{4,5},{5,4},{6,7},{7,6},{8,9},{9,8},{10,11... | collective-permute-start | bytes 983048 | tf_op jit(solution)/shard_map/ppermute | solution.py:229
  167.7 19.4 %collective-permute-start.23 = (bf16[4,5,32,256]{3,2,1,0:T(8,128)(2,1)}, bf16[4,5,32,256]{3,2,1,0:T(8,128)(2,1)S(1)}, u32[]{:S(2)}, u32[]{:S(2)}) collective-permute-start(bf16[4,5,32,256]{3,2,1,0:T(8,128)(2,1)} %bitcast.114), channel_id=1, source_target_pairs={{0,2},{1,3},{2,0},{3,1},{4,6},{5,7},{6,4},{7,5},{8,10},{9,11},{10,... | collective-permute-start | bytes 983048 | tf_op jit(solution)/shard_map/ppermute | solution.py:229
  167.7 19.4 %collective-permute-start.24 = (bf16[4,5,32,256]{3,2,1,0:T(8,128)(2,1)}, bf16[4,5,32,256]{3,2,1,0:T(8,128)(2,1)S(1)}, u32[]{:S(2)}, u32[]{:S(2)}) collective-permute-start(bf16[4,5,32,256]{3,2,1,0:T(8,128)(2,1)} %bitcast.115), channel_id=1, source_target_pairs={{0,3},{1,2},{2,1},{3,0},{4,7},{5,6},{6,5},{7,4},{8,11},{9,10},{10,... | collective-permute-start | bytes 983048 | tf_op jit(solution)/shard_map/ppermute | solution.py:229
  169.2 15.0 %collective-permute-start.14 = (bf16[11,32,256]{2,1,0:T(8,128)(2,1)S(1)}, bf16[11,32,256]{2,1,0:T(8,128)(2,1)S(1)}, u32[]{:S(2)}, u32[]{:S(2)}) collective-permute-start(bf16[11,32,256]{2,1,0:T(8,128)(2,1)S(1)} %slice.125), channel_id=1, source_target_pairs={{0,16},{4,20},{8,24},{12,28},{16,0},{20,4},{24,8},{28,12},{1,17},{... | collective-permute-start | bytes 540680 | tf_op jit(solution)/shard_map/ppermute | solution.py:229
  171.6 12.6 %copy-start.26 = (bf16[11,32,256]{2,1,0:T(8,128)(2,1)}, bf16[11,32,256]{2,1,0:T(8,128)(2,1)S(1)}, u32[]{:S(2)}) copy-start(bf16[11,32,256]{2,1,0:T(8,128)(2,1)S(1)} %collective-permute-done.13) | copy-start | bytes 540676
  171.6 12.6 %collective-permute-start.15 = (bf16[11,32,256]{2,1,0:T(8,128)(2,1)S(1)}, bf16[11,32,256]{2,1,0:T(8,128)(2,1)S(1)}, u32[]{:S(2)}, u32[]{:S(2)}) collective-permute-start(bf16[11,32,256]{2,1,0:T(8,128)(2,1)S(1)} %slice.125), channel_id=1, source_target_pairs={{0,24},{4,28},{8,16},{12,20},{16,8},{20,12},{24,0},{28,4},{1,25},{... | collective-permute-start | bytes 540680 | tf_op jit(solution)/shard_map/ppermute | solution.py:229
  190.6 7.9 %collective-permute-start.25 = (bf16[4,4,5,32,256]{4,3,2,1,0:T(8,128)(2,1)}, bf16[4,4,5,32,256]{4,3,2,1,0:T(8,128)(2,1)S(1)}, u32[]{:S(2)}, u32[]{:S(2)}) collective-permute-start(bf16[4,4,5,32,256]{4,3,2,1,0:T(8,128)(2,1)} %bitcast.107), channel_id=1, source_target_pairs={{0,4},{4,0},{8,12},{12,8},{16,20},{20,16},{24,28},{28,24},{1,5},{5... | collective-permute-start | bytes 3932168 | tf_op jit(solution)/shard_map/ppermute | solution.py:229
  195.0 43.2 %collective-permute-start.16 = (bf16[4,11,32,256]{3,2,1,0:T(8,128)(2,1)S(1)}, bf16[4,11,32,256]{3,2,1,0:T(8,128)(2,1)S(1)}, u32[]{:S(2)}, u32[]{:S(2)}) collective-permute-start(bf16[4,11,32,256]{3,2,1,0:T(8,128)(2,1)S(1)} %bitcast.104), channel_id=1, source_target_pairs={{0,1},{1,0},{2,3},{3,2},{4,5},{5,4},{6,7},{7,6},{8,9},{9,8},{10,11... | collective-permute-start | bytes 2162696 | tf_op jit(solution)/shard_map/ppermute | solution.py:229
  196.8 41.5 %collective-permute-start.17 = (bf16[4,11,32,256]{3,2,1,0:T(8,128)(2,1)S(1)}, bf16[4,11,32,256]{3,2,1,0:T(8,128)(2,1)S(1)}, u32[]{:S(2)}, u32[]{:S(2)}) collective-permute-start(bf16[4,11,32,256]{3,2,1,0:T(8,128)(2,1)S(1)} %bitcast.105), channel_id=1, source_target_pairs={{0,2},{1,3},{2,0},{3,1},{4,6},{5,7},{6,4},{7,5},{8,10},{9,11},{10,... | collective-permute-start | bytes 2162696 | tf_op jit(solution)/shard_map/ppermute | solution.py:229
  197.0 41.2 %collective-permute-start.18 = (bf16[4,11,32,256]{3,2,1,0:T(8,128)(2,1)S(1)}, bf16[4,11,32,256]{3,2,1,0:T(8,128)(2,1)S(1)}, u32[]{:S(2)}, u32[]{:S(2)}) collective-permute-start(bf16[4,11,32,256]{3,2,1,0:T(8,128)(2,1)S(1)} %bitcast.106), channel_id=1, source_target_pairs={{0,3},{1,2},{2,1},{3,0},{4,7},{5,6},{6,5},{7,4},{8,11},{9,10},{10,... | collective-permute-start | bytes 2162696 | tf_op jit(solution)/shard_map/ppermute | solution.py:229
  243.1 5.5 collective-permute-start.26
  325.9 4.9 collective-permute-start.27
  328.0 6.5 %collective-permute-start.28 = (f32[3,2,32,256]{3,2,1,0:T(8,128)S(1)}, f32[3,2,32,256]{3,2,1,0:T(8,128)S(1)}, u32[]{:S(2)}, u32[]{:S(2)}) collective-permute-start(f32[3,2,32,256]{3,2,1,0:T(8,128)S(1)} %get-tuple-element.162), channel_id=1, source_target_pairs={{4,0},{8,4},{12,8},{16,12},{20,16},{24,20},{28,24},{5,1},{9,5},{13... | collective-permute-start | bytes 589832 | tf_op jit(solution)/shard_map/ppermute | solution.py:53
  330.8 13.2 %copy-start.22 = (f32[3,2,32,256]{3,2,1,0:T(8,128)}, f32[3,2,32,256]{3,2,1,0:T(8,128)S(1)}, u32[]{:S(2)}) copy-start(f32[3,2,32,256]{3,2,1,0:T(8,128)S(1)} %collective-permute-done.27.refs_0_) | copy-start | bytes 589828
  334.6 7.8 %collective-permute-start.30 = (f32[3,36,2,256]{3,2,1,0:T(2,128)S(1)}, f32[3,36,2,256]{3,2,1,0:T(2,128)S(1)}, u32[]{:S(2)}, u32[]{:S(2)}) collective-permute-start(f32[3,36,2,256]{3,2,1,0:T(2,128)S(1)} %pad_maximum_fusion.4), channel_id=1, source_target_pairs={{1,0},{2,1},{3,2},{5,4},{6,5},{7,6},{9,8},{10,9},{11,10},{13,12},{... | collective-permute-start | bytes 663560 | tf_op jit(solution)/shard_map/ppermute | solution.py:53
  336.0 8.0 %collective-permute-start.29 = (f32[3,36,2,256]{3,2,1,0:T(2,128)S(1)}, f32[3,36,2,256]{3,2,1,0:T(2,128)S(1)}, u32[]{:S(2)}, u32[]{:S(2)}) collective-permute-start(f32[3,36,2,256]{3,2,1,0:T(2,128)S(1)} %pad_maximum_fusion.3), channel_id=1, source_target_pairs={{0,1},{1,2},{2,3},{4,5},{5,6},{6,7},{8,9},{9,10},{10,11},{12,13},{... | collective-permute-start | bytes 663560 | tf_op jit(solution)/shard_map/ppermute | solution.py:53
  360.3 53.3 %copy-start.62 = (s32[2]{0:T(128)S(1)}, s32[2]{0:T(128)}, u32[]{:S(2)}) copy-start(s32[2]{0:T(128)} %constant.471.clone.1) | copy-start | bytes 28
  409.9 10.2 %collective-permute-start.31 = (bf16[4,4,16,32,256]{4,3,2,1,0:T(8,128)(2,1)}, bf16[4,4,16,32,256]{4,3,2,1,0:T(8,128)(2,1)}, u32[]{:S(2)}, u32[]{:S(2)}) collective-permute-start(bf16[4,4,16,32,256]{4,3,2,1,0:T(8,128)(2,1)} %get-tuple-element.119), channel_id=1, source_target_pairs={{0,4},{4,0},{8,12},{12,8},{16,20},{20,16},{24,28},{28,24},{1,5},{5... | collective-permute-start | bytes 12582920 | tf_op jit(solution)/shard_map/ppermute | solution.py:229
  426.0 25.4 %collective-permute-start.32 = (bf16[4,8,32,256]{3,2,1,0:T(8,128)(2,1)}, bf16[4,8,32,256]{3,2,1,0:T(8,128)(2,1)S(1)}, u32[]{:S(2)}, u32[]{:S(2)}) collective-permute-start(bf16[4,8,32,256]{3,2,1,0:T(8,128)(2,1)} %get-tuple-element.121), channel_id=1, source_target_pairs={{0,1},{1,0},{2,3},{3,2},{4,5},{5,4},{6,7},{7,6},{8,9},{9,8},{10,11... | collective-permute-start | bytes 1572872 | tf_op jit(solution)/shard_map/ppermute | solution.py:229
  429.3 25.2 %collective-permute-start.33 = (bf16[4,8,32,256]{3,2,1,0:T(8,128)(2,1)}, bf16[4,8,32,256]{3,2,1,0:T(8,128)(2,1)S(1)}, u32[]{:S(2)}, u32[]{:S(2)}) collective-permute-start(bf16[4,8,32,256]{3,2,1,0:T(8,128)(2,1)} %get-tuple-element.122), channel_id=1, source_target_pairs={{0,2},{1,3},{2,0},{3,1},{4,6},{5,7},{6,4},{7,5},{8,10},{9,11},{10,... | collective-permute-start | bytes 1572872 | tf_op jit(solution)/shard_map/ppermute | solution.py:229
  431.6 24.1 %collective-permute-start.34 = (bf16[4,8,32,256]{3,2,1,0:T(8,128)(2,1)}, bf16[4,8,32,256]{3,2,1,0:T(8,128)(2,1)S(1)}, u32[]{:S(2)}, u32[]{:S(2)}) collective-permute-start(bf16[4,8,32,256]{3,2,1,0:T(8,128)(2,1)} %get-tuple-element.123), channel_id=1, source_target_pairs={{0,3},{1,2},{2,1},{3,0},{4,7},{5,6},{6,5},{7,4},{8,11},{9,10},{10,... | collective-permute-start | bytes 1572872 | tf_op jit(solution)/shard_map/ppermute | solution.py:229
  432.1 31.0 %copy-start.60 = (bf16[4,8,32,256]{3,2,1,0:T(8,128)(2,1)S(1)}, bf16[4,8,32,256]{3,2,1,0:T(8,128)(2,1)}, u32[]{:S(2)}) copy-start(bf16[4,8,32,256]{3,2,1,0:T(8,128)(2,1)} %get-tuple-element.128) | copy-start | bytes 1572868
  432.1 32.5 %copy-start.58 = (bf16[4,8,32,256]{3,2,1,0:T(8,128)(2,1)S(1)}, bf16[4,8,32,256]{3,2,1,0:T(8,128)(2,1)}, u32[]{:S(2)}) copy-start(bf16[4,8,32,256]{3,2,1,0:T(8,128)(2,1)} %get-tuple-element.129) | copy-start | bytes 1572868
  432.1 33.5 %copy-start.56 = (bf16[4,8,32,256]{3,2,1,0:T(8,128)(2,1)S(1)}, bf16[4,8,32,256]{3,2,1,0:T(8,128)(2,1)}, u32[]{:S(2)}) copy-start(bf16[4,8,32,256]{3,2,1,0:T(8,128)(2,1)} %get-tuple-element.130) | copy-start | bytes 1572868
  458.9 7.7 %collective-permute-start.38 = (bf16[8,32,256]{2,1,0:T(8,128)(2,1)}, bf16[8,32,256]{2,1,0:T(8,128)(2,1)S(1)}, u32[]{:S(2)}, u32[]{:S(2)}) collective-permute-start(bf16[8,32,256]{2,1,0:T(8,128)(2,1)} %bitcast.184), channel_id=1, source_target_pairs={{0,8},{4,12},{8,0},{12,4},{16,24},{20,28},{24,16},{28,20},{1,9},{5... | collective-permute-start | bytes 393224 | tf_op jit(solution)/shard_map/ppermute | solution.py:229
  463.1 21.8 %collective-permute-start.35 = (bf16[4,8,32,256]{3,2,1,0:T(8,128)(2,1)S(1)}, bf16[4,8,32,256]{3,2,1,0:T(8,128)(2,1)S(1)}, u32[]{:S(2)}, u32[]{:S(2)}) collective-permute-start(bf16[4,8,32,256]{3,2,1,0:T(8,128)(2,1)S(1)} %copy-done.60), channel_id=1, source_target_pairs={{0,1},{1,0},{2,3},{3,2},{4,5},{5,4},{6,7},{7,6},{8,9},{9,8},{10,11... | collective-permute-start | bytes 1572872 | tf_op jit(solution)/shard_map/ppermute | solution.py:229
  464.6 23.8 %collective-permute-start.36 = (bf16[4,8,32,256]{3,2,1,0:T(8,128)(2,1)S(1)}, bf16[4,8,32,256]{3,2,1,0:T(8,128)(2,1)S(1)}, u32[]{:S(2)}, u32[]{:S(2)}) collective-permute-start(bf16[4,8,32,256]{3,2,1,0:T(8,128)(2,1)S(1)} %copy-done.58), channel_id=1, source_target_pairs={{0,2},{1,3},{2,0},{3,1},{4,6},{5,7},{6,4},{7,5},{8,10},{9,11},{10,... | collective-permute-start | bytes 1572872 | tf_op jit(solution)/shard_map/ppermute | solution.py:229
  465.6 22.9 %collective-permute-start.37 = (bf16[4,8,32,256]{3,2,1,0:T(8,128)(2,1)S(1)}, bf16[4,8,32,256]{3,2,1,0:T(8,128)(2,1)S(1)}, u32[]{:S(2)}, u32[]{:S(2)}) collective-permute-start(bf16[4,8,32,256]{3,2,1,0:T(8,128)(2,1)S(1)} %copy-done.56), channel_id=1, source_target_pairs={{0,3},{1,2},{2,1},{3,0},{4,7},{5,6},{6,5},{7,4},{8,11},{9,10},{10,... | collective-permute-start | bytes 1572872 | tf_op jit(solution)/shard_map/ppermute | solution.py:229
  466.6 15.8 %collective-permute-start.39 = (bf16[8,32,256]{2,1,0:T(8,128)(2,1)}, bf16[8,32,256]{2,1,0:T(8,128)(2,1)S(1)}, u32[]{:S(2)}, u32[]{:S(2)}) collective-permute-start(bf16[8,32,256]{2,1,0:T(8,128)(2,1)} %bitcast.182), channel_id=1, source_target_pairs={{0,16},{4,20},{8,24},{12,28},{16,0},{20,4},{24,8},{28,12},{1,17},{... | collective-permute-start | bytes 393224 | tf_op jit(solution)/shard_map/ppermute | solution.py:229
  466.7 15.7 %copy-start.39 = (bf16[8,32,256]{2,1,0:T(8,128)(2,1)}, bf16[8,32,256]{2,1,0:T(8,128)(2,1)S(1)}, u32[]{:S(2)}) copy-start(bf16[8,32,256]{2,1,0:T(8,128)(2,1)S(1)} %collective-permute-done.38) | copy-start | bytes 393220
  466.7 15.7 %collective-permute-start.40 = (bf16[8,32,256]{2,1,0:T(8,128)(2,1)}, bf16[8,32,256]{2,1,0:T(8,128)(2,1)S(1)}, u32[]{:S(2)}, u32[]{:S(2)}) collective-permute-start(bf16[8,32,256]{2,1,0:T(8,128)(2,1)} %bitcast.180), channel_id=1, source_target_pairs={{0,24},{4,28},{8,16},{12,20},{16,8},{20,12},{24,0},{28,4},{1,25},{... | collective-permute-start | bytes 393224 | tf_op jit(solution)/shard_map/ppermute | solution.py:229
  469.0 30.0 %copy-start.53 = (f32[8,256]{1,0:T(8,128)S(1)}, f32[8,256]{1,0:T(8,128)}, u32[]{:S(2)}) copy-start(f32[8,256]{1,0:T(8,128)} %get-tuple-element.126) | copy-start | bytes 24580
  491.8 9.5 %collective-permute-start.41 = (bf16[8,32,256]{2,1,0:T(8,128)(2,1)}, bf16[8,32,256]{2,1,0:T(8,128)(2,1)S(1)}, u32[]{:S(2)}, u32[]{:S(2)}) collective-permute-start(bf16[8,32,256]{2,1,0:T(8,128)(2,1)} %bitcast.179), channel_id=1, source_target_pairs={{0,8},{4,12},{8,0},{12,4},{16,24},{20,28},{24,16},{28,20},{1,9},{5... | collective-permute-start | bytes 393224 | tf_op jit(solution)/shard_map/ppermute | solution.py:229
  492.1 11.0 %collective-permute-start.42 = (bf16[8,32,256]{2,1,0:T(8,128)(2,1)}, bf16[8,32,256]{2,1,0:T(8,128)(2,1)S(1)}, u32[]{:S(2)}, u32[]{:S(2)}) collective-permute-start(bf16[8,32,256]{2,1,0:T(8,128)(2,1)} %bitcast.178), channel_id=1, source_target_pairs={{0,16},{4,20},{8,24},{12,28},{16,0},{20,4},{24,8},{28,12},{1,17},{... | collective-permute-start | bytes 393224 | tf_op jit(solution)/shard_map/ppermute | solution.py:229
  493.7 9.4 %collective-permute-start.43 = (bf16[8,32,256]{2,1,0:T(8,128)(2,1)}, bf16[8,32,256]{2,1,0:T(8,128)(2,1)S(1)}, u32[]{:S(2)}, u32[]{:S(2)}) collective-permute-start(bf16[8,32,256]{2,1,0:T(8,128)(2,1)} %bitcast.177), channel_id=1, source_target_pairs={{0,24},{4,28},{8,16},{12,20},{16,8},{20,12},{24,0},{28,4},{1,25},{... | collective-permute-start | bytes 393224 | tf_op jit(solution)/shard_map/ppermute | solution.py:229
  508.3 7.7 %collective-permute-start.44 = (f32[72,128]{1,0:T(8,128)}, f32[72,128]{1,0:T(8,128)S(1)}, u32[]{:S(2)}, u32[]{:S(2)}) collective-permute-start(f32[72,128]{1,0:T(8,128)} %pack_sums.1), channel_id=1, source_target_pairs={{0,1},{1,0},{2,3},{3,2},{4,5},{5,4},{6,7},{7,6},{8,9},{9,8},{10,11... | collective-permute-start | bytes 110600 | tf_op jit(solution)/shard_map/ppermute | solution.py:229
  508.8 7.3 %collective-permute-start.45 = (f32[72,128]{1,0:T(8,128)}, f32[72,128]{1,0:T(8,128)S(1)}, u32[]{:S(2)}, u32[]{:S(2)}) collective-permute-start(f32[72,128]{1,0:T(8,128)} %pack_sums.1), channel_id=1, source_target_pairs={{0,2},{1,3},{2,0},{3,1},{4,6},{5,7},{6,4},{7,5},{8,10},{9,11},{10,... | collective-permute-start | bytes 110600 | tf_op jit(solution)/shard_map/ppermute | solution.py:229
  510.5 5.5 %collective-permute-start.46 = (f32[72,128]{1,0:T(8,128)}, f32[72,128]{1,0:T(8,128)S(1)}, u32[]{:S(2)}, u32[]{:S(2)}) collective-permute-start(f32[72,128]{1,0:T(8,128)} %pack_sums.1), channel_id=1, source_target_pairs={{0,3},{1,2},{2,1},{3,0},{4,7},{5,6},{6,5},{7,4},{8,11},{9,10},{10,... | collective-permute-start | bytes 110600 | tf_op jit(solution)/shard_map/ppermute | solution.py:229
  518.2 13.2 %collective-permute-start.47 = (f32[72,128]{1,0:T(8,128)}, f32[72,128]{1,0:T(8,128)S(1)}, u32[]{:S(2)}, u32[]{:S(2)}) collective-permute-start(f32[72,128]{1,0:T(8,128)} %sum_blocks.18.refs_0_), channel_id=1, source_target_pairs={{0,8},{4,12},{8,0},{12,4},{16,24},{20,28},{24,16},{28,20},{1,9},{5... | collective-permute-start | bytes 110600 | tf_op jit(solution)/shard_map/ppermute | solution.py:229
  520.1 11.3 %collective-permute-start.48 = (f32[72,128]{1,0:T(8,128)}, f32[72,128]{1,0:T(8,128)S(1)}, u32[]{:S(2)}, u32[]{:S(2)}) collective-permute-start(f32[72,128]{1,0:T(8,128)} %sum_blocks.18.refs_0_), channel_id=1, source_target_pairs={{0,16},{4,20},{8,24},{12,28},{16,0},{20,4},{24,8},{28,12},{1,17},{... | collective-permute-start | bytes 110600 | tf_op jit(solution)/shard_map/ppermute | solution.py:229
  520.1 11.3 %collective-permute-start.49 = (f32[72,128]{1,0:T(8,128)}, f32[72,128]{1,0:T(8,128)S(1)}, u32[]{:S(2)}, u32[]{:S(2)}) collective-permute-start(f32[72,128]{1,0:T(8,128)} %sum_blocks.18.refs_0_), channel_id=1, source_target_pairs={{0,24},{4,28},{8,16},{12,20},{16,8},{20,12},{24,0},{28,4},{1,25},{... | collective-permute-start | bytes 110600 | tf_op jit(solution)/shard_map/ppermute | solution.py:229
  533.5 8.8 %collective-permute-start.50 = (f32[72,128]{1,0:T(8,128)}, f32[72,128]{1,0:T(8,128)S(1)}, u32[]{:S(2)}, u32[]{:S(2)}) collective-permute-start(f32[72,128]{1,0:T(8,128)} %sum_blocks.19.refs_1_.left_ref), channel_id=1, source_target_pairs={{0,4},{4,0},{8,12},{12,8},{16,20},{20,16},{24,28},{28,24},{1,5},{5... | collective-permute-start | bytes 110600 | tf_op jit(solution)/shard_map/ppermute | solution.py:229
  (50 other events, 98.2 us)

commit v5 on v4

--- a/solution.py
+++ b/solution.py
@@ -267,23 +267,24 @@
 
 def core_kernel(own_ref, other_ref, *refs):
     count = own_ref.shape[0]
-    half = refs[0].shape[1]
+    cut = refs[0].shape[1]
     for n in range(count):
         total = (own_ref[n, 0].astype(F32) + other_ref[n, 0].astype(F32)).astype(BF16)
-        refs[n][0] = total[:half]
-        refs[count + n][0] = total[half:]
+        refs[n][0] = total[:cut]
+        refs[count + n][0] = total[cut:]
 
 
 def from_cores(lay, own, other):
     tail = (lay.own, 2 * LANES)
-    half = lay.groups // 2
+    cut = max(lay.groups * 5 // 8, 1)
     given = pl.BlockSpec((lay.n_gz, 1, lay.groups) + tail, lambda i: (0, i, 0, 0, 0))
+    sizes = [cut] * lay.n_gz + [lay.groups - cut] * lay.n_gz
     outs = pl.pallas_call(
         core_kernel,
         grid=(lay.chips,),
         in_specs=[given, given],
-        out_specs=[pl.BlockSpec((1, half) + tail, lambda i: (i, 0, 0, 0))] * (2 * lay.n_gz),
-        out_shape=[jax.ShapeDtypeStruct((lay.chips, half) + tail, BF16)] * (2 * lay.n_gz),
+        out_specs=[pl.BlockSpec((1, size) + tail, lambda i: (i, 0, 0, 0)) for size in sizes],
+        out_shape=[jax.ShapeDtypeStruct((lay.chips, size) + tail, BF16) for size in sizes],
         compiler_params=params(),
         cost_estimate=cost(own.size, own.size * 6),
         name="core_sums",
@@ -291,14 +292,14 @@
     return list(outs[: lay.n_gz]), list(outs[lay.n_gz :])
 
 
-def sum_all(lay, own, send, factor, work):
+def sum_all(lay, own, send, factor, work, last=()):
     early, late = from_cores(lay, own, exchange(send, "gy", 1))
     done = work(0, early[:1])
     early = sum_blocks(to_depth(early), True, after=[done])
     done = work(1, early[:1])
     first = from_chips(early, factor, [done])
     late = sum_blocks(to_depth(late), True, after=[first])
-    return [first, from_chips(late, factor)]
+    return [first, from_chips(late, factor, last)]
 
 
 def to_depth(blocks):
@@ -902,8 +903,9 @@
     total = refs[0][...]
     for ref in refs[1:n_parts]:
         total = total + ref[...]
-    out_ref[...] = small_ref[...]
+    out_ref[...] = jnp.zeros_like(out_ref)
     out_ref[:count, :count] = total
+    out_ref[count:] = small_ref[...]
 
 
 def pack_sums(lay, parts, small, after):
@@ -911,27 +913,29 @@
         functools.partial(pack_kernel, len(parts)),
         in_specs=[VMEM] * (len(parts) + 1) + [ANY] * len(after),
         out_specs=VMEM,
-        out_shape=jax.ShapeDtypeStruct(small.shape, F32),
+        out_shape=jax.ShapeDtypeStruct((lay.channels + small.shape[0], LANES), F32),
         name="pack_sums",
     )(*parts, small, *after)
 
 
-def unpack_kernel(left_ref, right_ref, *refs):
-    ends_ref, point_ref, bias_ref, outs_ref = refs[-4:]
+def unpack_kernel(cells, left_ref, right_ref, *refs):
+    loss_ref, point_ref, outs_ref, bias_ref, ends_ref = refs[-5:]
     count = point_ref.shape[0]
     total = left_ref[...] + right_ref[...]
     point_ref[...] = total[:count, :count]
-    outs_ref[...] = total[:count, count : count + 3]
-    bias_ref[...] = total[count : count + 1, :count]
-    ends_ref[...] = total[count + 1 : count + 2, :4]
+    outs_ref[...] = total[count : count + 3, :count]
+    bias_ref[...] = total[count + 3 : count + 4, :count]
+    ends_ref[...] = total[count + 4 : count + 5, :3]
+    loss_ref[...] = total[count + 4 : count + 5, 3:4] / cells
 
 
 def unpack_sums(lay, left, right, after):
-    shapes = [(1, 4), (lay.channels, lay.channels), (1, lay.channels), (lay.channels, 3)]
+    count = lay.channels
+    shapes = [(1, 1), (count, count), (3, count), (1, count), (1, 3)]
     return pl.pallas_call(
-        unpack_kernel,
+        functools.partial(unpack_kernel, lay.width * lay.ny * lay.nz),
         in_specs=[VMEM] * 2 + [ANY] * len(after),
-        out_specs=[VMEM] * 4,
+        out_specs=[VMEM] * len(shapes),
         out_shape=[jax.ShapeDtypeStruct(shape, F32) for shape in shapes],
         name="unpack_sums",
     )(left, right, *after)
@@ -943,7 +947,7 @@
     x_table, x_back = lay.x_tables()
     weights = out_weight.astype(F32)
     scale = math.sqrt(lay.mx * lay.my * lay.mz / (lay.width * lay.ny * lay.nz))
-    cuts = [0, lay.rows * 5 // 8, lay.rows]
+    cuts = [0, lay.rows * 3 // 4, lay.rows]
 
     def point(n, done, after):
         bias = point_bias.reshape(1, lay.channels)
@@ -957,15 +961,16 @@
         points.append(point(n, points[-1], after))
         return points[-1]
 
-    modes = sum_all(lay, own, send, scale, point_part)
+    b_field = jnp.broadcast_to(
+        out_bias[:, None, None, None], (3, lay.rows, lay.depth, lay.width)
+    ).astype(F32)
+    last = [x_back, tables[2], tables[3], b_field]
+    modes = sum_all(lay, own, send, scale, point_part, last)
     done = points[-1]
     modes_in = by_mode(lay, jnp.concatenate(modes))
     mixed = mix_modes(lay, modes_in, spectral_weight, after=[done])
     mine = by_group(lay, mixed.reshape(lay.kz, lay.ky, lay.mx, 2, lay.groups, lay.pack))
 
-    b_field = jnp.broadcast_to(
-        out_bias[:, None, None, None], (3, lay.rows, lay.depth, lay.width)
-    ).astype(F32)
     first = max(lay.groups * 5 // 16, 1)
     columns = [spread_chips(lay, mine[:first]), spread_chips(lay, mine[first:])]
     own = spread_depth(lay, columns[0], columns[1:])
@@ -991,13 +996,11 @@
         return point_parts[-1]
 
     grads = sum_all(lay, own, send, 1.0, grad_part)
-    outs = jnp.sum(sums[:, : 3 * lay.pack], axis=-1).reshape(lay.channels, 3)
+    outs = jnp.sum(sums[:, : 3 * lay.pack], axis=-1).reshape(lay.channels, 3).T
     bias = sums[:, 3 * lay.pack, :LANES].reshape(lay.groups, lay.pack, lay.mx)[..., 0]
-    ends = jnp.sum(edge[:4], axis=-1)
-    small = jnp.zeros((lay.channels + 8, LANES), F32)
-    small = small.at[: lay.channels, lay.channels : lay.channels + 3].set(outs)
-    small = small.at[lay.channels, : lay.channels].set(bias.reshape(lay.channels))
-    small = small.at[lay.channels + 1, :4].set(ends)
+    ends = jnp.pad(jnp.sum(edge[:4], axis=-1), (0, lay.channels - 4))
+    small = [outs, bias.reshape(1, lay.channels), ends.reshape(1, lay.channels)]
+    small = jnp.pad(jnp.concatenate(small), ((0, 3), (0, LANES - lay.channels)))
     flat = pack_sums(lay, point_parts, small, grads[-1:])
     rows = by_mode(lay, jnp.concatenate(grads))
     rows = jnp.concatenate([rows[:, :, : lay.mx], rows[:, :, lay.mx :]], axis=-1)
@@ -1011,14 +1014,14 @@
     flat = sum_blocks(gathered("gy", range(CORES, lay.n_gy, CORES)), False, 1.0, [grad_spectral])
     flat = flat[0]
     grad_spectral = weight_grad(lay, columns, rows, 1, [grad_spectral], [flat])
-    ends, grad_point, bias, outs = unpack_sums(lay, *gathered("gy", [1]), [grad_spectral])
+    loss, grad_point, outs, bias, ends = unpack_sums(lay, *gathered("gy", [1]), [grad_spectral])
     return (
-        ends[0, 3] / (lay.width * lay.ny * lay.nz),
+        loss.reshape(()),
         grad_spectral,
         grad_point,
         bias.reshape(lay.channels),
-        outs,
-        ends[0, :3],
+        outs.T,
+        ends.reshape(3),
     )
 
 

time: 559 us -> 544 us (0.973)
  local copies, waits for them, and re-layouts: 43.3 us -> 36.7 us
  starting transfers between devices: 77.4 us -> 71.4 us
    ppermute x47, starting transfers between devices: 68.2 us -> 61.9 us  [exchange(): return lax.ppermute(value, axis, [(i, i ^ distance) for i in range(count)])]
    unnamed x131 -> x124, local copies, waits for them, and re-layouts: 17.2 us -> 16.4 us
  transfers between devices with their start and end apart: 51 -> 51, of which waited for: 16 -> 14; matrix products, arithmetic and copies ran while one was open for 5% -> 4% of each run, Pallas kernels for 24% -> 24%
where the time goes in v5:
time: 544 us; the launch traced here: 533 us
  Pallas kernels  351 us (65%)
  starting transfers between devices  71.4 us (13%)
  waiting for transfers between devices  53.9 us (10%)
  local copies, waits for them, and re-layouts  36.7 us (7%)
  other arithmetic  17.6 us (3%)
    pallas_call x2, Pallas kernels, dense(): pl.pallas_call(functools.partial(dense_kernel, first), grid=(count,), in_...  112 us
    ppermute x47, starting transfers between devices, exchange(): return lax.ppermute(value, axis, [(i, i ^ distance) for i in range(count)])  61.9 us
    pallas_call x1, Pallas kernels, grad_modes(): pl.pallas_call(functools.partial(grad_kernel, first, len(after)), grid=(c...  49.5 us
    ppermute x47, waiting for transfers between devices, exchange(): return lax.ppermute(value, axis, [(i, i ^ distance) for i in range(count)])  45.2 us
    pallas_call x2, Pallas kernels, pointwise(): pl.pallas_call(functools.partial(pointwise_kernel, lay.tile), grid=(count...  35.1 us
    pallas_call x2, Pallas kernels, point_grad(): pl.pallas_call(functools.partial(point_kernel, lay.tile, len(after)), gri...  32 us
    pallas_call x1, Pallas kernels, forward_modes(): pl.pallas_call(functools.partial(modes_kernel, len(after)), grid=(count,)...  29 us
    pallas_call x10, Pallas kernels, sum_blocks(): pl.pallas_call(functools.partial(sum_kernel, len(values), n_out, factor),...  21.2 us
  transfers between devices with their start and end apart: 51, of which 14 were waited for; matrix products, arithmetic and copies ran while one was open for 4% of the time, Pallas kernels for 24%

profile of v5, /device:TPU:0, one launch (start us, length us, event | category | flops | bytes accessed | tf_op | source)
XLA Modules:
  0.0 532.9 jit_solution(2084155891570602696)
XLA Ops:
  0.8 2.9 compare_select_fusion.9
  7.4 29.0 %forward_modes.1 = (bf16[4,4,16,32,256]{4,3,2,1,0:T(8,128)(2,1)}, bf16[4,4,16,32,256]{4,3,2,1,0:T(8,128)(2,1)}) custom-call(bf16[64,32,32,256]{3,2,1,0:T(8,128)(2,1)} %field_ref.9, bf16[1024,256]{1,0:T(8,128)(2,1)} %pad_maximum_fusion.x_ref, bf16[128,256]{1,0:T(8,128)(2,1)} %select_convert_fusion.5.z_ref, bf16[128,256]{1,0:T(8,128)(2,1)} %select_convert_fusion.4.y_ref), custom_call_target="tpu_custom_call" | custom-call | flops 8589934592 | bytes 50331648 | tf_op jit(solution)/shard_map/forward_modes/pallas_call | solution.py:208
  37.6 1.6 select_convert_fusion.3.refs_5_.y_ref
  39.2 4.8 collective-permute-done.other_ref
  44.0 5.9 %core_sums.2 = (bf16[4,10,32,256]{3,2,1,0:T(8,128)(2,1)}, bf16[4,10,32,256]{3,2,1,0:T(8,128)(2,1)}, bf16[4,10,32,256]{3,2,1,0:T(8,128)(2,1)}, bf16[4,10,32,256]{...) custom-call(bf16[4,4,16,32,256]{4,3,2,1,0:T(8,128)(2,1)} %get-tuple-, ...), custom_call_target="tpu_custom_call" | custom-call | flops 2097152 | bytes 12582912 | tf_op jit(solution)/shard_map/core_sums/pallas_call | solution.py:282
  49.9 2.9 collective-permute-start.1
  52.8 1.5 collective-permute-start.2
  54.4 25.4 %pointwise.2.refs_4_.refs_0_ = bf16[64,32,32,256]{3,2,1,0:T(8,128)(2,1)} custom-call(bf16[64,32,32,256]{3,2,1,0:T(8,128)(2,1)} %field_ref.9, bf16[64,64]{1,0:T(8,128)(2,1)} %bitcast.155, f32[1,64]{1,0:T(1,128)} %bitcast.175, bf16[4,10,32,256]{3,2,1,0:T(8,128)(2,1)} %get-tuple-element.59.refs_0_), custom_call_target="tpu_custom_call" | custom-call | flops 12884901888 | bytes 50331648 | tf_op jit(solution)/shard_map/pointwise/pallas_call | solution.py:446
  79.7 3.8 collective-permute-done.2
  84.6 2.9 sum_blocks.10
  87.6 2.6 collective-permute-start.5
  94.9 1.6 collective-permute-start.4
  97.3 3.5 collective-permute-start.6
  100.8 9.8 %pointwise.3.refs_4_.refs_0_.point_ref = bf16[64,32,32,256]{3,2,1,0:T(8,128)(2,1)} custom-call(bf16[64,32,32,256]{3,2,1,0:T(8,128)(2,1)} %field_ref.9, bf16[64,64]{1,0:T(8,128)(2,1)} %bitcast.156, f32[1,64]{1,0:T(1,128)} %bitcast.176, bf16[64,32,32,256]{3,2,1,0:T(8,128)(2,1)} %pointwise.2.refs_4_.refs_0_, ...), custom_call_target="tpu_custom_call", output_to_operand_aliasing={{}: (3, {})} | custom-call | flops 4294967296 | bytes 16777216 | tf_op jit(solution)/shard_map/pointwise/pallas_call | solution.py:446
  111.3 1.9 sum_blocks.11
  114.2 2.3 sum_blocks.12
  117.4 3.5 collective-permute-start.12
  123.8 3.3 collective-permute-done.11
  127.1 2.1 broadcast_in_dim.26.refs_7_.b_in_ref
  129.3 2.1 sum_blocks.13
  132.9 1.6 maximum_bitcast_fusion
  136.1 15.2 %mix_modes.1 = bf16[8,4,32,128]{3,2,1,0:T(8,128)(2,1)} custom-call(bf16[8,4,64,64]{3,2,1,0:T(8,128)(2,1)} %copy.43.modes_ref, bf16[8,4,32,64,128]{4,3,2,1,0:T(8,128)(2,1)} %weight_ref.1, bf16[64,32,32,256]{3,2,1,0:T(8,128)(2,1)} %pointwise.3.refs_4_.refs_0_.point_ref), custom_call_target="tpu_custom_call" | custom-call | flops 67108864 | bytes 16777216 | tf_op jit(solution)/shard_map/mix_modes/pallas_call | solution.py:399
  154.6 1.7 collective-permute-start.20
  161.1 5.3 collective-permute-done.20
  167.1 1.8 stack_blocks.5
  170.2 2.0 collective-permute-start.23
  172.3 2.7 collective-permute-start.13
  176.2 3.8 collective-permute-done.14
  181.1 2.1 stack_blocks.4
  184.2 2.5 stack_blocks.6
  188.8 2.0 collective-permute-start.17
  192.0 37.0 %dense.2 = (bf16[64,32,32,256]{3,2,1,0:T(8,128)(2,1)}, bf16[64,32,32,256]{3,2,1,0:T(8,128)(2,1)}, f32[3,32,32,256]{3,2,1,0:T(8,128)}) custom-call(bf16[4,4,5,32,256]{4,3,2,1,0:T(8,128)(2,1)} %bitcast.108, bf16[4,4,5,32,256]{4,3,2,1,0:T(8,128)(2,1)} %copy-done.2, bf16[128,256]{1,0:T(8,128)(2,1)} %select_convert_fusion.3.refs_5_.y_ref, ...), custom_call_target="tpu_custom_call" | custom-call | flops 8053063680 | bytes 125829120 | tf_op jit(solution)/shard_map/dense/pallas_call | solution.py:554
  230.5 3.5 stack_blocks.7
  234.0 5.5 %collective-permute-done.26.other_ref = bf16[4,4,11,32,256]{4,3,2,1,0:T(8,128)(2,1)S(1)} collective-permute-done((bf16[4,4,11,32,256]{4,3,2,1,0:T(8,128)(2,1)}, bf16[4,4,11,32,256]{4,3,2,1,0:T(8,128)(2,1)S(1)}, u32[]{:S(2)}, u32[]{:S(2)}) %collective-permute-start.26) | collective-permute-done | bytes 2883616 | tf_op jit(solution)/shard_map/ppermute | solution.py:229
  239.5 1.7 copy-done.1
  241.3 74.5 %dense.3 = (bf16[64,32,32,256]{3,2,1,0:T(8,128)(2,1)}, bf16[64,32,32,256]{3,2,1,0:T(8,128)(2,1)}, f32[3,32,32,256]{3,2,1,0:T(8,128)}) custom-call(bf16[4,4,11,32,256]{4,3,2,1,0:T(8,128)(2,1)} %bitcast.99, bf16[4,4,11,32,256]{4,3,2,1,0:T(8,128)(2,1)} %copy-done.1, ...), custom_call_target="tpu_custom_call", output_to_operand_aliasing={{0}: (8, {}), {1}: (9, {})} | custom-call | flops 17716740096 | bytes 276824064 | tf_op jit(solution)/shard_map/dense/pallas_call | solution.py:554
  318.2 3.0 collective-permute-start.27
  322.9 3.9 collective-permute-start.29
  328.8 2.4 collective-permute-done.29.refs_2_
  331.2 6.3 %collective-permute-done.30.refs_3_ = f32[3,36,2,256]{3,2,1,0:T(2,128)S(1)} collective-permute-done((f32[3,36,2,256]{3,2,1,0:T(2,128)S(1)}, f32[3,36,2,256]{3,2,1,0:T(2,128)S(1)}, u32[]{:S(2)}, u32[]{:S(2)}) %collective-permute-start.30) | collective-permute-done | bytes 221216 | tf_op jit(solution)/shard_map/ppermute | solution.py:53
  338.2 15.7 %stencil.1 = (f32[3,32,32,256]{3,2,1,0:T(8,128)}, f32[8,256]{1,0:T(8,128)}) custom-call(s32[2]{0:T(128)} %pad_add_fusion.origin_ref, f32[3,32,32,256]{3,2,1,0:T(8,128)} %get-tuple-element.80.field_ref, f32[3,2,32,256]{3,2,1,0:T(8,128)} %copy-done.22, f32[3,2,32,256]{3,2,1,0:T(8,128)} %copy-done.21, f32[3,36,2,256]{3,2,1,0:T(2,128)} %copy-done.23, ...), custom_call_target="tpu_custom_call" | custom-call | tf_op jit(solution)/shard_map/stencil/pallas_call | solution.py:678
  353.9 49.5 %grad_modes.1 = (bf16[64,32,32,256]{3,2,1,0:T(8,128)(2,1)}, bf16[4,4,16,32,256]{4,3,2,1,0:T(8,128)(2,1)}, bf16[4,4,16,32,256]{4,3,2,1,0:T(8,128)(2,1)}, f32[16,16,256]{2,1,0:T(8,128)}) custom-call(f32[64,3]{1,0:T(8,128)} %convert_element_type.196.weight_ref, bf16[64,32,32,256]{3,2,1,0:T(8,128)(2,1)} %get-tuple-element.78.hidden_ref, ...), custom_call_target="tpu_custom_call" | custom-call | flops 8589934592 | bytes 167772160 | tf_op jit(solution)/shard_map/grad_modes/pallas_call | solution.py:755
  406.9 5.0 collective-permute-done.31.other_ref
  411.9 5.9 %core_sums.3 = (bf16[4,10,32,256]{3,2,1,0:T(8,128)(2,1)}, bf16[4,10,32,256]{3,2,1,0:T(8,128)(2,1)}, bf16[4,10,32,256]{3,2,1,0:T(8,128)(2,1)}, bf16[4,10,32,256]{...) custom-call(bf16[4,4,16,32,256]{4,3,2,1,0:T(8,128)(2,1)} %get-tuple-, ...), custom_call_target="tpu_custom_call" | custom-call | flops 2097152 | bytes 12582912 | tf_op jit(solution)/shard_map/core_sums/pallas_call | solution.py:282
  418.1 3.2 collective-permute-start.34
  421.3 22.1 %point_grad.2.refs_4_.refs_0_ = f32[64,64]{1,0:T(8,128)} custom-call(bf16[64,32,32,256]{3,2,1,0:T(8,128)(2,1)} %field_ref.9, bf16[64,32,32,256]{3,2,1,0:T(8,128)(2,1)} %get-tuple-element.82.grad_ref, bf16[4,10,32,256]{3,2,1,0:T(8,128)(2,1)} %get-tuple-element.85.refs_0_), custom_call_target="tpu_custom_call" | custom-call | flops 17179869184 | bytes 50331648 | tf_op jit(solution)/shard_map/point_grad/pallas_call | solution.py:839
  443.4 5.7 %collective-permute-done.33 = bf16[4,10,32,256]{3,2,1,0:T(8,128)(2,1)S(1)} collective-permute-done((bf16[4,10,32,256]{3,2,1,0:T(8,128)(2,1)}, bf16[4,10,32,256]{3,2,1,0:T(8,128)(2,1)S(1)}, u32[]{:S(2)}, u32[]{:S(2)}) %collective-permute-start.33) | collective-permute-done | bytes 655392 | tf_op jit(solution)/shard_map/ppermute | solution.py:229
  450.2 2.9 sum_blocks.14
  453.1 2.3 collective-permute-start.39
  455.8 1.7 collective-permute-start.35
  457.8 1.5 collective-permute-start.37
  460.1 3.1 collective-permute-done.39
  463.2 2.0 collective-permute-start.40
  465.3 9.9 %point_grad.3.refs_4_.refs_1_ = f32[64,64]{1,0:T(8,128)} custom-call(bf16[64,32,32,256]{3,2,1,0:T(8,128)(2,1)} %field_ref.9, bf16[64,32,32,256]{3,2,1,0:T(8,128)(2,1)} %get-tuple-element.82.grad_ref, bf16[10,32,256]{2,1,0:T(8,128)(2,1)} %bitcast.123), custom_call_target="tpu_custom_call" | custom-call | flops 17179869184 | bytes 50331648 | tf_op jit(solution)/shard_map/point_grad/pallas_call | solution.py:839
  475.9 1.9 sum_blocks.15
  478.9 2.3 sum_blocks.16
  481.2 2.4 collective-permute-start.42
  483.5 2.0 collective-permute-start.43
  488.1 3.5 collective-permute-done.42
  492.3 1.9 sum_blocks.17
  500.7 1.6 maximum_bitcast_fusion.1
  507.9 1.6 collective-permute-start.48
  510.9 8.8 %weight_grad.2.refs_4_.refs_0_ = f32[8,4,32,64,128]{4,3,2,1,0:T(8,128)} custom-call(bf16[8,4,64,64]{3,2,1,0:T(8,128)(2,1)} %bitcast.100, bf16[8,4,32,128]{3,2,1,0:T(8,128)(2,1)} %pad_maximum_fusion.2.refs_4_.grads_ref, f32[72,128]{1,0:T(8,128)} %sum_blocks.18.refs_0_), custom_call_target="tpu_custom_call" | custom-call | flops 16777216 | bytes 16777216 | tf_op jit(solution)/shard_map/weight_grad/pallas_call | solution.py:886
  521.8 8.8 %weight_grad.3.refs_0_ = f32[8,4,32,64,128]{4,3,2,1,0:T(8,128)} custom-call(bf16[8,4,64,64]{3,2,1,0:T(8,128)(2,1)} %bitcast.101, bf16[8,4,32,128]{3,2,1,0:T(8,128)(2,1)} %pad_maximum_fusion.2.refs_4_.grads_ref, f32[8,4,32,64,128]{4,3,2,1,0:T(8,128)} %weight_grad.2.refs_4_.refs_0_, f32[72,128]{1,0:T(8,128)} %sum_blocks.19.refs_1_.left_ref), custom_call_target="tpu_custom_call", output_to_operand_aliasing={{}: (2, {})} | custom-call | flops 16777216 | bytes 16777216 | tf_op jit(solution)/shard_map/weight_grad/pallas_call | solution.py:886
  (262 shorter events, 73.4 us)
Async XLA Ops:
  7.4 29.5 %copy-start.50 = (bf16[64,64]{1,0:T(8,128)(2,1)S(1)}, bf16[64,64]{1,0:T(8,128)(2,1)}, u32[]{:S(2)}) copy-start(bf16[64,64]{1,0:T(8,128)(2,1)} %param.8) | copy-start | bytes 24580
  36.4 7.6 %collective-permute-start = (bf16[4,4,16,32,256]{4,3,2,1,0:T(8,128)(2,1)}, bf16[4,4,16,32,256]{4,3,2,1,0:T(8,128)(2,1)}, u32[]{:S(2)}, u32[]{:S(2)}) collective-permute-start(bf16[4,4,16,32,256]{4,3,2,1,0:T(8,128)(2,1)} %get-tuple-element.58), channel_id=1, source_target_pairs={{0,4},{4,0},{8,12},{12,8},{16,20},{20,16},{24,28},{28,24},{1,5},{5... | collective-permute-start | bytes 12582920 | tf_op jit(solution)/shard_map/ppermute | solution.py:229
  49.9 29.8 %collective-permute-start.1 = (bf16[4,10,32,256]{3,2,1,0:T(8,128)(2,1)}, bf16[4,10,32,256]{3,2,1,0:T(8,128)(2,1)S(1)}, u32[]{:S(2)}, u32[]{:S(2)}) collective-permute-start(bf16[4,10,32,256]{3,2,1,0:T(8,128)(2,1)} %get-tuple-element.60), channel_id=1, source_target_pairs={{0,1},{1,0},{2,3},{3,2},{4,5},{5,4},{6,7},{7,6},{8,9},{9,8},{10,11... | collective-permute-start | bytes 1966088 | tf_op jit(solution)/shard_map/ppermute | solution.py:229
  52.8 30.7 %collective-permute-start.2 = (bf16[4,10,32,256]{3,2,1,0:T(8,128)(2,1)}, bf16[4,10,32,256]{3,2,1,0:T(8,128)(2,1)S(1)}, u32[]{:S(2)}, u32[]{:S(2)}) collective-permute-start(bf16[4,10,32,256]{3,2,1,0:T(8,128)(2,1)} %get-tuple-element.61), channel_id=1, source_target_pairs={{0,2},{1,3},{2,0},{3,1},{4,6},{5,7},{6,4},{7,5},{8,10},{9,11},{10,... | collective-permute-start | bytes 1966088 | tf_op jit(solution)/shard_map/ppermute | solution.py:229
  54.3 29.2 %collective-permute-start.3 = (bf16[4,10,32,256]{3,2,1,0:T(8,128)(2,1)}, bf16[4,10,32,256]{3,2,1,0:T(8,128)(2,1)S(1)}, u32[]{:S(2)}, u32[]{:S(2)}) collective-permute-start(bf16[4,10,32,256]{3,2,1,0:T(8,128)(2,1)} %get-tuple-element.62), channel_id=1, source_target_pairs={{0,3},{1,2},{2,1},{3,0},{4,7},{5,6},{6,5},{7,4},{8,11},{9,10},{10,... | collective-permute-start | bytes 1966088 | tf_op jit(solution)/shard_map/ppermute | solution.py:229
  84.6 8.9 %copy-start.54 = (bf16[4,6,32,256]{3,2,1,0:T(8,128)(2,1)S(1)}, bf16[4,6,32,256]{3,2,1,0:T(8,128)(2,1)}, u32[]{:S(2)}) copy-start(bf16[4,6,32,256]{3,2,1,0:T(8,128)(2,1)} %get-tuple-element.70) | copy-start | bytes 1179652
  87.6 9.7 %collective-permute-start.5 = (bf16[10,32,256]{2,1,0:T(8,128)(2,1)}, bf16[10,32,256]{2,1,0:T(8,128)(2,1)S(1)}, u32[]{:S(2)}, u32[]{:S(2)}) collective-permute-start(bf16[10,32,256]{2,1,0:T(8,128)(2,1)} %bitcast.180), channel_id=1, source_target_pairs={{0,16},{4,20},{8,24},{12,28},{16,0},{20,4},{24,8},{28,12},{1,17},{... | collective-permute-start | bytes 491528 | tf_op jit(solution)/shard_map/ppermute | solution.py:229
  91.4 21.8 %collective-permute-start.7 = (bf16[4,6,32,256]{3,2,1,0:T(8,128)(2,1)S(1)}, bf16[4,6,32,256]{3,2,1,0:T(8,128)(2,1)S(1)}, u32[]{:S(2)}, u32[]{:S(2)}) collective-permute-start(bf16[4,6,32,256]{3,2,1,0:T(8,128)(2,1)S(1)} %copy-done.56), channel_id=1, source_target_pairs={{0,1},{1,0},{2,3},{3,2},{4,5},{5,4},{6,7},{7,6},{8,9},{9,8},{10,11... | collective-permute-start | bytes 1179656 | tf_op jit(solution)/shard_map/ppermute | solution.py:229
  92.5 20.7 %collective-permute-start.8 = (bf16[4,6,32,256]{3,2,1,0:T(8,128)(2,1)S(1)}, bf16[4,6,32,256]{3,2,1,0:T(8,128)(2,1)S(1)}, u32[]{:S(2)}, u32[]{:S(2)}) collective-permute-start(bf16[4,6,32,256]{3,2,1,0:T(8,128)(2,1)S(1)} %copy-done.55), channel_id=1, source_target_pairs={{0,2},{1,3},{2,0},{3,1},{4,6},{5,7},{6,4},{7,5},{8,10},{9,11},{10,... | collective-permute-start | bytes 1179656 | tf_op jit(solution)/shard_map/ppermute | solution.py:229
  93.5 19.7 %collective-permute-start.9 = (bf16[4,6,32,256]{3,2,1,0:T(8,128)(2,1)S(1)}, bf16[4,6,32,256]{3,2,1,0:T(8,128)(2,1)S(1)}, u32[]{:S(2)}, u32[]{:S(2)}) collective-permute-start(bf16[4,6,32,256]{3,2,1,0:T(8,128)(2,1)S(1)} %copy-done.54), channel_id=1, source_target_pairs={{0,3},{1,2},{2,1},{3,0},{4,7},{5,6},{6,5},{7,4},{8,11},{9,10},{10,... | collective-permute-start | bytes 1179656 | tf_op jit(solution)/shard_map/ppermute | solution.py:229
  94.9 15.6 %collective-permute-start.4 = (bf16[10,32,256]{2,1,0:T(8,128)(2,1)}, bf16[10,32,256]{2,1,0:T(8,128)(2,1)S(1)}, u32[]{:S(2)}, u32[]{:S(2)}) collective-permute-start(bf16[10,32,256]{2,1,0:T(8,128)(2,1)} %bitcast.178), channel_id=1, source_target_pairs={{0,8},{4,12},{8,0},{12,4},{16,24},{20,28},{24,16},{28,20},{1,9},{5... | collective-permute-start | bytes 491528 | tf_op jit(solution)/shard_map/ppermute | solution.py:229
  97.3 13.3 %copy-start.28 = (bf16[10,32,256]{2,1,0:T(8,128)(2,1)}, bf16[10,32,256]{2,1,0:T(8,128)(2,1)S(1)}, u32[]{:S(2)}) copy-start(bf16[10,32,256]{2,1,0:T(8,128)(2,1)S(1)} %collective-permute-done.5) | copy-start | bytes 491524
  97.3 13.3 %collective-permute-start.6 = (bf16[10,32,256]{2,1,0:T(8,128)(2,1)}, bf16[10,32,256]{2,1,0:T(8,128)(2,1)S(1)}, u32[]{:S(2)}, u32[]{:S(2)}) collective-permute-start(bf16[10,32,256]{2,1,0:T(8,128)(2,1)} %bitcast.177), channel_id=1, source_target_pairs={{0,24},{4,28},{8,16},{12,20},{16,8},{20,12},{24,0},{28,4},{1,25},{... | collective-permute-start | bytes 491528 | tf_op jit(solution)/shard_map/ppermute | solution.py:229
  113.2 13.9 %copy-start.53 = (f32[3]{0:T(128)S(1)}, f32[3]{0:T(128)}, u32[]{:S(2)}) copy-start(f32[3]{0:T(128)} %param.11) | copy-start | bytes 40
  116.5 7.2 %collective-permute-start.10 = (bf16[6,32,256]{2,1,0:T(8,128)(2,1)}, bf16[6,32,256]{2,1,0:T(8,128)(2,1)S(1)}, u32[]{:S(2)}, u32[]{:S(2)}) collective-permute-start(bf16[6,32,256]{2,1,0:T(8,128)(2,1)} %bitcast.187), channel_id=1, source_target_pairs={{0,8},{4,12},{8,0},{12,4},{16,24},{20,28},{24,16},{28,20},{1,9},{5... | collective-permute-start | bytes 294920 | tf_op jit(solution)/shard_map/ppermute | solution.py:229
  116.5 10.6 %collective-permute-start.11 = (bf16[6,32,256]{2,1,0:T(8,128)(2,1)}, bf16[6,32,256]{2,1,0:T(8,128)(2,1)S(1)}, u32[]{:S(2)}, u32[]{:S(2)}) collective-permute-start(bf16[6,32,256]{2,1,0:T(8,128)(2,1)} %bitcast.185), channel_id=1, source_target_pairs={{0,16},{4,20},{8,24},{12,28},{16,0},{20,4},{24,8},{28,12},{1,17},{... | collective-permute-start | bytes 294920 | tf_op jit(solution)/shard_map/ppermute | solution.py:229
  117.4 9.7 %collective-permute-start.12 = (bf16[6,32,256]{2,1,0:T(8,128)(2,1)}, bf16[6,32,256]{2,1,0:T(8,128)(2,1)S(1)}, u32[]{:S(2)}, u32[]{:S(2)}) collective-permute-start(bf16[6,32,256]{2,1,0:T(8,128)(2,1)} %bitcast.183), channel_id=1, source_target_pairs={{0,24},{4,28},{8,16},{12,20},{16,8},{20,12},{24,0},{28,4},{1,25},{... | collective-permute-start | bytes 294920 | tf_op jit(solution)/shard_map/ppermute | solution.py:229
  135.0 16.2 %copy-start = (bf16[8,4,64,64]{2,3,1,0:T(8,128)(2,1)}, bf16[8,4,64,64]{2,3,1,0:T(8,128)(2,1)S(1)}, u32[]{:S(2)}) copy-start(bf16[8,4,64,64]{2,3,1,0:T(8,128)(2,1)S(1)} %reshape.290) | copy-start | bytes 786436
  153.2 7.9 %collective-permute-start.21 = (bf16[5,32,256]{2,1,0:T(8,128)(2,1)S(1)}, bf16[5,32,256]{2,1,0:T(8,128)(2,1)S(1)}, u32[]{:S(2)}, u32[]{:S(2)}) collective-permute-start(bf16[5,32,256]{2,1,0:T(8,128)(2,1)S(1)} %slice.57), channel_id=1, source_target_pairs={{0,24},{4,28},{8,16},{12,20},{16,8},{20,12},{24,0},{28,4},{1,25},{... | collective-permute-start | bytes 245768 | tf_op jit(solution)/shard_map/ppermute | solution.py:229
  154.6 11.8 %collective-permute-start.20 = (bf16[5,32,256]{2,1,0:T(8,128)(2,1)S(1)}, bf16[5,32,256]{2,1,0:T(8,128)(2,1)S(1)}, u32[]{:S(2)}, u32[]{:S(2)}) collective-permute-start(bf16[5,32,256]{2,1,0:T(8,128)(2,1)S(1)} %slice.57), channel_id=1, source_target_pairs={{0,16},{4,20},{8,24},{12,28},{16,0},{20,4},{24,8},{28,12},{1,17},{... | collective-permute-start | bytes 245768 | tf_op jit(solution)/shard_map/ppermute | solution.py:229
  156.3 10.1 %collective-permute-start.19 = (bf16[5,32,256]{2,1,0:T(8,128)(2,1)S(1)}, bf16[5,32,256]{2,1,0:T(8,128)(2,1)S(1)}, u32[]{:S(2)}, u32[]{:S(2)}) collective-permute-start(bf16[5,32,256]{2,1,0:T(8,128)(2,1)S(1)} %slice.57), channel_id=1, source_target_pairs={{0,8},{4,12},{8,0},{12,4},{16,24},{20,28},{24,16},{28,20},{1,9},{5... | collective-permute-start | bytes 245768 | tf_op jit(solution)/shard_map/ppermute | solution.py:229
  158.3 28.5 %copy-start.52 = (bf16[64,3]{0,1:T(4,128)(2,1)S(1)}, bf16[64,3]{0,1:T(4,128)(2,1)}, u32[]{:S(2)}) copy-start(bf16[64,3]{0,1:T(4,128)(2,1)} %param.10) | copy-start | bytes 1156
  158.8 13.6 %collective-permute-start.15 = (bf16[11,32,256]{2,1,0:T(8,128)(2,1)S(1)}, bf16[11,32,256]{2,1,0:T(8,128)(2,1)S(1)}, u32[]{:S(2)}, u32[]{:S(2)}) collective-permute-start(bf16[11,32,256]{2,1,0:T(8,128)(2,1)S(1)} %slice.55), channel_id=1, source_target_pairs={{0,24},{4,28},{8,16},{12,20},{16,8},{20,12},{24,0},{28,4},{1,25},{... | collective-permute-start | bytes 540680 | tf_op jit(solution)/shard_map/ppermute | solution.py:229
  168.8 14.4 %collective-permute-start.24 = (bf16[4,5,32,256]{3,2,1,0:T(8,128)(2,1)}, bf16[4,5,32,256]{3,2,1,0:T(8,128)(2,1)S(1)}, u32[]{:S(2)}, u32[]{:S(2)}) collective-permute-start(bf16[4,5,32,256]{3,2,1,0:T(8,128)(2,1)} %bitcast.115), channel_id=1, source_target_pairs={{0,3},{1,2},{2,1},{3,0},{4,7},{5,6},{6,5},{7,4},{8,11},{9,10},{10,... | collective-permute-start | bytes 983048 | tf_op jit(solution)/shard_map/ppermute | solution.py:229
  170.2 13.1 %collective-permute-start.23 = (bf16[4,5,32,256]{3,2,1,0:T(8,128)(2,1)}, bf16[4,5,32,256]{3,2,1,0:T(8,128)(2,1)S(1)}, u32[]{:S(2)}, u32[]{:S(2)}) collective-permute-start(bf16[4,5,32,256]{3,2,1,0:T(8,128)(2,1)} %bitcast.116), channel_id=1, source_target_pairs={{0,2},{1,3},{2,0},{3,1},{4,6},{5,7},{6,4},{7,5},{8,10},{9,11},{10,... | collective-permute-start | bytes 983048 | tf_op jit(solution)/shard_map/ppermute | solution.py:229
  172.2 11.1 %collective-permute-start.22 = (bf16[4,5,32,256]{3,2,1,0:T(8,128)(2,1)}, bf16[4,5,32,256]{3,2,1,0:T(8,128)(2,1)S(1)}, u32[]{:S(2)}, u32[]{:S(2)}) collective-permute-start(bf16[4,5,32,256]{3,2,1,0:T(8,128)(2,1)} %bitcast.117), channel_id=1, source_target_pairs={{0,1},{1,0},{2,3},{3,2},{4,5},{5,4},{6,7},{7,6},{8,9},{9,8},{10,11... | collective-permute-start | bytes 983048 | tf_op jit(solution)/shard_map/ppermute | solution.py:229
  172.3 7.7 %collective-permute-start.14 = (bf16[11,32,256]{2,1,0:T(8,128)(2,1)S(1)}, bf16[11,32,256]{2,1,0:T(8,128)(2,1)S(1)}, u32[]{:S(2)}, u32[]{:S(2)}) collective-permute-start(bf16[11,32,256]{2,1,0:T(8,128)(2,1)S(1)} %slice.55), channel_id=1, source_target_pairs={{0,16},{4,20},{8,24},{12,28},{16,0},{20,4},{24,8},{28,12},{1,17},{... | collective-permute-start | bytes 540680 | tf_op jit(solution)/shard_map/ppermute | solution.py:229
  172.3 8.1 %collective-permute-start.13 = (bf16[11,32,256]{2,1,0:T(8,128)(2,1)S(1)}, bf16[11,32,256]{2,1,0:T(8,128)(2,1)S(1)}, u32[]{:S(2)}, u32[]{:S(2)}) collective-permute-start(bf16[11,32,256]{2,1,0:T(8,128)(2,1)S(1)} %slice.55), channel_id=1, source_target_pairs={{0,8},{4,12},{8,0},{12,4},{16,24},{20,28},{24,16},{28,20},{1,9},{5... | collective-permute-start | bytes 540680 | tf_op jit(solution)/shard_map/ppermute | solution.py:229
  186.7 4.2 collective-permute-start.25
  187.5 41.6 %collective-permute-start.18 = (bf16[4,11,32,256]{3,2,1,0:T(8,128)(2,1)}, bf16[4,11,32,256]{3,2,1,0:T(8,128)(2,1)S(1)}, u32[]{:S(2)}, u32[]{:S(2)}) collective-permute-start(bf16[4,11,32,256]{3,2,1,0:T(8,128)(2,1)} %bitcast.103), channel_id=1, source_target_pairs={{0,3},{1,2},{2,1},{3,0},{4,7},{5,6},{6,5},{7,4},{8,11},{9,10},{10,... | collective-permute-start | bytes 2162696 | tf_op jit(solution)/shard_map/ppermute | solution.py:229
  188.8 40.3 %collective-permute-start.17 = (bf16[4,11,32,256]{3,2,1,0:T(8,128)(2,1)}, bf16[4,11,32,256]{3,2,1,0:T(8,128)(2,1)S(1)}, u32[]{:S(2)}, u32[]{:S(2)}) collective-permute-start(bf16[4,11,32,256]{3,2,1,0:T(8,128)(2,1)} %bitcast.104), channel_id=1, source_target_pairs={{0,2},{1,3},{2,0},{3,1},{4,6},{5,7},{6,4},{7,5},{8,10},{9,11},{10,... | collective-permute-start | bytes 2162696 | tf_op jit(solution)/shard_map/ppermute | solution.py:229
  190.8 38.3 %collective-permute-start.16 = (bf16[4,11,32,256]{3,2,1,0:T(8,128)(2,1)}, bf16[4,11,32,256]{3,2,1,0:T(8,128)(2,1)S(1)}, u32[]{:S(2)}, u32[]{:S(2)}) collective-permute-start(bf16[4,11,32,256]{3,2,1,0:T(8,128)(2,1)} %bitcast.105), channel_id=1, source_target_pairs={{0,1},{1,0},{2,3},{3,2},{4,5},{5,4},{6,7},{7,6},{8,9},{9,8},{10,11... | collective-permute-start | bytes 2162696 | tf_op jit(solution)/shard_map/ppermute | solution.py:229
  234.0 5.5 %collective-permute-start.26 = (bf16[4,4,11,32,256]{4,3,2,1,0:T(8,128)(2,1)}, bf16[4,4,11,32,256]{4,3,2,1,0:T(8,128)(2,1)S(1)}, u32[]{:S(2)}, u32[]{:S(2)}) collective-permute-start(bf16[4,4,11,32,256]{4,3,2,1,0:T(8,128)(2,1)} %bitcast.98), channel_id=1, source_target_pairs={{0,4},{4,0},{8,12},{12,8},{16,20},{20,16},{24,28},{28,24},{1,5},{5... | collective-permute-start | bytes 8650760 | tf_op jit(solution)/shard_map/ppermute | solution.py:229
  316.9 5.9 %collective-permute-start.28 = (f32[3,2,32,256]{3,2,1,0:T(8,128)S(1)}, f32[3,2,32,256]{3,2,1,0:T(8,128)S(1)}, u32[]{:S(2)}, u32[]{:S(2)}) collective-permute-start(f32[3,2,32,256]{3,2,1,0:T(8,128)S(1)} %get-tuple-element.110), channel_id=1, source_target_pairs={{4,0},{8,4},{12,8},{16,12},{20,16},{24,20},{28,24},{5,1},{9,5},{13... | collective-permute-start | bytes 589832 | tf_op jit(solution)/shard_map/ppermute | solution.py:53
  318.2 4.6 collective-permute-start.27
  322.7 14.8 %copy-start.21 = (f32[3,2,32,256]{3,2,1,0:T(8,128)}, f32[3,2,32,256]{3,2,1,0:T(8,128)S(1)}, u32[]{:S(2)}) copy-start(f32[3,2,32,256]{3,2,1,0:T(8,128)S(1)} %collective-permute-done.28.refs_1_) | copy-start | bytes 589828
  322.8 14.8 %copy-start.22 = (f32[3,2,32,256]{3,2,1,0:T(8,128)}, f32[3,2,32,256]{3,2,1,0:T(8,128)S(1)}, u32[]{:S(2)}) copy-start(f32[3,2,32,256]{3,2,1,0:T(8,128)S(1)} %collective-permute-done.27.refs_0_) | copy-start | bytes 589828
  322.9 8.3 %collective-permute-start.29 = (f32[3,36,2,256]{3,2,1,0:T(2,128)S(1)}, f32[3,36,2,256]{3,2,1,0:T(2,128)S(1)}, u32[]{:S(2)}, u32[]{:S(2)}) collective-permute-start(f32[3,36,2,256]{3,2,1,0:T(2,128)S(1)} %pad_maximum_fusion.3), channel_id=1, source_target_pairs={{0,1},{1,2},{2,3},{4,5},{5,6},{6,7},{8,9},{9,10},{10,11},{12,13},{... | collective-permute-start | bytes 663560 | tf_op jit(solution)/shard_map/ppermute | solution.py:53
  326.9 10.6 %collective-permute-start.30 = (f32[3,36,2,256]{3,2,1,0:T(2,128)S(1)}, f32[3,36,2,256]{3,2,1,0:T(2,128)S(1)}, u32[]{:S(2)}, u32[]{:S(2)}) collective-permute-start(f32[3,36,2,256]{3,2,1,0:T(2,128)S(1)} %pad_maximum_fusion.4), channel_id=1, source_target_pairs={{1,0},{2,1},{3,2},{5,4},{6,5},{7,6},{9,8},{10,9},{11,10},{13,12},{... | collective-permute-start | bytes 663560 | tf_op jit(solution)/shard_map/ppermute | solution.py:53
  403.4 8.5 %collective-permute-start.31 = (bf16[4,4,16,32,256]{4,3,2,1,0:T(8,128)(2,1)}, bf16[4,4,16,32,256]{4,3,2,1,0:T(8,128)(2,1)}, u32[]{:S(2)}, u32[]{:S(2)}) collective-permute-start(bf16[4,4,16,32,256]{4,3,2,1,0:T(8,128)(2,1)} %get-tuple-element.84), channel_id=1, source_target_pairs={{0,4},{4,0},{8,12},{12,8},{16,20},{20,16},{24,28},{28,24},{1,5},{5... | collective-permute-start | bytes 12582920 | tf_op jit(solution)/shard_map/ppermute | solution.py:229
  417.8 25.7 %collective-permute-start.32 = (bf16[4,10,32,256]{3,2,1,0:T(8,128)(2,1)}, bf16[4,10,32,256]{3,2,1,0:T(8,128)(2,1)S(1)}, u32[]{:S(2)}, u32[]{:S(2)}) collective-permute-start(bf16[4,10,32,256]{3,2,1,0:T(8,128)(2,1)} %get-tuple-element.86), channel_id=1, source_target_pairs={{0,1},{1,0},{2,3},{3,2},{4,5},{5,4},{6,7},{7,6},{8,9},{9,8},{10,11... | collective-permute-start | bytes 1966088 | tf_op jit(solution)/shard_map/ppermute | solution.py:229
  418.1 31.1 %collective-permute-start.33 = (bf16[4,10,32,256]{3,2,1,0:T(8,128)(2,1)}, bf16[4,10,32,256]{3,2,1,0:T(8,128)(2,1)S(1)}, u32[]{:S(2)}, u32[]{:S(2)}) collective-permute-start(bf16[4,10,32,256]{3,2,1,0:T(8,128)(2,1)} %get-tuple-element.87), channel_id=1, source_target_pairs={{0,2},{1,3},{2,0},{3,1},{4,6},{5,7},{6,4},{7,5},{8,10},{9,11},{10,... | collective-permute-start | bytes 1966088 | tf_op jit(solution)/shard_map/ppermute | solution.py:229
  418.1 31.1 %collective-permute-start.34 = (bf16[4,10,32,256]{3,2,1,0:T(8,128)(2,1)}, bf16[4,10,32,256]{3,2,1,0:T(8,128)(2,1)S(1)}, u32[]{:S(2)}, u32[]{:S(2)}) collective-permute-start(bf16[4,10,32,256]{3,2,1,0:T(8,128)(2,1)} %get-tuple-element.88), channel_id=1, source_target_pairs={{0,3},{1,2},{2,1},{3,0},{4,7},{5,6},{6,5},{7,4},{8,11},{9,10},{10,... | collective-permute-start | bytes 1966088 | tf_op jit(solution)/shard_map/ppermute | solution.py:229
  421.3 34.1 %copy-start.51 = (f32[8,256]{1,0:T(8,128)S(1)}, f32[8,256]{1,0:T(8,128)}, u32[]{:S(2)}) copy-start(f32[8,256]{1,0:T(8,128)} %get-tuple-element.91) | copy-start | bytes 24580
  421.3 34.5 %copy-start.59 = (bf16[4,6,32,256]{3,2,1,0:T(8,128)(2,1)S(1)}, bf16[4,6,32,256]{3,2,1,0:T(8,128)(2,1)}, u32[]{:S(2)}) copy-start(bf16[4,6,32,256]{3,2,1,0:T(8,128)(2,1)} %get-tuple-element.93) | copy-start | bytes 1179652
  421.3 36.2 %copy-start.58 = (bf16[4,6,32,256]{3,2,1,0:T(8,128)(2,1)S(1)}, bf16[4,6,32,256]{3,2,1,0:T(8,128)(2,1)}, u32[]{:S(2)}) copy-start(bf16[4,6,32,256]{3,2,1,0:T(8,128)(2,1)} %get-tuple-element.94) | copy-start | bytes 1179652
  421.3 36.5 %copy-start.57 = (bf16[4,6,32,256]{3,2,1,0:T(8,128)(2,1)S(1)}, bf16[4,6,32,256]{3,2,1,0:T(8,128)(2,1)}, u32[]{:S(2)}) copy-start(bf16[4,6,32,256]{3,2,1,0:T(8,128)(2,1)} %get-tuple-element.95) | copy-start | bytes 1179652
  453.1 10.2 %collective-permute-start.39 = (bf16[10,32,256]{2,1,0:T(8,128)(2,1)}, bf16[10,32,256]{2,1,0:T(8,128)(2,1)S(1)}, u32[]{:S(2)}, u32[]{:S(2)}) collective-permute-start(bf16[10,32,256]{2,1,0:T(8,128)(2,1)} %bitcast.182), channel_id=1, source_target_pairs={{0,16},{4,20},{8,24},{12,28},{16,0},{20,4},{24,8},{28,12},{1,17},{... | collective-permute-start | bytes 491528 | tf_op jit(solution)/shard_map/ppermute | solution.py:229
  455.8 22.1 %collective-permute-start.35 = (bf16[4,6,32,256]{3,2,1,0:T(8,128)(2,1)S(1)}, bf16[4,6,32,256]{3,2,1,0:T(8,128)(2,1)S(1)}, u32[]{:S(2)}, u32[]{:S(2)}) collective-permute-start(bf16[4,6,32,256]{3,2,1,0:T(8,128)(2,1)S(1)} %copy-done.59), channel_id=1, source_target_pairs={{0,1},{1,0},{2,3},{3,2},{4,5},{5,4},{6,7},{7,6},{8,9},{9,8},{10,11... | collective-permute-start | bytes 1179656 | tf_op jit(solution)/shard_map/ppermute | solution.py:229
  457.5 20.3 %collective-permute-start.36 = (bf16[4,6,32,256]{3,2,1,0:T(8,128)(2,1)S(1)}, bf16[4,6,32,256]{3,2,1,0:T(8,128)(2,1)S(1)}, u32[]{:S(2)}, u32[]{:S(2)}) collective-permute-start(bf16[4,6,32,256]{3,2,1,0:T(8,128)(2,1)S(1)} %copy-done.58), channel_id=1, source_target_pairs={{0,2},{1,3},{2,0},{3,1},{4,6},{5,7},{6,4},{7,5},{8,10},{9,11},{10,... | collective-permute-start | bytes 1179656 | tf_op jit(solution)/shard_map/ppermute | solution.py:229
  457.8 20.1 %collective-permute-start.37 = (bf16[4,6,32,256]{3,2,1,0:T(8,128)(2,1)S(1)}, bf16[4,6,32,256]{3,2,1,0:T(8,128)(2,1)S(1)}, u32[]{:S(2)}, u32[]{:S(2)}) collective-permute-start(bf16[4,6,32,256]{3,2,1,0:T(8,128)(2,1)S(1)} %copy-done.57), channel_id=1, source_target_pairs={{0,3},{1,2},{2,1},{3,0},{4,7},{5,6},{6,5},{7,4},{8,11},{9,10},{10,... | collective-permute-start | bytes 1179656 | tf_op jit(solution)/shard_map/ppermute | solution.py:229
  459.3 15.9 %collective-permute-start.38 = (bf16[10,32,256]{2,1,0:T(8,128)(2,1)}, bf16[10,32,256]{2,1,0:T(8,128)(2,1)S(1)}, u32[]{:S(2)}, u32[]{:S(2)}) collective-permute-start(bf16[10,32,256]{2,1,0:T(8,128)(2,1)} %bitcast.181), channel_id=1, source_target_pairs={{0,8},{4,12},{8,0},{12,4},{16,24},{20,28},{24,16},{28,20},{1,9},{5... | collective-permute-start | bytes 491528 | tf_op jit(solution)/shard_map/ppermute | solution.py:229
  463.2 12.0 %copy-start.31 = (bf16[10,32,256]{2,1,0:T(8,128)(2,1)}, bf16[10,32,256]{2,1,0:T(8,128)(2,1)S(1)}, u32[]{:S(2)}) copy-start(bf16[10,32,256]{2,1,0:T(8,128)(2,1)S(1)} %collective-permute-done.39) | copy-start | bytes 491524
  463.2 12.0 %collective-permute-start.40 = (bf16[10,32,256]{2,1,0:T(8,128)(2,1)}, bf16[10,32,256]{2,1,0:T(8,128)(2,1)S(1)}, u32[]{:S(2)}, u32[]{:S(2)}) collective-permute-start(bf16[10,32,256]{2,1,0:T(8,128)(2,1)} %bitcast.179), channel_id=1, source_target_pairs={{0,24},{4,28},{8,16},{12,20},{16,8},{20,12},{24,0},{28,4},{1,25},{... | collective-permute-start | bytes 491528 | tf_op jit(solution)/shard_map/ppermute | solution.py:229
  481.2 7.0 %collective-permute-start.41 = (bf16[6,32,256]{2,1,0:T(8,128)(2,1)}, bf16[6,32,256]{2,1,0:T(8,128)(2,1)S(1)}, u32[]{:S(2)}, u32[]{:S(2)}) collective-permute-start(bf16[6,32,256]{2,1,0:T(8,128)(2,1)} %bitcast.188), channel_id=1, source_target_pairs={{0,8},{4,12},{8,0},{12,4},{16,24},{20,28},{24,16},{28,20},{1,9},{5... | collective-permute-start | bytes 294920 | tf_op jit(solution)/shard_map/ppermute | solution.py:229
  481.2 10.4 %collective-permute-start.42 = (bf16[6,32,256]{2,1,0:T(8,128)(2,1)}, bf16[6,32,256]{2,1,0:T(8,128)(2,1)S(1)}, u32[]{:S(2)}, u32[]{:S(2)}) collective-permute-start(bf16[6,32,256]{2,1,0:T(8,128)(2,1)} %bitcast.186), channel_id=1, source_target_pairs={{0,16},{4,20},{8,24},{12,28},{16,0},{20,4},{24,8},{28,12},{1,17},{... | collective-permute-start | bytes 294920 | tf_op jit(solution)/shard_map/ppermute | solution.py:229
  483.5 8.1 %collective-permute-start.43 = (bf16[6,32,256]{2,1,0:T(8,128)(2,1)}, bf16[6,32,256]{2,1,0:T(8,128)(2,1)S(1)}, u32[]{:S(2)}, u32[]{:S(2)}) collective-permute-start(bf16[6,32,256]{2,1,0:T(8,128)(2,1)} %bitcast.184), channel_id=1, source_target_pairs={{0,24},{4,28},{8,16},{12,20},{16,8},{20,12},{24,0},{28,4},{1,25},{... | collective-permute-start | bytes 294920 | tf_op jit(solution)/shard_map/ppermute | solution.py:229
  495.6 8.7 %collective-permute-start.46 = (f32[72,128]{1,0:T(8,128)}, f32[72,128]{1,0:T(8,128)S(1)}, u32[]{:S(2)}, u32[]{:S(2)}) collective-permute-start(f32[72,128]{1,0:T(8,128)} %pack_sums.1), channel_id=1, source_target_pairs={{0,3},{1,2},{2,1},{3,0},{4,7},{5,6},{6,5},{7,4},{8,11},{9,10},{10,... | collective-permute-start | bytes 110600 | tf_op jit(solution)/shard_map/ppermute | solution.py:229
  496.7 7.7 %collective-permute-start.45 = (f32[72,128]{1,0:T(8,128)}, f32[72,128]{1,0:T(8,128)S(1)}, u32[]{:S(2)}, u32[]{:S(2)}) collective-permute-start(f32[72,128]{1,0:T(8,128)} %pack_sums.1), channel_id=1, source_target_pairs={{0,2},{1,3},{2,0},{3,1},{4,6},{5,7},{6,4},{7,5},{8,10},{9,11},{10,... | collective-permute-start | bytes 110600 | tf_op jit(solution)/shard_map/ppermute | solution.py:229
  497.8 6.6 %collective-permute-start.44 = (f32[72,128]{1,0:T(8,128)}, f32[72,128]{1,0:T(8,128)S(1)}, u32[]{:S(2)}, u32[]{:S(2)}) collective-permute-start(f32[72,128]{1,0:T(8,128)} %pack_sums.1), channel_id=1, source_target_pairs={{0,1},{1,0},{2,3},{3,2},{4,5},{5,4},{6,7},{7,6},{8,9},{9,8},{10,11... | collective-permute-start | bytes 110600 | tf_op jit(solution)/shard_map/ppermute | solution.py:229
  506.5 13.2 %collective-permute-start.49 = (f32[72,128]{1,0:T(8,128)}, f32[72,128]{1,0:T(8,128)S(1)}, u32[]{:S(2)}, u32[]{:S(2)}) collective-permute-start(f32[72,128]{1,0:T(8,128)} %sum_blocks.18.refs_0_), channel_id=1, source_target_pairs={{0,24},{4,28},{8,16},{12,20},{16,8},{20,12},{24,0},{28,4},{1,25},{... | collective-permute-start | bytes 110600 | tf_op jit(solution)/shard_map/ppermute | solution.py:229
  507.9 11.8 %collective-permute-start.48 = (f32[72,128]{1,0:T(8,128)}, f32[72,128]{1,0:T(8,128)S(1)}, u32[]{:S(2)}, u32[]{:S(2)}) collective-permute-start(f32[72,128]{1,0:T(8,128)} %sum_blocks.18.refs_0_), channel_id=1, source_target_pairs={{0,16},{4,20},{8,24},{12,28},{16,0},{20,4},{24,8},{28,12},{1,17},{... | collective-permute-start | bytes 110600 | tf_op jit(solution)/shard_map/ppermute | solution.py:229
  509.5 10.2 %collective-permute-start.47 = (f32[72,128]{1,0:T(8,128)}, f32[72,128]{1,0:T(8,128)S(1)}, u32[]{:S(2)}, u32[]{:S(2)}) collective-permute-start(f32[72,128]{1,0:T(8,128)} %sum_blocks.18.refs_0_), channel_id=1, source_target_pairs={{0,8},{4,12},{8,0},{12,4},{16,24},{20,28},{24,16},{28,20},{1,9},{5... | collective-permute-start | bytes 110600 | tf_op jit(solution)/shard_map/ppermute | solution.py:229
  521.8 8.8 %collective-permute-start.50 = (f32[72,128]{1,0:T(8,128)}, f32[72,128]{1,0:T(8,128)S(1)}, u32[]{:S(2)}, u32[]{:S(2)}) collective-permute-start(f32[72,128]{1,0:T(8,128)} %sum_blocks.19.refs_1_.left_ref), channel_id=1, source_target_pairs={{0,4},{4,0},{8,12},{12,8},{16,20},{20,16},{24,28},{28,24},{1,5},{5... | collective-permute-start | bytes 110600 | tf_op jit(solution)/shard_map/ppermute | solution.py:229
  (47 other events, 86.6 us)

commit v6 on v5

--- a/solution.py
+++ b/solution.py
@@ -971,7 +971,7 @@
     mixed = mix_modes(lay, modes_in, spectral_weight, after=[done])
     mine = by_group(lay, mixed.reshape(lay.kz, lay.ky, lay.mx, 2, lay.groups, lay.pack))
 
-    first = max(lay.groups * 5 // 16, 1)
+    first = max(lay.groups // 4, 1)
     columns = [spread_chips(lay, mine[:first]), spread_chips(lay, mine[first:])]
     own = spread_depth(lay, columns[0], columns[1:])
     *kept, b_field = dense(

time: 544 us -> 551 us (1.013)
  transfers between devices with their start and end apart: 51 -> 51, of which waited for: 14 -> 16; matrix products, arithmetic and copies ran while one was open for 4% -> 4% of each run, Pallas kernels for 24% -> 23%
where the time goes in v6:
time: 551 us; the launch traced here: 540 us
  Pallas kernels  352 us (64%)
  starting transfers between devices  74.1 us (13%)
  waiting for transfers between devices  58.7 us (11%)
  local copies, waits for them, and re-layouts  36.4 us (7%)
  other arithmetic  17.6 us (3%)
    pallas_call x2, Pallas kernels, dense(): pl.pallas_call(functools.partial(dense_kernel, first), grid=(count,), in_...  112 us
    ppermute x47, starting transfers between devices, exchange(): return lax.ppermute(value, axis, [(i, i ^ distance) for i in range(count)])  64.9 us
    ppermute x47, waiting for transfers between devices, exchange(): return lax.ppermute(value, axis, [(i, i ^ distance) for i in range(count)])  50 us
    pallas_call x1, Pallas kernels, grad_modes(): pl.pallas_call(functools.partial(grad_kernel, first, len(after)), grid=(c...  49.5 us
    pallas_call x2, Pallas kernels, pointwise(): pl.pallas_call(functools.partial(pointwise_kernel, lay.tile), grid=(count...  35.1 us
    pallas_call x2, Pallas kernels, point_grad(): pl.pallas_call(functools.partial(point_kernel, lay.tile, len(after)), gri...  32 us
    pallas_call x1, Pallas kernels, forward_modes(): pl.pallas_call(functools.partial(modes_kernel, len(after)), grid=(count,)...  29 us
    pallas_call x10, Pallas kernels, sum_blocks(): pl.pallas_call(functools.partial(sum_kernel, len(values), n_out, factor),...  21.2 us
  transfers between devices with their start and end apart: 51, of which 16 were waited for; matrix products, arithmetic and copies ran while one was open for 4% of the time, Pallas kernels for 23%

profile of v6, /device:TPU:0, one launch (start us, length us, event | category | flops | bytes accessed | tf_op | source)
XLA Modules:
  0.0 540.0 jit_solution(14139248290386174056)
XLA Ops:
  0.8 2.9 compare_select_fusion.9
  7.4 29.0 %forward_modes.1 = (bf16[4,4,16,32,256]{4,3,2,1,0:T(8,128)(2,1)}, bf16[4,4,16,32,256]{4,3,2,1,0:T(8,128)(2,1)}) custom-call(bf16[64,32,32,256]{3,2,1,0:T(8,128)(2,1)} %field_ref.9, bf16[1024,256]{1,0:T(8,128)(2,1)} %pad_maximum_fusion.x_ref, bf16[128,256]{1,0:T(8,128)(2,1)} %select_convert_fusion.5.z_ref, bf16[128,256]{1,0:T(8,128)(2,1)} %select_convert_fusion.4.y_ref), custom_call_target="tpu_custom_call" | custom-call | flops 8589934592 | bytes 50331648 | tf_op jit(solution)/shard_map/forward_modes/pallas_call | solution.py:208
  39.1 4.8 collective-permute-done.other_ref
  43.9 5.9 %core_sums.2 = (bf16[4,10,32,256]{3,2,1,0:T(8,128)(2,1)}, bf16[4,10,32,256]{3,2,1,0:T(8,128)(2,1)}, bf16[4,10,32,256]{3,2,1,0:T(8,128)(2,1)}, bf16[4,10,32,256]{...) custom-call(bf16[4,4,16,32,256]{4,3,2,1,0:T(8,128)(2,1)} %get-tuple-, ...), custom_call_target="tpu_custom_call" | custom-call | flops 2097152 | bytes 12582912 | tf_op jit(solution)/shard_map/core_sums/pallas_call | solution.py:282
  49.9 2.9 collective-permute-start.1
  54.3 25.4 %pointwise.2.refs_4_.refs_0_ = bf16[64,32,32,256]{3,2,1,0:T(8,128)(2,1)} custom-call(bf16[64,32,32,256]{3,2,1,0:T(8,128)(2,1)} %field_ref.9, bf16[64,64]{1,0:T(8,128)(2,1)} %bitcast.155, f32[1,64]{1,0:T(1,128)} %bitcast.175, bf16[4,10,32,256]{3,2,1,0:T(8,128)(2,1)} %get-tuple-element.59.refs_0_), custom_call_target="tpu_custom_call" | custom-call | flops 12884901888 | bytes 50331648 | tf_op jit(solution)/shard_map/pointwise/pallas_call | solution.py:446
  79.7 3.8 collective-permute-done.2
  84.6 2.9 sum_blocks.10
  87.5 2.6 collective-permute-start.5
  97.2 3.5 collective-permute-start.6
  100.7 9.8 %pointwise.3.refs_4_.refs_0_.point_ref = bf16[64,32,32,256]{3,2,1,0:T(8,128)(2,1)} custom-call(bf16[64,32,32,256]{3,2,1,0:T(8,128)(2,1)} %field_ref.9, bf16[64,64]{1,0:T(8,128)(2,1)} %bitcast.156, f32[1,64]{1,0:T(1,128)} %bitcast.176, bf16[64,32,32,256]{3,2,1,0:T(8,128)(2,1)} %pointwise.2.refs_4_.refs_0_, ...), custom_call_target="tpu_custom_call", output_to_operand_aliasing={{}: (3, {})} | custom-call | flops 4294967296 | bytes 16777216 | tf_op jit(solution)/shard_map/pointwise/pallas_call | solution.py:446
  111.2 1.9 sum_blocks.11
  114.2 2.3 sum_blocks.12
  117.4 3.5 collective-permute-start.12
  123.7 3.3 collective-permute-done.11
  127.1 2.1 broadcast_in_dim.26.refs_7_.b_in_ref
  129.2 2.1 sum_blocks.13
  132.9 1.6 maximum_bitcast_fusion
  136.0 15.2 %mix_modes.1 = bf16[8,4,32,128]{3,2,1,0:T(8,128)(2,1)} custom-call(bf16[8,4,64,64]{3,2,1,0:T(8,128)(2,1)} %copy.43.modes_ref, bf16[8,4,32,64,128]{4,3,2,1,0:T(8,128)(2,1)} %weight_ref.1, bf16[64,32,32,256]{3,2,1,0:T(8,128)(2,1)} %pointwise.3.refs_4_.refs_0_.point_ref), custom_call_target="tpu_custom_call" | custom-call | flops 67108864 | bytes 16777216 | tf_op jit(solution)/shard_map/mix_modes/pallas_call | solution.py:399
  155.8 2.5 collective-permute-start.21
  158.3 1.9 collective-permute-start.19
  161.0 2.3 collective-permute-done.21
  163.3 5.1 collective-permute-done.20
  169.1 1.6 stack_blocks.5
  172.0 2.2 collective-permute-start.23
  174.9 2.8 collective-permute-start.13
  178.8 5.5 %collective-permute-done.14 = bf16[12,32,256]{2,1,0:T(8,128)(2,1)S(1)} collective-permute-done((bf16[12,32,256]{2,1,0:T(8,128)(2,1)S(1)}, bf16[12,32,256]{2,1,0:T(8,128)(2,1)S(1)}, u32[]{:S(2)}, u32[]{:S(2)}) %collective-permute-start.14) | collective-permute-done | bytes 196640 | tf_op jit(solution)/shard_map/ppermute | solution.py:229
  185.1 2.2 stack_blocks.4
  188.1 2.3 stack_blocks.6
  191.9 1.7 collective-permute-start.17
  195.7 30.9 %dense.2 = (bf16[64,32,32,256]{3,2,1,0:T(8,128)(2,1)}, bf16[64,32,32,256]{3,2,1,0:T(8,128)(2,1)}, f32[3,32,32,256]{3,2,1,0:T(8,128)}) custom-call(bf16[4,4,4,32,256]{4,3,2,1,0:T(8,128)(2,1)} %bitcast.110, bf16[4,4,4,32,256]{4,3,2,1,0:T(8,128)(2,1)} %copy-done.2, bf16[128,256]{1,0:T(8,128)(2,1)} %select_convert_fusion.3.refs_5_.y_ref, ...), custom_call_target="tpu_custom_call" | custom-call | flops 6442450944 | bytes 100663296 | tf_op jit(solution)/shard_map/dense/pallas_call | solution.py:554
  226.6 1.8 collective-permute-done.17
  229.5 3.7 stack_blocks.7
  233.2 5.8 %collective-permute-done.26.other_ref = bf16[4,4,12,32,256]{4,3,2,1,0:T(8,128)(2,1)S(1)} collective-permute-done((bf16[4,4,12,32,256]{4,3,2,1,0:T(8,128)(2,1)}, bf16[4,4,12,32,256]{4,3,2,1,0:T(8,128)(2,1)S(1)}, u32[]{:S(2)}, u32[]{:S(2)}) %collective-permute-start.26) | collective-permute-done | bytes 3145760 | tf_op jit(solution)/shard_map/ppermute | solution.py:229
  239.1 1.8 copy-done.1
  240.8 80.8 %dense.3 = (bf16[64,32,32,256]{3,2,1,0:T(8,128)(2,1)}, bf16[64,32,32,256]{3,2,1,0:T(8,128)(2,1)}, f32[3,32,32,256]{3,2,1,0:T(8,128)}) custom-call(bf16[4,4,12,32,256]{4,3,2,1,0:T(8,128)(2,1)} %bitcast.99, bf16[4,4,12,32,256]{4,3,2,1,0:T(8,128)(2,1)} %copy-done.1, ...), custom_call_target="tpu_custom_call", output_to_operand_aliasing={{0}: (8, {}), {1}: (9, {})} | custom-call | flops 19327352832 | bytes 301989888 | tf_op jit(solution)/shard_map/dense/pallas_call | solution.py:554
  324.0 3.0 collective-permute-start.27
  328.7 3.5 collective-permute-start.29
  334.3 2.3 collective-permute-done.29.refs_2_
  336.6 6.4 %collective-permute-done.30.refs_3_ = f32[3,36,2,256]{3,2,1,0:T(2,128)S(1)} collective-permute-done((f32[3,36,2,256]{3,2,1,0:T(2,128)S(1)}, f32[3,36,2,256]{3,2,1,0:T(2,128)S(1)}, u32[]{:S(2)}, u32[]{:S(2)}) %collective-permute-start.30) | collective-permute-done | bytes 221216 | tf_op jit(solution)/shard_map/ppermute | solution.py:53
  343.7 15.6 %stencil.1 = (f32[3,32,32,256]{3,2,1,0:T(8,128)}, f32[8,256]{1,0:T(8,128)}) custom-call(s32[2]{0:T(128)} %pad_add_fusion.origin_ref, f32[3,32,32,256]{3,2,1,0:T(8,128)} %get-tuple-element.80.field_ref, f32[3,2,32,256]{3,2,1,0:T(8,128)} %copy-done.22, f32[3,2,32,256]{3,2,1,0:T(8,128)} %copy-done.21, f32[3,36,2,256]{3,2,1,0:T(2,128)} %copy-done.23, ...), custom_call_target="tpu_custom_call" | custom-call | tf_op jit(solution)/shard_map/stencil/pallas_call | solution.py:678
  359.3 49.5 %grad_modes.1 = (bf16[64,32,32,256]{3,2,1,0:T(8,128)(2,1)}, bf16[4,4,16,32,256]{4,3,2,1,0:T(8,128)(2,1)}, bf16[4,4,16,32,256]{4,3,2,1,0:T(8,128)(2,1)}, f32[16,16,256]{2,1,0:T(8,128)}) custom-call(f32[64,3]{1,0:T(8,128)} %convert_element_type.196.weight_ref, bf16[64,32,32,256]{3,2,1,0:T(8,128)(2,1)} %get-tuple-element.78.hidden_ref, ...), custom_call_target="tpu_custom_call" | custom-call | flops 8589934592 | bytes 167772160 | tf_op jit(solution)/shard_map/grad_modes/pallas_call | solution.py:755
  412.3 5.0 collective-permute-done.31.other_ref
  417.3 5.9 %core_sums.3 = (bf16[4,10,32,256]{3,2,1,0:T(8,128)(2,1)}, bf16[4,10,32,256]{3,2,1,0:T(8,128)(2,1)}, bf16[4,10,32,256]{3,2,1,0:T(8,128)(2,1)}, bf16[4,10,32,256]{...) custom-call(bf16[4,4,16,32,256]{4,3,2,1,0:T(8,128)(2,1)} %get-tuple-, ...), custom_call_target="tpu_custom_call" | custom-call | flops 2097152 | bytes 12582912 | tf_op jit(solution)/shard_map/core_sums/pallas_call | solution.py:282
  424.1 2.6 collective-permute-start.34
  426.8 22.1 %point_grad.2.refs_4_.refs_0_ = f32[64,64]{1,0:T(8,128)} custom-call(bf16[64,32,32,256]{3,2,1,0:T(8,128)(2,1)} %field_ref.9, bf16[64,32,32,256]{3,2,1,0:T(8,128)(2,1)} %get-tuple-element.82.grad_ref, bf16[4,10,32,256]{3,2,1,0:T(8,128)(2,1)} %get-tuple-element.85.refs_0_), custom_call_target="tpu_custom_call" | custom-call | flops 17179869184 | bytes 50331648 | tf_op jit(solution)/shard_map/point_grad/pallas_call | solution.py:839
  448.9 6.2 %collective-permute-done.33 = bf16[4,10,32,256]{3,2,1,0:T(8,128)(2,1)S(1)} collective-permute-done((bf16[4,10,32,256]{3,2,1,0:T(8,128)(2,1)}, bf16[4,10,32,256]{3,2,1,0:T(8,128)(2,1)S(1)}, u32[]{:S(2)}, u32[]{:S(2)}) %collective-permute-start.33) | collective-permute-done | bytes 655392 | tf_op jit(solution)/shard_map/ppermute | solution.py:229
  456.2 2.9 sum_blocks.14
  459.0 3.4 collective-permute-start.39
  462.8 1.7 collective-permute-start.35
  464.7 1.6 collective-permute-start.37
  467.3 2.2 collective-permute-done.39
  469.6 3.0 collective-permute-start.40
  472.6 9.9 %point_grad.3.refs_4_.refs_1_ = f32[64,64]{1,0:T(8,128)} custom-call(bf16[64,32,32,256]{3,2,1,0:T(8,128)(2,1)} %field_ref.9, bf16[64,32,32,256]{3,2,1,0:T(8,128)(2,1)} %get-tuple-element.82.grad_ref, bf16[10,32,256]{2,1,0:T(8,128)(2,1)} %bitcast.123), custom_call_target="tpu_custom_call" | custom-call | flops 17179869184 | bytes 50331648 | tf_op jit(solution)/shard_map/point_grad/pallas_call | solution.py:839
  483.3 1.9 sum_blocks.15
  486.2 2.3 sum_blocks.16
  489.8 3.0 collective-permute-start.43
  495.5 3.3 collective-permute-done.42
  499.4 1.9 sum_blocks.17
  504.0 2.2 collective-permute-start.44
  507.8 1.6 maximum_bitcast_fusion.1
  515.0 1.6 collective-permute-start.48
  518.0 8.8 %weight_grad.2.refs_4_.refs_0_ = f32[8,4,32,64,128]{4,3,2,1,0:T(8,128)} custom-call(bf16[8,4,64,64]{3,2,1,0:T(8,128)(2,1)} %bitcast.100, bf16[8,4,32,128]{3,2,1,0:T(8,128)(2,1)} %pad_maximum_fusion.2.refs_4_.grads_ref, f32[72,128]{1,0:T(8,128)} %sum_blocks.18.refs_0_), custom_call_target="tpu_custom_call" | custom-call | flops 16777216 | bytes 16777216 | tf_op jit(solution)/shard_map/weight_grad/pallas_call | solution.py:886
  528.9 8.8 %weight_grad.3.refs_0_ = f32[8,4,32,64,128]{4,3,2,1,0:T(8,128)} custom-call(bf16[8,4,64,64]{3,2,1,0:T(8,128)(2,1)} %bitcast.101, bf16[8,4,32,128]{3,2,1,0:T(8,128)(2,1)} %pad_maximum_fusion.2.refs_4_.grads_ref, f32[8,4,32,64,128]{4,3,2,1,0:T(8,128)} %weight_grad.2.refs_4_.refs_0_, f32[72,128]{1,0:T(8,128)} %sum_blocks.19.refs_1_.left_ref), custom_call_target="tpu_custom_call", output_to_operand_aliasing={{}: (2, {})} | custom-call | flops 16777216 | bytes 16777216 | tf_op jit(solution)/shard_map/weight_grad/pallas_call | solution.py:886
  (262 shorter events, 75.2 us)
Async XLA Ops:
  7.4 29.5 %copy-start.50 = (bf16[64,64]{1,0:T(8,128)(2,1)S(1)}, bf16[64,64]{1,0:T(8,128)(2,1)}, u32[]{:S(2)}) copy-start(bf16[64,64]{1,0:T(8,128)(2,1)} %param.8) | copy-start | bytes 24580
  36.4 7.6 %collective-permute-start = (bf16[4,4,16,32,256]{4,3,2,1,0:T(8,128)(2,1)}, bf16[4,4,16,32,256]{4,3,2,1,0:T(8,128)(2,1)}, u32[]{:S(2)}, u32[]{:S(2)}) collective-permute-start(bf16[4,4,16,32,256]{4,3,2,1,0:T(8,128)(2,1)} %get-tuple-element.58), channel_id=1, source_target_pairs={{0,4},{4,0},{8,12},{12,8},{16,20},{20,16},{24,28},{28,24},{1,5},{5... | collective-permute-start | bytes 12582920 | tf_op jit(solution)/shard_map/ppermute | solution.py:229
  49.9 29.8 %collective-permute-start.1 = (bf16[4,10,32,256]{3,2,1,0:T(8,128)(2,1)}, bf16[4,10,32,256]{3,2,1,0:T(8,128)(2,1)S(1)}, u32[]{:S(2)}, u32[]{:S(2)}) collective-permute-start(bf16[4,10,32,256]{3,2,1,0:T(8,128)(2,1)} %get-tuple-element.60), channel_id=1, source_target_pairs={{0,1},{1,0},{2,3},{3,2},{4,5},{5,4},{6,7},{7,6},{8,9},{9,8},{10,11... | collective-permute-start | bytes 1966088 | tf_op jit(solution)/shard_map/ppermute | solution.py:229
  52.8 30.7 %collective-permute-start.2 = (bf16[4,10,32,256]{3,2,1,0:T(8,128)(2,1)}, bf16[4,10,32,256]{3,2,1,0:T(8,128)(2,1)S(1)}, u32[]{:S(2)}, u32[]{:S(2)}) collective-permute-start(bf16[4,10,32,256]{3,2,1,0:T(8,128)(2,1)} %get-tuple-element.61), channel_id=1, source_target_pairs={{0,2},{1,3},{2,0},{3,1},{4,6},{5,7},{6,4},{7,5},{8,10},{9,11},{10,... | collective-permute-start | bytes 1966088 | tf_op jit(solution)/shard_map/ppermute | solution.py:229
  54.3 29.2 %collective-permute-start.3 = (bf16[4,10,32,256]{3,2,1,0:T(8,128)(2,1)}, bf16[4,10,32,256]{3,2,1,0:T(8,128)(2,1)S(1)}, u32[]{:S(2)}, u32[]{:S(2)}) collective-permute-start(bf16[4,10,32,256]{3,2,1,0:T(8,128)(2,1)} %get-tuple-element.62), channel_id=1, source_target_pairs={{0,3},{1,2},{2,1},{3,0},{4,7},{5,6},{6,5},{7,4},{8,11},{9,10},{10,... | collective-permute-start | bytes 1966088 | tf_op jit(solution)/shard_map/ppermute | solution.py:229
  87.5 9.7 %collective-permute-start.5 = (bf16[10,32,256]{2,1,0:T(8,128)(2,1)}, bf16[10,32,256]{2,1,0:T(8,128)(2,1)S(1)}, u32[]{:S(2)}, u32[]{:S(2)}) collective-permute-start(bf16[10,32,256]{2,1,0:T(8,128)(2,1)} %bitcast.180), channel_id=1, source_target_pairs={{0,16},{4,20},{8,24},{12,28},{16,0},{20,4},{24,8},{28,12},{1,17},{... | collective-permute-start | bytes 491528 | tf_op jit(solution)/shard_map/ppermute | solution.py:229
  91.4 21.8 %collective-permute-start.7 = (bf16[4,6,32,256]{3,2,1,0:T(8,128)(2,1)S(1)}, bf16[4,6,32,256]{3,2,1,0:T(8,128)(2,1)S(1)}, u32[]{:S(2)}, u32[]{:S(2)}) collective-permute-start(bf16[4,6,32,256]{3,2,1,0:T(8,128)(2,1)S(1)} %copy-done.56), channel_id=1, source_target_pairs={{0,1},{1,0},{2,3},{3,2},{4,5},{5,4},{6,7},{7,6},{8,9},{9,8},{10,11... | collective-permute-start | bytes 1179656 | tf_op jit(solution)/shard_map/ppermute | solution.py:229
  92.4 20.7 %collective-permute-start.8 = (bf16[4,6,32,256]{3,2,1,0:T(8,128)(2,1)S(1)}, bf16[4,6,32,256]{3,2,1,0:T(8,128)(2,1)S(1)}, u32[]{:S(2)}, u32[]{:S(2)}) collective-permute-start(bf16[4,6,32,256]{3,2,1,0:T(8,128)(2,1)S(1)} %copy-done.55), channel_id=1, source_target_pairs={{0,2},{1,3},{2,0},{3,1},{4,6},{5,7},{6,4},{7,5},{8,10},{9,11},{10,... | collective-permute-start | bytes 1179656 | tf_op jit(solution)/shard_map/ppermute | solution.py:229
  93.5 19.7 %collective-permute-start.9 = (bf16[4,6,32,256]{3,2,1,0:T(8,128)(2,1)S(1)}, bf16[4,6,32,256]{3,2,1,0:T(8,128)(2,1)S(1)}, u32[]{:S(2)}, u32[]{:S(2)}) collective-permute-start(bf16[4,6,32,256]{3,2,1,0:T(8,128)(2,1)S(1)} %copy-done.54), channel_id=1, source_target_pairs={{0,3},{1,2},{2,1},{3,0},{4,7},{5,6},{6,5},{7,4},{8,11},{9,10},{10,... | collective-permute-start | bytes 1179656 | tf_op jit(solution)/shard_map/ppermute | solution.py:229
  94.9 15.6 %collective-permute-start.4 = (bf16[10,32,256]{2,1,0:T(8,128)(2,1)}, bf16[10,32,256]{2,1,0:T(8,128)(2,1)S(1)}, u32[]{:S(2)}, u32[]{:S(2)}) collective-permute-start(bf16[10,32,256]{2,1,0:T(8,128)(2,1)} %bitcast.178), channel_id=1, source_target_pairs={{0,8},{4,12},{8,0},{12,4},{16,24},{20,28},{24,16},{28,20},{1,9},{5... | collective-permute-start | bytes 491528 | tf_op jit(solution)/shard_map/ppermute | solution.py:229
  97.2 13.3 %copy-start.28 = (bf16[10,32,256]{2,1,0:T(8,128)(2,1)}, bf16[10,32,256]{2,1,0:T(8,128)(2,1)S(1)}, u32[]{:S(2)}) copy-start(bf16[10,32,256]{2,1,0:T(8,128)(2,1)S(1)} %collective-permute-done.5) | copy-start | bytes 491524
  97.2 13.3 %collective-permute-start.6 = (bf16[10,32,256]{2,1,0:T(8,128)(2,1)}, bf16[10,32,256]{2,1,0:T(8,128)(2,1)S(1)}, u32[]{:S(2)}, u32[]{:S(2)}) collective-permute-start(bf16[10,32,256]{2,1,0:T(8,128)(2,1)} %bitcast.177), channel_id=1, source_target_pairs={{0,24},{4,28},{8,16},{12,20},{16,8},{20,12},{24,0},{28,4},{1,25},{... | collective-permute-start | bytes 491528 | tf_op jit(solution)/shard_map/ppermute | solution.py:229
  113.2 13.9 %copy-start.53 = (f32[3]{0:T(128)S(1)}, f32[3]{0:T(128)}, u32[]{:S(2)}) copy-start(f32[3]{0:T(128)} %param.11) | copy-start | bytes 40
  116.5 7.2 %collective-permute-start.10 = (bf16[6,32,256]{2,1,0:T(8,128)(2,1)}, bf16[6,32,256]{2,1,0:T(8,128)(2,1)S(1)}, u32[]{:S(2)}, u32[]{:S(2)}) collective-permute-start(bf16[6,32,256]{2,1,0:T(8,128)(2,1)} %bitcast.187), channel_id=1, source_target_pairs={{0,8},{4,12},{8,0},{12,4},{16,24},{20,28},{24,16},{28,20},{1,9},{5... | collective-permute-start | bytes 294920 | tf_op jit(solution)/shard_map/ppermute | solution.py:229
  116.5 10.6 %collective-permute-start.11 = (bf16[6,32,256]{2,1,0:T(8,128)(2,1)}, bf16[6,32,256]{2,1,0:T(8,128)(2,1)S(1)}, u32[]{:S(2)}, u32[]{:S(2)}) collective-permute-start(bf16[6,32,256]{2,1,0:T(8,128)(2,1)} %bitcast.185), channel_id=1, source_target_pairs={{0,16},{4,20},{8,24},{12,28},{16,0},{20,4},{24,8},{28,12},{1,17},{... | collective-permute-start | bytes 294920 | tf_op jit(solution)/shard_map/ppermute | solution.py:229
  117.4 9.7 %collective-permute-start.12 = (bf16[6,32,256]{2,1,0:T(8,128)(2,1)}, bf16[6,32,256]{2,1,0:T(8,128)(2,1)S(1)}, u32[]{:S(2)}, u32[]{:S(2)}) collective-permute-start(bf16[6,32,256]{2,1,0:T(8,128)(2,1)} %bitcast.183), channel_id=1, source_target_pairs={{0,24},{4,28},{8,16},{12,20},{16,8},{20,12},{24,0},{28,4},{1,25},{... | collective-permute-start | bytes 294920 | tf_op jit(solution)/shard_map/ppermute | solution.py:229
  135.0 16.2 %copy-start = (bf16[8,4,64,64]{2,3,1,0:T(8,128)(2,1)}, bf16[8,4,64,64]{2,3,1,0:T(8,128)(2,1)S(1)}, u32[]{:S(2)}) copy-start(bf16[8,4,64,64]{2,3,1,0:T(8,128)(2,1)S(1)} %reshape.290) | copy-start | bytes 786436
  153.4 40.6 %copy-start.52 = (bf16[64,3]{0,1:T(4,128)(2,1)S(1)}, bf16[64,3]{0,1:T(4,128)(2,1)}, u32[]{:S(2)}) copy-start(bf16[64,3]{0,1:T(4,128)(2,1)} %param.10) | copy-start | bytes 1156
  153.9 21.0 %collective-permute-start.15 = (bf16[12,32,256]{2,1,0:T(8,128)(2,1)S(1)}, bf16[12,32,256]{2,1,0:T(8,128)(2,1)S(1)}, u32[]{:S(2)}, u32[]{:S(2)}) collective-permute-start(bf16[12,32,256]{2,1,0:T(8,128)(2,1)S(1)} %slice.55), channel_id=1, source_target_pairs={{0,24},{4,28},{8,16},{12,20},{16,8},{20,12},{24,0},{28,4},{1,25},{... | collective-permute-start | bytes 589832 | tf_op jit(solution)/shard_map/ppermute | solution.py:229
  155.8 7.6 %collective-permute-start.21 = (bf16[4,32,256]{2,1,0:T(8,128)(2,1)S(1)}, bf16[4,32,256]{2,1,0:T(8,128)(2,1)S(1)}, u32[]{:S(2)}, u32[]{:S(2)}) collective-permute-start(bf16[4,32,256]{2,1,0:T(8,128)(2,1)S(1)} %slice.57), channel_id=1, source_target_pairs={{0,24},{4,28},{8,16},{12,20},{16,8},{20,12},{24,0},{28,4},{1,25},{... | collective-permute-start | bytes 196616 | tf_op jit(solution)/shard_map/ppermute | solution.py:229
  158.3 10.1 %collective-permute-start.20 = (bf16[4,32,256]{2,1,0:T(8,128)(2,1)S(1)}, bf16[4,32,256]{2,1,0:T(8,128)(2,1)S(1)}, u32[]{:S(2)}, u32[]{:S(2)}) collective-permute-start(bf16[4,32,256]{2,1,0:T(8,128)(2,1)S(1)} %slice.57), channel_id=1, source_target_pairs={{0,16},{4,20},{8,24},{12,28},{16,0},{20,4},{24,8},{28,12},{1,17},{... | collective-permute-start | bytes 196616 | tf_op jit(solution)/shard_map/ppermute | solution.py:229
  158.3 10.1 %collective-permute-start.19 = (bf16[4,32,256]{2,1,0:T(8,128)(2,1)S(1)}, bf16[4,32,256]{2,1,0:T(8,128)(2,1)S(1)}, u32[]{:S(2)}, u32[]{:S(2)}) collective-permute-start(bf16[4,32,256]{2,1,0:T(8,128)(2,1)S(1)} %slice.57), channel_id=1, source_target_pairs={{0,8},{4,12},{8,0},{12,4},{16,24},{20,28},{24,16},{28,20},{1,9},{5... | collective-permute-start | bytes 196616 | tf_op jit(solution)/shard_map/ppermute | solution.py:229
  170.7 16.5 %collective-permute-start.24 = (bf16[4,4,32,256]{3,2,1,0:T(8,128)(2,1)}, bf16[4,4,32,256]{3,2,1,0:T(8,128)(2,1)S(1)}, u32[]{:S(2)}, u32[]{:S(2)}) collective-permute-start(bf16[4,4,32,256]{3,2,1,0:T(8,128)(2,1)} %bitcast.115), channel_id=1, source_target_pairs={{0,3},{1,2},{2,1},{3,0},{4,7},{5,6},{6,5},{7,4},{8,11},{9,10},{10,... | collective-permute-start | bytes 786440 | tf_op jit(solution)/shard_map/ppermute | solution.py:229
  172.0 15.3 %collective-permute-start.23 = (bf16[4,4,32,256]{3,2,1,0:T(8,128)(2,1)}, bf16[4,4,32,256]{3,2,1,0:T(8,128)(2,1)S(1)}, u32[]{:S(2)}, u32[]{:S(2)}) collective-permute-start(bf16[4,4,32,256]{3,2,1,0:T(8,128)(2,1)} %bitcast.116), channel_id=1, source_target_pairs={{0,2},{1,3},{2,0},{3,1},{4,6},{5,7},{6,4},{7,5},{8,10},{9,11},{10,... | collective-permute-start | bytes 786440 | tf_op jit(solution)/shard_map/ppermute | solution.py:229
  174.2 13.1 %collective-permute-start.22 = (bf16[4,4,32,256]{3,2,1,0:T(8,128)(2,1)}, bf16[4,4,32,256]{3,2,1,0:T(8,128)(2,1)S(1)}, u32[]{:S(2)}, u32[]{:S(2)}) collective-permute-start(bf16[4,4,32,256]{3,2,1,0:T(8,128)(2,1)} %bitcast.117), channel_id=1, source_target_pairs={{0,1},{1,0},{2,3},{3,2},{4,5},{5,4},{6,7},{7,6},{8,9},{9,8},{10,11... | collective-permute-start | bytes 786440 | tf_op jit(solution)/shard_map/ppermute | solution.py:229
  174.2 10.1 %collective-permute-start.14 = (bf16[12,32,256]{2,1,0:T(8,128)(2,1)S(1)}, bf16[12,32,256]{2,1,0:T(8,128)(2,1)S(1)}, u32[]{:S(2)}, u32[]{:S(2)}) collective-permute-start(bf16[12,32,256]{2,1,0:T(8,128)(2,1)S(1)} %slice.55), channel_id=1, source_target_pairs={{0,16},{4,20},{8,24},{12,28},{16,0},{20,4},{24,8},{28,12},{1,17},{... | collective-permute-start | bytes 589832 | tf_op jit(solution)/shard_map/ppermute | solution.py:229
  174.9 9.5 %copy-start.25 = (bf16[12,32,256]{2,1,0:T(8,128)(2,1)}, bf16[12,32,256]{2,1,0:T(8,128)(2,1)S(1)}, u32[]{:S(2)}) copy-start(bf16[12,32,256]{2,1,0:T(8,128)(2,1)S(1)} %collective-permute-done.15) | copy-start | bytes 589828
  174.9 9.5 %collective-permute-start.13 = (bf16[12,32,256]{2,1,0:T(8,128)(2,1)S(1)}, bf16[12,32,256]{2,1,0:T(8,128)(2,1)S(1)}, u32[]{:S(2)}, u32[]{:S(2)}) collective-permute-start(bf16[12,32,256]{2,1,0:T(8,128)(2,1)S(1)} %slice.55), channel_id=1, source_target_pairs={{0,8},{4,12},{8,0},{12,4},{16,24},{20,28},{24,16},{28,20},{1,9},{5... | collective-permute-start | bytes 589832 | tf_op jit(solution)/shard_map/ppermute | solution.py:229
  190.4 4.2 collective-permute-start.25
  190.4 36.1 %collective-permute-start.18 = (bf16[4,12,32,256]{3,2,1,0:T(8,128)(2,1)}, bf16[4,12,32,256]{3,2,1,0:T(8,128)(2,1)S(1)}, u32[]{:S(2)}, u32[]{:S(2)}) collective-permute-start(bf16[4,12,32,256]{3,2,1,0:T(8,128)(2,1)} %bitcast.103), channel_id=1, source_target_pairs={{0,3},{1,2},{2,1},{3,0},{4,7},{5,6},{6,5},{7,4},{8,11},{9,10},{10,... | collective-permute-start | bytes 2359304 | tf_op jit(solution)/shard_map/ppermute | solution.py:229
  191.9 36.5 %collective-permute-start.17 = (bf16[4,12,32,256]{3,2,1,0:T(8,128)(2,1)}, bf16[4,12,32,256]{3,2,1,0:T(8,128)(2,1)S(1)}, u32[]{:S(2)}, u32[]{:S(2)}) collective-permute-start(bf16[4,12,32,256]{3,2,1,0:T(8,128)(2,1)} %bitcast.104), channel_id=1, source_target_pairs={{0,2},{1,3},{2,0},{3,1},{4,6},{5,7},{6,4},{7,5},{8,10},{9,11},{10,... | collective-permute-start | bytes 2359304 | tf_op jit(solution)/shard_map/ppermute | solution.py:229
  193.6 34.7 %collective-permute-start.16 = (bf16[4,12,32,256]{3,2,1,0:T(8,128)(2,1)}, bf16[4,12,32,256]{3,2,1,0:T(8,128)(2,1)S(1)}, u32[]{:S(2)}, u32[]{:S(2)}) collective-permute-start(bf16[4,12,32,256]{3,2,1,0:T(8,128)(2,1)} %bitcast.105), channel_id=1, source_target_pairs={{0,1},{1,0},{2,3},{3,2},{4,5},{5,4},{6,7},{7,6},{8,9},{9,8},{10,11... | collective-permute-start | bytes 2359304 | tf_op jit(solution)/shard_map/ppermute | solution.py:229
  233.2 5.9 %collective-permute-start.26 = (bf16[4,4,12,32,256]{4,3,2,1,0:T(8,128)(2,1)}, bf16[4,4,12,32,256]{4,3,2,1,0:T(8,128)(2,1)S(1)}, u32[]{:S(2)}, u32[]{:S(2)}) collective-permute-start(bf16[4,4,12,32,256]{4,3,2,1,0:T(8,128)(2,1)} %bitcast.98), channel_id=1, source_target_pairs={{0,4},{4,0},{8,12},{12,8},{16,20},{20,16},{24,28},{28,24},{1,5},{5... | collective-permute-start | bytes 9437192 | tf_op jit(solution)/shard_map/ppermute | solution.py:229
  322.7 5.9 %collective-permute-start.28 = (f32[3,2,32,256]{3,2,1,0:T(8,128)S(1)}, f32[3,2,32,256]{3,2,1,0:T(8,128)S(1)}, u32[]{:S(2)}, u32[]{:S(2)}) collective-permute-start(f32[3,2,32,256]{3,2,1,0:T(8,128)S(1)} %get-tuple-element.110), channel_id=1, source_target_pairs={{4,0},{8,4},{12,8},{16,12},{20,16},{24,20},{28,24},{5,1},{9,5},{13... | collective-permute-start | bytes 589832 | tf_op jit(solution)/shard_map/ppermute | solution.py:53
  324.0 4.6 collective-permute-start.27
  328.6 14.4 %copy-start.21 = (f32[3,2,32,256]{3,2,1,0:T(8,128)}, f32[3,2,32,256]{3,2,1,0:T(8,128)S(1)}, u32[]{:S(2)}) copy-start(f32[3,2,32,256]{3,2,1,0:T(8,128)S(1)} %collective-permute-done.28.refs_1_) | copy-start | bytes 589828
  328.6 14.4 %copy-start.22 = (f32[3,2,32,256]{3,2,1,0:T(8,128)}, f32[3,2,32,256]{3,2,1,0:T(8,128)S(1)}, u32[]{:S(2)}) copy-start(f32[3,2,32,256]{3,2,1,0:T(8,128)S(1)} %collective-permute-done.27.refs_0_) | copy-start | bytes 589828
  328.7 7.9 %collective-permute-start.29 = (f32[3,36,2,256]{3,2,1,0:T(2,128)S(1)}, f32[3,36,2,256]{3,2,1,0:T(2,128)S(1)}, u32[]{:S(2)}, u32[]{:S(2)}) collective-permute-start(f32[3,36,2,256]{3,2,1,0:T(2,128)S(1)} %pad_maximum_fusion.3), channel_id=1, source_target_pairs={{0,1},{1,2},{2,3},{4,5},{5,6},{6,7},{8,9},{9,10},{10,11},{12,13},{... | collective-permute-start | bytes 663560 | tf_op jit(solution)/shard_map/ppermute | solution.py:53
  332.4 10.6 %collective-permute-start.30 = (f32[3,36,2,256]{3,2,1,0:T(2,128)S(1)}, f32[3,36,2,256]{3,2,1,0:T(2,128)S(1)}, u32[]{:S(2)}, u32[]{:S(2)}) collective-permute-start(f32[3,36,2,256]{3,2,1,0:T(2,128)S(1)} %pad_maximum_fusion.4), channel_id=1, source_target_pairs={{1,0},{2,1},{3,2},{5,4},{6,5},{7,6},{9,8},{10,9},{11,10},{13,12},{... | collective-permute-start | bytes 663560 | tf_op jit(solution)/shard_map/ppermute | solution.py:53
  408.9 8.5 %collective-permute-start.31 = (bf16[4,4,16,32,256]{4,3,2,1,0:T(8,128)(2,1)}, bf16[4,4,16,32,256]{4,3,2,1,0:T(8,128)(2,1)}, u32[]{:S(2)}, u32[]{:S(2)}) collective-permute-start(bf16[4,4,16,32,256]{4,3,2,1,0:T(8,128)(2,1)} %get-tuple-element.84), channel_id=1, source_target_pairs={{0,4},{4,0},{8,12},{12,8},{16,20},{20,16},{24,28},{28,24},{1,5},{5... | collective-permute-start | bytes 12582920 | tf_op jit(solution)/shard_map/ppermute | solution.py:229
  423.2 25.7 %collective-permute-start.32 = (bf16[4,10,32,256]{3,2,1,0:T(8,128)(2,1)}, bf16[4,10,32,256]{3,2,1,0:T(8,128)(2,1)S(1)}, u32[]{:S(2)}, u32[]{:S(2)}) collective-permute-start(bf16[4,10,32,256]{3,2,1,0:T(8,128)(2,1)} %get-tuple-element.86), channel_id=1, source_target_pairs={{0,1},{1,0},{2,3},{3,2},{4,5},{5,4},{6,7},{7,6},{8,9},{9,8},{10,11... | collective-permute-start | bytes 1966088 | tf_op jit(solution)/shard_map/ppermute | solution.py:229
  424.1 31.0 %collective-permute-start.33 = (bf16[4,10,32,256]{3,2,1,0:T(8,128)(2,1)}, bf16[4,10,32,256]{3,2,1,0:T(8,128)(2,1)S(1)}, u32[]{:S(2)}, u32[]{:S(2)}) collective-permute-start(bf16[4,10,32,256]{3,2,1,0:T(8,128)(2,1)} %get-tuple-element.87), channel_id=1, source_target_pairs={{0,2},{1,3},{2,0},{3,1},{4,6},{5,7},{6,4},{7,5},{8,10},{9,11},{10,... | collective-permute-start | bytes 1966088 | tf_op jit(solution)/shard_map/ppermute | solution.py:229
  424.1 31.0 %collective-permute-start.34 = (bf16[4,10,32,256]{3,2,1,0:T(8,128)(2,1)}, bf16[4,10,32,256]{3,2,1,0:T(8,128)(2,1)S(1)}, u32[]{:S(2)}, u32[]{:S(2)}) collective-permute-start(bf16[4,10,32,256]{3,2,1,0:T(8,128)(2,1)} %get-tuple-element.88), channel_id=1, source_target_pairs={{0,3},{1,2},{2,1},{3,0},{4,7},{5,6},{6,5},{7,4},{8,11},{9,10},{10,... | collective-permute-start | bytes 1966088 | tf_op jit(solution)/shard_map/ppermute | solution.py:229
  426.8 35.6 %copy-start.51 = (f32[8,256]{1,0:T(8,128)S(1)}, f32[8,256]{1,0:T(8,128)}, u32[]{:S(2)}) copy-start(f32[8,256]{1,0:T(8,128)} %get-tuple-element.91) | copy-start | bytes 24580
  426.8 36.0 %copy-start.59 = (bf16[4,6,32,256]{3,2,1,0:T(8,128)(2,1)S(1)}, bf16[4,6,32,256]{3,2,1,0:T(8,128)(2,1)}, u32[]{:S(2)}) copy-start(bf16[4,6,32,256]{3,2,1,0:T(8,128)(2,1)} %get-tuple-element.93) | copy-start | bytes 1179652
  426.8 37.7 %copy-start.58 = (bf16[4,6,32,256]{3,2,1,0:T(8,128)(2,1)S(1)}, bf16[4,6,32,256]{3,2,1,0:T(8,128)(2,1)}, u32[]{:S(2)}) copy-start(bf16[4,6,32,256]{3,2,1,0:T(8,128)(2,1)} %get-tuple-element.94) | copy-start | bytes 1179652
  426.8 38.0 %copy-start.57 = (bf16[4,6,32,256]{3,2,1,0:T(8,128)(2,1)S(1)}, bf16[4,6,32,256]{3,2,1,0:T(8,128)(2,1)}, u32[]{:S(2)}) copy-start(bf16[4,6,32,256]{3,2,1,0:T(8,128)(2,1)} %get-tuple-element.95) | copy-start | bytes 1179652
  459.0 10.5 %collective-permute-start.39 = (bf16[10,32,256]{2,1,0:T(8,128)(2,1)}, bf16[10,32,256]{2,1,0:T(8,128)(2,1)S(1)}, u32[]{:S(2)}, u32[]{:S(2)}) collective-permute-start(bf16[10,32,256]{2,1,0:T(8,128)(2,1)} %bitcast.182), channel_id=1, source_target_pairs={{0,16},{4,20},{8,24},{12,28},{16,0},{20,4},{24,8},{28,12},{1,17},{... | collective-permute-start | bytes 491528 | tf_op jit(solution)/shard_map/ppermute | solution.py:229
  462.8 22.4 %collective-permute-start.35 = (bf16[4,6,32,256]{3,2,1,0:T(8,128)(2,1)S(1)}, bf16[4,6,32,256]{3,2,1,0:T(8,128)(2,1)S(1)}, u32[]{:S(2)}, u32[]{:S(2)}) collective-permute-start(bf16[4,6,32,256]{3,2,1,0:T(8,128)(2,1)S(1)} %copy-done.59), channel_id=1, source_target_pairs={{0,1},{1,0},{2,3},{3,2},{4,5},{5,4},{6,7},{7,6},{8,9},{9,8},{10,11... | collective-permute-start | bytes 1179656 | tf_op jit(solution)/shard_map/ppermute | solution.py:229
  464.5 20.7 %collective-permute-start.36 = (bf16[4,6,32,256]{3,2,1,0:T(8,128)(2,1)S(1)}, bf16[4,6,32,256]{3,2,1,0:T(8,128)(2,1)S(1)}, u32[]{:S(2)}, u32[]{:S(2)}) collective-permute-start(bf16[4,6,32,256]{3,2,1,0:T(8,128)(2,1)S(1)} %copy-done.58), channel_id=1, source_target_pairs={{0,2},{1,3},{2,0},{3,1},{4,6},{5,7},{6,4},{7,5},{8,10},{9,11},{10,... | collective-permute-start | bytes 1179656 | tf_op jit(solution)/shard_map/ppermute | solution.py:229
  464.7 20.5 %collective-permute-start.37 = (bf16[4,6,32,256]{3,2,1,0:T(8,128)(2,1)S(1)}, bf16[4,6,32,256]{3,2,1,0:T(8,128)(2,1)S(1)}, u32[]{:S(2)}, u32[]{:S(2)}) collective-permute-start(bf16[4,6,32,256]{3,2,1,0:T(8,128)(2,1)S(1)} %copy-done.57), channel_id=1, source_target_pairs={{0,3},{1,2},{2,1},{3,0},{4,7},{5,6},{6,5},{7,4},{8,11},{9,10},{10,... | collective-permute-start | bytes 1179656 | tf_op jit(solution)/shard_map/ppermute | solution.py:229
  466.3 16.2 %collective-permute-start.38 = (bf16[10,32,256]{2,1,0:T(8,128)(2,1)}, bf16[10,32,256]{2,1,0:T(8,128)(2,1)S(1)}, u32[]{:S(2)}, u32[]{:S(2)}) collective-permute-start(bf16[10,32,256]{2,1,0:T(8,128)(2,1)} %bitcast.181), channel_id=1, source_target_pairs={{0,8},{4,12},{8,0},{12,4},{16,24},{20,28},{24,16},{28,20},{1,9},{5... | collective-permute-start | bytes 491528 | tf_op jit(solution)/shard_map/ppermute | solution.py:229
  469.6 13.0 %copy-start.31 = (bf16[10,32,256]{2,1,0:T(8,128)(2,1)}, bf16[10,32,256]{2,1,0:T(8,128)(2,1)S(1)}, u32[]{:S(2)}) copy-start(bf16[10,32,256]{2,1,0:T(8,128)(2,1)S(1)} %collective-permute-done.39) | copy-start | bytes 491524
  469.6 13.0 %collective-permute-start.40 = (bf16[10,32,256]{2,1,0:T(8,128)(2,1)}, bf16[10,32,256]{2,1,0:T(8,128)(2,1)S(1)}, u32[]{:S(2)}, u32[]{:S(2)}) collective-permute-start(bf16[10,32,256]{2,1,0:T(8,128)(2,1)} %bitcast.179), channel_id=1, source_target_pairs={{0,24},{4,28},{8,16},{12,20},{16,8},{20,12},{24,0},{28,4},{1,25},{... | collective-permute-start | bytes 491528 | tf_op jit(solution)/shard_map/ppermute | solution.py:229
  488.5 7.0 %collective-permute-start.41 = (bf16[6,32,256]{2,1,0:T(8,128)(2,1)}, bf16[6,32,256]{2,1,0:T(8,128)(2,1)S(1)}, u32[]{:S(2)}, u32[]{:S(2)}) collective-permute-start(bf16[6,32,256]{2,1,0:T(8,128)(2,1)} %bitcast.188), channel_id=1, source_target_pairs={{0,8},{4,12},{8,0},{12,4},{16,24},{20,28},{24,16},{28,20},{1,9},{5... | collective-permute-start | bytes 294920 | tf_op jit(solution)/shard_map/ppermute | solution.py:229
  488.5 10.2 %collective-permute-start.42 = (bf16[6,32,256]{2,1,0:T(8,128)(2,1)}, bf16[6,32,256]{2,1,0:T(8,128)(2,1)S(1)}, u32[]{:S(2)}, u32[]{:S(2)}) collective-permute-start(bf16[6,32,256]{2,1,0:T(8,128)(2,1)} %bitcast.186), channel_id=1, source_target_pairs={{0,16},{4,20},{8,24},{12,28},{16,0},{20,4},{24,8},{28,12},{1,17},{... | collective-permute-start | bytes 294920 | tf_op jit(solution)/shard_map/ppermute | solution.py:229
  489.8 8.9 %collective-permute-start.43 = (bf16[6,32,256]{2,1,0:T(8,128)(2,1)}, bf16[6,32,256]{2,1,0:T(8,128)(2,1)S(1)}, u32[]{:S(2)}, u32[]{:S(2)}) collective-permute-start(bf16[6,32,256]{2,1,0:T(8,128)(2,1)} %bitcast.184), channel_id=1, source_target_pairs={{0,24},{4,28},{8,16},{12,20},{16,8},{20,12},{24,0},{28,4},{1,25},{... | collective-permute-start | bytes 294920 | tf_op jit(solution)/shard_map/ppermute | solution.py:229
  502.7 8.7 %collective-permute-start.46 = (f32[72,128]{1,0:T(8,128)}, f32[72,128]{1,0:T(8,128)S(1)}, u32[]{:S(2)}, u32[]{:S(2)}) collective-permute-start(f32[72,128]{1,0:T(8,128)} %pack_sums.1), channel_id=1, source_target_pairs={{0,3},{1,2},{2,1},{3,0},{4,7},{5,6},{6,5},{7,4},{8,11},{9,10},{10,... | collective-permute-start | bytes 110600 | tf_op jit(solution)/shard_map/ppermute | solution.py:229
  504.0 7.5 %collective-permute-start.45 = (f32[72,128]{1,0:T(8,128)}, f32[72,128]{1,0:T(8,128)S(1)}, u32[]{:S(2)}, u32[]{:S(2)}) collective-permute-start(f32[72,128]{1,0:T(8,128)} %pack_sums.1), channel_id=1, source_target_pairs={{0,2},{1,3},{2,0},{3,1},{4,6},{5,7},{6,4},{7,5},{8,10},{9,11},{10,... | collective-permute-start | bytes 110600 | tf_op jit(solution)/shard_map/ppermute | solution.py:229
  504.0 7.5 %collective-permute-start.44 = (f32[72,128]{1,0:T(8,128)}, f32[72,128]{1,0:T(8,128)S(1)}, u32[]{:S(2)}, u32[]{:S(2)}) collective-permute-start(f32[72,128]{1,0:T(8,128)} %pack_sums.1), channel_id=1, source_target_pairs={{0,1},{1,0},{2,3},{3,2},{4,5},{5,4},{6,7},{7,6},{8,9},{9,8},{10,11... | collective-permute-start | bytes 110600 | tf_op jit(solution)/shard_map/ppermute | solution.py:229
  513.6 13.2 %collective-permute-start.49 = (f32[72,128]{1,0:T(8,128)}, f32[72,128]{1,0:T(8,128)S(1)}, u32[]{:S(2)}, u32[]{:S(2)}) collective-permute-start(f32[72,128]{1,0:T(8,128)} %sum_blocks.18.refs_0_), channel_id=1, source_target_pairs={{0,24},{4,28},{8,16},{12,20},{16,8},{20,12},{24,0},{28,4},{1,25},{... | collective-permute-start | bytes 110600 | tf_op jit(solution)/shard_map/ppermute | solution.py:229
  515.0 11.8 %collective-permute-start.48 = (f32[72,128]{1,0:T(8,128)}, f32[72,128]{1,0:T(8,128)S(1)}, u32[]{:S(2)}, u32[]{:S(2)}) collective-permute-start(f32[72,128]{1,0:T(8,128)} %sum_blocks.18.refs_0_), channel_id=1, source_target_pairs={{0,16},{4,20},{8,24},{12,28},{16,0},{20,4},{24,8},{28,12},{1,17},{... | collective-permute-start | bytes 110600 | tf_op jit(solution)/shard_map/ppermute | solution.py:229
  516.6 10.2 %collective-permute-start.47 = (f32[72,128]{1,0:T(8,128)}, f32[72,128]{1,0:T(8,128)S(1)}, u32[]{:S(2)}, u32[]{:S(2)}) collective-permute-start(f32[72,128]{1,0:T(8,128)} %sum_blocks.18.refs_0_), channel_id=1, source_target_pairs={{0,8},{4,12},{8,0},{12,4},{16,24},{20,28},{24,16},{28,20},{1,9},{5... | collective-permute-start | bytes 110600 | tf_op jit(solution)/shard_map/ppermute | solution.py:229
  528.9 8.8 %collective-permute-start.50 = (f32[72,128]{1,0:T(8,128)}, f32[72,128]{1,0:T(8,128)S(1)}, u32[]{:S(2)}, u32[]{:S(2)}) collective-permute-start(f32[72,128]{1,0:T(8,128)} %sum_blocks.19.refs_1_.left_ref), channel_id=1, source_target_pairs={{0,4},{4,0},{8,12},{12,8},{16,20},{20,16},{24,28},{28,24},{1,5},{5... | collective-permute-start | bytes 110600 | tf_op jit(solution)/shard_map/ppermute | solution.py:229
  (47 other events, 87.7 us)
